TPU v7x, 128 devices: a whole 4x4x4 slice. The times are simulated.
128 devices in a mesh: grp: 32 (over y, x, core), sub: 4 (over z).
Axes of the slice: x: 4, y: 4, z: 4, core: 2. Of those that a mesh axis runs over, the one named last changes fastest.
Arguments:
- rhs: float32 [8, 8, 8, 32768], P(None, None, None, ('grp', 'sub')), may hold values from -6 to 6
- spacing_z: float32 [32], P('grp'), may hold values from 0.5 to 2
- spacing_a: float32 [64], replicated, may hold values from 0.5 to 2
- spacing_b: float32 [16], replicated, may hold values from 0.5 to 2
- rotation: int32 [32], replicated, may hold values from 0 to 3, as said below
Outputs:
- solution: float32 [8, 8, 8, 32768], P(None, None, None, ('grp', 'sub'))
- residual: float32 [8, 8, 8, 32768], P(None, None, None, ('grp', 'sub'))
Inputs may be any that keep to these rules, and one draw needn't show every extreme that they name: Device (g, s) holds columns (rotation[g] + s * 16 + j) mod 64; some group has 3 and some 0.
All inputs are finite; a program needn't handle non-finite values.
Results may differ from a plain program's by a relative error of at most 0.0003.
Values sent between devices are 32-bit elements; how exact they have to be, the bound alone decides.
No kernel may reach another device: no remote copies, remote signals or barrier semaphores. Data moves between devices by JAX's collectives and lax.ppermute only.
A program may use at most 128 MiB of HBM per device.

v0:
```python
import jax
import jax.numpy as jnp
import numpy as np
from jax import lax
from jax.sharding import PartitionSpec as P

PTS = 8
CPTS = 4
LAYERS_DEV = 1
COLS_DEV = 16
RADIAL = 16
SMOOTH = 2
DRIFT = 4


highest = lax.Precision.HIGHEST
cheb_upper = 2.0
cheb_ratio = 0.1


def from_behind(value, axis, steps):
    count = lax.axis_size(axis)
    pairs = [(source, (source + steps) % count) for source in range(count)]
    return lax.ppermute(value, axis, pairs)


def padded(block, sides, width):
    for axis, dim in sides:
        count = lax.axis_size(axis)
        forward = [(i, i + 1) for i in range(count - 1)]
        forward.append((count - 1, 0))
        backward = [(target, source) for source, target in forward]
        low = lax.ppermute(
            lax.slice_in_dim(block, block.shape[dim] - width, None, axis=dim), axis, forward
        )
        high = lax.ppermute(lax.slice_in_dim(block, 0, width, axis=dim), axis, backward)
        block = jnp.concatenate([low, block, high], axis=dim)
    return block


def legendre_rows(gll_nodes, poly_order):
    values = np.zeros((gll_nodes.size, poly_order + 1))
    values[:, 0] = 1.0
    values[:, 1] = gll_nodes
    for degree in range(2, poly_order + 1):
        values[:, degree] = (
            (2 * degree - 1) * gll_nodes * values[:, degree - 1]
            - (degree - 1) * values[:, degree - 2]
        ) / degree
    return values


def jacobi_eigen(matrix):
    order = matrix.shape[0]
    current = matrix.copy()
    vectors = np.eye(order)
    for sweep in range(12):
        for first in range(order - 1):
            for second in range(first + 1, order):
                off_value = current[first, second]
                spread = current[second, second] - current[first, first]
                sense = np.where(spread >= 0.0, 1.0, -1.0)
                denom = spread + sense * np.sqrt(spread * spread + 4.0 * off_value * off_value)
                denom = np.where(denom == 0.0, 1.0, denom)
                tangent = 2.0 * off_value / denom
                cosine = 1.0 / np.sqrt(1.0 + tangent * tangent)
                sine = tangent * cosine
                rotate = np.eye(order)
                rotate[first, first] = cosine
                rotate[second, second] = cosine
                rotate[first, second] = sine
                rotate[second, first] = -sine
                current = rotate.T @ current @ rotate
                vectors = vectors @ rotate
    diag_ids = np.arange(order)
    return (current[diag_ids, diag_ids].copy(), vectors)


def lobatto(poly_order):
    gll_nodes = np.cos(np.pi * np.arange(poly_order + 1) / poly_order)
    for newton in range(100):
        values = legendre_rows(gll_nodes, poly_order)
        gll_nodes = gll_nodes - (gll_nodes * values[:, poly_order] - values[:, poly_order - 1]) / (
            (poly_order + 1) * values[:, poly_order]
        )
    values = legendre_rows(gll_nodes, poly_order)
    gll_nodes = gll_nodes[::-1].copy()
    top_poly = values[::-1, poly_order].copy()
    weights = 2.0 / (poly_order * (poly_order + 1) * top_poly**2)
    derivative = np.zeros((poly_order + 1, poly_order + 1))
    for row_index in range(poly_order + 1):
        for col_index in range(poly_order + 1):
            if row_index != col_index:
                derivative[row_index, col_index] = top_poly[row_index] / (
                    top_poly[col_index] * (gll_nodes[row_index] - gll_nodes[col_index])
                )
    derivative[0, 0] = -poly_order * (poly_order + 1) / 4.0
    derivative[poly_order, poly_order] = poly_order * (poly_order + 1) / 4.0
    stiffness = derivative.T @ (weights[:, None] * derivative)
    return (gll_nodes, weights, stiffness)


def basis_tables(fine_count, coarse_count):
    fine_nodes, fine_weights, fine_stiff = lobatto(fine_count - 1)
    coarse_nodes, coarse_weights, coarse_stiff = lobatto(coarse_count - 1)
    interp = np.ones((fine_count, coarse_count))
    for target_col in range(coarse_count):
        for other_col in range(coarse_count):
            if other_col != target_col:
                interp[:, target_col] *= (fine_nodes - coarse_nodes[other_col]) / (
                    coarse_nodes[target_col] - coarse_nodes[other_col]
                )
    poly_order = fine_count - 1
    node_count = 3 * poly_order + 1
    joined_stiff = np.zeros((node_count, node_count))
    joined_mass = np.zeros(node_count)
    for piece_index in range(3):
        first_node = piece_index * poly_order
        joined_stiff[
            first_node : first_node + fine_count, first_node : first_node + fine_count
        ] += fine_stiff
        joined_mass[first_node : first_node + fine_count] += fine_weights
    kept_stiff = joined_stiff[
        poly_order - 1 : 2 * poly_order + 2, poly_order - 1 : 2 * poly_order + 2
    ]
    root_mass = np.sqrt(joined_mass[poly_order - 1 : 2 * poly_order + 2])
    eigen_values, eigen_vectors = jacobi_eigen(kept_stiff / root_mass[:, None] / root_mass[None, :])
    eigen_basis = eigen_vectors / root_mass[:, None]
    coarse_ids = np.arange(coarse_count)
    coarse_diag = coarse_stiff[coarse_ids, coarse_ids].copy()
    coarse_z = (
        coarse_diag[:, None, None] * coarse_weights[None, :, None] * coarse_weights[None, None, :]
    )
    coarse_a = (
        coarse_weights[:, None, None] * coarse_diag[None, :, None] * coarse_weights[None, None, :]
    )
    coarse_b = (
        coarse_weights[:, None, None] * coarse_weights[None, :, None] * coarse_diag[None, None, :]
    )
    tables = (
        fine_stiff,
        fine_weights,
        eigen_basis,
        eigen_values,
        interp,
        coarse_z,
        coarse_a,
        coarse_b,
    )
    return tuple((jnp.asarray(table, dtype=jnp.float32) for table in tables))


def contract(matrix, field, dimension):
    product = jnp.tensordot(matrix, field, axes=(1, dimension), precision=highest)
    return jnp.moveaxis(product, 0, dimension)


def per_device(rhs, spacing_z, spacing_a, spacing_b, rotation):
    stiffness, weights, eigen_basis, eigen_values, interp, coarse_z, coarse_a, coarse_b = (
        basis_tables(PTS, CPTS)
    )
    width = COLS_DEV * RADIAL
    field_shape = (1, PTS, PTS, PTS, LAYERS_DEV, width)
    group = lax.axis_index("grp")
    groups = lax.axis_size("grp")
    member = lax.axis_index("sub")
    rot_here = rotation[group]
    rot_down = rotation[(group + groups - 1) % groups]
    rot_up = rotation[(group + 1) % groups]
    doubled = jnp.concatenate([spacing_a, spacing_a])
    start_column = rot_here + member * COLS_DEV
    length_a = jnp.repeat(lax.dynamic_slice_in_dim(doubled, start_column, COLS_DEV), RADIAL)[
        None, :
    ]
    length_b = jnp.tile(spacing_b, COLS_DEV)[None, :]
    length_z = spacing_z[:, None]
    coef_z = length_a * length_b / (2.0 * length_z)
    coef_a = length_z * length_b / (2.0 * length_a)
    coef_b = length_z * length_a / (2.0 * length_b)
    pair = weights[:, None] * weights[None, :]
    pair_jk = pair[:, :, None, None]
    pair_ik = pair[:, None, :, None, None]
    pair_ij = pair[:, :, None, None, None]
    lam_inv = 1.0 / (
        coef_z * eigen_values[:, None, None, None, None]
        + coef_a * eigen_values[None, :, None, None, None]
        + coef_b * eigen_values[None, None, :, None, None]
    )
    radial_pos = jnp.arange(width) % RADIAL
    keep_upper = (radial_pos < RADIAL - 1).astype(jnp.float32)
    keep_lower = (radial_pos > 0).astype(jnp.float32)
    point_ids = jnp.arange(PTS)
    first_point = (point_ids == 0).astype(jnp.float32)
    last_point = (point_ids == PTS - 1).astype(jnp.float32)
    face_factor = 1.0 + first_point + last_point
    radial_factor = (
        1.0 + first_point[:, None] * keep_lower[None, :] + last_point[:, None] * keep_upper[None, :]
    )
    multiplicity = (
        face_factor[:, None, None, None, None]
        * face_factor[None, :, None, None, None]
        * radial_factor[None, None, :, None, :]
    )
    inv_mult = 1.0 / multiplicity

    def windowed(plane, offset, extra):
        start = (DRIFT + offset - extra) * RADIAL
        return lax.dynamic_slice_in_dim(
            plane, start, (COLS_DEV + 2 * extra) * RADIAL, axis=plane.ndim - 1
        )

    def fetch_planes(upper_plane, lower_plane, extra):
        from_below = from_behind(upper_plane, "grp", 1)
        from_above = from_behind(lower_plane, "grp", -1)
        rimmed = padded(jnp.stack([from_below, from_above]), (("sub", 4),), DRIFT * RADIAL)
        from_below = windowed(rimmed[0], rot_here - rot_down, extra)
        from_above = windowed(rimmed[1], rot_here - rot_up, extra)
        return (from_below, from_above)

    def fetch_sides(leading_cols, trailing_cols):
        shape = leading_cols.shape
        from_next = from_behind(leading_cols.reshape(-1), "sub", -1).reshape(shape)
        from_prev = from_behind(trailing_cols.reshape(-1), "sub", 1).reshape(shape)
        return (from_next, from_prev)

    def pass_z(field, from_below, from_above):
        upper_face, lower_face = (field[:, -1], field[:, 0])
        over = jnp.concatenate([lower_face[:, :, :, 1:], from_above[:, :, :, None]], axis=3)
        under = jnp.concatenate([from_below[:, :, :, None], upper_face[:, :, :, :-1]], axis=3)
        return field.at[:, -1].set(upper_face + over).at[:, 0].set(lower_face + under)

    def pass_a(field, from_next, from_prev):
        left_face, right_face = (field[:, :, 0], field[:, :, -1])
        over = jnp.concatenate([left_face[..., RADIAL:], from_next], axis=4)
        under = jnp.concatenate([from_prev, right_face[..., :-RADIAL]], axis=4)
        return field.at[:, :, -1].set(right_face + over).at[:, :, 0].set(left_face + under)

    def pass_b(field):
        inner_face, outer_face = (field[:, :, :, 0], field[:, :, :, -1])
        over = jnp.roll(inner_face, -1, axis=4) * keep_upper
        under = jnp.roll(outer_face, 1, axis=4) * keep_lower
        return field.at[:, :, :, -1].set(outer_face + over).at[:, :, :, 0].set(inner_face + under)

    def assemble(field):
        upper_face, lower_face = (field[:, -1], field[:, 0])
        from_below, from_above = fetch_planes(upper_face[:, :, :, -1], lower_face[:, :, :, 0], 0)
        field = pass_z(field, from_below, from_above)
        ghost_next, ghost_prev = fetch_sides(
            field[:, :, 0, :, :, :RADIAL], field[:, :, -1, :, :, -RADIAL:]
        )
        field = pass_a(field, ghost_next, ghost_prev)
        return pass_b(field)

    def apply_op(field):
        term_z = contract(stiffness, field, 1) * pair_jk
        term_a = contract(stiffness, field, 2) * pair_ik
        term_b = contract(stiffness, field, 3) * pair_ij
        return assemble(coef_z * term_z + coef_a * term_a + coef_b * term_b)

    def precondition(resid):
        from_below, from_above = fetch_planes(resid[:, -2, :, :, -1], resid[:, 1, :, :, 0], 0)
        from_next, from_prev = fetch_sides(
            resid[:, :, 1, :, :, :RADIAL], resid[:, :, -2, :, :, -RADIAL:]
        )
        extended = jnp.zeros((1, PTS + 2, PTS + 2, PTS + 2, LAYERS_DEV, width), jnp.float32)
        extended = extended.at[:, 1:-1, 1:-1, 1:-1].set(resid)
        extended = extended.at[:, 0, 1:-1, 1:-1].set(
            jnp.concatenate([from_below[:, :, :, None], resid[:, -2, :, :, :-1]], axis=3)
        )
        extended = extended.at[:, -1, 1:-1, 1:-1].set(
            jnp.concatenate([resid[:, 1, :, :, 1:], from_above[:, :, :, None]], axis=3)
        )
        extended = extended.at[:, 1:-1, 0, 1:-1].set(
            jnp.concatenate([from_prev, resid[:, :, -2, :, :, :-RADIAL]], axis=4)
        )
        extended = extended.at[:, 1:-1, -1, 1:-1].set(
            jnp.concatenate([resid[:, :, 1, :, :, RADIAL:], from_next], axis=4)
        )
        extended = extended.at[:, 1:-1, 1:-1, 0].set(
            jnp.roll(resid[:, :, :, -2], 1, axis=4) * keep_lower
        )
        extended = extended.at[:, 1:-1, 1:-1, -1].set(
            jnp.roll(resid[:, :, :, 1], -1, axis=4) * keep_upper
        )
        for dimension in (1, 2, 3):
            extended = contract(eigen_basis.T, extended, dimension)
        extended = extended * lam_inv
        for dimension in (1, 2, 3):
            extended = contract(eigen_basis, extended, dimension)
        return assemble(extended[:, 1:-1, 1:-1, 1:-1] * inv_mult)

    def smooth(solution, resid):
        theta = 0.5 * (cheb_upper + cheb_upper * cheb_ratio)
        delta = 0.5 * (cheb_upper - cheb_upper * cheb_ratio)
        sigma = theta / delta
        rho_now = 1.0 / sigma
        step = precondition(resid) / theta
        for turn in range(SMOOTH):
            solution = solution + step
            resid = resid - apply_op(step)
            if turn + 1 < SMOOTH:
                rho_next = 1.0 / (2.0 * sigma - rho_now)
                step = rho_next * rho_now * step + 2.0 * rho_next / delta * precondition(resid)
                rho_now = rho_next
        return (solution, resid)

    source = rhs.reshape(field_shape)
    target = assemble(source * inv_mult)
    solution, resid = smooth(jnp.zeros(field_shape, jnp.float32), target)
    weighted = resid * inv_mult
    for dimension in (1, 2, 3):
        weighted = contract(interp.T, weighted, dimension)
    coarse_local = (
        coef_z * coarse_z[:, :, :, None, None]
        + coef_a * coarse_a[:, :, :, None, None]
        + coef_b * coarse_b[:, :, :, None, None]
    )
    assembled = assemble(jnp.concatenate([weighted, coarse_local[None]], axis=0))
    correction = assembled[0:1] / assembled[1:2]
    for dimension in (1, 2, 3):
        correction = contract(interp, correction, dimension)
    solution = solution + correction
    resid = resid - apply_op(correction)
    solution, resid = smooth(solution, resid)
    return (solution.reshape(rhs.shape), resid.reshape(rhs.shape))


def solution(mesh):
    return jax.shard_map(
        per_device,
        mesh=mesh,
        in_specs=(P(None, None, None, ("grp", "sub")), P("grp"), P(), P(), P()),
        out_specs=(P(None, None, None, ("grp", "sub")), P(None, None, None, ("grp", "sub"))),
        check_vma=False,
    )
```

profile of v0, /device:TPU:0, one launch (start us, length us, event | category | flops | bytes accessed | tf_op | source)
XLA Modules:
  0.0 460.8 jit_solution(9863616698275583389)
XLA Ops:
  2.5 5.1 %collective-permute-start.1 = (f32[1,8,8,256]{3,0,2,1:T(1,128)S(1)}, f32[1,8,8,256]{3,0,2,1:T(1,128)S(1)}, u32[]{:S(2)}, u32[]{:S(2)}) collective-permute-start(f32[1,8,8,256]{3,0,2,1:T(1,128)S(1)} %get-tuple-element.1254), channel_id=1, source_target_pairs={{0,124},{4,0},{8,4},{12,8},{16,12},{20,16},{24,20},{28,24},{32,28}... | collective-permute-start | bytes 196616 | tf_op jit(solution)/shard_map/ppermute | solution.py:24
  10.7 4.2 collective-permute-start.3
  18.1 2.2 collective-permute-done.2
  27.2 2.0 collective-permute-done.5
  31.6 3.2 collective-permute-start.11
  35.2 4.5 collective-permute-start.7
  44.1 2.0 collective-permute-done.9
  54.6 2.0 fusion.3
  58.5 2.0 fusion.57
  60.5 14.9 %fusion.40 = f32[10,10,10,256]{3,0,2,1:T(8,128)S(1)} fusion(f32[10,10,1,1]{0,1,3,2:T(8,128)S(1)} %copy-done.2, f32[10,10,10,256]{3,1,2,0:T(8,128)S(1)} %fusion.57), kind=kOutput, calls=%fused_computation.45 | convolution fusion | flops 30720000 | bytes 2048400 | tf_op jit(solution)/shard_map/dot_general | solution.py:154
  77.0 5.1 %collective-permute-start.13 = (f32[1,8,8,256]{3,0,2,1:T(1,128)S(1)}, f32[1,8,8,256]{3,0,2,1:T(1,128)S(1)}, u32[]{:S(2)}, u32[]{:S(2)}) collective-permute-start(f32[1,8,8,256]{3,0,2,1:T(1,128)S(1)} %get-tuple-element.1237), channel_id=1, source_target_pairs={{0,124},{4,0},{8,4},{12,8},{16,12},{20,16},{24,20},{28,24},{32,28}... | collective-permute-start | bytes 196616 | tf_op jit(solution)/shard_map/ppermute | solution.py:24
  84.3 2.0 collective-permute-start.14
  86.4 2.2 collective-permute-done.15
  92.9 2.0 collective-permute-start.17
  101.9 5.1 %collective-permute-start.19 = (f32[1,8,8,256]{3,2,1,0:T(8,128)S(1)}, f32[1,8,8,256]{3,2,1,0:T(8,128)S(1)}, u32[]{:S(2)}, u32[]{:S(2)}) collective-permute-start(f32[1,8,8,256]{3,2,1,0:T(8,128)S(1)} %slice_bitcast_fusion.83), channel_id=1, source_target_pairs={{0,124},{4,0},{8,4},{12,8},{16,12},{20,16},{24,20},{28,24},{32,28}... | collective-permute-start | bytes 196616 | tf_op jit(solution)/shard_map/ppermute | solution.py:24
  111.1 2.2 collective-permute-done.21
  125.2 2.7 collective-permute-start.29
  129.5 4.5 collective-permute-start.25
  138.3 2.0 collective-permute-done.27
  145.3 2.3 scatter.360
  147.6 2.4 scatter.361
  153.4 3.4 fusion.38
  164.7 2.1 fusion.28
  168.4 5.1 %collective-permute-start.31 = (f32[1,8,8,256]{3,0,2,1:T(1,128)S(1)}, f32[1,8,8,256]{3,0,2,1:T(1,128)S(1)}, u32[]{:S(2)}, u32[]{:S(2)}) collective-permute-start(f32[1,8,8,256]{3,0,2,1:T(1,128)S(1)} %get-tuple-element.1213), channel_id=1, source_target_pairs={{0,124},{4,0},{8,4},{12,8},{16,12},{20,16},{24,20},{28,24},{32,28}... | collective-permute-start | bytes 196616 | tf_op jit(solution)/shard_map/ppermute | solution.py:24
  175.7 2.0 collective-permute-start.32
  177.7 2.2 collective-permute-done.33
  184.3 2.0 collective-permute-start.35
  193.4 5.1 %collective-permute-start.37 = (f32[1,8,8,256]{3,2,1,0:T(8,128)S(1)}, f32[1,8,8,256]{3,2,1,0:T(8,128)S(1)}, u32[]{:S(2)}, u32[]{:S(2)}) collective-permute-start(f32[1,8,8,256]{3,2,1,0:T(8,128)S(1)} %slice_bitcast_fusion.76), channel_id=1, source_target_pairs={{0,124},{4,0},{8,4},{12,8},{16,12},{20,16},{24,20},{28,24},{32,28}... | collective-permute-start | bytes 196616 | tf_op jit(solution)/shard_map/ppermute | solution.py:24
  217.3 5.1 %collective-permute-start.43 = (f32[2,4,4,256]{3,0,2,1:T(2,128)S(1)}, f32[2,4,4,256]{3,0,2,1:T(2,128)S(1)}, u32[]{:S(2)}, u32[]{:S(2)}) collective-permute-start(f32[2,4,4,256]{3,0,2,1:T(2,128)S(1)} %bitcast.1208), channel_id=1, source_target_pairs={{0,124},{4,0},{8,4},{12,8},{16,12},{20,16},{24,20},{28,24},{32,28}... | collective-permute-start | bytes 98312 | tf_op jit(solution)/shard_map/ppermute | solution.py:24
  230.5 2.0 collective-permute-start.47
  240.2 5.4 %collective-permute-start.49 = (f32[1,8,8,256]{3,2,1,0:T(8,128)S(1)}, f32[1,8,8,256]{3,2,1,0:T(8,128)S(1)}, u32[]{:S(2)}, u32[]{:S(2)}) collective-permute-start(f32[1,8,8,256]{3,2,1,0:T(8,128)S(1)} %slice_bitcast_fusion.72), channel_id=1, source_target_pairs={{0,124},{4,0},{8,4},{12,8},{16,12},{20,16},{24,20},{28,24},{32,28}... | collective-permute-start | bytes 196616 | tf_op jit(solution)/shard_map/ppermute | solution.py:24
  249.8 2.2 collective-permute-done.51
  259.9 2.3 collective-permute-done.53
  268.0 2.3 scatter.404
  270.3 2.3 scatter.405
  275.3 2.7 collective-permute-start.59
  279.7 4.5 collective-permute-start.55
  288.4 2.0 collective-permute-done.57
  295.4 2.3 scatter.411
  297.7 2.4 scatter.414
  303.3 3.4 fusion.26
  308.7 2.0 fusion.1
  314.6 2.2 fusion.16
  318.4 5.1 %collective-permute-start.61 = (f32[1,8,8,256]{3,0,2,1:T(1,128)S(1)}, f32[1,8,8,256]{3,0,2,1:T(1,128)S(1)}, u32[]{:S(2)}, u32[]{:S(2)}) collective-permute-start(f32[1,8,8,256]{3,0,2,1:T(1,128)S(1)} %get-tuple-element.1182), channel_id=1, source_target_pairs={{0,124},{4,0},{8,4},{12,8},{16,12},{20,16},{24,20},{28,24},{32,28}... | collective-permute-start | bytes 196616 | tf_op jit(solution)/shard_map/ppermute | solution.py:24
  325.7 2.0 collective-permute-start.62
  327.7 2.2 collective-permute-done.63
  334.2 2.0 collective-permute-start.65
  344.4 5.1 %collective-permute-start.67 = (f32[1,8,8,256]{3,0,2,1:T(1,128)S(1)}, f32[1,8,8,256]{3,0,2,1:T(1,128)S(1)}, u32[]{:S(2)}, u32[]{:S(2)}) collective-permute-start(f32[1,8,8,256]{3,0,2,1:T(1,128)S(1)} %get-tuple-element.1173), channel_id=1, source_target_pairs={{0,124},{4,0},{8,4},{12,8},{16,12},{20,16},{24,20},{28,24},{32,28}... | collective-permute-start | bytes 196616 | tf_op jit(solution)/shard_map/ppermute | solution.py:24
  355.9 2.2 collective-permute-done.68
  369.3 2.8 collective-permute-start.77
  373.6 4.5 collective-permute-start.73
  382.4 2.0 collective-permute-done.75
  389.4 2.3 scatter.444
  391.7 2.4 scatter.445
  397.3 3.4 fusion.14
  406.6 2.0 fusion.81
  408.6 2.2 fusion.4
  411.7 5.1 %collective-permute-start.79 = (f32[1,8,8,256]{3,1,2,0:T(8,128)S(1)}, f32[1,8,8,256]{3,1,2,0:T(8,128)S(1)}, u32[]{:S(2)}, u32[]{:S(2)}) collective-permute-start(f32[1,8,8,256]{3,1,2,0:T(8,128)S(1)} %get-tuple-element.1155), channel_id=1, source_target_pairs={{0,124},{4,0},{8,4},{12,8},{16,12},{20,16},{24,20},{28,24},{32,28}... | collective-permute-start | bytes 196616 | tf_op jit(solution)/shard_map/ppermute | solution.py:24
  418.8 2.0 collective-permute-start.80
  420.9 2.2 collective-permute-done.81
  425.1 2.0 collective-permute-start.83
  436.7 5.1 %collective-permute-start.85 = (f32[1,8,8,256]{3,0,2,1:T(1,128)S(1)}, f32[1,8,8,256]{3,0,2,1:T(1,128)S(1)}, u32[]{:S(2)}, u32[]{:S(2)}) collective-permute-start(f32[1,8,8,256]{3,0,2,1:T(1,128)S(1)} %get-tuple-element.1147), channel_id=1, source_target_pairs={{0,124},{4,0},{8,4},{12,8},{16,12},{20,16},{24,20},{28,24},{32,28}... | collective-permute-start | bytes 196616 | tf_op jit(solution)/shard_map/ppermute | solution.py:24
  448.3 2.0 collective-permute-done.86
  452.4 3.1 collective-permute-start.88
  (727 shorter events, 251.4 us)
Async XLA Ops:
  2.4 8.0 %collective-permute-start = (f32[1,8,8,256]{3,0,2,1:T(1,128)S(1)}, f32[1,8,8,256]{3,0,2,1:T(1,128)S(1)}, u32[]{:S(2)}, u32[]{:S(2)}) collective-permute-start(f32[1,8,8,256]{3,0,2,1:T(1,128)S(1)} %get-tuple-element.1253), channel_id=1, source_target_pairs={{0,4},{4,8},{8,12},{12,16},{16,20},{20,24},{24,28},{28,32},{32,36}... | collective-permute-start | bytes 196616 | tf_op jit(solution)/shard_map/ppermute | solution.py:24
  2.5 7.9 %collective-permute-start.1 = (f32[1,8,8,256]{3,0,2,1:T(1,128)S(1)}, f32[1,8,8,256]{3,0,2,1:T(1,128)S(1)}, u32[]{:S(2)}, u32[]{:S(2)}) collective-permute-start(f32[1,8,8,256]{3,0,2,1:T(1,128)S(1)} %get-tuple-element.1254), channel_id=1, source_target_pairs={{0,124},{4,0},{8,4},{12,8},{16,12},{20,16},{24,20},{28,24},{32,28}... | collective-permute-start | bytes 196616 | tf_op jit(solution)/shard_map/ppermute | solution.py:24
  10.7 7.4 %collective-permute-start.3 = (f32[2,1,8,8,64]{4,0,3,2,1:T(2,128)S(1)}, f32[2,1,8,8,64]{4,0,3,2,1:T(2,128)S(1)}, u32[]{:S(2)}, u32[]{:S(2)}) collective-permute-start(f32[2,1,8,8,64]{4,0,3,2,1:T(2,128)S(1)} %get-tuple-element.1319), channel_id=1, source_target_pairs={{1,0},{2,1},{3,2},{0,3},{5,4},{6,5},{7,6},{4,7},{9,8},{10,9},{11,1... | collective-permute-start | bytes 98312 | tf_op jit(solution)/shard_map/ppermute | solution.py:36
  14.9 5.5 %collective-permute-start.2 = (f32[2,1,8,8,64]{4,0,3,2,1:T(2,128)S(1)}, f32[2,1,8,8,64]{4,0,3,2,1:T(2,128)S(1)}, u32[]{:S(2)}, u32[]{:S(2)}) collective-permute-start(f32[2,1,8,8,64]{4,0,3,2,1:T(2,128)S(1)} %get-tuple-element.1318), channel_id=1, source_target_pairs={{0,1},{1,2},{2,3},{3,0},{4,5},{5,6},{6,7},{7,4},{8,9},{9,10},{10,1... | collective-permute-start | bytes 98312 | tf_op jit(solution)/shard_map/ppermute | solution.py:33
  24.4 4.8 %collective-permute-start.5 = (f32[1024]{0:T(1024)S(1)}, f32[1024]{0:T(1024)S(1)}, u32[]{:S(2)}, u32[]{:S(2)}) collective-permute-start(f32[1024]{0:T(1024)S(1)} %reshape_squeeze.91), channel_id=1, source_target_pairs={{0,1},{1,2},{2,3},{3,0},{4,5},{5,6},{6,7},{7,4},{8,9},{9,10},{10,1... | collective-permute-start | bytes 12296 | tf_op jit(solution)/shard_map/ppermute | solution.py:24
  31.3 8.7 %collective-permute-start.6 = (f32[1,8,8,256]{3,1,2,0:T(8,128)S(1)}, f32[1,8,8,256]{3,1,2,0:T(8,128)S(1)}, u32[]{:S(2)}, u32[]{:S(2)}) collective-permute-start(f32[1,8,8,256]{3,1,2,0:T(8,128)S(1)} %get-tuple-element.1244), channel_id=1, source_target_pairs={{0,4},{4,8},{8,12},{12,16},{16,20},{20,24},{24,28},{28,32},{32,36}... | collective-permute-start | bytes 196616 | tf_op jit(solution)/shard_map/ppermute | solution.py:24
  31.5 8.3 %collective-permute-start.10 = (f32[1024]{0:T(1024)S(1)}, f32[1024]{0:T(1024)S(1)}, u32[]{:S(2)}, u32[]{:S(2)}) collective-permute-start(f32[1024]{0:T(1024)S(1)} %reshape_squeeze.92), channel_id=1, source_target_pairs={{0,1},{1,2},{2,3},{3,0},{4,5},{5,6},{6,7},{7,4},{8,9},{9,10},{10,1... | collective-permute-start | bytes 12296 | tf_op jit(solution)/shard_map/ppermute | solution.py:24
  31.6 8.3 %collective-permute-start.11 = (f32[1024]{0:T(1024)S(1)}, f32[1024]{0:T(1024)S(1)}, u32[]{:S(2)}, u32[]{:S(2)}) collective-permute-start(f32[1024]{0:T(1024)S(1)} %reshape_squeeze.93), channel_id=1, source_target_pairs={{0,3},{1,0},{2,1},{3,2},{4,7},{5,4},{6,5},{7,6},{8,11},{9,8},{10,9... | collective-permute-start | bytes 12296 | tf_op jit(solution)/shard_map/ppermute | solution.py:24
  35.2 6.5 %collective-permute-start.7 = (f32[1,8,8,256]{3,1,2,0:T(8,128)S(1)}, f32[1,8,8,256]{3,1,2,0:T(8,128)S(1)}, u32[]{:S(2)}, u32[]{:S(2)}) collective-permute-start(f32[1,8,8,256]{3,1,2,0:T(8,128)S(1)} %get-tuple-element.1245), channel_id=1, source_target_pairs={{0,124},{4,0},{8,4},{12,8},{16,12},{20,16},{24,20},{28,24},{32,28}... | collective-permute-start | bytes 196616 | tf_op jit(solution)/shard_map/ppermute | solution.py:24
  42.1 5.5 %collective-permute-start.8 = (f32[2,1,8,8,64]{4,2,3,1,0:T(8,128)S(1)}, f32[2,1,8,8,64]{4,2,3,1,0:T(8,128)S(1)}, u32[]{:S(2)}, u32[]{:S(2)}) collective-permute-start(f32[2,1,8,8,64]{4,2,3,1,0:T(8,128)S(1)} %get-tuple-element.1316), channel_id=1, source_target_pairs={{0,1},{1,2},{2,3},{3,0},{4,5},{5,6},{6,7},{7,4},{8,9},{9,10},{10,1... | collective-permute-start | bytes 98312 | tf_op jit(solution)/shard_map/ppermute | solution.py:33
  77.0 7.1 %collective-permute-start.12 = (f32[1,8,8,256]{3,0,2,1:T(1,128)S(1)}, f32[1,8,8,256]{3,0,2,1:T(1,128)S(1)}, u32[]{:S(2)}, u32[]{:S(2)}) collective-permute-start(f32[1,8,8,256]{3,0,2,1:T(1,128)S(1)} %get-tuple-element.1236), channel_id=1, source_target_pairs={{0,4},{4,8},{8,12},{12,16},{16,20},{20,24},{24,28},{28,32},{32,36}... | collective-permute-start | bytes 196616 | tf_op jit(solution)/shard_map/ppermute | solution.py:24
  77.0 7.0 %collective-permute-start.13 = (f32[1,8,8,256]{3,0,2,1:T(1,128)S(1)}, f32[1,8,8,256]{3,0,2,1:T(1,128)S(1)}, u32[]{:S(2)}, u32[]{:S(2)}) collective-permute-start(f32[1,8,8,256]{3,0,2,1:T(1,128)S(1)} %get-tuple-element.1237), channel_id=1, source_target_pairs={{0,124},{4,0},{8,4},{12,8},{16,12},{20,16},{24,20},{28,24},{32,28}... | collective-permute-start | bytes 196616 | tf_op jit(solution)/shard_map/ppermute | solution.py:24
  84.3 5.5 %collective-permute-start.14 = (f32[2,1,8,8,64]{4,0,3,2,1:T(2,128)S(1)}, f32[2,1,8,8,64]{4,0,3,2,1:T(2,128)S(1)}, u32[]{:S(2)}, u32[]{:S(2)}) collective-permute-start(f32[2,1,8,8,64]{4,0,3,2,1:T(2,128)S(1)} %get-tuple-element.1314), channel_id=1, source_target_pairs={{0,1},{1,2},{2,3},{3,0},{4,5},{5,6},{6,7},{7,4},{8,9},{9,10},{10,1... | collective-permute-start | bytes 98312 | tf_op jit(solution)/shard_map/ppermute | solution.py:33
  92.9 4.8 %collective-permute-start.17 = (f32[1024]{0:T(1024)S(1)}, f32[1024]{0:T(1024)S(1)}, u32[]{:S(2)}, u32[]{:S(2)}) collective-permute-start(f32[1024]{0:T(1024)S(1)} %reshape_squeeze.95), channel_id=1, source_target_pairs={{0,1},{1,2},{2,3},{3,0},{4,5},{5,6},{6,7},{7,4},{8,9},{9,10},{10,1... | collective-permute-start | bytes 12296 | tf_op jit(solution)/shard_map/ppermute | solution.py:24
  101.8 7.1 %collective-permute-start.18 = (f32[1,8,8,256]{3,2,1,0:T(8,128)S(1)}, f32[1,8,8,256]{3,2,1,0:T(8,128)S(1)}, u32[]{:S(2)}, u32[]{:S(2)}) collective-permute-start(f32[1,8,8,256]{3,2,1,0:T(8,128)S(1)} %slice_bitcast_fusion.84), channel_id=1, source_target_pairs={{0,4},{4,8},{8,12},{12,16},{16,20},{20,24},{24,28},{28,32},{32,36}... | collective-permute-start | bytes 196616 | tf_op jit(solution)/shard_map/ppermute | solution.py:24
  101.9 7.0 %collective-permute-start.19 = (f32[1,8,8,256]{3,2,1,0:T(8,128)S(1)}, f32[1,8,8,256]{3,2,1,0:T(8,128)S(1)}, u32[]{:S(2)}, u32[]{:S(2)}) collective-permute-start(f32[1,8,8,256]{3,2,1,0:T(8,128)S(1)} %slice_bitcast_fusion.83), channel_id=1, source_target_pairs={{0,124},{4,0},{8,4},{12,8},{16,12},{20,16},{24,20},{28,24},{32,28}... | collective-permute-start | bytes 196616 | tf_op jit(solution)/shard_map/ppermute | solution.py:24
  109.6 5.5 %collective-permute-start.20 = (f32[2,1,8,8,64]{4,3,2,1,0:T(8,128)S(1)}, f32[2,1,8,8,64]{4,3,2,1,0:T(8,128)S(1)}, u32[]{:S(2)}, u32[]{:S(2)}) collective-permute-start(f32[2,1,8,8,64]{4,3,2,1,0:T(8,128)S(1)} %get-tuple-element.1312), channel_id=1, source_target_pairs={{0,1},{1,2},{2,3},{3,0},{4,5},{5,6},{6,7},{7,4},{8,9},{9,10},{10,1... | collective-permute-start | bytes 98312 | tf_op jit(solution)/shard_map/ppermute | solution.py:33
  116.2 4.8 %collective-permute-start.23 = (f32[1024]{0:T(1024)S(1)}, f32[1024]{0:T(1024)S(1)}, u32[]{:S(2)}, u32[]{:S(2)}) collective-permute-start(f32[1024]{0:T(1024)S(1)} %reshape_squeeze.97), channel_id=1, source_target_pairs={{0,1},{1,2},{2,3},{3,0},{4,5},{5,6},{6,7},{7,4},{8,9},{9,10},{10,1... | collective-permute-start | bytes 12296 | tf_op jit(solution)/shard_map/ppermute | solution.py:24
  124.5 9.8 %collective-permute-start.24 = (f32[1,8,8,256]{3,1,2,0:T(8,128)S(1)}, f32[1,8,8,256]{3,1,2,0:T(8,128)S(1)}, u32[]{:S(2)}, u32[]{:S(2)}) collective-permute-start(f32[1,8,8,256]{3,1,2,0:T(8,128)S(1)} %get-tuple-element.1220), channel_id=1, source_target_pairs={{0,4},{4,8},{8,12},{12,16},{16,20},{20,24},{24,28},{28,32},{32,36}... | collective-permute-start | bytes 196616 | tf_op jit(solution)/shard_map/ppermute | solution.py:24
  124.6 9.4 %collective-permute-start.28 = (f32[1024]{0:T(1024)S(1)}, f32[1024]{0:T(1024)S(1)}, u32[]{:S(2)}, u32[]{:S(2)}) collective-permute-start(f32[1024]{0:T(1024)S(1)} %reshape_squeeze.98), channel_id=1, source_target_pairs={{0,1},{1,2},{2,3},{3,0},{4,5},{5,6},{6,7},{7,4},{8,9},{9,10},{10,1... | collective-permute-start | bytes 12296 | tf_op jit(solution)/shard_map/ppermute | solution.py:24
  125.2 8.9 %collective-permute-start.29 = (f32[1024]{0:T(1024)S(1)}, f32[1024]{0:T(1024)S(1)}, u32[]{:S(2)}, u32[]{:S(2)}) collective-permute-start(f32[1024]{0:T(1024)S(1)} %reshape_squeeze.99), channel_id=1, source_target_pairs={{0,3},{1,0},{2,1},{3,2},{4,7},{5,4},{6,5},{7,6},{8,11},{9,8},{10,9... | collective-permute-start | bytes 12296 | tf_op jit(solution)/shard_map/ppermute | solution.py:24
  129.5 6.4 %collective-permute-start.25 = (f32[1,8,8,256]{3,1,2,0:T(8,128)S(1)}, f32[1,8,8,256]{3,1,2,0:T(8,128)S(1)}, u32[]{:S(2)}, u32[]{:S(2)}) collective-permute-start(f32[1,8,8,256]{3,1,2,0:T(8,128)S(1)} %get-tuple-element.1221), channel_id=1, source_target_pairs={{0,124},{4,0},{8,4},{12,8},{16,12},{20,16},{24,20},{28,24},{32,28}... | collective-permute-start | bytes 196616 | tf_op jit(solution)/shard_map/ppermute | solution.py:24
  136.3 5.5 %collective-permute-start.26 = (f32[2,1,8,8,64]{4,2,3,1,0:T(8,128)S(1)}, f32[2,1,8,8,64]{4,2,3,1,0:T(8,128)S(1)}, u32[]{:S(2)}, u32[]{:S(2)}) collective-permute-start(f32[2,1,8,8,64]{4,2,3,1,0:T(8,128)S(1)} %get-tuple-element.1310), channel_id=1, source_target_pairs={{0,1},{1,2},{2,3},{3,0},{4,5},{5,6},{6,7},{7,4},{8,9},{9,10},{10,1... | collective-permute-start | bytes 98312 | tf_op jit(solution)/shard_map/ppermute | solution.py:33
  168.3 7.1 %collective-permute-start.30 = (f32[1,8,8,256]{3,0,2,1:T(1,128)S(1)}, f32[1,8,8,256]{3,0,2,1:T(1,128)S(1)}, u32[]{:S(2)}, u32[]{:S(2)}) collective-permute-start(f32[1,8,8,256]{3,0,2,1:T(1,128)S(1)} %get-tuple-element.1212), channel_id=1, source_target_pairs={{0,4},{4,8},{8,12},{12,16},{16,20},{20,24},{24,28},{28,32},{32,36}... | collective-permute-start | bytes 196616 | tf_op jit(solution)/shard_map/ppermute | solution.py:24
  168.4 7.0 %collective-permute-start.31 = (f32[1,8,8,256]{3,0,2,1:T(1,128)S(1)}, f32[1,8,8,256]{3,0,2,1:T(1,128)S(1)}, u32[]{:S(2)}, u32[]{:S(2)}) collective-permute-start(f32[1,8,8,256]{3,0,2,1:T(1,128)S(1)} %get-tuple-element.1213), channel_id=1, source_target_pairs={{0,124},{4,0},{8,4},{12,8},{16,12},{20,16},{24,20},{28,24},{32,28}... | collective-permute-start | bytes 196616 | tf_op jit(solution)/shard_map/ppermute | solution.py:24
  175.7 5.5 %collective-permute-start.32 = (f32[2,1,8,8,64]{4,0,3,2,1:T(2,128)S(1)}, f32[2,1,8,8,64]{4,0,3,2,1:T(2,128)S(1)}, u32[]{:S(2)}, u32[]{:S(2)}) collective-permute-start(f32[2,1,8,8,64]{4,0,3,2,1:T(2,128)S(1)} %get-tuple-element.1308), channel_id=1, source_target_pairs={{0,1},{1,2},{2,3},{3,0},{4,5},{5,6},{6,7},{7,4},{8,9},{9,10},{10,1... | collective-permute-start | bytes 98312 | tf_op jit(solution)/shard_map/ppermute | solution.py:33
  184.3 4.8 %collective-permute-start.35 = (f32[1024]{0:T(1024)S(1)}, f32[1024]{0:T(1024)S(1)}, u32[]{:S(2)}, u32[]{:S(2)}) collective-permute-start(f32[1024]{0:T(1024)S(1)} %reshape_squeeze.101), channel_id=1, source_target_pairs={{0,1},{1,2},{2,3},{3,0},{4,5},{5,6},{6,7},{7,4},{8,9},{9,10},{10,1... | collective-permute-start | bytes 12296 | tf_op jit(solution)/shard_map/ppermute | solution.py:24
  193.3 7.1 %collective-permute-start.36 = (f32[1,8,8,256]{3,2,1,0:T(8,128)S(1)}, f32[1,8,8,256]{3,2,1,0:T(8,128)S(1)}, u32[]{:S(2)}, u32[]{:S(2)}) collective-permute-start(f32[1,8,8,256]{3,2,1,0:T(8,128)S(1)} %slice_bitcast_fusion.77), channel_id=1, source_target_pairs={{0,4},{4,8},{8,12},{12,16},{16,20},{20,24},{24,28},{28,32},{32,36}... | collective-permute-start | bytes 196616 | tf_op jit(solution)/shard_map/ppermute | solution.py:24
  193.4 7.0 %collective-permute-start.37 = (f32[1,8,8,256]{3,2,1,0:T(8,128)S(1)}, f32[1,8,8,256]{3,2,1,0:T(8,128)S(1)}, u32[]{:S(2)}, u32[]{:S(2)}) collective-permute-start(f32[1,8,8,256]{3,2,1,0:T(8,128)S(1)} %slice_bitcast_fusion.76), channel_id=1, source_target_pairs={{0,124},{4,0},{8,4},{12,8},{16,12},{20,16},{24,20},{28,24},{32,28}... | collective-permute-start | bytes 196616 | tf_op jit(solution)/shard_map/ppermute | solution.py:24
  201.1 5.5 %collective-permute-start.38 = (f32[2,1,8,8,64]{4,3,2,1,0:T(8,128)S(1)}, f32[2,1,8,8,64]{4,3,2,1,0:T(8,128)S(1)}, u32[]{:S(2)}, u32[]{:S(2)}) collective-permute-start(f32[2,1,8,8,64]{4,3,2,1,0:T(8,128)S(1)} %get-tuple-element.1306), channel_id=1, source_target_pairs={{0,1},{1,2},{2,3},{3,0},{4,5},{5,6},{6,7},{7,4},{8,9},{9,10},{10,1... | collective-permute-start | bytes 98312 | tf_op jit(solution)/shard_map/ppermute | solution.py:33
  207.9 4.8 %collective-permute-start.41 = (f32[1024]{0:T(1024)S(1)}, f32[1024]{0:T(1024)S(1)}, u32[]{:S(2)}, u32[]{:S(2)}) collective-permute-start(f32[1024]{0:T(1024)S(1)} %reshape_squeeze.103), channel_id=1, source_target_pairs={{0,1},{1,2},{2,3},{3,0},{4,5},{5,6},{6,7},{7,4},{8,9},{9,10},{10,1... | collective-permute-start | bytes 12296 | tf_op jit(solution)/shard_map/ppermute | solution.py:24
  217.2 6.7 %collective-permute-start.42 = (f32[2,4,4,256]{3,0,2,1:T(2,128)S(1)}, f32[2,4,4,256]{3,0,2,1:T(2,128)S(1)}, u32[]{:S(2)}, u32[]{:S(2)}) collective-permute-start(f32[2,4,4,256]{3,0,2,1:T(2,128)S(1)} %get-tuple-element.1304), channel_id=1, source_target_pairs={{0,4},{4,8},{8,12},{12,16},{16,20},{20,24},{24,28},{28,32},{32,36}... | collective-permute-start | bytes 98312 | tf_op jit(solution)/shard_map/ppermute | solution.py:24
  217.3 6.7 %collective-permute-start.43 = (f32[2,4,4,256]{3,0,2,1:T(2,128)S(1)}, f32[2,4,4,256]{3,0,2,1:T(2,128)S(1)}, u32[]{:S(2)}, u32[]{:S(2)}) collective-permute-start(f32[2,4,4,256]{3,0,2,1:T(2,128)S(1)} %bitcast.1208), channel_id=1, source_target_pairs={{0,124},{4,0},{8,4},{12,8},{16,12},{20,16},{24,20},{28,24},{32,28}... | collective-permute-start | bytes 98312 | tf_op jit(solution)/shard_map/ppermute | solution.py:24
  224.2 5.1 %collective-permute-start.44 = (f32[2,2,4,4,64]{4,1,3,2,0:T(2,128)S(1)}, f32[2,2,4,4,64]{4,1,3,2,0:T(2,128)S(1)}, u32[]{:S(2)}, u32[]{:S(2)}) collective-permute-start(f32[2,2,4,4,64]{4,1,3,2,0:T(2,128)S(1)} %get-tuple-element.1322), channel_id=1, source_target_pairs={{0,1},{1,2},{2,3},{3,0},{4,5},{5,6},{6,7},{7,4},{8,9},{9,10},{10,1... | collective-permute-start | bytes 49160 | tf_op jit(solution)/shard_map/ppermute | solution.py:33
  240.2 7.1 %collective-permute-start.48 = (f32[1,8,8,256]{3,2,1,0:T(8,128)S(1)}, f32[1,8,8,256]{3,2,1,0:T(8,128)S(1)}, u32[]{:S(2)}, u32[]{:S(2)}) collective-permute-start(f32[1,8,8,256]{3,2,1,0:T(8,128)S(1)} %slice_bitcast_fusion.73), channel_id=1, source_target_pairs={{0,4},{4,8},{8,12},{12,16},{16,20},{20,24},{24,28},{28,32},{32,36}... | collective-permute-start | bytes 196616 | tf_op jit(solution)/shard_map/ppermute | solution.py:24
  240.2 7.3 %collective-permute-start.49 = (f32[1,8,8,256]{3,2,1,0:T(8,128)S(1)}, f32[1,8,8,256]{3,2,1,0:T(8,128)S(1)}, u32[]{:S(2)}, u32[]{:S(2)}) collective-permute-start(f32[1,8,8,256]{3,2,1,0:T(8,128)S(1)} %slice_bitcast_fusion.72), channel_id=1, source_target_pairs={{0,124},{4,0},{8,4},{12,8},{16,12},{20,16},{24,20},{28,24},{32,28}... | collective-permute-start | bytes 196616 | tf_op jit(solution)/shard_map/ppermute | solution.py:24
  248.3 5.5 %collective-permute-start.50 = (f32[2,1,8,8,64]{4,3,2,1,0:T(8,128)S(1)}, f32[2,1,8,8,64]{4,3,2,1,0:T(8,128)S(1)}, u32[]{:S(2)}, u32[]{:S(2)}) collective-permute-start(f32[2,1,8,8,64]{4,3,2,1,0:T(8,128)S(1)} %get-tuple-element.1295), channel_id=1, source_target_pairs={{0,1},{1,2},{2,3},{3,0},{4,5},{5,6},{6,7},{7,4},{8,9},{9,10},{10,1... | collective-permute-start | bytes 98312 | tf_op jit(solution)/shard_map/ppermute | solution.py:33
  257.4 4.8 %collective-permute-start.53 = (f32[1024]{0:T(1024)S(1)}, f32[1024]{0:T(1024)S(1)}, u32[]{:S(2)}, u32[]{:S(2)}) collective-permute-start(f32[1024]{0:T(1024)S(1)} %reshape_squeeze.107), channel_id=1, source_target_pairs={{0,1},{1,2},{2,3},{3,0},{4,5},{5,6},{6,7},{7,4},{8,9},{9,10},{10,1... | collective-permute-start | bytes 12296 | tf_op jit(solution)/shard_map/ppermute | solution.py:24
  274.6 9.8 %collective-permute-start.54 = (f32[1,8,8,256]{3,1,2,0:T(8,128)S(1)}, f32[1,8,8,256]{3,1,2,0:T(8,128)S(1)}, u32[]{:S(2)}, u32[]{:S(2)}) collective-permute-start(f32[1,8,8,256]{3,1,2,0:T(8,128)S(1)} %get-tuple-element.1189), channel_id=1, source_target_pairs={{0,4},{4,8},{8,12},{12,16},{16,20},{20,24},{24,28},{28,32},{32,36}... | collective-permute-start | bytes 196616 | tf_op jit(solution)/shard_map/ppermute | solution.py:24
  274.7 9.4 %collective-permute-start.58 = (f32[1024]{0:T(1024)S(1)}, f32[1024]{0:T(1024)S(1)}, u32[]{:S(2)}, u32[]{:S(2)}) collective-permute-start(f32[1024]{0:T(1024)S(1)} %reshape_squeeze.108), channel_id=1, source_target_pairs={{0,1},{1,2},{2,3},{3,0},{4,5},{5,6},{6,7},{7,4},{8,9},{9,10},{10,1... | collective-permute-start | bytes 12296 | tf_op jit(solution)/shard_map/ppermute | solution.py:24
  275.3 8.9 %collective-permute-start.59 = (f32[1024]{0:T(1024)S(1)}, f32[1024]{0:T(1024)S(1)}, u32[]{:S(2)}, u32[]{:S(2)}) collective-permute-start(f32[1024]{0:T(1024)S(1)} %reshape_squeeze.109), channel_id=1, source_target_pairs={{0,3},{1,0},{2,1},{3,2},{4,7},{5,4},{6,5},{7,6},{8,11},{9,8},{10,9... | collective-permute-start | bytes 12296 | tf_op jit(solution)/shard_map/ppermute | solution.py:24
  279.7 6.4 %collective-permute-start.55 = (f32[1,8,8,256]{3,1,2,0:T(8,128)S(1)}, f32[1,8,8,256]{3,1,2,0:T(8,128)S(1)}, u32[]{:S(2)}, u32[]{:S(2)}) collective-permute-start(f32[1,8,8,256]{3,1,2,0:T(8,128)S(1)} %get-tuple-element.1190), channel_id=1, source_target_pairs={{0,124},{4,0},{8,4},{12,8},{16,12},{20,16},{24,20},{28,24},{32,28}... | collective-permute-start | bytes 196616 | tf_op jit(solution)/shard_map/ppermute | solution.py:24
  286.5 5.5 %collective-permute-start.56 = (f32[2,1,8,8,64]{4,2,3,1,0:T(8,128)S(1)}, f32[2,1,8,8,64]{4,2,3,1,0:T(8,128)S(1)}, u32[]{:S(2)}, u32[]{:S(2)}) collective-permute-start(f32[2,1,8,8,64]{4,2,3,1,0:T(8,128)S(1)} %get-tuple-element.1293), channel_id=1, source_target_pairs={{0,1},{1,2},{2,3},{3,0},{4,5},{5,6},{6,7},{7,4},{8,9},{9,10},{10,1... | collective-permute-start | bytes 98312 | tf_op jit(solution)/shard_map/ppermute | solution.py:33
  318.3 7.1 %collective-permute-start.60 = (f32[1,8,8,256]{3,0,2,1:T(1,128)S(1)}, f32[1,8,8,256]{3,0,2,1:T(1,128)S(1)}, u32[]{:S(2)}, u32[]{:S(2)}) collective-permute-start(f32[1,8,8,256]{3,0,2,1:T(1,128)S(1)} %get-tuple-element.1181), channel_id=1, source_target_pairs={{0,4},{4,8},{8,12},{12,16},{16,20},{20,24},{24,28},{28,32},{32,36}... | collective-permute-start | bytes 196616 | tf_op jit(solution)/shard_map/ppermute | solution.py:24
  318.4 7.0 %collective-permute-start.61 = (f32[1,8,8,256]{3,0,2,1:T(1,128)S(1)}, f32[1,8,8,256]{3,0,2,1:T(1,128)S(1)}, u32[]{:S(2)}, u32[]{:S(2)}) collective-permute-start(f32[1,8,8,256]{3,0,2,1:T(1,128)S(1)} %get-tuple-element.1182), channel_id=1, source_target_pairs={{0,124},{4,0},{8,4},{12,8},{16,12},{20,16},{24,20},{28,24},{32,28}... | collective-permute-start | bytes 196616 | tf_op jit(solution)/shard_map/ppermute | solution.py:24
  325.7 5.5 %collective-permute-start.62 = (f32[2,1,8,8,64]{4,0,3,2,1:T(2,128)S(1)}, f32[2,1,8,8,64]{4,0,3,2,1:T(2,128)S(1)}, u32[]{:S(2)}, u32[]{:S(2)}) collective-permute-start(f32[2,1,8,8,64]{4,0,3,2,1:T(2,128)S(1)} %get-tuple-element.1291), channel_id=1, source_target_pairs={{0,1},{1,2},{2,3},{3,0},{4,5},{5,6},{6,7},{7,4},{8,9},{9,10},{10,1... | collective-permute-start | bytes 98312 | tf_op jit(solution)/shard_map/ppermute | solution.py:33
  334.2 4.8 %collective-permute-start.65 = (f32[1024]{0:T(1024)S(1)}, f32[1024]{0:T(1024)S(1)}, u32[]{:S(2)}, u32[]{:S(2)}) collective-permute-start(f32[1024]{0:T(1024)S(1)} %reshape_squeeze.111), channel_id=1, source_target_pairs={{0,1},{1,2},{2,3},{3,0},{4,5},{5,6},{6,7},{7,4},{8,9},{9,10},{10,1... | collective-permute-start | bytes 12296 | tf_op jit(solution)/shard_map/ppermute | solution.py:24
  344.3 7.1 %collective-permute-start.66 = (f32[1,8,8,256]{3,0,2,1:T(1,128)S(1)}, f32[1,8,8,256]{3,0,2,1:T(1,128)S(1)}, u32[]{:S(2)}, u32[]{:S(2)}) collective-permute-start(f32[1,8,8,256]{3,0,2,1:T(1,128)S(1)} %get-tuple-element.1172), channel_id=1, source_target_pairs={{0,4},{4,8},{8,12},{12,16},{16,20},{20,24},{24,28},{28,32},{32,36}... | collective-permute-start | bytes 196616 | tf_op jit(solution)/shard_map/ppermute | solution.py:24
  344.4 7.0 %collective-permute-start.67 = (f32[1,8,8,256]{3,0,2,1:T(1,128)S(1)}, f32[1,8,8,256]{3,0,2,1:T(1,128)S(1)}, u32[]{:S(2)}, u32[]{:S(2)}) collective-permute-start(f32[1,8,8,256]{3,0,2,1:T(1,128)S(1)} %get-tuple-element.1173), channel_id=1, source_target_pairs={{0,124},{4,0},{8,4},{12,8},{16,12},{20,16},{24,20},{28,24},{32,28}... | collective-permute-start | bytes 196616 | tf_op jit(solution)/shard_map/ppermute | solution.py:24
  352.3 5.9 %collective-permute-start.68 = (f32[2,1,8,8,64]{4,0,3,2,1:T(2,128)S(1)}, f32[2,1,8,8,64]{4,0,3,2,1:T(2,128)S(1)}, u32[]{:S(2)}, u32[]{:S(2)}) collective-permute-start(f32[2,1,8,8,64]{4,0,3,2,1:T(2,128)S(1)} %get-tuple-element.1289), channel_id=1, source_target_pairs={{0,1},{1,2},{2,3},{3,0},{4,5},{5,6},{6,7},{7,4},{8,9},{9,10},{10,1... | collective-permute-start | bytes 98312 | tf_op jit(solution)/shard_map/ppermute | solution.py:33
  361.5 4.8 %collective-permute-start.71 = (f32[1024]{0:T(1024)S(1)}, f32[1024]{0:T(1024)S(1)}, u32[]{:S(2)}, u32[]{:S(2)}) collective-permute-start(f32[1024]{0:T(1024)S(1)} %reshape_squeeze.113), channel_id=1, source_target_pairs={{0,1},{1,2},{2,3},{3,0},{4,5},{5,6},{6,7},{7,4},{8,9},{9,10},{10,1... | collective-permute-start | bytes 12296 | tf_op jit(solution)/shard_map/ppermute | solution.py:24
  368.6 9.8 %collective-permute-start.72 = (f32[1,8,8,256]{3,1,2,0:T(8,128)S(1)}, f32[1,8,8,256]{3,1,2,0:T(8,128)S(1)}, u32[]{:S(2)}, u32[]{:S(2)}) collective-permute-start(f32[1,8,8,256]{3,1,2,0:T(8,128)S(1)} %get-tuple-element.1163), channel_id=1, source_target_pairs={{0,4},{4,8},{8,12},{12,16},{16,20},{20,24},{24,28},{28,32},{32,36}... | collective-permute-start | bytes 196616 | tf_op jit(solution)/shard_map/ppermute | solution.py:24
  368.7 9.4 %collective-permute-start.76 = (f32[1024]{0:T(1024)S(1)}, f32[1024]{0:T(1024)S(1)}, u32[]{:S(2)}, u32[]{:S(2)}) collective-permute-start(f32[1024]{0:T(1024)S(1)} %reshape_squeeze.114), channel_id=1, source_target_pairs={{0,1},{1,2},{2,3},{3,0},{4,5},{5,6},{6,7},{7,4},{8,9},{9,10},{10,1... | collective-permute-start | bytes 12296 | tf_op jit(solution)/shard_map/ppermute | solution.py:24
  369.3 8.9 %collective-permute-start.77 = (f32[1024]{0:T(1024)S(1)}, f32[1024]{0:T(1024)S(1)}, u32[]{:S(2)}, u32[]{:S(2)}) collective-permute-start(f32[1024]{0:T(1024)S(1)} %reshape_squeeze.115), channel_id=1, source_target_pairs={{0,3},{1,0},{2,1},{3,2},{4,7},{5,4},{6,5},{7,6},{8,11},{9,8},{10,9... | collective-permute-start | bytes 12296 | tf_op jit(solution)/shard_map/ppermute | solution.py:24
  373.6 6.4 %collective-permute-start.73 = (f32[1,8,8,256]{3,1,2,0:T(8,128)S(1)}, f32[1,8,8,256]{3,1,2,0:T(8,128)S(1)}, u32[]{:S(2)}, u32[]{:S(2)}) collective-permute-start(f32[1,8,8,256]{3,1,2,0:T(8,128)S(1)} %get-tuple-element.1164), channel_id=1, source_target_pairs={{0,124},{4,0},{8,4},{12,8},{16,12},{20,16},{24,20},{28,24},{32,28}... | collective-permute-start | bytes 196616 | tf_op jit(solution)/shard_map/ppermute | solution.py:24
  380.4 5.5 %collective-permute-start.74 = (f32[2,1,8,8,64]{4,2,3,1,0:T(8,128)S(1)}, f32[2,1,8,8,64]{4,2,3,1,0:T(8,128)S(1)}, u32[]{:S(2)}, u32[]{:S(2)}) collective-permute-start(f32[2,1,8,8,64]{4,2,3,1,0:T(8,128)S(1)} %get-tuple-element.1287), channel_id=1, source_target_pairs={{0,1},{1,2},{2,3},{3,0},{4,5},{5,6},{6,7},{7,4},{8,9},{9,10},{10,1... | collective-permute-start | bytes 98312 | tf_op jit(solution)/shard_map/ppermute | solution.py:33
  411.6 7.1 %collective-permute-start.78 = (f32[1,8,8,256]{3,1,2,0:T(8,128)S(1)}, f32[1,8,8,256]{3,1,2,0:T(8,128)S(1)}, u32[]{:S(2)}, u32[]{:S(2)}) collective-permute-start(f32[1,8,8,256]{3,1,2,0:T(8,128)S(1)} %get-tuple-element.1154), channel_id=1, source_target_pairs={{0,4},{4,8},{8,12},{12,16},{16,20},{20,24},{24,28},{28,32},{32,36}... | collective-permute-start | bytes 196616 | tf_op jit(solution)/shard_map/ppermute | solution.py:24
  411.7 7.0 %collective-permute-start.79 = (f32[1,8,8,256]{3,1,2,0:T(8,128)S(1)}, f32[1,8,8,256]{3,1,2,0:T(8,128)S(1)}, u32[]{:S(2)}, u32[]{:S(2)}) collective-permute-start(f32[1,8,8,256]{3,1,2,0:T(8,128)S(1)} %get-tuple-element.1155), channel_id=1, source_target_pairs={{0,124},{4,0},{8,4},{12,8},{16,12},{20,16},{24,20},{28,24},{32,28}... | collective-permute-start | bytes 196616 | tf_op jit(solution)/shard_map/ppermute | solution.py:24
  418.8 5.5 %collective-permute-start.80 = (f32[2,1,8,8,64]{4,2,3,1,0:T(8,128)S(1)}, f32[2,1,8,8,64]{4,2,3,1,0:T(8,128)S(1)}, u32[]{:S(2)}, u32[]{:S(2)}) collective-permute-start(f32[2,1,8,8,64]{4,2,3,1,0:T(8,128)S(1)} %get-tuple-element.1285), channel_id=1, source_target_pairs={{0,1},{1,2},{2,3},{3,0},{4,5},{5,6},{6,7},{7,4},{8,9},{9,10},{10,1... | collective-permute-start | bytes 98312 | tf_op jit(solution)/shard_map/ppermute | solution.py:33
  425.1 4.8 %collective-permute-start.83 = (f32[1024]{0:T(1024)S(1)}, f32[1024]{0:T(1024)S(1)}, u32[]{:S(2)}, u32[]{:S(2)}) collective-permute-start(f32[1024]{0:T(1024)S(1)} %reshape_squeeze.117), channel_id=1, source_target_pairs={{0,1},{1,2},{2,3},{3,0},{4,5},{5,6},{6,7},{7,4},{8,9},{9,10},{10,1... | collective-permute-start | bytes 12296 | tf_op jit(solution)/shard_map/ppermute | solution.py:24
  436.6 7.1 %collective-permute-start.84 = (f32[1,8,8,256]{3,0,2,1:T(1,128)S(1)}, f32[1,8,8,256]{3,0,2,1:T(1,128)S(1)}, u32[]{:S(2)}, u32[]{:S(2)}) collective-permute-start(f32[1,8,8,256]{3,0,2,1:T(1,128)S(1)} %get-tuple-element.1146), channel_id=1, source_target_pairs={{0,4},{4,8},{8,12},{12,16},{16,20},{20,24},{24,28},{28,32},{32,36}... | collective-permute-start | bytes 196616 | tf_op jit(solution)/shard_map/ppermute | solution.py:24
  436.7 7.0 %collective-permute-start.85 = (f32[1,8,8,256]{3,0,2,1:T(1,128)S(1)}, f32[1,8,8,256]{3,0,2,1:T(1,128)S(1)}, u32[]{:S(2)}, u32[]{:S(2)}) collective-permute-start(f32[1,8,8,256]{3,0,2,1:T(1,128)S(1)} %get-tuple-element.1147), channel_id=1, source_target_pairs={{0,124},{4,0},{8,4},{12,8},{16,12},{20,16},{24,20},{28,24},{32,28}... | collective-permute-start | bytes 196616 | tf_op jit(solution)/shard_map/ppermute | solution.py:24
  444.6 5.7 %collective-permute-start.86 = (f32[2,1,8,8,64]{4,0,3,2,1:T(2,128)S(1)}, f32[2,1,8,8,64]{4,0,3,2,1:T(2,128)S(1)}, u32[]{:S(2)}, u32[]{:S(2)}) collective-permute-start(f32[2,1,8,8,64]{4,0,3,2,1:T(2,128)S(1)} %get-tuple-element.1283), channel_id=1, source_target_pairs={{0,1},{1,2},{2,3},{3,0},{4,5},{5,6},{6,7},{7,4},{8,9},{9,10},{10,1... | collective-permute-start | bytes 98312 | tf_op jit(solution)/shard_map/ppermute | solution.py:33
  452.1 4.8 %collective-permute-start.89 = (f32[1024]{0:T(1024)S(1)}, f32[1024]{0:T(1024)S(1)}, u32[]{:S(2)}, u32[]{:S(2)}) collective-permute-start(f32[1024]{0:T(1024)S(1)} %reshape_squeeze.119), channel_id=1, source_target_pairs={{0,1},{1,2},{2,3},{3,0},{4,5},{5,6},{6,7},{7,4},{8,9},{9,10},{10,1... | collective-permute-start | bytes 12296 | tf_op jit(solution)/shard_map/ppermute | solution.py:24
  (44 other events, 218.5 us)
where the time goes:
time: 470 us; the launch traced here: 461 us
  starting transfers between devices  146 us (31%)
  waiting for transfers between devices  105 us (22%)
  local copies, waits for them, and re-layouts  89 us (19%)
  matrix products  79.1 us (17%)
  other arithmetic  33.6 us (7%)
  between operations  8.38 us (2%)
    ppermute x60, starting transfers between devices, from_behind(): return lax.ppermute(value, axis, pairs)  112 us
    dot_general x45, matrix products, contract(): jnp.tensordot(matrix, field, axes=(1, dimension), precision=highest)  79.1 us
    ppermute x60, waiting for transfers between devices, from_behind(): return lax.ppermute(value, axis, pairs)  53.1 us
    ppermute x15, waiting for transfers between devices, padded(): lax.ppermute(lax.slice_in_dim(block, 0, width, axis=dim), axis, backward)  27.3 us
    ppermute x15, starting transfers between devices, padded(): lax.ppermute(lax.slice_in_dim(block, block.shape[dim] - width, None, axis...  24.6 us
    ppermute x15, waiting for transfers between devices, padded(): lax.ppermute(lax.slice_in_dim(block, block.shape[dim] - width, None, axis...  24.4 us
  transfers between devices with their start and end apart: 90, of which 64 were waited for; matrix products, arithmetic and copies ran while one was open for 4% of the time, Pallas kernels for 0%

commit v1 on v0

v1 whole, which is shorter than its diff:
```python
import functools

import jax
import jax.numpy as jnp
import ml_dtypes
import numpy as np
from jax import lax
from jax.experimental import pallas as pl
from jax.experimental.pallas import tpu as pltpu
from jax.sharding import PartitionSpec as P

PTS = 8
CPTS = 4
COLS_DEV = 16
RADIAL = 16
SMOOTH = 2

WIN = 40
LEFT = 10
LANES = WIN * RADIAL
OWN = COLS_DEV * RADIAL
CLASSES = ((0, 0), (0, 1), (1, 0), (1, 1))
EXT = 224
MODES = 256
CHUNKS = ((0, 256), (256, 512), (512, 640))
TILE = 128
TILES = LANES // TILE

cheb_upper = 2.0
cheb_ratio = 0.1
theta = 0.5 * (cheb_upper + cheb_upper * cheb_ratio)
delta = 0.5 * (cheb_upper - cheb_upper * cheb_ratio)
sigma = theta / delta
rho_first = 1.0 / sigma
rho_second = 1.0 / (2.0 * sigma - rho_first)


def legendre_rows(gll_nodes, poly_order):
    values = np.zeros((gll_nodes.size, poly_order + 1))
    values[:, 0] = 1.0
    values[:, 1] = gll_nodes
    for degree in range(2, poly_order + 1):
        values[:, degree] = (
            (2 * degree - 1) * gll_nodes * values[:, degree - 1]
            - (degree - 1) * values[:, degree - 2]
        ) / degree
    return values


def jacobi_eigen(matrix):
    order = matrix.shape[0]
    current = matrix.copy()
    vectors = np.eye(order)
    for sweep in range(12):
        for first in range(order - 1):
            for second in range(first + 1, order):
                off_value = current[first, second]
                spread = current[second, second] - current[first, first]
                sense = np.where(spread >= 0.0, 1.0, -1.0)
                denom = spread + sense * np.sqrt(spread * spread + 4.0 * off_value * off_value)
                denom = np.where(denom == 0.0, 1.0, denom)
                tangent = 2.0 * off_value / denom
                cosine = 1.0 / np.sqrt(1.0 + tangent * tangent)
                sine = tangent * cosine
                rotate = np.eye(order)
                rotate[first, first] = cosine
                rotate[second, second] = cosine
                rotate[first, second] = sine
                rotate[second, first] = -sine
                current = rotate.T @ current @ rotate
                vectors = vectors @ rotate
    diag_ids = np.arange(order)
    return (current[diag_ids, diag_ids].copy(), vectors)


def lobatto(poly_order):
    gll_nodes = np.cos(np.pi * np.arange(poly_order + 1) / poly_order)
    for newton in range(100):
        values = legendre_rows(gll_nodes, poly_order)
        gll_nodes = gll_nodes - (gll_nodes * values[:, poly_order] - values[:, poly_order - 1]) / (
            (poly_order + 1) * values[:, poly_order]
        )
    values = legendre_rows(gll_nodes, poly_order)
    gll_nodes = gll_nodes[::-1].copy()
    top_poly = values[::-1, poly_order].copy()
    weights = 2.0 / (poly_order * (poly_order + 1) * top_poly**2)
    derivative = np.zeros((poly_order + 1, poly_order + 1))
    for row_index in range(poly_order + 1):
        for col_index in range(poly_order + 1):
            if row_index != col_index:
                derivative[row_index, col_index] = top_poly[row_index] / (
                    top_poly[col_index] * (gll_nodes[row_index] - gll_nodes[col_index])
                )
    derivative[0, 0] = -poly_order * (poly_order + 1) / 4.0
    derivative[poly_order, poly_order] = poly_order * (poly_order + 1) / 4.0
    stiffness = derivative.T @ (weights[:, None] * derivative)
    return (gll_nodes, weights, stiffness)


def element_tables():
    fine_nodes, fine_weights, fine_stiff = lobatto(PTS - 1)
    coarse_nodes, coarse_weights, coarse_stiff = lobatto(CPTS - 1)
    interp = np.ones((PTS, CPTS))
    for target_col in range(CPTS):
        for other_col in range(CPTS):
            if other_col != target_col:
                interp[:, target_col] *= (fine_nodes - coarse_nodes[other_col]) / (
                    coarse_nodes[target_col] - coarse_nodes[other_col]
                )
    poly_order = PTS - 1
    node_count = 3 * poly_order + 1
    joined_stiff = np.zeros((node_count, node_count))
    joined_mass = np.zeros(node_count)
    for piece_index in range(3):
        first_node = piece_index * poly_order
        joined_stiff[first_node : first_node + PTS, first_node : first_node + PTS] += fine_stiff
        joined_mass[first_node : first_node + PTS] += fine_weights
    kept = slice(poly_order - 1, 2 * poly_order + 2)
    root_mass = np.sqrt(joined_mass[kept])
    eigen_values, eigen_vectors = jacobi_eigen(
        joined_stiff[kept, kept] / root_mass[:, None] / root_mass[None, :]
    )
    eigen_basis = eigen_vectors / root_mass[:, None]
    coarse_diag = np.diag(coarse_stiff).copy()
    return fine_stiff, fine_weights, eigen_basis, eigen_values, interp, coarse_diag, coarse_weights


def split(table):
    high = table.astype(np.float32).astype(ml_dtypes.bfloat16)
    low = (table - high.astype(np.float64)).astype(np.float32).astype(ml_dtypes.bfloat16)
    return high, low


def kron3(first, second, third):
    return np.kron(first, np.kron(second, third))


def matrices():
    stiff, weights, basis, values, interp, coarse_diag, coarse_weights = element_tables()
    parts = ([], [])
    for mode in range(PTS + 2):
        column = basis[:, mode]
        odd = np.abs(column + column[::-1]).sum() < np.abs(column - column[::-1]).sum()
        parts[int(odd)].append(mode)
    signs = (1.0, -1.0)
    pure = basis.copy()
    for parity in (0, 1):
        for mode in parts[parity]:
            pure[:, mode] = 0.5 * (basis[:, mode] + signs[parity] * basis[::-1, mode])
    center = pure[1:-1, :]
    edges = pure[[0, -1], :]

    def folded(matrix, parity):
        half = PTS // 2
        return 0.5 * (matrix[:half, :half] + signs[parity] * matrix[:half, ::-1][:, :half])

    mass = np.diag(weights)
    halved = np.ones(PTS // 2)
    halved[0] = 0.5
    forward = np.zeros((4, MODES, EXT))
    backward = np.zeros((4, PTS * 16, MODES))
    apply_rows = np.zeros((4, 3 * PTS * 16, PTS * 16))
    mode_values = np.ones((4, MODES, 8))
    for at, (pi, pk) in enumerate(CLASSES):
        ci, ck = center[:4, parts[pi]], center[:4, parts[pk]]
        ei, ek = edges[:1, parts[pi]], edges[:1, parts[pk]]
        count = len(parts[pi]) * len(parts[pk]) * (PTS + 2)
        columns = np.concatenate(
            [
                kron3(ci, ck, center),
                kron3(ei, ck, center),
                kron3(ci, ek, center),
                kron3(ci, ck, edges[:1]),
                kron3(ci, ck, edges[1:]),
            ],
            axis=0,
        )
        forward[at, :count] = columns.T
        backward[at, :, :count] = kron3(halved[:, None] * ci, halved[:, None] * ck, center)
        vi, vk = values[parts[pi]], values[parts[pk]]
        ones = np.ones
        mode_values[at, :count, 0] = kron3(vi, ones(len(vk)), ones(PTS + 2))
        mode_values[at, :count, 1] = kron3(ones(len(vi)), vk, ones(PTS + 2))
        mode_values[at, :count, 2] = kron3(ones(len(vi)), ones(len(vk)), values)
        si, sk = folded(stiff, pi), folded(stiff, pk)
        mi, mk = folded(mass, pi), folded(mass, pk)
        apply_rows[at] = np.concatenate(
            [kron3(si, mk, mass), kron3(mi, sk, mass), kron3(mi, mk, stiff)], axis=0
        )
    mass_up, stiff_up = mass @ interp, stiff @ interp
    prolong = np.concatenate(
        [
            kron3(interp, interp, interp),
            kron3(stiff_up, mass_up, mass_up),
            kron3(mass_up, stiff_up, mass_up),
            kron3(mass_up, mass_up, stiff_up),
        ],
        axis=0,
    )
    restrict = kron3(interp.T, interp.T, interp.T)
    coarse = np.zeros((CPTS**3, 8))
    coarse[:, 0] = kron3(coarse_diag, coarse_weights, coarse_weights)
    coarse[:, 1] = kron3(coarse_weights, coarse_diag, coarse_weights)
    coarse[:, 2] = kron3(coarse_weights, coarse_weights, coarse_diag)

    def pair(table):
        high, low = split(table)
        return jnp.asarray(np.concatenate([high, high], axis=-1)), jnp.asarray(low)

    high, low = split(prolong)
    return {
        "forward": pair(forward),
        "backward": pair(backward),
        "apply": pair(apply_rows),
        "restrict": pair(restrict),
        "prolong": jnp.asarray(np.concatenate([high, high, low], axis=-1)),
        "modes": jnp.asarray(mode_values.reshape(4 * MODES, 8).astype(np.float32)),
        "coarse": jnp.asarray(coarse.astype(np.float32)),
    }


def halves(value):
    high = value.astype(jnp.bfloat16)
    low = (value - high.astype(jnp.float32)).astype(jnp.bfloat16)
    return high, low


def dot(left, right):
    return jnp.dot(left, right, preferred_element_type=jnp.float32)


def turn(value, steps):
    return pltpu.roll(value, steps % value.shape[-1], axis=value.ndim - 1)


def lane_masks(rows):
    radial = lax.broadcasted_iota(jnp.int32, (rows, LANES), 1) % RADIAL
    keep_upper = (radial < RADIAL - 1).astype(jnp.float32)
    keep_lower = (radial > 0).astype(jnp.float32)
    return keep_upper, keep_lower


def point_factor():
    point = lax.broadcasted_iota(jnp.int32, (PTS, LANES), 0)
    radial = lax.broadcasted_iota(jnp.int32, (PTS, LANES), 1) % RADIAL
    shared = ((point == 0) & (radial > 0)) | ((point == PTS - 1) & (radial < RADIAL - 1))
    return jnp.where(shared, 0.5, 1.0)


def side_factor(i, k):
    return (0.5 if i in (0, PTS - 1) else 1.0) * (0.5 if k in (0, PTS - 1) else 1.0)


def block(plane, k):
    start = plane * 64 + k * PTS
    return slice(start, start + PTS)


def load(ref, rows, base=0):
    return jnp.concatenate([ref[base + t, rows, :] for t in range(TILES)], axis=1)


def store(ref, rows, value, base=0, first=0):
    for t in range(value.shape[1] // TILE):
        ref[base + first + t, rows, :] = value[:, t * TILE : (t + 1) * TILE]


def assemble_sides(field, planes):
    keep_upper, keep_lower = lane_masks(PTS)
    for plane in range(planes):
        left = load(field, block(plane, 0))
        right = load(field, block(plane, PTS - 1))
        store(field, block(plane, PTS - 1), right + turn(left, -RADIAL))
        store(field, block(plane, 0), left + turn(right, RADIAL))
    for plane in range(planes):
        inner_at = pl.ds(plane * 64, PTS, stride=PTS)
        outer_at = pl.ds(plane * 64 + PTS - 1, PTS, stride=PTS)
        inner = load(field, inner_at)
        outer = load(field, outer_at)
        store(field, outer_at, outer + turn(inner, -1) * keep_upper)
        store(field, inner_at, inner + turn(outer, 1) * keep_lower)


def fold(a, b, c, d):
    sum_k, diff_k = a + b, a - b
    sum_m, diff_m = c + d, c - d
    return sum_k + sum_m, sum_k - sum_m, diff_k + diff_m, diff_k - diff_m


def pack(parts, packed, rows):
    for c in range(4):
        for t in range(TILES):
            lanes = slice(t * TILE, (t + 1) * TILE)
            high, low = halves(parts[c * TILES + t, 0:rows, :])
            packed[c, 0:rows, lanes] = high
            packed[c, rows : 2 * rows, lanes] = low


def unfold(parts, at):
    ss, sa, as_, aa = (load(parts, at, c * TILES) for c in range(4))
    sum_k, sum_m = ss + sa, ss - sa
    diff_k, diff_m = as_ + aa, as_ - aa
    return sum_k + diff_k, sum_k - diff_k, sum_m + diff_m, sum_m - diff_m


def mirrored(i, k):
    return (i, k), (PTS - 1 - i, k), (i, PTS - 1 - k), (PTS - 1 - i, PTS - 1 - k)


def tables_kernel(geo, modes, lam, coef):
    la, lb, lz = (jnp.broadcast_to(geo[n : n + 1], (PTS, LANES)) for n in range(3))
    cz = la * lb / (2.0 * lz)
    ca = lz * lb / (2.0 * la)
    cb = lz * la / (2.0 * lb)
    coef[0:8] = cz
    coef[8:16] = ca
    coef[16:24] = cb

    def rows(at, carry):
        here = pl.ds(pl.multiple_of(at * 8, 8), 8)
        mu = modes[here, :]
        lam[here, :] = 1.0 / (cz * mu[:, 0:1] + ca * mu[:, 1:2] + cb * mu[:, 2:3])
        return carry

    lax.fori_loop(0, 4 * MODES // 8, rows, 0)


def window_kernel(rot, left, own, right, geo, field, up, down):
    factor = point_factor()
    for case in range(4):

        @pl.when(rot[0] == case)
        def _(case=case):
            shift = (COLS_DEV - LEFT - case) * RADIAL

            for i in range(PTS):
                for k in range(PTS):
                    here = block(i, k)
                    joined = jnp.concatenate([left[here], own[here], right[here]], axis=1)
                    value = turn(joined, -shift)[:, :LANES]
                    field[here] = value * (factor * side_factor(i, k))

    up[0:128] = field[384:512]
    down[0:128] = field[0:128]
    length = jnp.broadcast_to(geo[2:3], (PTS, LANES))
    up[128:136] = length
    down[128:136] = length


def solve_kernel(
    field, below, above, lam, fwd, fwd_low, bwd, bwd_low, share, out, up, down, ext, parts, packed, modes
):
    store(ext, slice(0, 64), below[0:64])
    store(ext, slice(64, 128), field[0:64] + below[64:128])
    for i in range(1, PTS - 1):
        store(ext, slice(i * 64 + 64, i * 64 + 128), field[i * 64 : i * 64 + 64])
    store(ext, slice(512, 576), field[448:512] + above[0:64])
    store(ext, slice(576, 640), above[64:128])
    assemble_sides(ext, PTS + 2)
    factor = point_factor()
    for i in range(PTS):
        for k in range(PTS):
            share[block(i, k)] = load(ext, block(i + 1, k)) * (factor * side_factor(i, k))

    def put(at, values):
        for c in range(4):
            store(parts, at, values[c], c * TILES)

    for i in range(4):
        for k in range(4):
            put(block(0, i * 4 + k), fold(*(load(ext, block(p + 1, q)) for p, q in mirrored(i, k))))
    for k in range(4):
        put(
            block(2, k),
            fold(*(load(ext, block(p, q)) for p, q in ((0, k), (9, k), (0, 7 - k), (9, 7 - k)))),
        )
    for i in range(4):
        before = [turn(load(ext, block(p + 1, PTS - 2)), RADIAL) for p in (i, 7 - i)]
        after = [turn(load(ext, block(p + 1, 1)), -RADIAL) for p in (i, 7 - i)]
        put(block(2, 4 + i), fold(*before, *after))
    keep_upper, keep_lower = lane_masks(16)
    for c in range(4):
        base = c * TILES
        lower = load(parts, pl.ds(PTS - 2, 16, stride=PTS), base)
        upper = load(parts, pl.ds(1, 16, stride=PTS), base)
        store(parts, slice(192, 208), turn(lower, 1) * keep_lower, base)
        store(parts, slice(208, 224), turn(upper, -1) * keep_upper, base)
    pack(parts, packed, EXT)
    for c in range(4):
        for start, stop in CHUNKS:
            spectrum = dot(fwd[c], packed[c, :, start:stop])
            spectrum = spectrum + dot(fwd_low[c], packed[c, 0:EXT, start:stop])
            spectrum = spectrum * lam[c * MODES : (c + 1) * MODES, start:stop]
            modes[0:MODES, start:stop], modes[MODES:, start:stop] = halves(spectrum)
        for start, stop in CHUNKS:
            value = dot(bwd[c], modes[:, start:stop])
            value = value + dot(bwd_low[c], modes[0:MODES, start:stop])
            store(parts, slice(0, 128), value, c * TILES, start // TILE)
    for i in range(4):
        for k in range(4):
            values = unfold(parts, block(0, i * 4 + k))
            for (p, q), value in zip(mirrored(i, k), values):
                out[block(p, q)] = value * factor
    up[...] = out[448:512]
    down[...] = out[0:64]


def step_kernel(kind, *refs):
    take = iter(refs)
    local, below, above = next(take), next(take), next(take)
    before = next(take) if kind in (1, 3) else None
    total = next(take) if kind != 0 else None
    share, coef, app, app_low = (next(take) for _ in range(4))
    res, res_low = (next(take), next(take)) if kind == 1 else (None, None)
    step = next(take) if kind in (0, 2) else None
    sum_out = next(take) if kind != 0 else None
    field, up, down = next(take), next(take), next(take)
    coarse = next(take) if kind == 1 else None
    ext, parts, packed = next(take), next(take), next(take)
    wide = next(take) if kind == 1 else None
    store(ext, slice(0, 64), local[0:64] + below[...])
    for i in range(1, PTS - 1):
        store(ext, slice(i * 64, i * 64 + 64), local[i * 64 : i * 64 + 64])
    store(ext, slice(448, 512), local[448:512] + above[...])
    assemble_sides(ext, PTS)
    for i in range(PTS):
        here = slice(i * 64, i * 64 + 64)
        value = load(ext, here)
        if kind in (0, 2):
            value = value * (1.0 / theta)
            step[here] = value
        else:
            value = before[here] * (rho_second * rho_first) + value * (2.0 * rho_second / delta)
        store(ext, here, value)
        if kind != 0:
            sum_out[here] = total[here] + value
    for i in range(4):
        for k in range(4):
            values = fold(*(load(ext, block(p, q)) for p, q in mirrored(i, k)))
            for c in range(4):
                store(parts, block(0, i * 4 + k), values[c], c * TILES)
    pack(parts, packed, 128)
    for c in range(4):
        for start, stop in CHUNKS:
            terms = dot(app[c], packed[c, :, start:stop])
            terms = terms + dot(app_low[c], packed[c, 0:128, start:stop])
            terms = terms.reshape(3, 16, PTS, stop - start)
            value = (
                terms[0] * coef[0:8, start:stop]
                + terms[1] * coef[8:16, start:stop]
                + terms[2] * coef[16:24, start:stop]
            )
            store(parts, slice(0, 128), value.reshape(128, stop - start), c * TILES, start // TILE)
    for i in range(4):
        for k in range(4):
            values = unfold(parts, block(0, i * 4 + k))
            for (p, q), value in zip(mirrored(i, k), values):
                field[block(p, q)] = share[block(p, q)] - value
    if kind == 1:
        wide[0:512], wide[512:1024] = halves(field[...])
        for start, stop in CHUNKS:
            value = dot(res[...], wide[:, start:stop])
            coarse[:, start:stop] = value + dot(res_low[...], wide[0:512, start:stop])
        up[...] = coarse[48:64]
        down[...] = coarse[0:16]
    elif kind == 3:
        up[...] = field[448:512]
        down[...] = field[0:64]
    else:
        up[...] = field[384:512]
        down[...] = field[0:128]


def assemble_coarse(value):
    row = lax.broadcasted_iota(jnp.int32, (64, LANES), 0)
    keep_upper, keep_lower = lane_masks(64)
    first = (row % 16) < 4
    last = (row % 16) >= 12
    over = pltpu.roll(turn(value, -RADIAL), 12, axis=0)
    under = pltpu.roll(turn(value, RADIAL), 64 - 12, axis=0)
    value = value + jnp.where(last, over, 0.0) + jnp.where(first, under, 0.0)
    first = (row % 4) == 0
    last = (row % 4) == 3
    over = pltpu.roll(turn(value, -1) * keep_upper, 3, axis=0)
    under = pltpu.roll(turn(value, 1) * keep_lower, 64 - 3, axis=0)
    return value + jnp.where(last, over, 0.0) + jnp.where(first, under, 0.0)


def coarse_kernel(
    local, below, above, lower, upper, geo, coef, table, prolong, total, field, sum_out, out, up, down, packed
):
    value = local[...]
    value = jnp.concatenate([value[0:16] + below[...], value[16:48], value[48:64] + above[...]])
    value = assemble_coarse(value)
    la, lb = geo[0:1], geo[1:2]

    def diagonal(lz, rows):
        return (
            la * lb / (2.0 * lz) * table[rows, 0:1]
            + lz * lb / (2.0 * la) * table[rows, 1:2]
            + lz * la / (2.0 * lb) * table[rows, 2:3]
        )

    scale = diagonal(geo[2:3], slice(0, 64))
    scale = jnp.concatenate(
        [
            scale[0:16] + diagonal(lower[128:129], slice(48, 64)),
            scale[16:48],
            scale[48:64] + diagonal(upper[128:129], slice(0, 16)),
        ]
    )
    value = value / assemble_coarse(scale)
    high, low = halves(value)
    packed[0:64] = high
    packed[64:128] = low
    packed[128:192] = high
    for start, stop in CHUNKS:
        for i in range(PTS):
            here = slice(i * 64, i * 64 + 64)
            sides = (8, PTS, stop - start)
            terms = [
                dot(prolong[n * 512 + i * 64 : n * 512 + i * 64 + 64], packed[:, start:stop]) for n in range(4)
            ]
            sum_out[here, start:stop] = total[here, start:stop] + terms[0]
            value = (
                terms[1].reshape(sides) * coef[0:8, start:stop]
                + terms[2].reshape(sides) * coef[8:16, start:stop]
                + terms[3].reshape(sides) * coef[16:24, start:stop]
            )
            out[here, start:stop] = field[here, start:stop] - value.reshape(64, stop - start)
    up[...] = out[384:512]
    down[...] = out[0:128]


def finish_kernel(rot, local, below, above, total, sol, res, ext):
    store(ext, slice(0, 64), local[0:64] + below[...])
    for i in range(1, PTS - 1):
        store(ext, slice(i * 64, i * 64 + 64), local[i * 64 : i * 64 + 64])
    store(ext, slice(448, 512), local[448:512] + above[...])
    assemble_sides(ext, PTS)
    for case in range(4):

        @pl.when(rot[0] == case)
        def _(case=case):
            start = (LEFT + case) * RADIAL
            for plane in range(PTS):
                here = slice(plane * 64, plane * 64 + 64)
                sol[here] = total[here, start : start + OWN]
                res[here] = load(ext, here)[:, start : start + OWN]


def call(kernel, name, args, outs, scratch=(), scalars=0, flops=0):
    shape = lambda rows, lanes=LANES: jax.ShapeDtypeStruct((rows, lanes), jnp.float32)
    in_specs = [
        pl.BlockSpec(memory_space=pltpu.SMEM if n < scalars else pltpu.VMEM) for n in range(len(args))
    ]
    return pl.pallas_call(
        kernel,
        out_shape=[shape(*out) if isinstance(out, tuple) else shape(out) for out in outs],
        in_specs=in_specs,
        out_specs=[pl.BlockSpec(memory_space=pltpu.VMEM) for _ in outs],
        scratch_shapes=list(scratch),
        name=name,
        cost_estimate=pl.CostEstimate(flops=flops, bytes_accessed=8_000_000, transcendentals=0),
        compiler_params=pltpu.CompilerParams(vmem_limit_bytes=40 * 1024 * 1024),
    )(*args)


def per_device(rhs, spacing_z, spacing_a, spacing_b, rotation):
    mats = matrices()
    group = lax.axis_index("grp")
    member = lax.axis_index("sub")
    groups = lax.axis_size("grp")
    members = lax.axis_size("sub")
    wide, narrow = jnp.float32, jnp.bfloat16
    vmem = pltpu.VMEM

    def shifted(value, axis, count, steps):
        return lax.ppermute(value, axis, [(n, (n + steps) % count) for n in range(count)])

    def neighbours(up, down):
        return shifted(up, "grp", groups, 1), shifted(down, "grp", groups, -1)

    own = rhs.reshape(512, OWN)
    left = shifted(own, "sub", members, 1)
    right = shifted(own, "sub", members, -1)
    rot = lax.dynamic_slice(rotation, (group,), (1,))
    ring = jnp.concatenate([spacing_a, spacing_a, spacing_a])
    columns = lax.dynamic_slice(ring, (spacing_a.shape[0] + member * COLS_DEV - LEFT,), (WIN,))
    geo = jnp.stack(
        [
            jnp.repeat(columns, RADIAL),
            jnp.tile(spacing_b, WIN),
            jnp.broadcast_to(spacing_z, (LANES,)),
        ]
    )
    geo = jnp.concatenate([geo, jnp.ones((5, LANES), wide)])
    lam, coef = call(tables_kernel, "tables", (geo, mats["modes"]), (4 * MODES, 24))
    field, up, down = call(
        window_kernel, "window", (rot, left, own, right, geo), (512, 136, 136), scalars=1
    )

    def solve(field, below, above):
        return call(
            solve_kernel,
            "solve",
            (field, below, above, lam, *mats["forward"], *mats["backward"]),
            (512, 512, 64, 64),
            (
                vmem((TILES, 640, TILE), wide),
                vmem((4 * TILES, EXT, TILE), wide),
                vmem((4, 2 * EXT, LANES), narrow),
                vmem((2 * MODES, LANES), narrow),
            ),
        )

    def advance(kind, args, outs):
        scratch = [
            vmem((TILES, 512, TILE), wide),
            vmem((4 * TILES, 128, TILE), wide),
            vmem((4, 256, LANES), narrow),
        ]
        if kind == 1:
            scratch.append(vmem((1024, LANES), narrow))
        return call(functools.partial(step_kernel, kind), f"step{kind}", args, outs, scratch)

    lower, upper = neighbours(up, down)
    share, local, up, down = solve(field, lower, upper)
    below, above = neighbours(up, down)
    total, field, up, down = advance(
        0, (local, below, above, share, coef, *mats["apply"]), (512, 512, 128, 128)
    )
    below, above = neighbours(up, down)
    share, local, up, down = solve(field, below, above)
    below, above = neighbours(up, down)
    total, field, up, down, coarse = advance(
        1,
        (local, below, above, total, total, share, coef, *mats["apply"], *mats["restrict"]),
        (512, 512, 16, 16, 64),
    )
    below, above = neighbours(up, down)
    total, field, up, down = call(
        coarse_kernel,
        "coarse",
        (coarse, below, above, lower, upper, geo, coef, mats["coarse"], mats["prolong"], total, field),
        (512, 512, 128, 128),
        (vmem((192, LANES), narrow),),
    )
    below, above = neighbours(up, down)
    share, local, up, down = solve(field, below, above)
    below, above = neighbours(up, down)
    step, total, field, up, down = advance(
        2, (local, below, above, total, share, coef, *mats["apply"]), (512, 512, 512, 128, 128)
    )
    below, above = neighbours(up, down)
    share, local, up, down = solve(field, below, above)
    below, above = neighbours(up, down)
    total, field, up, down = advance(
        3, (local, below, above, step, total, share, coef, *mats["apply"]), (512, 512, 64, 64)
    )
    below, above = neighbours(up, down)
    sol, res = call(
        finish_kernel,
        "finish",
        (rot, field, below, above, total),
        ((512, OWN), (512, OWN)),
        (vmem((TILES, 512, TILE), wide),),
        scalars=1,
    )
    return sol.reshape(rhs.shape), res.reshape(rhs.shape)


def solution(mesh):
    return jax.shard_map(
        per_device,
        mesh=mesh,
        in_specs=(P(None, None, None, ("grp", "sub")), P("grp"), P(), P(), P()),
        out_specs=(P(None, None, None, ("grp", "sub")), P(None, None, None, ("grp", "sub"))),
        check_vma=False,
    )
```

time: 470 us -> 145 us (0.31)
  the two profiles are of different devices: /device:TPU:0 before, /device:TPU:31 now
where the time goes in v1:
time: 145 us
  waiting for transfers between devices  83.5 us (58%)
  Pallas kernels  38.3 us (26%)
  starting transfers between devices  15.5 us (11%)
  local copies, waits for them, and re-layouts  5.42 us (4%)
  between operations  1.53 us (1%)
    ppermute x22, waiting for transfers between devices, shifted(): lax.ppermute(value, axis, [(n, (n + steps) % count) for n in range(count)])  83.5 us
    pallas_call x12, Pallas kernels, call(): pl.pallas_call(kernel, out_shape=[shape(*out) if isinstance(out, tuple) e...  38.3 us
    ppermute x22, starting transfers between devices, shifted(): lax.ppermute(value, axis, [(n, (n + steps) % count) for n in range(count)])  15.5 us
    unnamed x26, local copies, waits for them, and re-layouts  3.07 us
  transfers between devices with their start and end apart: 22, of which 20 were waited for; matrix products, arithmetic and copies ran while one was open for 2% of the time, Pallas kernels for 7%

profile of v1, /device:TPU:31, one launch (start us, length us, event | category | flops | bytes accessed | tf_op | source)
XLA Modules:
  0.0 145.1 jit_solution(1969885865091623468)
XLA Ops:
  0.7 3.8 %collective-permute-start.1 = (f32[512,256]{1,0:T(8,128)}, f32[512,256]{1,0:T(8,128)S(1)}, u32[]{:S(2)}, u32[]{:S(2)}) collective-permute-start(f32[512,256]{1,0:T(8,128)} %bitcast.4), channel_id=1, source_target_pairs={{0,3},{1,0},{2,1},{3,2},{4,7},{5,4},{6,5},{7,6},{8,11},{9,8},{10,9... | collective-permute-start | bytes 1572872 | tf_op jit(solution)/shard_map/ppermute | solution.py:579
  5.1 0.1 pad.2.clone
  5.2 0.1 pad.3.clone
  5.3 0.8 pad_maximum_fusion
  6.1 0.1 dynamic_slice.7
  6.2 0.1 broadcast_in_dim.6
  6.3 0.1 stack_reshape.3
  6.4 0.7 tile.2
  7.0 0.1 stack_tile.3
  7.1 1.2 dynamic_slice.6.rot
  8.4 7.0 %collective-permute-done.1.right = f32[512,256]{1,0:T(8,128)S(1)} collective-permute-done((f32[512,256]{1,0:T(8,128)}, f32[512,256]{1,0:T(8,128)S(1)}, u32[]{:S(2)}, u32[]{:S(2)}) %collective-permute-start.1) | collective-permute-done | bytes 524320 | tf_op jit(solution)/shard_map/ppermute | solution.py:579
  15.4 3.0 %collective-permute-done.left = f32[512,256]{1,0:T(8,128)S(1)} collective-permute-done((f32[512,256]{1,0:T(8,128)}, f32[512,256]{1,0:T(8,128)S(1)}, u32[]{:S(2)}, u32[]{:S(2)}) %collective-permute-start) | collective-permute-done | bytes 524320 | tf_op jit(solution)/shard_map/ppermute | solution.py:579
  18.4 1.0 copy-done.8
  19.4 1.1 window.1
  20.5 1.7 %collective-permute-start.2 = (f32[136,640]{1,0:T(8,128)S(1)}, f32[136,640]{1,0:T(8,128)S(1)}, u32[]{:S(2)}, u32[]{:S(2)}) collective-permute-start(f32[136,640]{1,0:T(8,128)S(1)} %get-tuple-element.48), channel_id=1, source_target_pairs={{0,4},{4,8},{8,12},{12,16},{16,20},{20,24},{24,28},{28,32},{32,36}... | collective-permute-start | bytes 1044488 | tf_op jit(solution)/shard_map/ppermute | solution.py:579
  22.2 0.3 collective-permute-start.3
  22.5 1.0 copy-done.9
  23.6 10.7 %tables.1 = (f32[1024,640]{1,0:T(8,128)S(1)}, f32[24,640]{1,0:T(8,128)S(1)}) custom-call(f32[8,640]{1,0:T(8,128)S(1)} %maximum_maximum_fusion.geo, f32[1024,8]{1,0:T(8,128)S(1)} %copy-done.9), custom_call_target="tpu_custom_call" | custom-call | bytes 8000000 | tf_op jit(solution)/shard_map/tables/pallas_call | solution.py:557
  34.3 0.9 copy-done.5
  35.3 3.3 %solve.4 = (f32[512,640]{1,0:T(8,128)S(1)}, f32[512,640]{1,0:T(8,128)S(1)}, f32[64,640]{1,0:T(8,128)S(1)}, f32[64,640]{1,0:T(8,128)S(1)}) custom-call(f32[512,640]{1,0:T(8,128)S(1)} %get-tuple-element.47.field, f32[136,640]{1,0:T(8,128)S(1)} %collective-permute-done.2.below.lower, f32[136,640]{1,0:T(8,128)S(1)} %collective-permute-done.3.above.upper, ...), custom_call_target="tpu_custom_call" | custom-call | bytes 8000000 | tf_op jit(solution)/shard_map/solve/pallas_call | solution.py:557
  38.5 4.8 %collective-permute-start.4 = (f32[64,640]{1,0:T(8,128)S(1)}, f32[64,640]{1,0:T(8,128)S(1)}, u32[]{:S(2)}, u32[]{:S(2)}) collective-permute-start(f32[64,640]{1,0:T(8,128)S(1)} %get-tuple-element.52), channel_id=1, source_target_pairs={{0,4},{4,8},{8,12},{12,16},{16,20},{20,24},{24,28},{28,32},{32,36}... | collective-permute-start | bytes 491528 | tf_op jit(solution)/shard_map/ppermute | solution.py:579
  43.3 2.3 %collective-permute-done.4.refs_1_ = f32[64,640]{1,0:T(8,128)S(1)} collective-permute-done((f32[64,640]{1,0:T(8,128)S(1)}, f32[64,640]{1,0:T(8,128)S(1)}, u32[]{:S(2)}, u32[]{:S(2)}) %collective-permute-start.4) | collective-permute-done | bytes 163872 | tf_op jit(solution)/shard_map/ppermute | solution.py:579
  45.6 5.8 %collective-permute-done.5.refs_2_ = f32[64,640]{1,0:T(8,128)S(1)} collective-permute-done((f32[64,640]{1,0:T(8,128)S(1)}, f32[64,640]{1,0:T(8,128)S(1)}, u32[]{:S(2)}, u32[]{:S(2)}) %collective-permute-start.5) | collective-permute-done | bytes 163872 | tf_op jit(solution)/shard_map/ppermute | solution.py:579
  51.4 2.0 %step0.1 = (f32[512,640]{1,0:T(8,128)S(1)}, f32[512,640]{1,0:T(8,128)S(1)}, f32[128,640]{1,0:T(8,128)S(1)}, f32[128,640]{1,0:T(8,128)S(1)}) custom-call(f32[512,640]{1,0:T(8,128)S(1)} %get-tuple-element.51.refs_0_, f32[64,640]{1,0:T(8,128)S(1)} %collective-permute-done.4.refs_1_, f32[64,640]{1,0:T(8,128)S(1)} %collective-permute-done.5.refs_2_, ...), custom_call_target="tpu_custom_call" | custom-call | bytes 8000000 | tf_op jit(solution)/shard_map/step0/pallas_call | solution.py:557
  53.4 0.1 collective-permute-start.6
  53.5 0.5 collective-permute-start.7
  54.0 3.5 %collective-permute-done.6.below = f32[128,640]{1,0:T(8,128)S(1)} collective-permute-done((f32[128,640]{1,0:T(8,128)S(1)}, f32[128,640]{1,0:T(8,128)S(1)}, u32[]{:S(2)}, u32[]{:S(2)}) %collective-permute-start.6) | collective-permute-done | bytes 327712 | tf_op jit(solution)/shard_map/ppermute | solution.py:579
  57.5 6.0 %collective-permute-done.7.above = f32[128,640]{1,0:T(8,128)S(1)} collective-permute-done((f32[128,640]{1,0:T(8,128)S(1)}, f32[128,640]{1,0:T(8,128)S(1)}, u32[]{:S(2)}, u32[]{:S(2)}) %collective-permute-start.7) | collective-permute-done | bytes 327712 | tf_op jit(solution)/shard_map/ppermute | solution.py:579
  63.6 3.2 %solve.5 = (f32[512,640]{1,0:T(8,128)S(1)}, f32[512,640]{1,0:T(8,128)S(1)}, f32[64,640]{1,0:T(8,128)S(1)}, f32[64,640]{1,0:T(8,128)S(1)}) custom-call(f32[512,640]{1,0:T(8,128)S(1)} %get-tuple-element.56.field, f32[128,640]{1,0:T(8,128)S(1)} %collective-permute-done.6.below, f32[128,640]{1,0:T(8,128)S(1)} %collective-permute-done.7.above, ...), custom_call_target="tpu_custom_call" | custom-call | bytes 8000000 | tf_op jit(solution)/shard_map/solve/pallas_call | solution.py:557
  66.8 0.1 collective-permute-start.8
  66.9 0.5 collective-permute-start.9
  67.4 1.8 %collective-permute-done.8.refs_1_ = f32[64,640]{1,0:T(8,128)S(1)} collective-permute-done((f32[64,640]{1,0:T(8,128)S(1)}, f32[64,640]{1,0:T(8,128)S(1)}, u32[]{:S(2)}, u32[]{:S(2)}) %collective-permute-start.8) | collective-permute-done | bytes 163872 | tf_op jit(solution)/shard_map/ppermute | solution.py:579
  69.2 5.9 %collective-permute-done.9.refs_2_ = f32[64,640]{1,0:T(8,128)S(1)} collective-permute-done((f32[64,640]{1,0:T(8,128)S(1)}, f32[64,640]{1,0:T(8,128)S(1)}, u32[]{:S(2)}, u32[]{:S(2)}) %collective-permute-start.9) | collective-permute-done | bytes 163872 | tf_op jit(solution)/shard_map/ppermute | solution.py:579
  75.1 2.6 %step1.1 = (f32[512,640]{1,0:T(8,128)S(1)}, f32[512,640]{1,0:T(8,128)S(1)}, f32[16,640]{1,0:T(8,128)S(1)}, f32[16,640]{1,0:T(8,128)S(1)}, f32[64,640]{1,0:T(8,128)S(1)}) custom-call(f32[512,640]{1,0:T(8,128)S(1)} %get-tuple-element.59.refs_0_, f32[64,640]{1,0:T(8,128)S(1)} %collective-permute-done.8.refs_1_, f32[64,640]{1,0:T(8,128)S(1)} %collective-permute-done.9.refs_2_, ...), custom_call_target="tpu_custom_call" | custom-call | bytes 8000000 | tf_op jit(solution)/shard_map/step1/pallas_call | solution.py:557
  77.6 0.1 collective-permute-start.10
  77.7 0.5 collective-permute-start.11
  78.2 0.7 collective-permute-done.10.below
  78.9 5.6 %collective-permute-done.11.above = f32[16,640]{1,0:T(8,128)S(1)} collective-permute-done((f32[16,640]{1,0:T(8,128)S(1)}, f32[16,640]{1,0:T(8,128)S(1)}, u32[]{:S(2)}, u32[]{:S(2)}) %collective-permute-start.11) | collective-permute-done | bytes 40992 | tf_op jit(solution)/shard_map/ppermute | solution.py:579
  84.5 2.5 %coarse.1 = (f32[512,640]{1,0:T(8,128)S(1)}, f32[512,640]{1,0:T(8,128)S(1)}, f32[128,640]{1,0:T(8,128)S(1)}, f32[128,640]{1,0:T(8,128)S(1)}) custom-call(f32[64,640]{1,0:T(8,128)S(1)} %get-tuple-element.64.local, f32[16,640]{1,0:T(8,128)S(1)} %collective-permute-done.10.below, f32[16,640]{1,0:T(8,128)S(1)} %collective-permute-done.11.above, ...), custom_call_target="tpu_custom_call" | custom-call | bytes 8000000 | tf_op jit(solution)/shard_map/coarse/pallas_call | solution.py:557
  87.0 0.1 collective-permute-start.12
  87.1 0.5 collective-permute-start.13
  87.6 3.5 %collective-permute-done.12.below = f32[128,640]{1,0:T(8,128)S(1)} collective-permute-done((f32[128,640]{1,0:T(8,128)S(1)}, f32[128,640]{1,0:T(8,128)S(1)}, u32[]{:S(2)}, u32[]{:S(2)}) %collective-permute-start.12) | collective-permute-done | bytes 327712 | tf_op jit(solution)/shard_map/ppermute | solution.py:579
  91.1 6.1 %collective-permute-done.13.above = f32[128,640]{1,0:T(8,128)S(1)} collective-permute-done((f32[128,640]{1,0:T(8,128)S(1)}, f32[128,640]{1,0:T(8,128)S(1)}, u32[]{:S(2)}, u32[]{:S(2)}) %collective-permute-start.13) | collective-permute-done | bytes 327712 | tf_op jit(solution)/shard_map/ppermute | solution.py:579
  97.2 3.2 %solve.6 = (f32[512,640]{1,0:T(8,128)S(1)}, f32[512,640]{1,0:T(8,128)S(1)}, f32[64,640]{1,0:T(8,128)S(1)}, f32[64,640]{1,0:T(8,128)S(1)}) custom-call(f32[512,640]{1,0:T(8,128)S(1)} %get-tuple-element.69.field, f32[128,640]{1,0:T(8,128)S(1)} %collective-permute-done.12.below, f32[128,640]{1,0:T(8,128)S(1)} %collective-permute-done.13.above, ...), custom_call_target="tpu_custom_call" | custom-call | bytes 8000000 | tf_op jit(solution)/shard_map/solve/pallas_call | solution.py:557
  100.4 0.1 collective-permute-start.14
  100.5 0.5 collective-permute-start.15
  101.0 1.8 %collective-permute-done.14.refs_1_ = f32[64,640]{1,0:T(8,128)S(1)} collective-permute-done((f32[64,640]{1,0:T(8,128)S(1)}, f32[64,640]{1,0:T(8,128)S(1)}, u32[]{:S(2)}, u32[]{:S(2)}) %collective-permute-start.14) | collective-permute-done | bytes 163872 | tf_op jit(solution)/shard_map/ppermute | solution.py:579
  102.8 5.9 %collective-permute-done.15.refs_2_ = f32[64,640]{1,0:T(8,128)S(1)} collective-permute-done((f32[64,640]{1,0:T(8,128)S(1)}, f32[64,640]{1,0:T(8,128)S(1)}, u32[]{:S(2)}, u32[]{:S(2)}) %collective-permute-start.15) | collective-permute-done | bytes 163872 | tf_op jit(solution)/shard_map/ppermute | solution.py:579
  108.7 2.1 %step2.1 = (f32[512,640]{1,0:T(8,128)S(1)}, f32[512,640]{1,0:T(8,128)S(1)}, f32[512,640]{1,0:T(8,128)S(1)}, f32[128,640]{1,0:T(8,128)S(1)}, f32[128,640]{1,0:T(8,128)S(1)}) custom-call(f32[512,640]{1,0:T(8,128)S(1)} %get-tuple-element.72.refs_0_, f32[64,640]{1,0:T(8,128)S(1)} %collective-permute-done.14.refs_1_, ...), custom_call_target="tpu_custom_call" | custom-call | bytes 8000000 | tf_op jit(solution)/shard_map/step2/pallas_call | solution.py:557
  110.8 0.1 collective-permute-start.16
  110.9 0.5 collective-permute-start.17
  111.4 3.5 %collective-permute-done.16.below = f32[128,640]{1,0:T(8,128)S(1)} collective-permute-done((f32[128,640]{1,0:T(8,128)S(1)}, f32[128,640]{1,0:T(8,128)S(1)}, u32[]{:S(2)}, u32[]{:S(2)}) %collective-permute-start.16) | collective-permute-done | bytes 327712 | tf_op jit(solution)/shard_map/ppermute | solution.py:579
  114.9 5.9 %collective-permute-done.17.above = f32[128,640]{1,0:T(8,128)S(1)} collective-permute-done((f32[128,640]{1,0:T(8,128)S(1)}, f32[128,640]{1,0:T(8,128)S(1)}, u32[]{:S(2)}, u32[]{:S(2)}) %collective-permute-start.17) | collective-permute-done | bytes 327712 | tf_op jit(solution)/shard_map/ppermute | solution.py:579
  120.7 3.3 %solve.7 = (f32[512,640]{1,0:T(8,128)S(1)}, f32[512,640]{1,0:T(8,128)S(1)}, f32[64,640]{1,0:T(8,128)S(1)}, f32[64,640]{1,0:T(8,128)S(1)}) custom-call(f32[512,640]{1,0:T(8,128)S(1)} %get-tuple-element.77.field, f32[128,640]{1,0:T(8,128)S(1)} %collective-permute-done.16.below, f32[128,640]{1,0:T(8,128)S(1)} %collective-permute-done.17.above, ...), custom_call_target="tpu_custom_call" | custom-call | bytes 8000000 | tf_op jit(solution)/shard_map/solve/pallas_call | solution.py:557
  124.0 0.1 collective-permute-start.18
  124.1 0.5 collective-permute-start.19
  124.6 1.8 %collective-permute-done.18.refs_1_ = f32[64,640]{1,0:T(8,128)S(1)} collective-permute-done((f32[64,640]{1,0:T(8,128)S(1)}, f32[64,640]{1,0:T(8,128)S(1)}, u32[]{:S(2)}, u32[]{:S(2)}) %collective-permute-start.18) | collective-permute-done | bytes 163872 | tf_op jit(solution)/shard_map/ppermute | solution.py:579
  126.3 5.9 %collective-permute-done.19.refs_2_ = f32[64,640]{1,0:T(8,128)S(1)} collective-permute-done((f32[64,640]{1,0:T(8,128)S(1)}, f32[64,640]{1,0:T(8,128)S(1)}, u32[]{:S(2)}, u32[]{:S(2)}) %collective-permute-start.19) | collective-permute-done | bytes 163872 | tf_op jit(solution)/shard_map/ppermute | solution.py:579
  132.2 2.2 %step3.1 = (f32[512,640]{1,0:T(8,128)S(1)}, f32[512,640]{1,0:T(8,128)S(1)}, f32[64,640]{1,0:T(8,128)S(1)}, f32[64,640]{1,0:T(8,128)S(1)}) custom-call(f32[512,640]{1,0:T(8,128)S(1)} %get-tuple-element.80.refs_0_, f32[64,640]{1,0:T(8,128)S(1)} %collective-permute-done.18.refs_1_, f32[64,640]{1,0:T(8,128)S(1)} %collective-permute-done.19.refs_2_, ...), custom_call_target="tpu_custom_call" | custom-call | bytes 8000000 | tf_op jit(solution)/shard_map/step3/pallas_call | solution.py:557
  134.4 0.3 collective-permute-start.20
  134.7 0.5 collective-permute-start.21
  135.2 1.8 %collective-permute-done.20.below = f32[64,640]{1,0:T(8,128)S(1)} collective-permute-done((f32[64,640]{1,0:T(8,128)S(1)}, f32[64,640]{1,0:T(8,128)S(1)}, u32[]{:S(2)}, u32[]{:S(2)}) %collective-permute-start.20) | collective-permute-done | bytes 163872 | tf_op jit(solution)/shard_map/ppermute | solution.py:579
  137.0 5.9 %collective-permute-done.21.above = f32[64,640]{1,0:T(8,128)S(1)} collective-permute-done((f32[64,640]{1,0:T(8,128)S(1)}, f32[64,640]{1,0:T(8,128)S(1)}, u32[]{:S(2)}, u32[]{:S(2)}) %collective-permute-start.21) | collective-permute-done | bytes 163872 | tf_op jit(solution)/shard_map/ppermute | solution.py:579
  142.9 2.3 %finish.1 = (f32[512,256]{1,0:T(8,128)}, f32[512,256]{1,0:T(8,128)}) custom-call(s32[1]{0:T(128)} %dynamic_slice.6.rot, f32[512,640]{1,0:T(8,128)S(1)} %get-tuple-element.86.local, f32[64,640]{1,0:T(8,128)S(1)} %collective-permute-done.20.below, f32[64,640]{1,0:T(8,128)S(1)} %collective-permute-done.21.above, f32[512,640]{1,0:T(8,128)S(1)} %get-tuple-element.89.total), custom_call_target="tpu_custom_call" | custom-call | bytes 8000000 | tf_op jit(solution)/shard_map/finish/pallas_call | solution.py:557
  (29 shorter events, 0.1 us)
Async XLA Ops:
  0.6 33.6 %copy-start.2 = (bf16[4,128,512]{2,1,0:T(8,128)(2,1)S(1)}, bf16[4,128,512]{2,1,0:T(8,128)(2,1)}, u32[]{:S(2)}) copy-start(bf16[4,128,512]{2,1,0:T(8,128)(2,1)} %constant.49.clone.bwd) | copy-start | bytes 1572868
  0.6 33.6 %copy-start.3 = (bf16[4,256,224]{2,1,0:T(8,128)(2,1)S(1)}, bf16[4,256,224]{2,1,0:T(8,128)(2,1)}, u32[]{:S(2)}) copy-start(bf16[4,256,224]{2,1,0:T(8,128)(2,1)} %constant.48.clone.fwd_low) | copy-start | bytes 1376260
  0.7 33.6 %copy-start = (bf16[4,256,448]{2,1,0:T(8,128)(2,1)S(1)}, bf16[4,256,448]{2,1,0:T(8,128)(2,1)}, u32[]{:S(2)}) copy-start(bf16[4,256,448]{2,1,0:T(8,128)(2,1)} %constant.47.clone.fwd) | copy-start | bytes 2752516
  0.7 14.7 %collective-permute-start.1 = (f32[512,256]{1,0:T(8,128)}, f32[512,256]{1,0:T(8,128)S(1)}, u32[]{:S(2)}, u32[]{:S(2)}) collective-permute-start(f32[512,256]{1,0:T(8,128)} %bitcast.4), channel_id=1, source_target_pairs={{0,3},{1,0},{2,1},{3,2},{4,7},{5,4},{6,5},{7,6},{8,11},{9,8},{10,9... | collective-permute-start | bytes 1572872 | tf_op jit(solution)/shard_map/ppermute | solution.py:579
  4.5 13.9 %collective-permute-start = (f32[512,256]{1,0:T(8,128)}, f32[512,256]{1,0:T(8,128)S(1)}, u32[]{:S(2)}, u32[]{:S(2)}) collective-permute-start(f32[512,256]{1,0:T(8,128)} %bitcast.5), channel_id=1, source_target_pairs={{0,1},{1,2},{2,3},{3,0},{4,5},{5,6},{6,7},{7,4},{8,9},{9,10},{10,1... | collective-permute-start | bytes 1572872 | tf_op jit(solution)/shard_map/ppermute | solution.py:579
  18.4 1.0 copy-start.8
  20.5 13.7 %collective-permute-start.2 = (f32[136,640]{1,0:T(8,128)S(1)}, f32[136,640]{1,0:T(8,128)S(1)}, u32[]{:S(2)}, u32[]{:S(2)}) collective-permute-start(f32[136,640]{1,0:T(8,128)S(1)} %get-tuple-element.48), channel_id=1, source_target_pairs={{0,4},{4,8},{8,12},{12,16},{16,20},{20,24},{24,28},{28,32},{32,36}... | collective-permute-start | bytes 1044488 | tf_op jit(solution)/shard_map/ppermute | solution.py:579
  22.2 12.0 %collective-permute-start.3 = (f32[136,640]{1,0:T(8,128)S(1)}, f32[136,640]{1,0:T(8,128)S(1)}, u32[]{:S(2)}, u32[]{:S(2)}) collective-permute-start(f32[136,640]{1,0:T(8,128)S(1)} %get-tuple-element.49), channel_id=1, source_target_pairs={{0,124},{4,0},{8,4},{12,8},{16,12},{20,16},{24,20},{28,24},{32,28}... | collective-permute-start | bytes 1044488 | tf_op jit(solution)/shard_map/ppermute | solution.py:579
  22.5 1.0 copy-start.9
  34.3 1.0 copy-start.5
  35.3 16.1 %copy-start.1 = (bf16[4,384,256]{2,1,0:T(8,128)(2,1)S(1)}, bf16[4,384,256]{2,1,0:T(8,128)(2,1)}, u32[]{:S(2)}) copy-start(bf16[4,384,256]{2,1,0:T(8,128)(2,1)} %constant.51.clone.refs_5_.refs_7_.refs_6_) | copy-start | bytes 2359300
  35.3 16.1 %copy-start.4 = (bf16[4,384,128]{2,1,0:T(8,128)(2,1)S(1)}, bf16[4,384,128]{2,1,0:T(8,128)(2,1)}, u32[]{:S(2)}) copy-start(bf16[4,384,128]{2,1,0:T(8,128)(2,1)} %constant.52.clone.refs_6_.refs_8_.refs_7_) | copy-start | bytes 1179652
  38.5 7.1 %collective-permute-start.4 = (f32[64,640]{1,0:T(8,128)S(1)}, f32[64,640]{1,0:T(8,128)S(1)}, u32[]{:S(2)}, u32[]{:S(2)}) collective-permute-start(f32[64,640]{1,0:T(8,128)S(1)} %get-tuple-element.52), channel_id=1, source_target_pairs={{0,4},{4,8},{8,12},{12,16},{16,20},{20,24},{24,28},{28,32},{32,36}... | collective-permute-start | bytes 491528 | tf_op jit(solution)/shard_map/ppermute | solution.py:579
  43.3 8.1 %collective-permute-start.5 = (f32[64,640]{1,0:T(8,128)S(1)}, f32[64,640]{1,0:T(8,128)S(1)}, u32[]{:S(2)}, u32[]{:S(2)}) collective-permute-start(f32[64,640]{1,0:T(8,128)S(1)} %get-tuple-element.53), channel_id=1, source_target_pairs={{0,124},{4,0},{8,4},{12,8},{16,12},{20,16},{24,20},{28,24},{32,28}... | collective-permute-start | bytes 491528 | tf_op jit(solution)/shard_map/ppermute | solution.py:579
  53.4 4.1 %collective-permute-start.6 = (f32[128,640]{1,0:T(8,128)S(1)}, f32[128,640]{1,0:T(8,128)S(1)}, u32[]{:S(2)}, u32[]{:S(2)}) collective-permute-start(f32[128,640]{1,0:T(8,128)S(1)} %get-tuple-element.57), channel_id=1, source_target_pairs={{0,4},{4,8},{8,12},{12,16},{16,20},{20,24},{24,28},{28,32},{32,36}... | collective-permute-start | bytes 983048 | tf_op jit(solution)/shard_map/ppermute | solution.py:579
  53.5 10.1 %collective-permute-start.7 = (f32[128,640]{1,0:T(8,128)S(1)}, f32[128,640]{1,0:T(8,128)S(1)}, u32[]{:S(2)}, u32[]{:S(2)}) collective-permute-start(f32[128,640]{1,0:T(8,128)S(1)} %get-tuple-element.58), channel_id=1, source_target_pairs={{0,124},{4,0},{8,4},{12,8},{16,12},{20,16},{24,20},{28,24},{32,28}... | collective-permute-start | bytes 983048 | tf_op jit(solution)/shard_map/ppermute | solution.py:579
  63.6 11.5 %copy-start.10 = (bf16[64,1024]{1,0:T(8,128)(2,1)S(1)}, bf16[64,1024]{1,0:T(8,128)(2,1)}, u32[]{:S(2)}) copy-start(bf16[64,1024]{1,0:T(8,128)(2,1)} %constant.53.clone.refs_9_) | copy-start | bytes 393220
  63.6 11.5 %copy-start.11 = (bf16[64,512]{1,0:T(8,128)(2,1)S(1)}, bf16[64,512]{1,0:T(8,128)(2,1)}, u32[]{:S(2)}) copy-start(bf16[64,512]{1,0:T(8,128)(2,1)} %constant.54.clone.refs_10_) | copy-start | bytes 196612
  66.8 2.3 %collective-permute-start.8 = (f32[64,640]{1,0:T(8,128)S(1)}, f32[64,640]{1,0:T(8,128)S(1)}, u32[]{:S(2)}, u32[]{:S(2)}) collective-permute-start(f32[64,640]{1,0:T(8,128)S(1)} %get-tuple-element.60), channel_id=1, source_target_pairs={{0,4},{4,8},{8,12},{12,16},{16,20},{20,24},{24,28},{28,32},{32,36}... | collective-permute-start | bytes 491528 | tf_op jit(solution)/shard_map/ppermute | solution.py:579
  66.9 8.1 %collective-permute-start.9 = (f32[64,640]{1,0:T(8,128)S(1)}, f32[64,640]{1,0:T(8,128)S(1)}, u32[]{:S(2)}, u32[]{:S(2)}) collective-permute-start(f32[64,640]{1,0:T(8,128)S(1)} %get-tuple-element.61), channel_id=1, source_target_pairs={{0,124},{4,0},{8,4},{12,8},{16,12},{20,16},{24,20},{28,24},{32,28}... | collective-permute-start | bytes 491528 | tf_op jit(solution)/shard_map/ppermute | solution.py:579
  75.1 9.5 %copy-start.7 = (bf16[2048,192]{1,0:T(8,128)(2,1)S(1)}, bf16[2048,192]{1,0:T(8,128)(2,1)}, u32[]{:S(2)}) copy-start(bf16[2048,192]{1,0:T(8,128)(2,1)} %constant.55.clone.prolong) | copy-start | bytes 2359300
  75.1 9.5 %copy-start.12 = (f32[64,8]{1,0:T(8,128)S(1)}, f32[64,8]{1,0:T(8,128)}, u32[]{:S(2)}) copy-start(f32[64,8]{1,0:T(8,128)} %constant.57.clone.table) | copy-start | bytes 6148
  77.6 1.3 collective-permute-start.10
  77.7 6.8 %collective-permute-start.11 = (f32[16,640]{1,0:T(8,128)S(1)}, f32[16,640]{1,0:T(8,128)S(1)}, u32[]{:S(2)}, u32[]{:S(2)}) collective-permute-start(f32[16,640]{1,0:T(8,128)S(1)} %get-tuple-element.66), channel_id=1, source_target_pairs={{0,124},{4,0},{8,4},{12,8},{16,12},{20,16},{24,20},{28,24},{32,28}... | collective-permute-start | bytes 122888 | tf_op jit(solution)/shard_map/ppermute | solution.py:579
  84.5 12.7 %copy-start.6 = (bf16[4,128,256]{2,1,0:T(8,128)(2,1)S(1)}, bf16[4,128,256]{2,1,0:T(8,128)(2,1)}, u32[]{:S(2)}) copy-start(bf16[4,128,256]{2,1,0:T(8,128)(2,1)} %constant.50.clone.bwd_low) | copy-start | bytes 786436
  87.0 4.1 %collective-permute-start.12 = (f32[128,640]{1,0:T(8,128)S(1)}, f32[128,640]{1,0:T(8,128)S(1)}, u32[]{:S(2)}, u32[]{:S(2)}) collective-permute-start(f32[128,640]{1,0:T(8,128)S(1)} %get-tuple-element.70), channel_id=1, source_target_pairs={{0,4},{4,8},{8,12},{12,16},{16,20},{20,24},{24,28},{28,32},{32,36}... | collective-permute-start | bytes 983048 | tf_op jit(solution)/shard_map/ppermute | solution.py:579
  87.1 10.1 %collective-permute-start.13 = (f32[128,640]{1,0:T(8,128)S(1)}, f32[128,640]{1,0:T(8,128)S(1)}, u32[]{:S(2)}, u32[]{:S(2)}) collective-permute-start(f32[128,640]{1,0:T(8,128)S(1)} %get-tuple-element.71), channel_id=1, source_target_pairs={{0,124},{4,0},{8,4},{12,8},{16,12},{20,16},{24,20},{28,24},{32,28}... | collective-permute-start | bytes 983048 | tf_op jit(solution)/shard_map/ppermute | solution.py:579
  100.4 2.3 %collective-permute-start.14 = (f32[64,640]{1,0:T(8,128)S(1)}, f32[64,640]{1,0:T(8,128)S(1)}, u32[]{:S(2)}, u32[]{:S(2)}) collective-permute-start(f32[64,640]{1,0:T(8,128)S(1)} %get-tuple-element.73), channel_id=1, source_target_pairs={{0,4},{4,8},{8,12},{12,16},{16,20},{20,24},{24,28},{28,32},{32,36}... | collective-permute-start | bytes 491528 | tf_op jit(solution)/shard_map/ppermute | solution.py:579
  100.5 8.1 %collective-permute-start.15 = (f32[64,640]{1,0:T(8,128)S(1)}, f32[64,640]{1,0:T(8,128)S(1)}, u32[]{:S(2)}, u32[]{:S(2)}) collective-permute-start(f32[64,640]{1,0:T(8,128)S(1)} %get-tuple-element.74), channel_id=1, source_target_pairs={{0,124},{4,0},{8,4},{12,8},{16,12},{20,16},{24,20},{28,24},{32,28}... | collective-permute-start | bytes 491528 | tf_op jit(solution)/shard_map/ppermute | solution.py:579
  110.8 4.1 %collective-permute-start.16 = (f32[128,640]{1,0:T(8,128)S(1)}, f32[128,640]{1,0:T(8,128)S(1)}, u32[]{:S(2)}, u32[]{:S(2)}) collective-permute-start(f32[128,640]{1,0:T(8,128)S(1)} %get-tuple-element.78), channel_id=1, source_target_pairs={{0,4},{4,8},{8,12},{12,16},{16,20},{20,24},{24,28},{28,32},{32,36}... | collective-permute-start | bytes 983048 | tf_op jit(solution)/shard_map/ppermute | solution.py:579
  110.9 9.9 %collective-permute-start.17 = (f32[128,640]{1,0:T(8,128)S(1)}, f32[128,640]{1,0:T(8,128)S(1)}, u32[]{:S(2)}, u32[]{:S(2)}) collective-permute-start(f32[128,640]{1,0:T(8,128)S(1)} %get-tuple-element.79), channel_id=1, source_target_pairs={{0,124},{4,0},{8,4},{12,8},{16,12},{20,16},{24,20},{28,24},{32,28}... | collective-permute-start | bytes 983048 | tf_op jit(solution)/shard_map/ppermute | solution.py:579
  124.0 2.3 %collective-permute-start.18 = (f32[64,640]{1,0:T(8,128)S(1)}, f32[64,640]{1,0:T(8,128)S(1)}, u32[]{:S(2)}, u32[]{:S(2)}) collective-permute-start(f32[64,640]{1,0:T(8,128)S(1)} %get-tuple-element.81), channel_id=1, source_target_pairs={{0,4},{4,8},{8,12},{12,16},{16,20},{20,24},{24,28},{28,32},{32,36}... | collective-permute-start | bytes 491528 | tf_op jit(solution)/shard_map/ppermute | solution.py:579
  124.1 8.1 %collective-permute-start.19 = (f32[64,640]{1,0:T(8,128)S(1)}, f32[64,640]{1,0:T(8,128)S(1)}, u32[]{:S(2)}, u32[]{:S(2)}) collective-permute-start(f32[64,640]{1,0:T(8,128)S(1)} %get-tuple-element.82), channel_id=1, source_target_pairs={{0,124},{4,0},{8,4},{12,8},{16,12},{20,16},{24,20},{28,24},{32,28}... | collective-permute-start | bytes 491528 | tf_op jit(solution)/shard_map/ppermute | solution.py:579
  134.4 2.6 %collective-permute-start.20 = (f32[64,640]{1,0:T(8,128)S(1)}, f32[64,640]{1,0:T(8,128)S(1)}, u32[]{:S(2)}, u32[]{:S(2)}) collective-permute-start(f32[64,640]{1,0:T(8,128)S(1)} %get-tuple-element.87), channel_id=1, source_target_pairs={{0,4},{4,8},{8,12},{12,16},{16,20},{20,24},{24,28},{28,32},{32,36}... | collective-permute-start | bytes 491528 | tf_op jit(solution)/shard_map/ppermute | solution.py:579
  134.7 8.1 %collective-permute-start.21 = (f32[64,640]{1,0:T(8,128)S(1)}, f32[64,640]{1,0:T(8,128)S(1)}, u32[]{:S(2)}, u32[]{:S(2)}) collective-permute-start(f32[64,640]{1,0:T(8,128)S(1)} %get-tuple-element.88), channel_id=1, source_target_pairs={{0,124},{4,0},{8,4},{12,8},{16,12},{20,16},{24,20},{28,24},{32,28}... | collective-permute-start | bytes 491528 | tf_op jit(solution)/shard_map/ppermute | solution.py:579

commit v2 on v1

v2 whole, which is shorter than its diff:
```python
import functools

import jax
import jax.numpy as jnp
import ml_dtypes
import numpy as np
from jax import lax
from jax.experimental import pallas as pl
from jax.experimental.pallas import tpu as pltpu
from jax.sharding import PartitionSpec as P

PTS = 8
CPTS = 4
COLS_DEV = 16
RADIAL = 16
SMOOTH = 2

WIN = 40
LEFT = 10
LANES = WIN * RADIAL
RINGS = ((8, 32), (4, 8), (32, 36), (0, 4), (36, 40))
OWN = COLS_DEV * RADIAL
CLASSES = ((0, 0), (0, 1), (1, 0), (1, 1))
INNER = 160
OUTER = 80
MODES = 256
TILE = 128
TILES = LANES // TILE
TERMS = 32
BATCH = 4

cheb_upper = 2.0
cheb_ratio = 0.1
theta = 0.5 * (cheb_upper + cheb_upper * cheb_ratio)
delta = 0.5 * (cheb_upper - cheb_upper * cheb_ratio)
sigma = theta / delta
rho_first = 1.0 / sigma
rho_second = 1.0 / (2.0 * sigma - rho_first)


def legendre_rows(gll_nodes, poly_order):
    values = np.zeros((gll_nodes.size, poly_order + 1))
    values[:, 0] = 1.0
    values[:, 1] = gll_nodes
    for degree in range(2, poly_order + 1):
        values[:, degree] = (
            (2 * degree - 1) * gll_nodes * values[:, degree - 1]
            - (degree - 1) * values[:, degree - 2]
        ) / degree
    return values


def jacobi_eigen(matrix):
    order = matrix.shape[0]
    current = matrix.copy()
    vectors = np.eye(order)
    for sweep in range(12):
        for first in range(order - 1):
            for second in range(first + 1, order):
                off_value = current[first, second]
                spread = current[second, second] - current[first, first]
                sense = np.where(spread >= 0.0, 1.0, -1.0)
                denom = spread + sense * np.sqrt(spread * spread + 4.0 * off_value * off_value)
                denom = np.where(denom == 0.0, 1.0, denom)
                tangent = 2.0 * off_value / denom
                cosine = 1.0 / np.sqrt(1.0 + tangent * tangent)
                sine = tangent * cosine
                rotate = np.eye(order)
                rotate[first, first] = cosine
                rotate[second, second] = cosine
                rotate[first, second] = sine
                rotate[second, first] = -sine
                current = rotate.T @ current @ rotate
                vectors = vectors @ rotate
    diag_ids = np.arange(order)
    return (current[diag_ids, diag_ids].copy(), vectors)


def lobatto(poly_order):
    gll_nodes = np.cos(np.pi * np.arange(poly_order + 1) / poly_order)
    for newton in range(100):
        values = legendre_rows(gll_nodes, poly_order)
        gll_nodes = gll_nodes - (gll_nodes * values[:, poly_order] - values[:, poly_order - 1]) / (
            (poly_order + 1) * values[:, poly_order]
        )
    values = legendre_rows(gll_nodes, poly_order)
    gll_nodes = gll_nodes[::-1].copy()
    top_poly = values[::-1, poly_order].copy()
    weights = 2.0 / (poly_order * (poly_order + 1) * top_poly**2)
    derivative = np.zeros((poly_order + 1, poly_order + 1))
    for row_index in range(poly_order + 1):
        for col_index in range(poly_order + 1):
            if row_index != col_index:
                derivative[row_index, col_index] = top_poly[row_index] / (
                    top_poly[col_index] * (gll_nodes[row_index] - gll_nodes[col_index])
                )
    derivative[0, 0] = -poly_order * (poly_order + 1) / 4.0
    derivative[poly_order, poly_order] = poly_order * (poly_order + 1) / 4.0
    stiffness = derivative.T @ (weights[:, None] * derivative)
    return (gll_nodes, weights, stiffness)


def element_tables():
    fine_nodes, fine_weights, fine_stiff = lobatto(PTS - 1)
    coarse_nodes, coarse_weights, coarse_stiff = lobatto(CPTS - 1)
    interp = np.ones((PTS, CPTS))
    for target_col in range(CPTS):
        for other_col in range(CPTS):
            if other_col != target_col:
                interp[:, target_col] *= (fine_nodes - coarse_nodes[other_col]) / (
                    coarse_nodes[target_col] - coarse_nodes[other_col]
                )
    poly_order = PTS - 1
    node_count = 3 * poly_order + 1
    joined_stiff = np.zeros((node_count, node_count))
    joined_mass = np.zeros(node_count)
    for piece_index in range(3):
        first_node = piece_index * poly_order
        joined_stiff[first_node : first_node + PTS, first_node : first_node + PTS] += fine_stiff
        joined_mass[first_node : first_node + PTS] += fine_weights
    kept = slice(poly_order - 1, 2 * poly_order + 2)
    root_mass = np.sqrt(joined_mass[kept])
    eigen_values, eigen_vectors = jacobi_eigen(
        joined_stiff[kept, kept] / root_mass[:, None] / root_mass[None, :]
    )
    eigen_basis = eigen_vectors / root_mass[:, None]
    coarse_diag = np.diag(coarse_stiff).copy()
    return fine_stiff, fine_weights, eigen_basis, eigen_values, interp, coarse_diag, coarse_weights


def split(table):
    high = table.astype(np.float32).astype(ml_dtypes.bfloat16)
    low = (table - high.astype(np.float64)).astype(np.float32).astype(ml_dtypes.bfloat16)
    return high, low


def kron3(first, second, third):
    return np.kron(first, np.kron(second, third))


def spread(values):
    terms = np.zeros((values.shape[0], TERMS), ml_dtypes.bfloat16)
    for at in range(3):
        high, rest = split(values[:, at])
        middle, low = split(values[:, at] - high.astype(np.float64))
        for n, part in enumerate((high, high, high, middle, middle, low)):
            terms[:, at * 6 + n] = part
    return terms


def matrices():
    stiff, weights, basis, values, interp, coarse_diag, coarse_weights = element_tables()
    parts = ([], [])
    for mode in range(PTS + 2):
        column = basis[:, mode]
        odd = np.abs(column + column[::-1]).sum() < np.abs(column - column[::-1]).sum()
        parts[int(odd)].append(mode)
    signs = (1.0, -1.0)
    pure = basis.copy()
    for parity in (0, 1):
        for mode in parts[parity]:
            pure[:, mode] = 0.5 * (basis[:, mode] + signs[parity] * basis[::-1, mode])
    center = pure[1:-1, :]
    edges = pure[[0, -1], :]

    def folded(matrix, parity):
        half = PTS // 2
        return 0.5 * (matrix[:half, :half] + signs[parity] * matrix[:half, ::-1][:, :half])

    mass = np.diag(weights)
    halved = np.ones(PTS // 2)
    halved[0] = 0.5
    forward_inner = np.zeros((4, MODES, INNER))
    forward_outer = np.zeros((4, MODES, OUTER))
    backward = np.zeros((4, PTS * 16, MODES))
    apply_inner = np.zeros((4, 320, 96))
    apply_outer = np.zeros((4, 192, 32))
    mode_values = np.ones((4, MODES, 3))
    for at, (pi, pk) in enumerate(CLASSES):
        ci, ck = center[:4, parts[pi]], center[:4, parts[pk]]
        ei, ek = edges[:1, parts[pi]], edges[:1, parts[pk]]
        count = len(parts[pi]) * len(parts[pk]) * (PTS + 2)
        rest = ci[1:]
        gap = lambda rows: np.zeros((rows, count))
        columns = [kron3(rest, ck, center), kron3(rest, ek, center), gap(8)]
        columns += [kron3(rest, ck, edges[:1]), gap(4), kron3(rest, ck, edges[1:]), gap(4)]
        forward_inner[at, :count] = np.concatenate(columns, axis=0).T
        columns = [kron3(ci[:1], ck, center), kron3(ei, ck, center), kron3(ci[:1], ek, center)]
        columns += [kron3(ci[:1], ck, edges[:1]), kron3(ci[:1], ck, edges[1:])]
        forward_outer[at, :count] = np.concatenate(columns, axis=0).T
        backward[at, :, :count] = kron3(halved[:, None] * ci, halved[:, None] * ck, center)
        vi, vk = values[parts[pi]], values[parts[pk]]
        ones = np.ones
        mode_values[at, :count, 0] = kron3(vi, ones(len(vk)), ones(PTS + 2))
        mode_values[at, :count, 1] = kron3(ones(len(vi)), vk, ones(PTS + 2))
        mode_values[at, :count, 2] = kron3(ones(len(vi)), ones(len(vk)), values)
        si, sk = folded(stiff, pi), folded(stiff, pk)
        mi, mk = folded(mass, pi), folded(mass, pk)
        along_z, along_a, along_b = kron3(si, mk, mass), kron3(mi, sk, mass), kron3(mi, mk, stiff)
        apply_inner[at] = np.concatenate([along_z[:, 32:], along_a[32:, 32:], along_b[32:, 32:]])
        apply_outer[at] = np.concatenate([along_z[:, :32], along_a[:32, :32], along_b[:32, :32]])
    mass_up, stiff_up = mass @ interp, stiff @ interp
    prolong = np.concatenate(
        [
            kron3(interp, interp, interp),
            kron3(stiff_up, mass_up, mass_up),
            kron3(mass_up, stiff_up, mass_up),
            kron3(mass_up, mass_up, stiff_up),
        ],
        axis=0,
    )
    restrict = kron3(interp.T, interp.T, interp.T)
    coarse = np.zeros((CPTS**3, 8))
    coarse[:, 0] = kron3(coarse_diag, coarse_weights, coarse_weights)
    coarse[:, 1] = kron3(coarse_weights, coarse_diag, coarse_weights)
    coarse[:, 2] = kron3(coarse_weights, coarse_weights, coarse_diag)

    def pair(table):
        high, low = split(table)
        return jnp.asarray(np.concatenate([high, high], axis=-1)), jnp.asarray(low)

    def triple(table):
        high, low = split(table)
        return jnp.asarray(np.concatenate([high, high, low], axis=-1))

    return {
        "forward_inner": triple(forward_inner),
        "forward_outer": triple(forward_outer),
        "backward": pair(backward),
        "apply_inner": triple(apply_inner),
        "apply_outer": triple(apply_outer),
        "restrict": pair(restrict),
        "prolong": triple(prolong),
        "modes": jnp.asarray(spread(mode_values.reshape(4 * MODES, 3))),
        "coarse": jnp.asarray(coarse.astype(np.float32)),
    }


def halves(value):
    high = value.astype(jnp.bfloat16)
    low = (value - high.astype(jnp.float32)).astype(jnp.bfloat16)
    return high, low


def dot(left, right):
    return jnp.dot(left, right, preferred_element_type=jnp.float32)


def join(tiles):
    return jnp.concatenate(tiles, axis=1)


def tiles_of(value):
    return [value[:, t * TILE : (t + 1) * TILE] for t in range(value.shape[1] // TILE)]


def radial_turn(value, steps):
    return join([pltpu.roll(tile, steps % TILE, axis=1) for tile in tiles_of(value)])


def column_turn(value, direction):
    tiles = tiles_of(value)
    count = len(tiles)
    lane = lax.broadcasted_iota(jnp.int32, tiles[0].shape, 1)
    near = [pltpu.roll(tile, (direction * RADIAL) % TILE, axis=1) for tile in tiles]
    far = lambda at: pltpu.roll(tiles[at], (TILE // 2 + direction * RADIAL) % TILE, axis=1)
    out = list(near)
    if direction < 0:
        high_end, low_end = lane >= TILE - RADIAL, (lane >= TILE // 2 - RADIAL) & (lane < TILE // 2)
        out[0] = jnp.where(high_end, near[1], near[0])
        out[1] = jnp.where(high_end, near[2], near[1])
        inner, outer, middle = 2, high_end, low_end
        edge = 0
    else:
        high_end, low_end = lane < RADIAL, (lane >= TILE // 2) & (lane < TILE // 2 + RADIAL)
        out[1] = jnp.where(high_end, near[0], near[1])
        out[2] = jnp.where(high_end, near[1], near[2])
        inner, outer, middle = 0, high_end, low_end
        edge = 2
    if count > 3:
        first_ring = far(3)
        out[inner] = jnp.where(outer, first_ring, out[inner])
        out[3] = jnp.where(middle, far(edge), near[3])
    if count > 4:
        out[3] = jnp.where(outer, far(4), out[3])
        out[4] = jnp.where(middle, first_ring, near[4])
    return join(out)


def lane_masks(rows, lanes):
    radial = lax.broadcasted_iota(jnp.int32, (rows, lanes), 1) % RADIAL
    keep_upper = (radial < RADIAL - 1).astype(jnp.float32)
    keep_lower = (radial > 0).astype(jnp.float32)
    return keep_upper, keep_lower


def chunks(lanes):
    return [(start, min(start + 2 * TILE, lanes)) for start in range(0, lanes, 2 * TILE)]


def point_factor(lanes):
    point = lax.broadcasted_iota(jnp.int32, (PTS, lanes), 0)
    radial = lax.broadcasted_iota(jnp.int32, (PTS, lanes), 1) % RADIAL
    shared = ((point == 0) & (radial > 0)) | ((point == PTS - 1) & (radial < RADIAL - 1))
    return jnp.where(shared, 0.5, 1.0)


def side_factor(i, k):
    return (0.5 if i in (0, PTS - 1) else 1.0) * (0.5 if k in (0, PTS - 1) else 1.0)


def plane_factor(factor, i):
    return jnp.concatenate([factor * side_factor(i, k) for k in range(PTS)])


def block(plane, k):
    start = plane * 64 + k * PTS
    return slice(start, start + PTS)


def load(ref, rows, tiles, base=0):
    return join([ref[base + t, rows, :] for t in range(tiles)])


def store(ref, rows, value, base=0):
    for t, tile in enumerate(tiles_of(value)):
        ref[base + t, rows, :] = tile


def assemble_sides(field, planes, tiles):
    batches = [planes[start : start + BATCH] for start in range(0, len(planes), BATCH)]
    for batch in batches:
        left = jnp.concatenate([load(field, block(plane, 0), tiles) for plane in batch])
        right = jnp.concatenate([load(field, block(plane, PTS - 1), tiles) for plane in batch])
        new_right = right + column_turn(left, -1)
        new_left = left + column_turn(right, 1)
        for at, plane in enumerate(batch):
            store(field, block(plane, PTS - 1), new_right[at * PTS : (at + 1) * PTS])
            store(field, block(plane, 0), new_left[at * PTS : (at + 1) * PTS])
    keep_upper, keep_lower = lane_masks(PTS * BATCH, tiles * TILE)
    for batch in batches:
        rows = len(batch) * PTS
        inner_at = [pl.ds(plane * 64, PTS, stride=PTS) for plane in batch]
        outer_at = [pl.ds(plane * 64 + PTS - 1, PTS, stride=PTS) for plane in batch]
        inner = jnp.concatenate([load(field, at, tiles) for at in inner_at])
        outer = jnp.concatenate([load(field, at, tiles) for at in outer_at])
        new_outer = outer + radial_turn(inner, -1) * keep_upper[:rows]
        new_inner = inner + radial_turn(outer, 1) * keep_lower[:rows]
        for at in range(len(batch)):
            store(field, outer_at[at], new_outer[at * PTS : (at + 1) * PTS])
            store(field, inner_at[at], new_inner[at * PTS : (at + 1) * PTS])


def fold(a, b, c, d):
    sum_k, diff_k = a + b, a - b
    sum_m, diff_m = c + d, c - d
    return sum_k + sum_m, sum_k - sum_m, diff_k + diff_m, diff_k - diff_m


def pack(parts, packed, rows, tiles):
    for c in range(4):
        for t in range(tiles):
            lanes = slice(t * TILE, (t + 1) * TILE)
            high, low = halves(parts[c * tiles + t, 0:rows, :])
            packed[c, 0:rows, lanes] = high
            packed[c, rows : 2 * rows, lanes] = low
            packed[c, 2 * rows : 3 * rows, lanes] = high


def unfold(ss, sa, as_, aa):
    sum_k, sum_m = ss + sa, ss - sa
    diff_k, diff_m = as_ + aa, as_ - aa
    return sum_k + diff_k, sum_k - diff_k, sum_m + diff_m, sum_m - diff_m


def mirrored(i, k):
    return (i, k), (PTS - 1 - i, k), (i, PTS - 1 - k), (PTS - 1 - i, PTS - 1 - k)


def coefficient_terms(values):
    rows = []
    for value in values:
        parts = []
        for _ in range(3):
            part = value.astype(jnp.bfloat16).astype(jnp.float32)
            parts.append(part)
            value = value - part
        high, middle, low = parts
        rows += [high, middle, low, high, middle, high]
    rows.append(jnp.zeros((TERMS - len(rows), value.shape[1]), jnp.float32))
    return jnp.concatenate(rows).astype(jnp.bfloat16)


def tables_kernel(geo, modes, own, lam, coef, kept):
    kept[...] = own[...]
    la, lb, lz = (geo[n : n + 1] for n in range(3))
    cz = la * lb / (2.0 * lz)
    ca = lz * lb / (2.0 * la)
    cb = lz * la / (2.0 * lb)
    for at, value in enumerate((cz, ca, cb)):
        coef[at * PTS : (at + 1) * PTS] = jnp.broadcast_to(value, (PTS, LANES))
    terms = coefficient_terms((cz, ca, cb))
    for start, stop in chunks(LANES):
        for c in range(4):
            here = slice(c * MODES, (c + 1) * MODES)
            lam[here, start:stop] = 1.0 / dot(modes[here], terms[:, start:stop])


def window(case, left, own, right, rows):
    shift = (COLS_DEV - LEFT - case) * RADIAL
    joined = join([left[rows], own, right[rows]])
    joined = pltpu.roll(joined, joined.shape[1] - shift, axis=1)[:, :LANES]
    first, *center, last = tiles_of(joined)
    lane = lax.broadcasted_iota(jnp.int32, first.shape, 1)
    half = TILE // 2
    near = jnp.where(lane < half, pltpu.roll(first, half, axis=1), pltpu.roll(last, half, axis=1))
    return join([*center, near, jnp.where(lane < half, first, last)])


def outer_kernel(rot, left, own, right, geo, field, up, down, inner):
    factor = point_factor(LANES)
    for case in range(4):

        @pl.when(rot[0] == case)
        def _(case=case):
            for at, i in enumerate((0, 1, 6, 7)):
                here = slice(at * 64, at * 64 + 64)
                value = window(case, left, own[i * 64 : i * 64 + 64], right, here)
                field[here] = value * plane_factor(factor, i)

    up[0:128] = field[128:256]
    down[0:128] = field[0:128]
    length = jnp.broadcast_to(geo[2:3], (PTS, LANES))
    up[128:136] = length
    down[128:136] = length
    inner[...] = own[128:384]


def inner_kernel(rot, left, own, right, field):
    factor = point_factor(LANES)
    for case in range(4):

        @pl.when(rot[0] == case)
        def _(case=case):
            for at, i in enumerate((2, 3, 4, 5)):
                here = slice(at * 64, at * 64 + 64)
                field[here] = window(case, left, own[here], right, here) * plane_factor(factor, i)


def put(parts, tiles, at, values):
    for c in range(4):
        store(parts, at, values[c], c * tiles)


def layer(value, at):
    return value[at * PTS : (at + 1) * PTS]


def column_halos(field, planes, wide, lanes):
    before = jnp.concatenate([load(field, block(plane, PTS - 2), wide) for plane in planes])
    after = jnp.concatenate([load(field, block(plane, 1), wide) for plane in planes])
    return column_turn(before, 1)[:, :lanes], column_turn(after, -1)[:, :lanes]


def radial_halos(parts, tiles, count):
    masks = lane_masks(4 * count, tiles * TILE)
    found = []
    for first, steps, keep in ((PTS - 2, 1, masks[1]), (1, -1, masks[0])):
        rows = pl.ds(first, count, stride=PTS)
        values = [load(parts, rows, tiles, c * tiles) for c in range(4)]
        values = radial_turn(jnp.concatenate(values), steps) * keep
        found.append([values[c * count : (c + 1) * count] for c in range(4)])
    return found


def solve_inner_kernel(start_up, wide, tiles, *refs):
    if start_up:
        outer, inner, *refs = refs
        planes = [outer[64:128]] + [inner[i * 64 : i * 64 + 64] for i in range(4)] + [outer[128:192]]
    else:
        field, *refs = refs
        planes = [field[i * 64 : i * 64 + 64] for i in range(1, 7)]
    fwd, share, spectrum, ext, parts, packed = refs
    lanes = tiles * TILE
    factor = point_factor(lanes)
    for at, plane in enumerate(planes):
        store(ext, slice(at * 64, at * 64 + 64), plane)
    assemble_sides(ext, range(6), wide)
    for at in range(6):
        here = slice(at * 64, at * 64 + 64)
        share[here] = load(ext, here, tiles) * plane_factor(factor, at + 1)
    for i in range(3):
        for k in range(4):
            corners = ((i, k), (5 - i, k), (i, 7 - k), (5 - i, 7 - k))
            values = fold(*(load(ext, block(p, q), tiles) for p, q in corners))
            put(parts, tiles, block(0, i * 4 + k), values)
    before, after = column_halos(ext, range(6), wide, lanes)
    for i in range(3):
        values = fold(layer(before, i), layer(before, 5 - i), layer(after, i), layer(after, 5 - i))
        put(parts, tiles, slice(96 + i * 8, 104 + i * 8), values)
    put(parts, tiles, slice(120, 128), [jnp.zeros((PTS, lanes), jnp.float32)] * 4)
    lower, upper = radial_halos(parts, tiles, 16)
    put(parts, tiles, slice(128, 144), lower)
    put(parts, tiles, slice(144, 160), upper)
    pack(parts, packed, INNER, tiles)
    for c in range(4):
        for start, stop in chunks(lanes):
            spectrum[c * MODES : (c + 1) * MODES, start:stop] = dot(fwd[c], packed[c, :, start:stop])


def solve_outer_kernel(start_up, wide, tiles, *refs):
    field, below, above, spectrum, lam, fwd, bwd, bwd_low = refs[:8]
    share, out, up, down, ext, parts, packed, modes = refs[8:]
    lanes = tiles * TILE
    factor = point_factor(lanes)
    last = 192 if start_up else 448
    store(ext, slice(0, 64), below[0:64])
    store(ext, slice(64, 128), field[0:64] + below[64:128])
    store(ext, slice(128, 192), field[last : last + 64] + above[0:64])
    store(ext, slice(192, 256), above[64:128])
    assemble_sides(ext, range(4), wide)
    share[0:64] = load(ext, slice(64, 128), tiles) * plane_factor(factor, 0)
    share[64:128] = load(ext, slice(128, 192), tiles) * plane_factor(factor, 7)
    for k in range(4):
        for at, (p, q) in enumerate(((1, 2), (0, 3))):
            corners = ((p, k), (q, k), (p, 7 - k), (q, 7 - k))
            values = fold(*(load(ext, block(*corner), tiles) for corner in corners))
            put(parts, tiles, block(0, at * 4 + k), values)
    before, after = column_halos(ext, (1, 2), wide, lanes)
    values = fold(layer(before, 0), layer(before, 1), layer(after, 0), layer(after, 1))
    put(parts, tiles, slice(64, 72), values)
    lower, upper = radial_halos(parts, tiles, 4)
    put(parts, tiles, slice(72, 80), [jnp.concatenate(pair) for pair in zip(lower, upper)])
    pack(parts, packed, OUTER, tiles)
    for c in range(4):
        for start, stop in chunks(lanes):
            here = slice(c * MODES, (c + 1) * MODES)
            value = dot(fwd[c], packed[c, :, start:stop]) + spectrum[here, start:stop]
            modes[0:MODES, start:stop], modes[MODES:, start:stop] = halves(value * lam[here, start:stop])
        for start, stop in chunks(lanes):
            value = dot(bwd[c], modes[:, start:stop])
            value = value + dot(bwd_low[c], modes[0:MODES, start:stop])
            store(parts, slice(0, 128), value, c * tiles + start // TILE)
    for i in range(4):
        for k in range(4):
            classes = (load(parts, block(0, i * 4 + k), tiles, c * tiles) for c in range(4))
            for (p, q), value in zip(mirrored(i, k), unfold(*classes)):
                out[block(p, q)] = value * factor
    up[...] = out[448:512]
    down[...] = out[0:64]


def stepped(kind, value, before):
    if kind in (0, 2):
        return value * (1.0 / theta)
    return before * (rho_second * rho_first) + value * (2.0 * rho_second / delta)


def step_inner_kernel(kind, wide, tiles, *refs):
    take = iter(refs)
    local = next(take)
    before = next(take) if kind in (1, 3) else None
    total = next(take) if kind != 0 else None
    coef, app = next(take), next(take)
    step = next(take) if kind in (0, 2) else None
    sum_out = next(take) if kind != 0 else None
    image, ext, parts, packed = take
    lanes = tiles * TILE
    for i in range(6):
        store(ext, slice(i * 64, i * 64 + 64), local[i * 64 + 64 : i * 64 + 128])
    assemble_sides(ext, range(6), wide)
    for i in range(6):
        here = slice(i * 64, i * 64 + 64)
        value = stepped(kind, load(ext, here, tiles), None if before is None else before[here, :lanes])
        if step is not None:
            step[here] = value
        if sum_out is not None:
            sum_out[here] = total[here, :lanes] + value
        store(ext, here, value)
    for i in range(3):
        for k in range(4):
            corners = ((i, k), (5 - i, k), (i, 7 - k), (5 - i, 7 - k))
            values = fold(*(load(ext, block(p, q), tiles) for p, q in corners))
            put(parts, tiles, block(0, i * 4 + k), values)
    pack(parts, packed, 96, tiles)
    for c in range(4):
        for start, stop in chunks(lanes):
            terms = dot(app[c], packed[c, :, start:stop]).reshape(40, PTS, stop - start)
            value = terms[0:16] * coef[0:8, start:stop]
            sides = terms[16:28] * coef[8:16, start:stop] + terms[28:40] * coef[16:24, start:stop]
            value = jnp.concatenate([value[0:4], value[4:16] + sides])
            image[c * 128 : (c + 1) * 128, start:stop] = value.reshape(128, stop - start)


def step_outer_kernel(kind, wide, tiles, *refs):
    take = iter(refs)
    local, below, above = next(take), next(take), next(take)
    before = next(take) if kind in (1, 3) else None
    total = next(take) if kind != 0 else None
    share_inner, share_outer, image, coef, app = (next(take) for _ in range(5))
    res, res_low = (next(take), next(take)) if kind == 1 else (None, None)
    step = next(take) if kind in (0, 2) else None
    sum_out = next(take) if kind != 0 else None
    field, up, down = next(take), next(take), next(take)
    coarse = next(take) if kind == 1 else None
    ext, parts, packed = next(take), next(take), next(take)
    split_field = next(take) if kind == 1 else None
    lanes = tiles * TILE
    store(ext, slice(0, 64), local[0:64] + below[...])
    store(ext, slice(64, 128), local[448:512] + above[...])
    assemble_sides(ext, range(2), wide)
    for at in range(2):
        here = slice(at * 64, at * 64 + 64)
        value = stepped(kind, load(ext, here, tiles), None if before is None else before[here, :lanes])
        if step is not None:
            step[here] = value
        if sum_out is not None:
            sum_out[here] = total[here, :lanes] + value
        store(ext, here, value)
    for k in range(4):
        corners = ((0, k), (1, k), (0, 7 - k), (1, 7 - k))
        values = fold(*(load(ext, block(p, q), tiles) for p, q in corners))
        put(parts, tiles, block(0, k), values)
    pack(parts, packed, 32, tiles)
    for c in range(4):
        for start, stop in chunks(lanes):
            terms = dot(app[c], packed[c, :, start:stop]).reshape(24, PTS, stop - start)
            value = terms[0:16] * coef[0:8, start:stop]
            sides = terms[16:20] * coef[8:16, start:stop] + terms[20:24] * coef[16:24, start:stop]
            value = jnp.concatenate([value[0:4] + sides, value[4:16]]).reshape(128, stop - start)
            value = value + image[c * 128 : (c + 1) * 128, start:stop]
            store(parts, slice(0, 128), value, c * tiles + start // TILE)
    for i in range(4):
        for k in range(4):
            classes = (load(parts, block(0, i * 4 + k), tiles, c * tiles) for c in range(4))
            for (p, q), value in zip(mirrored(i, k), unfold(*classes)):
                if p in (0, 7):
                    shared = share_outer[block(p // 7, q), :lanes]
                else:
                    shared = share_inner[block(p - 1, q), :lanes]
                field[block(p, q)] = shared - value
    if kind == 1:
        split_field[0:512], split_field[512:1024] = halves(field[...])
        for start, stop in chunks(lanes):
            value = dot(res[...], split_field[:, start:stop])
            coarse[:, start:stop] = value + dot(res_low[...], split_field[0:512, start:stop])
        up[...] = coarse[48:64]
        down[...] = coarse[0:16]
    elif kind == 3:
        up[...] = field[448:512]
        down[...] = field[0:64]
    else:
        up[...] = field[384:512]
        down[...] = field[0:128]


def assemble_coarse(value):
    lanes = value.shape[1]
    row = lax.broadcasted_iota(jnp.int32, (64, lanes), 0)
    keep_upper, keep_lower = lane_masks(64, lanes)
    first = (row % 16) < 4
    last = (row % 16) >= 12
    over = pltpu.roll(column_turn(value, -1), 12, axis=0)
    under = pltpu.roll(column_turn(value, 1), 64 - 12, axis=0)
    value = value + jnp.where(last, over, 0.0) + jnp.where(first, under, 0.0)
    first = (row % 4) == 0
    last = (row % 4) == 3
    over = pltpu.roll(radial_turn(value, -1) * keep_upper, 3, axis=0)
    under = pltpu.roll(radial_turn(value, 1) * keep_lower, 64 - 3, axis=0)
    return value + jnp.where(last, over, 0.0) + jnp.where(first, under, 0.0)


def diagonal_kernel(lower, upper, geo, table, scale):
    lanes = scale.shape[1]
    la, lb = geo[0:1, :lanes], geo[1:2, :lanes]

    def local(lz, rows):
        return (
            la * lb / (2.0 * lz) * table[rows, 0:1]
            + lz * lb / (2.0 * la) * table[rows, 1:2]
            + lz * la / (2.0 * lb) * table[rows, 2:3]
        )

    value = local(geo[2:3, :lanes], slice(0, 64))
    first = value[0:16] + local(lower[128:129, :lanes], slice(48, 64))
    last = value[48:64] + local(upper[128:129, :lanes], slice(0, 16))
    scale[...] = assemble_coarse(jnp.concatenate([first, value[16:48], last]))


def coarse_kernel(local, below, above, scale, coef, prolong, *refs):
    total_inner, total_outer, field, sum_inner, sum_outer, out, up, down, packed = refs
    lanes = local.shape[1]
    value = local[...]
    value = jnp.concatenate([value[0:16] + below[...], value[16:48], value[48:64] + above[...]])
    value = assemble_coarse(value) / scale[...]
    high, low = halves(value)
    packed[0:64] = high
    packed[64:128] = low
    packed[128:192] = high
    for start, stop in chunks(lanes):
        for i in range(PTS):
            here = slice(i * 64, i * 64 + 64)
            sides = (8, PTS, stop - start)
            terms = [
                dot(prolong[n * 512 + i * 64 : n * 512 + i * 64 + 64], packed[:, start:stop]) for n in range(4)
            ]
            if i in (0, 7):
                at = slice(i // 7 * 64, i // 7 * 64 + 64)
                sum_outer[at, start:stop] = total_outer[at, start:stop] + terms[0]
            else:
                at = slice(i * 64 - 64, i * 64)
                sum_inner[at, start:stop] = total_inner[at, start:stop] + terms[0]
            value = (
                terms[1].reshape(sides) * coef[0:8, start:stop]
                + terms[2].reshape(sides) * coef[8:16, start:stop]
                + terms[3].reshape(sides) * coef[16:24, start:stop]
            )
            out[here, start:stop] = field[here, start:stop] - value.reshape(64, stop - start)
    up[...] = out[384:512]
    down[...] = out[0:128]


def finish_inner_kernel(rot, local, total_inner, total_outer, sol, res, ext):
    tiles = local.shape[1] // TILE
    for i in range(6):
        store(ext, slice(i * 64, i * 64 + 64), local[i * 64 + 64 : i * 64 + 128])
    assemble_sides(ext, range(6), tiles)
    for case in range(4):

        @pl.when(rot[0] == case)
        def _(case=case):
            start = (LEFT + case - RINGS[0][0]) * RADIAL
            for plane in range(PTS):
                here = slice(plane * 64, plane * 64 + 64)
                if plane in (0, 7):
                    at = plane // 7 * 64
                    sol[here] = total_outer[at : at + 64, start : start + OWN]
                else:
                    before = slice(plane * 64 - 64, plane * 64)
                    sol[here] = total_inner[before, start : start + OWN]
                    res[before] = load(ext, before, tiles)[:, start : start + OWN]


def finish_outer_kernel(rot, local, below, above, inner, res, ext):
    tiles = local.shape[1] // TILE
    store(ext, slice(0, 64), local[0:64] + below[...])
    store(ext, slice(64, 128), local[448:512] + above[...])
    assemble_sides(ext, range(2), tiles)
    res[64:448] = inner[...]
    for case in range(4):

        @pl.when(rot[0] == case)
        def _(case=case):
            start = (LEFT + case - RINGS[0][0]) * RADIAL
            res[0:64] = load(ext, slice(0, 64), tiles)[:, start : start + OWN]
            res[448:512] = load(ext, slice(64, 128), tiles)[:, start : start + OWN]


def call(kernel, name, args, outs, scratch=(), scalars=0, flops=0):
    in_specs = [
        pl.BlockSpec(memory_space=pltpu.SMEM if n < scalars else pltpu.VMEM) for n in range(len(args))
    ]
    return pl.pallas_call(
        kernel,
        out_shape=[jax.ShapeDtypeStruct(out, jnp.float32) for out in outs],
        in_specs=in_specs,
        out_specs=[pl.BlockSpec(memory_space=pltpu.VMEM) for _ in outs],
        scratch_shapes=list(scratch),
        name=name,
        cost_estimate=pl.CostEstimate(flops=flops, bytes_accessed=4_000_000, transcendentals=0),
        compiler_params=pltpu.CompilerParams(vmem_limit_bytes=40 * 1024 * 1024),
    )(*args)


def per_device(rhs, spacing_z, spacing_a, spacing_b, rotation):
    mats = matrices()
    group = lax.axis_index("grp")
    member = lax.axis_index("sub")
    groups = lax.axis_size("grp")
    members = lax.axis_size("sub")
    wide, narrow = jnp.float32, jnp.bfloat16
    vmem = pltpu.VMEM

    def shifted(value, axis, count, steps):
        return lax.ppermute(value, axis, [(n, (n + steps) % count) for n in range(count)])

    def neighbours(up, down):
        return shifted(up, "grp", groups, 1), shifted(down, "grp", groups, -1)

    def beside(value):
        return shifted(value, "sub", members, 1), shifted(value, "sub", members, -1)

    def shapes(tiles, *rows):
        return tuple((count, tiles * TILE) for count in rows)

    own = rhs.reshape(512, OWN)
    left, right = beside(jnp.concatenate([own[0:128], own[384:512]]))
    rot = lax.dynamic_slice(rotation, (group,), (1,))
    ring = jnp.concatenate([spacing_a, spacing_a, spacing_a])
    columns = lax.dynamic_slice(ring, (spacing_a.shape[0] + member * COLS_DEV - LEFT,), (WIN,))
    columns = jnp.concatenate([columns[start:stop] for start, stop in RINGS])
    geo = jnp.stack(
        [
            jnp.repeat(columns, RADIAL),
            jnp.tile(spacing_b, WIN),
            jnp.broadcast_to(spacing_z, (LANES,)),
        ]
    )
    geo = jnp.concatenate([geo, jnp.ones((5, LANES), wide)])
    lam, coef, own = call(
        tables_kernel, "tables", (geo, mats["modes"], own), ((4 * MODES, LANES), (24, LANES), (512, OWN))
    )
    outer, up, down, inner = call(
        outer_kernel,
        "outer",
        (rot, left, own, right, geo),
        ((256, LANES), (136, LANES), (136, LANES), (256, OWN)),
        scalars=1,
    )
    lower, upper = neighbours(up, down)
    left, right = beside(inner)
    (inner,) = call(inner_kernel, "inner", (rot, left, inner, right), ((256, LANES),), scalars=1)

    def solve(fields, below, above, before, tiles):
        lanes = tiles * TILE
        start_up = len(fields) == 2
        share_inner, spectrum = call(
            functools.partial(solve_inner_kernel, start_up, before, tiles),
            "solve_inner",
            (*fields, mats["forward_inner"]),
            shapes(tiles, 384, 4 * MODES),
            (
                vmem((before, 384, TILE), wide),
                vmem((4 * tiles, INNER, TILE), wide),
                vmem((4, 3 * INNER, lanes), narrow),
            ),
        )
        share_outer, local, up, down = call(
            functools.partial(solve_outer_kernel, start_up, before, tiles),
            "solve_outer",
            (fields[0], below, above, spectrum, lam, mats["forward_outer"], *mats["backward"]),
            shapes(tiles, 128, 512, 64, 64),
            (
                vmem((before, 256, TILE), wide),
                vmem((4 * tiles, 128, TILE), wide),
                vmem((4, 3 * OUTER, lanes), narrow),
                vmem((2 * MODES, lanes), narrow),
            ),
        )
        return (share_inner, share_outer), local, neighbours(up, down)

    def advance(kind, local, messages, share, before, total, width, tiles):
        lanes = tiles * TILE

        def scratch(rows, folded):
            return [
                vmem((width, rows, TILE), wide),
                vmem((4 * tiles, 128, TILE), wide),
                vmem((4, folded, lanes), narrow),
            ]

        def pick(at):
            return [pair[at] for pair in (before, total) if pair is not None]

        kept = [count for count, used in ((1, kind in (0, 2)), (1, kind != 0)) if used]
        *inner, image = call(
            functools.partial(step_inner_kernel, kind, width, tiles),
            f"step{kind}_inner",
            (local, *pick(0), coef, mats["apply_inner"]),
            shapes(tiles, *(384 for _ in kept), 512),
            scratch(384, 288),
        )
        sent = {0: 128, 1: 16, 2: 128, 3: 64}[kind]
        extra = scratch(128, 96)
        if kind == 1:
            extra.append(vmem((1024, lanes), narrow))
        out = call(
            functools.partial(step_outer_kernel, kind, width, tiles),
            f"step{kind}_outer",
            (
                *(local, *messages, *pick(1), *share, image, coef, mats["apply_outer"]),
                *(mats["restrict"] if kind == 1 else ()),
            ),
            shapes(tiles, *(128 for _ in kept), 512, sent, sent, *((64,) if kind == 1 else ())),
            extra,
        )
        outer, (field, up, down, *coarse) = out[: len(kept)], out[len(kept) :]
        return list(zip(inner, outer)), field, neighbours(up, down), *coarse

    share, local, messages = solve((outer, inner), lower, upper, 5, 5)
    (step,), field, messages = advance(0, local, messages, share, None, None, 5, 5)
    share, local, messages = solve((field,), *messages, 5, 5)
    (total,), field, messages, coarse = advance(1, local, messages, share, step, step, 5, 4)
    (scale,) = call(diagonal_kernel, "diagonal", (lower, upper, geo, mats["coarse"]), shapes(4, 64))
    *total, field, up, down = call(
        coarse_kernel,
        "coarse",
        (coarse, *messages, scale, coef, mats["prolong"], *total, field),
        shapes(4, 384, 128, 512, 128, 128),
        (vmem((192, 4 * TILE), narrow),),
    )
    share, local, messages = solve((field,), *neighbours(up, down), 4, 4)
    (step, total), field, messages = advance(2, local, messages, share, None, total, 4, 4)
    share, local, messages = solve((field,), *messages, 4, 3)
    (total,), field, messages = advance(3, local, messages, share, step, total, 3, 3)
    sol, inner = call(
        finish_inner_kernel,
        "finish_inner",
        (rot, field, *total),
        ((512, OWN), (384, OWN)),
        (vmem((3, 384, TILE), wide),),
        scalars=1,
    )
    (res,) = call(
        finish_outer_kernel,
        "finish_outer",
        (rot, field, *messages, inner),
        ((512, OWN),),
        (vmem((3, 128, TILE), wide),),
        scalars=1,
    )
    return sol.reshape(rhs.shape), res.reshape(rhs.shape)


def solution(mesh):
    return jax.shard_map(
        per_device,
        mesh=mesh,
        in_specs=(P(None, None, None, ("grp", "sub")), P("grp"), P(), P(), P()),
        out_specs=(P(None, None, None, ("grp", "sub")), P(None, None, None, ("grp", "sub"))),
        check_vma=False,
    )
```

time: 145 us -> 122 us (0.84)
  waiting for transfers between devices: 83.5 us -> 65.6 us
  Pallas kernels: 38.3 us -> 32 us
  starting transfers between devices: 15.5 us -> 17.3 us
    ppermute x22 -> x24, waiting for transfers between devices: 83.5 us -> 65.6 us  [shifted(): lax.ppermute(value, axis, [(n, (n + steps) % count) for n in range(count)])]
    pallas_call x12 -> x23, Pallas kernels: 38.3 us -> 32 us  [call(): pl.pallas_call(kernel, out_shape=[jax.ShapeDtypeStruct(out, jnp.float32)...]
    unnamed x26 -> x24, local copies, waits for them, and re-layouts: 3.07 us -> 1 us
    ppermute x22 -> x24, starting transfers between devices: 15.5 us -> 17.3 us  [shifted(): lax.ppermute(value, axis, [(n, (n + steps) % count) for n in range(count)])]
  transfers between devices with their start and end apart: 22 -> 24, of which waited for: 20 -> 18; matrix products, arithmetic and copies ran while one was open for 2% -> 3% of each run, Pallas kernels for 7% -> 13%
where the time goes in v2:
time: 122 us
  waiting for transfers between devices  65.6 us (54%)
  Pallas kernels  32 us (26%)
  starting transfers between devices  17.3 us (14%)
  local copies, waits for them, and re-layouts  4.7 us (4%)
  between operations  1.64 us (1%)
    ppermute x24, waiting for transfers between devices, shifted(): lax.ppermute(value, axis, [(n, (n + steps) % count) for n in range(count)])  65.6 us
    pallas_call x23, Pallas kernels, call(): pl.pallas_call(kernel, out_shape=[jax.ShapeDtypeStruct(out, jnp.float32)...  32 us
    ppermute x24, starting transfers between devices, shifted(): lax.ppermute(value, axis, [(n, (n + steps) % count) for n in range(count)])  17.3 us
  transfers between devices with their start and end apart: 24, of which 18 were waited for; matrix products, arithmetic and copies ran while one was open for 3% of the time, Pallas kernels for 13%

profile of v2, /device:TPU:31, one launch (start us, length us, event | category | flops | bytes accessed | tf_op | source)
XLA Modules:
  0.0 122.2 jit_solution(4915685065742833912)
XLA Ops:
  0.6 1.0 fusion
  1.7 3.8 %collective-permute-start.1 = (f32[256,256]{1,0:T(8,128)S(1)}, f32[256,256]{1,0:T(8,128)S(1)}, u32[]{:S(2)}, u32[]{:S(2)}) collective-permute-start(f32[256,256]{1,0:T(8,128)S(1)} %pad_maximum_fusion), channel_id=1, source_target_pairs={{0,3},{1,0},{2,1},{3,2},{4,7},{5,4},{6,5},{7,6},{8,11},{9,8},{10,9... | collective-permute-start | bytes 786440 | tf_op jit(solution)/shard_map/ppermute | solution.py:785
  5.5 0.8 pad_maximum_fusion.1
  6.4 0.1 dynamic_slice.7
  7.3 0.1 pad.3.clone
  7.4 0.1 concatenate.14
  7.6 0.1 stack_reshape.3
  7.7 0.7 tile.2
  8.3 0.1 stack_tile.3
  8.4 1.3 %dynamic_slice.6.rot = s32[1]{0:T(128)} dynamic-slice(s32[32]{0:T(128)} %param.20, s32[]{:T(128)S(6)} %select_n.6), dynamic_slice_sizes={1} | dynamic-slice | bytes 12 | tf_op jit(solution)/shard_map/dynamic_slice | solution.py:798
  9.8 0.9 copy-done.8
  10.7 0.6 tables.1
  11.3 2.3 %collective-permute-done.left = f32[256,256]{1,0:T(8,128)S(1)} collective-permute-done((f32[256,256]{1,0:T(8,128)S(1)}, f32[256,256]{1,0:T(8,128)S(1)}, u32[]{:S(2)}, u32[]{:S(2)}) %collective-permute-start) | collective-permute-done | bytes 262176 | tf_op jit(solution)/shard_map/ppermute | solution.py:785
  13.6 1.2 %outer.1 = (f32[256,640]{1,0:T(8,128)S(1)}, f32[136,640]{1,0:T(8,128)S(1)}, f32[136,640]{1,0:T(8,128)S(1)}, f32[256,256]{1,0:T(8,128)S(1)}) custom-call(s32[1]{0:T(128)} %dynamic_slice.6.rot, f32[256,256]{1,0:T(8,128)S(1)} %collective-permute-done.left, f32[512,256]{1,0:T(8,128)S(1)} %get-tuple-element.67.own, f32[256,256]{1,0:T(8,128)S(1)} %collective-permute-done.1.right, ...), custom_call_target="tpu_custom_call" | custom-call | bytes 4000000 | tf_op jit(solution)/shard_map/outer/pallas_call | solution.py:763
  14.8 1.7 %collective-permute-start.2 = (f32[136,640]{1,0:T(8,128)S(1)}, f32[136,640]{1,0:T(8,128)S(1)}, u32[]{:S(2)}, u32[]{:S(2)}) collective-permute-start(f32[136,640]{1,0:T(8,128)S(1)} %get-tuple-element.69), channel_id=1, source_target_pairs={{0,4},{4,8},{8,12},{12,16},{16,20},{20,24},{24,28},{28,32},{32,36}... | collective-permute-start | bytes 1044488 | tf_op jit(solution)/shard_map/ppermute | solution.py:785
  16.5 0.3 collective-permute-start.3
  16.9 1.5 %collective-permute-start.4 = (f32[256,256]{1,0:T(8,128)S(1)}, f32[256,256]{1,0:T(8,128)S(1)}, u32[]{:S(2)}, u32[]{:S(2)}) collective-permute-start(f32[256,256]{1,0:T(8,128)S(1)} %get-tuple-element.71.own), channel_id=1, source_target_pairs={{0,1},{1,2},{2,3},{3,0},{4,5},{5,6},{6,7},{7,4},{8,9},{9,10},{10,1... | collective-permute-start | bytes 786440 | tf_op jit(solution)/shard_map/ppermute | solution.py:785
  18.3 4.7 %collective-permute-done.5.right = f32[256,256]{1,0:T(8,128)S(1)} collective-permute-done((f32[256,256]{1,0:T(8,128)S(1)}, f32[256,256]{1,0:T(8,128)S(1)}, u32[]{:S(2)}, u32[]{:S(2)}) %collective-permute-start.5) | collective-permute-done | bytes 262176 | tf_op jit(solution)/shard_map/ppermute | solution.py:785
  23.0 1.1 collective-permute-done.4.left
  24.1 1.2 inner.1.refs_1_
  25.3 1.7 %solve_inner.4 = (f32[384,640]{1,0:T(8,128)S(1)}, f32[1024,640]{1,0:T(8,128)S(1)}) custom-call(f32[256,640]{1,0:T(8,128)S(1)} %get-tuple-element.68.refs_0_, f32[256,640]{1,0:T(8,128)S(1)} %inner.1.refs_1_, bf16[4,256,480]{2,1,0:T(8,128)(2,1)S(1)} %copy-done), custom_call_target="tpu_custom_call" | custom-call | bytes 4000000 | tf_op jit(solution)/shard_map/solve_inner/pallas_call | solution.py:763
  27.0 2.2 %solve_outer.4 = (f32[128,640]{1,0:T(8,128)S(1)}, f32[512,640]{1,0:T(8,128)S(1)}, f32[64,640]{1,0:T(8,128)S(1)}, f32[64,640]{1,0:T(8,128)S(1)}) custom-call(f32[256,640]{1,0:T(8,128)S(1)} %get-tuple-element.68.refs_0_, f32[136,640]{1,0:T(8,128)S(1)} %collective-permute-done.2.refs_1_.lower, f32[136,640]{1,0:T(8,128)S(1)} %collective-permute-done.3.refs_2_.upper, ...), custom_call_target="tpu_custom_call" | custom-call | bytes 4000000 | tf_op jit(solution)/shard_map/solve_outer/pallas_call | solution.py:763
  29.3 5.5 %collective-permute-start.6 = (f32[64,640]{1,0:T(8,128)S(1)}, f32[64,640]{1,0:T(8,128)S(1)}, u32[]{:S(2)}, u32[]{:S(2)}) collective-permute-start(f32[64,640]{1,0:T(8,128)S(1)} %get-tuple-element.75), channel_id=1, source_target_pairs={{0,4},{4,8},{8,12},{12,16},{16,20},{20,24},{24,28},{28,32},{32,36}... | collective-permute-start | bytes 491528 | tf_op jit(solution)/shard_map/ppermute | solution.py:785
  34.8 1.6 %step0_inner.1 = (f32[384,640]{1,0:T(8,128)S(1)}, f32[512,640]{1,0:T(8,128)S(1)}) custom-call(f32[512,640]{1,0:T(8,128)S(1)} %get-tuple-element.74.refs_0_, f32[24,640]{1,0:T(8,128)S(1)} %get-tuple-element.79.refs_1_.refs_6_.refs_3_.refs_8_.coef.refs_2_.refs_7_, bf16[4,320,288]{2,1,0:T(8,128)(2,1)S(1)} %copy-done.1), custom_call_target="tpu_custom_call" | custom-call | bytes 4000000 | tf_op jit(solution)/shard_map/step0_inner/pallas_call | solution.py:763
  36.3 0.7 collective-permute-done.6.refs_1_
  37.0 5.8 %collective-permute-done.7.refs_2_ = f32[64,640]{1,0:T(8,128)S(1)} collective-permute-done((f32[64,640]{1,0:T(8,128)S(1)}, f32[64,640]{1,0:T(8,128)S(1)}, u32[]{:S(2)}, u32[]{:S(2)}) %collective-permute-start.7) | collective-permute-done | bytes 163872 | tf_op jit(solution)/shard_map/ppermute | solution.py:785
  42.8 0.9 step0_outer.1
  43.8 0.5 collective-permute-start.9
  44.3 1.7 %solve_inner.5 = (f32[384,640]{1,0:T(8,128)S(1)}, f32[1024,640]{1,0:T(8,128)S(1)}) custom-call(f32[512,640]{1,0:T(8,128)S(1)} %get-tuple-element.81.refs_0_, bf16[4,256,480]{2,1,0:T(8,128)(2,1)S(1)} %copy-done), custom_call_target="tpu_custom_call" | custom-call | bytes 4000000 | tf_op jit(solution)/shard_map/solve_inner/pallas_call | solution.py:763
  46.0 1.8 %collective-permute-done.8.refs_1_ = f32[128,640]{1,0:T(8,128)S(1)} collective-permute-done((f32[128,640]{1,0:T(8,128)S(1)}, f32[128,640]{1,0:T(8,128)S(1)}, u32[]{:S(2)}, u32[]{:S(2)}) %collective-permute-start.8) | collective-permute-done | bytes 327712 | tf_op jit(solution)/shard_map/ppermute | solution.py:785
  47.8 5.9 %collective-permute-done.9.refs_2_ = f32[128,640]{1,0:T(8,128)S(1)} collective-permute-done((f32[128,640]{1,0:T(8,128)S(1)}, f32[128,640]{1,0:T(8,128)S(1)}, u32[]{:S(2)}, u32[]{:S(2)}) %collective-permute-start.9) | collective-permute-done | bytes 327712 | tf_op jit(solution)/shard_map/ppermute | solution.py:785
  53.6 2.1 %solve_outer.5 = (f32[128,640]{1,0:T(8,128)S(1)}, f32[512,640]{1,0:T(8,128)S(1)}, f32[64,640]{1,0:T(8,128)S(1)}, f32[64,640]{1,0:T(8,128)S(1)}) custom-call(f32[512,640]{1,0:T(8,128)S(1)} %get-tuple-element.81.refs_0_, f32[128,640]{1,0:T(8,128)S(1)} %collective-permute-done.8.refs_1_, f32[128,640]{1,0:T(8,128)S(1)} %collective-permute-done.9.refs_2_, ...), custom_call_target="tpu_custom_call" | custom-call | bytes 4000000 | tf_op jit(solution)/shard_map/solve_outer/pallas_call | solution.py:763
  55.9 0.5 collective-permute-start.11
  56.4 1.4 %step1_inner.1 = (f32[384,512]{1,0:T(8,128)S(1)}, f32[512,512]{1,0:T(8,128)S(1)}) custom-call(f32[512,640]{1,0:T(8,128)S(1)} %get-tuple-element.85.refs_0_, f32[384,640]{1,0:T(8,128)S(1)} %get-tuple-element.91.refs_1_.refs_2_, f32[384,640]{1,0:T(8,128)S(1)} %get-tuple-element.91.refs_1_.refs_2_, ...), custom_call_target="tpu_custom_call" | custom-call | bytes 4000000 | tf_op jit(solution)/shard_map/step1_inner/pallas_call | solution.py:763
  57.8 0.3 collective-permute-done.10.refs_1_
  58.1 5.9 %collective-permute-done.11.refs_2_ = f32[64,640]{1,0:T(8,128)S(1)} collective-permute-done((f32[64,640]{1,0:T(8,128)S(1)}, f32[64,640]{1,0:T(8,128)S(1)}, u32[]{:S(2)}, u32[]{:S(2)}) %collective-permute-start.11) | collective-permute-done | bytes 163872 | tf_op jit(solution)/shard_map/ppermute | solution.py:785
  64.0 1.2 step1_outer.1
  65.3 0.5 collective-permute-start.13
  65.8 0.4 diagonal.1.scale
  66.2 0.3 collective-permute-done.12.below
  66.5 5.5 %collective-permute-done.13.above = f32[16,512]{1,0:T(8,128)S(1)} collective-permute-done((f32[16,512]{1,0:T(8,128)S(1)}, f32[16,512]{1,0:T(8,128)S(1)}, u32[]{:S(2)}, u32[]{:S(2)}) %collective-permute-start.13) | collective-permute-done | bytes 32800 | tf_op jit(solution)/shard_map/ppermute | solution.py:785
  72.0 1.5 %coarse.1 = (f32[384,512]{1,0:T(8,128)S(1)}, f32[128,512]{1,0:T(8,128)S(1)}, f32[512,512]{1,0:T(8,128)S(1)}, f32[128,512]{1,0:T(8,128)S(1)}, f32[128,512]{1,0:T(8,128)S(1)}) custom-call(f32[64,512]{1,0:T(8,128)S(1)} %get-tuple-element.93.local, f32[16,512]{1,0:T(8,128)S(1)} %collective-permute-done.12.below, f32[16,512]{1,0:T(8,128)S(1)} %collective-permute-done.13.above, ...), custom_call_target="tpu_custom_call" | custom-call | bytes 4000000 | tf_op jit(solution)/shard_map/coarse/pallas_call | solution.py:763
  73.6 0.5 collective-permute-start.15
  74.1 1.4 %solve_inner.6 = (f32[384,512]{1,0:T(8,128)S(1)}, f32[1024,512]{1,0:T(8,128)S(1)}) custom-call(f32[512,512]{1,0:T(8,128)S(1)} %get-tuple-element.99.refs_0_, bf16[4,256,480]{2,1,0:T(8,128)(2,1)S(1)} %copy-done), custom_call_target="tpu_custom_call" | custom-call | bytes 4000000 | tf_op jit(solution)/shard_map/solve_inner/pallas_call | solution.py:763
  75.6 1.4 %collective-permute-done.14.refs_1_ = f32[128,512]{1,0:T(8,128)S(1)} collective-permute-done((f32[128,512]{1,0:T(8,128)S(1)}, f32[128,512]{1,0:T(8,128)S(1)}, u32[]{:S(2)}, u32[]{:S(2)}) %collective-permute-start.14) | collective-permute-done | bytes 262176 | tf_op jit(solution)/shard_map/ppermute | solution.py:785
  76.9 6.1 %collective-permute-done.15.refs_2_ = f32[128,512]{1,0:T(8,128)S(1)} collective-permute-done((f32[128,512]{1,0:T(8,128)S(1)}, f32[128,512]{1,0:T(8,128)S(1)}, u32[]{:S(2)}, u32[]{:S(2)}) %collective-permute-start.15) | collective-permute-done | bytes 262176 | tf_op jit(solution)/shard_map/ppermute | solution.py:785
  83.0 1.9 %solve_outer.6 = (f32[128,512]{1,0:T(8,128)S(1)}, f32[512,512]{1,0:T(8,128)S(1)}, f32[64,512]{1,0:T(8,128)S(1)}, f32[64,512]{1,0:T(8,128)S(1)}) custom-call(f32[512,512]{1,0:T(8,128)S(1)} %get-tuple-element.99.refs_0_, f32[128,512]{1,0:T(8,128)S(1)} %collective-permute-done.14.refs_1_, f32[128,512]{1,0:T(8,128)S(1)} %collective-permute-done.15.refs_2_, ...), custom_call_target="tpu_custom_call" | custom-call | bytes 4000000 | tf_op jit(solution)/shard_map/solve_outer/pallas_call | solution.py:763
  85.1 0.5 collective-permute-start.17
  85.5 1.5 %step2_inner.1 = (f32[384,512]{1,0:T(8,128)S(1)}, f32[384,512]{1,0:T(8,128)S(1)}, f32[512,512]{1,0:T(8,128)S(1)}) custom-call(f32[512,512]{1,0:T(8,128)S(1)} %get-tuple-element.103.refs_0_, f32[384,512]{1,0:T(8,128)S(1)} %get-tuple-element.109.refs_1_, f32[24,640]{1,0:T(8,128)S(1)} %get-tuple-element.79.refs_1_.refs_6_.refs_3_.refs_8_.coef.refs_2_.refs_7_, ...), custom_call_target="tpu_custom_call" | custom-call | bytes 4000000 | tf_op jit(solution)/shard_map/step2_inner/pallas_call | solution.py:763
  87.0 5.8 %collective-permute-done.17.refs_2_ = f32[64,512]{1,0:T(8,128)S(1)} collective-permute-done((f32[64,512]{1,0:T(8,128)S(1)}, f32[64,512]{1,0:T(8,128)S(1)}, u32[]{:S(2)}, u32[]{:S(2)}) %collective-permute-start.17) | collective-permute-done | bytes 131104 | tf_op jit(solution)/shard_map/ppermute | solution.py:785
  92.8 0.8 step2_outer.1
  93.7 0.5 collective-permute-start.19
  94.2 1.2 %solve_inner.7 = (f32[384,384]{1,0:T(8,128)S(1)}, f32[1024,384]{1,0:T(8,128)S(1)}) custom-call(f32[512,512]{1,0:T(8,128)S(1)} %get-tuple-element.111.refs_0_, bf16[4,256,480]{2,1,0:T(8,128)(2,1)S(1)} %copy-done), custom_call_target="tpu_custom_call" | custom-call | bytes 4000000 | tf_op jit(solution)/shard_map/solve_inner/pallas_call | solution.py:763
  95.5 1.6 %collective-permute-done.18.refs_1_ = f32[128,512]{1,0:T(8,128)S(1)} collective-permute-done((f32[128,512]{1,0:T(8,128)S(1)}, f32[128,512]{1,0:T(8,128)S(1)}, u32[]{:S(2)}, u32[]{:S(2)}) %collective-permute-start.18) | collective-permute-done | bytes 262176 | tf_op jit(solution)/shard_map/ppermute | solution.py:785
  97.0 5.9 %collective-permute-done.19.refs_2_ = f32[128,512]{1,0:T(8,128)S(1)} collective-permute-done((f32[128,512]{1,0:T(8,128)S(1)}, f32[128,512]{1,0:T(8,128)S(1)}, u32[]{:S(2)}, u32[]{:S(2)}) %collective-permute-start.19) | collective-permute-done | bytes 262176 | tf_op jit(solution)/shard_map/ppermute | solution.py:785
  102.9 1.9 %solve_outer.7 = (f32[128,384]{1,0:T(8,128)S(1)}, f32[512,384]{1,0:T(8,128)S(1)}, f32[64,384]{1,0:T(8,128)S(1)}, f32[64,384]{1,0:T(8,128)S(1)}) custom-call(f32[512,512]{1,0:T(8,128)S(1)} %get-tuple-element.111.refs_0_, f32[128,512]{1,0:T(8,128)S(1)} %collective-permute-done.18.refs_1_, f32[128,512]{1,0:T(8,128)S(1)} %collective-permute-done.19.refs_2_, ...), custom_call_target="tpu_custom_call" | custom-call | bytes 4000000 | tf_op jit(solution)/shard_map/solve_outer/pallas_call | solution.py:763
  104.9 0.5 collective-permute-start.21
  105.4 1.2 step3_inner.1
  106.5 5.8 %collective-permute-done.21.refs_2_ = f32[64,384]{1,0:T(8,128)S(1)} collective-permute-done((f32[64,384]{1,0:T(8,128)S(1)}, f32[64,384]{1,0:T(8,128)S(1)}, u32[]{:S(2)}, u32[]{:S(2)}) %collective-permute-start.21) | collective-permute-done | bytes 98336 | tf_op jit(solution)/shard_map/ppermute | solution.py:785
  112.3 0.6 step3_outer.1
  113.0 0.5 collective-permute-start.23
  113.5 2.1 %finish_inner.1 = (f32[512,256]{1,0:T(8,128)}, f32[384,256]{1,0:T(8,128)S(1)}) custom-call(s32[1]{0:T(128)} %dynamic_slice.6.rot, f32[512,384]{1,0:T(8,128)S(1)} %get-tuple-element.125.local, f32[384,384]{1,0:T(8,128)S(1)} %get-tuple-element.126.total_inner, f32[128,384]{1,0:T(8,128)S(1)} %get-tuple-element.127.total_outer), custom_call_target="tpu_custom_call" | custom-call | bytes 4000000 | tf_op jit(solution)/shard_map/finish_inner/pallas_call | solution.py:763
  115.6 4.9 %collective-permute-done.23.above = f32[64,384]{1,0:T(8,128)S(1)} collective-permute-done((f32[64,384]{1,0:T(8,128)S(1)}, f32[64,384]{1,0:T(8,128)S(1)}, u32[]{:S(2)}, u32[]{:S(2)}) %collective-permute-start.23) | collective-permute-done | bytes 98336 | tf_op jit(solution)/shard_map/ppermute | solution.py:785
  120.4 1.7 %finish_outer.1 = f32[512,256]{1,0:T(8,128)} custom-call(s32[1]{0:T(128)} %dynamic_slice.6.rot, f32[512,384]{1,0:T(8,128)S(1)} %get-tuple-element.125.local, f32[64,384]{1,0:T(8,128)S(1)} %collective-permute-done.22.below, f32[64,384]{1,0:T(8,128)S(1)} %collective-permute-done.23.above, f32[384,256]{1,0:T(8,128)S(1)} %get-tuple-element.131.inner), custom_call_target="tpu_custom_call" | custom-call | bytes 4000000 | tf_op jit(solution)/shard_map/finish_outer/pallas_call | solution.py:763
  (47 shorter events, 1.1 us)
Async XLA Ops:
  0.6 9.2 %copy-start.6 = (f32[8,8,8,256]{3,2,1,0:T(8,128)S(1)}, f32[8,8,8,256]{3,2,1,0:T(8,128)}, u32[]{:S(2)}) copy-start(f32[8,8,8,256]{3,2,1,0:T(8,128)} %param.16) | copy-start | bytes 1572868
  1.7 9.6 %collective-permute-start.1 = (f32[256,256]{1,0:T(8,128)S(1)}, f32[256,256]{1,0:T(8,128)S(1)}, u32[]{:S(2)}, u32[]{:S(2)}) collective-permute-start(f32[256,256]{1,0:T(8,128)S(1)} %pad_maximum_fusion), channel_id=1, source_target_pairs={{0,3},{1,0},{2,1},{3,2},{4,7},{5,4},{6,5},{7,6},{8,11},{9,8},{10,9... | collective-permute-start | bytes 786440 | tf_op jit(solution)/shard_map/ppermute | solution.py:785
  5.5 8.1 %collective-permute-start = (f32[256,256]{1,0:T(8,128)S(1)}, f32[256,256]{1,0:T(8,128)S(1)}, u32[]{:S(2)}, u32[]{:S(2)}) collective-permute-start(f32[256,256]{1,0:T(8,128)S(1)} %pad_maximum_fusion), channel_id=1, source_target_pairs={{0,1},{1,2},{2,3},{3,0},{4,5},{5,6},{6,7},{7,4},{8,9},{9,10},{10,1... | collective-permute-start | bytes 786440 | tf_op jit(solution)/shard_map/ppermute | solution.py:785
  9.8 1.0 copy-start.8
  10.7 14.5 %copy-start = (bf16[4,256,480]{2,1,0:T(8,128)(2,1)S(1)}, bf16[4,256,480]{2,1,0:T(8,128)(2,1)}, u32[]{:S(2)}) copy-start(bf16[4,256,480]{2,1,0:T(8,128)(2,1)} %constant.47.clone.refs_2_.refs_1_) | copy-start | bytes 2949124
  14.8 12.1 %collective-permute-start.2 = (f32[136,640]{1,0:T(8,128)S(1)}, f32[136,640]{1,0:T(8,128)S(1)}, u32[]{:S(2)}, u32[]{:S(2)}) collective-permute-start(f32[136,640]{1,0:T(8,128)S(1)} %get-tuple-element.69), channel_id=1, source_target_pairs={{0,4},{4,8},{8,12},{12,16},{16,20},{20,24},{24,28},{28,32},{32,36}... | collective-permute-start | bytes 1044488 | tf_op jit(solution)/shard_map/ppermute | solution.py:785
  16.5 10.5 %collective-permute-start.3 = (f32[136,640]{1,0:T(8,128)S(1)}, f32[136,640]{1,0:T(8,128)S(1)}, u32[]{:S(2)}, u32[]{:S(2)}) collective-permute-start(f32[136,640]{1,0:T(8,128)S(1)} %get-tuple-element.70), channel_id=1, source_target_pairs={{0,124},{4,0},{8,4},{12,8},{16,12},{20,16},{24,20},{28,24},{32,28}... | collective-permute-start | bytes 1044488 | tf_op jit(solution)/shard_map/ppermute | solution.py:785
  16.9 10.2 %copy-start.2 = (bf16[4,128,512]{2,1,0:T(8,128)(2,1)S(1)}, bf16[4,128,512]{2,1,0:T(8,128)(2,1)}, u32[]{:S(2)}) copy-start(bf16[4,128,512]{2,1,0:T(8,128)(2,1)} %constant.49.clone.refs_6_) | copy-start | bytes 1572868
  16.9 10.2 %copy-start.3 = (bf16[4,256,240]{2,1,0:T(8,128)(2,1)S(1)}, bf16[4,256,240]{2,1,0:T(8,128)(2,1)}, u32[]{:S(2)}) copy-start(bf16[4,256,240]{2,1,0:T(8,128)(2,1)} %constant.48.clone.refs_5_) | copy-start | bytes 1474564
  16.9 10.2 %copy-start.4 = (bf16[4,128,256]{2,1,0:T(8,128)(2,1)S(1)}, bf16[4,128,256]{2,1,0:T(8,128)(2,1)}, u32[]{:S(2)}) copy-start(bf16[4,128,256]{2,1,0:T(8,128)(2,1)} %constant.50.clone.refs_7_) | copy-start | bytes 786436
  16.9 6.1 %collective-permute-start.5 = (f32[256,256]{1,0:T(8,128)S(1)}, f32[256,256]{1,0:T(8,128)S(1)}, u32[]{:S(2)}, u32[]{:S(2)}) collective-permute-start(f32[256,256]{1,0:T(8,128)S(1)} %get-tuple-element.71.own), channel_id=1, source_target_pairs={{0,3},{1,0},{2,1},{3,2},{4,7},{5,4},{6,5},{7,6},{8,11},{9,8},{10,9... | collective-permute-start | bytes 786440 | tf_op jit(solution)/shard_map/ppermute | solution.py:785
  16.9 7.2 %collective-permute-start.4 = (f32[256,256]{1,0:T(8,128)S(1)}, f32[256,256]{1,0:T(8,128)S(1)}, u32[]{:S(2)}, u32[]{:S(2)}) collective-permute-start(f32[256,256]{1,0:T(8,128)S(1)} %get-tuple-element.71.own), channel_id=1, source_target_pairs={{0,1},{1,2},{2,3},{3,0},{4,5},{5,6},{6,7},{7,4},{8,9},{9,10},{10,1... | collective-permute-start | bytes 786440 | tf_op jit(solution)/shard_map/ppermute | solution.py:785
  27.0 7.7 %copy-start.1 = (bf16[4,320,288]{2,1,0:T(8,128)(2,1)S(1)}, bf16[4,320,288]{2,1,0:T(8,128)(2,1)}, u32[]{:S(2)}) copy-start(bf16[4,320,288]{2,1,0:T(8,128)(2,1)} %constant.51.clone.refs_2_.refs_4_.refs_3_) | copy-start | bytes 2211844
  29.3 13.5 %copy-start.5 = (bf16[4,192,96]{2,1,0:T(8,128)(2,1)S(1)}, bf16[4,192,96]{2,1,0:T(8,128)(2,1)}, u32[]{:S(2)}) copy-start(bf16[4,192,96]{2,1,0:T(8,128)(2,1)} %constant.52.clone.refs_7_.refs_9_.refs_8_) | copy-start | bytes 442372
  29.3 7.7 %collective-permute-start.6 = (f32[64,640]{1,0:T(8,128)S(1)}, f32[64,640]{1,0:T(8,128)S(1)}, u32[]{:S(2)}, u32[]{:S(2)}) collective-permute-start(f32[64,640]{1,0:T(8,128)S(1)} %get-tuple-element.75), channel_id=1, source_target_pairs={{0,4},{4,8},{8,12},{12,16},{16,20},{20,24},{24,28},{28,32},{32,36}... | collective-permute-start | bytes 491528 | tf_op jit(solution)/shard_map/ppermute | solution.py:785
  34.7 8.1 %collective-permute-start.7 = (f32[64,640]{1,0:T(8,128)S(1)}, f32[64,640]{1,0:T(8,128)S(1)}, u32[]{:S(2)}, u32[]{:S(2)}) collective-permute-start(f32[64,640]{1,0:T(8,128)S(1)} %get-tuple-element.76), channel_id=1, source_target_pairs={{0,124},{4,0},{8,4},{12,8},{16,12},{20,16},{24,20},{28,24},{32,28}... | collective-permute-start | bytes 491528 | tf_op jit(solution)/shard_map/ppermute | solution.py:785
  43.7 4.1 %collective-permute-start.8 = (f32[128,640]{1,0:T(8,128)S(1)}, f32[128,640]{1,0:T(8,128)S(1)}, u32[]{:S(2)}, u32[]{:S(2)}) collective-permute-start(f32[128,640]{1,0:T(8,128)S(1)} %get-tuple-element.82), channel_id=1, source_target_pairs={{0,4},{4,8},{8,12},{12,16},{16,20},{20,24},{24,28},{28,32},{32,36}... | collective-permute-start | bytes 983048 | tf_op jit(solution)/shard_map/ppermute | solution.py:785
  43.8 9.9 %collective-permute-start.9 = (f32[128,640]{1,0:T(8,128)S(1)}, f32[128,640]{1,0:T(8,128)S(1)}, u32[]{:S(2)}, u32[]{:S(2)}) collective-permute-start(f32[128,640]{1,0:T(8,128)S(1)} %get-tuple-element.83), channel_id=1, source_target_pairs={{0,124},{4,0},{8,4},{12,8},{16,12},{20,16},{24,20},{28,24},{32,28}... | collective-permute-start | bytes 983048 | tf_op jit(solution)/shard_map/ppermute | solution.py:785
  55.8 2.3 %collective-permute-start.10 = (f32[64,640]{1,0:T(8,128)S(1)}, f32[64,640]{1,0:T(8,128)S(1)}, u32[]{:S(2)}, u32[]{:S(2)}) collective-permute-start(f32[64,640]{1,0:T(8,128)S(1)} %get-tuple-element.86), channel_id=1, source_target_pairs={{0,4},{4,8},{8,12},{12,16},{16,20},{20,24},{24,28},{28,32},{32,36}... | collective-permute-start | bytes 491528 | tf_op jit(solution)/shard_map/ppermute | solution.py:785
  55.9 8.1 %collective-permute-start.11 = (f32[64,640]{1,0:T(8,128)S(1)}, f32[64,640]{1,0:T(8,128)S(1)}, u32[]{:S(2)}, u32[]{:S(2)}) collective-permute-start(f32[64,640]{1,0:T(8,128)S(1)} %get-tuple-element.87), channel_id=1, source_target_pairs={{0,124},{4,0},{8,4},{12,8},{16,12},{20,16},{24,20},{28,24},{32,28}... | collective-permute-start | bytes 491528 | tf_op jit(solution)/shard_map/ppermute | solution.py:785
  56.4 7.6 %copy-start.9 = (bf16[64,1024]{1,0:T(8,128)(2,1)S(1)}, bf16[64,1024]{1,0:T(8,128)(2,1)}, u32[]{:S(2)}) copy-start(bf16[64,1024]{1,0:T(8,128)(2,1)} %constant.53.clone.refs_10_) | copy-start | bytes 393220
  56.4 7.6 %copy-start.10 = (bf16[64,512]{1,0:T(8,128)(2,1)S(1)}, bf16[64,512]{1,0:T(8,128)(2,1)}, u32[]{:S(2)}) copy-start(bf16[64,512]{1,0:T(8,128)(2,1)} %constant.54.clone.refs_11_) | copy-start | bytes 196612
  64.0 1.8 %copy-start.11 = (f32[64,8]{1,0:T(8,128)S(1)}, f32[64,8]{1,0:T(8,128)}, u32[]{:S(2)}) copy-start(f32[64,8]{1,0:T(8,128)} %constant.57.clone.table) | copy-start | bytes 6148
  64.0 8.0 %copy-start.7 = (bf16[2048,192]{1,0:T(8,128)(2,1)S(1)}, bf16[2048,192]{1,0:T(8,128)(2,1)}, u32[]{:S(2)}) copy-start(bf16[2048,192]{1,0:T(8,128)(2,1)} %constant.55.clone.prolong) | copy-start | bytes 2359300
  65.2 1.3 %collective-permute-start.12 = (f32[16,512]{1,0:T(8,128)S(1)}, f32[16,512]{1,0:T(8,128)S(1)}, u32[]{:S(2)}, u32[]{:S(2)}) collective-permute-start(f32[16,512]{1,0:T(8,128)S(1)} %get-tuple-element.94), channel_id=1, source_target_pairs={{0,4},{4,8},{8,12},{12,16},{16,20},{20,24},{24,28},{28,32},{32,36}... | collective-permute-start | bytes 98312 | tf_op jit(solution)/shard_map/ppermute | solution.py:785
  65.3 6.7 %collective-permute-start.13 = (f32[16,512]{1,0:T(8,128)S(1)}, f32[16,512]{1,0:T(8,128)S(1)}, u32[]{:S(2)}, u32[]{:S(2)}) collective-permute-start(f32[16,512]{1,0:T(8,128)S(1)} %get-tuple-element.95), channel_id=1, source_target_pairs={{0,124},{4,0},{8,4},{12,8},{16,12},{20,16},{24,20},{28,24},{32,28}... | collective-permute-start | bytes 98312 | tf_op jit(solution)/shard_map/ppermute | solution.py:785
  73.6 3.4 %collective-permute-start.14 = (f32[128,512]{1,0:T(8,128)S(1)}, f32[128,512]{1,0:T(8,128)S(1)}, u32[]{:S(2)}, u32[]{:S(2)}) collective-permute-start(f32[128,512]{1,0:T(8,128)S(1)} %get-tuple-element.100), channel_id=1, source_target_pairs={{0,4},{4,8},{8,12},{12,16},{16,20},{20,24},{24,28},{28,32},{32,36}... | collective-permute-start | bytes 786440 | tf_op jit(solution)/shard_map/ppermute | solution.py:785
  73.6 9.4 %collective-permute-start.15 = (f32[128,512]{1,0:T(8,128)S(1)}, f32[128,512]{1,0:T(8,128)S(1)}, u32[]{:S(2)}, u32[]{:S(2)}) collective-permute-start(f32[128,512]{1,0:T(8,128)S(1)} %get-tuple-element.101), channel_id=1, source_target_pairs={{0,124},{4,0},{8,4},{12,8},{16,12},{20,16},{24,20},{28,24},{32,28}... | collective-permute-start | bytes 786440 | tf_op jit(solution)/shard_map/ppermute | solution.py:785
  85.0 2.0 %collective-permute-start.16 = (f32[64,512]{1,0:T(8,128)S(1)}, f32[64,512]{1,0:T(8,128)S(1)}, u32[]{:S(2)}, u32[]{:S(2)}) collective-permute-start(f32[64,512]{1,0:T(8,128)S(1)} %get-tuple-element.104), channel_id=1, source_target_pairs={{0,4},{4,8},{8,12},{12,16},{16,20},{20,24},{24,28},{28,32},{32,36}... | collective-permute-start | bytes 393224 | tf_op jit(solution)/shard_map/ppermute | solution.py:785
  85.1 7.8 %collective-permute-start.17 = (f32[64,512]{1,0:T(8,128)S(1)}, f32[64,512]{1,0:T(8,128)S(1)}, u32[]{:S(2)}, u32[]{:S(2)}) collective-permute-start(f32[64,512]{1,0:T(8,128)S(1)} %get-tuple-element.105), channel_id=1, source_target_pairs={{0,124},{4,0},{8,4},{12,8},{16,12},{20,16},{24,20},{28,24},{32,28}... | collective-permute-start | bytes 393224 | tf_op jit(solution)/shard_map/ppermute | solution.py:785
  93.6 3.4 %collective-permute-start.18 = (f32[128,512]{1,0:T(8,128)S(1)}, f32[128,512]{1,0:T(8,128)S(1)}, u32[]{:S(2)}, u32[]{:S(2)}) collective-permute-start(f32[128,512]{1,0:T(8,128)S(1)} %get-tuple-element.112), channel_id=1, source_target_pairs={{0,4},{4,8},{8,12},{12,16},{16,20},{20,24},{24,28},{28,32},{32,36}... | collective-permute-start | bytes 786440 | tf_op jit(solution)/shard_map/ppermute | solution.py:785
  93.7 9.2 %collective-permute-start.19 = (f32[128,512]{1,0:T(8,128)S(1)}, f32[128,512]{1,0:T(8,128)S(1)}, u32[]{:S(2)}, u32[]{:S(2)}) collective-permute-start(f32[128,512]{1,0:T(8,128)S(1)} %get-tuple-element.113), channel_id=1, source_target_pairs={{0,124},{4,0},{8,4},{12,8},{16,12},{20,16},{24,20},{28,24},{32,28}... | collective-permute-start | bytes 786440 | tf_op jit(solution)/shard_map/ppermute | solution.py:785
  104.8 1.7 %collective-permute-start.20 = (f32[64,384]{1,0:T(8,128)S(1)}, f32[64,384]{1,0:T(8,128)S(1)}, u32[]{:S(2)}, u32[]{:S(2)}) collective-permute-start(f32[64,384]{1,0:T(8,128)S(1)} %get-tuple-element.116), channel_id=1, source_target_pairs={{0,4},{4,8},{8,12},{12,16},{16,20},{20,24},{24,28},{28,32},{32,36}... | collective-permute-start | bytes 294920 | tf_op jit(solution)/shard_map/ppermute | solution.py:785
  104.9 7.4 %collective-permute-start.21 = (f32[64,384]{1,0:T(8,128)S(1)}, f32[64,384]{1,0:T(8,128)S(1)}, u32[]{:S(2)}, u32[]{:S(2)}) collective-permute-start(f32[64,384]{1,0:T(8,128)S(1)} %get-tuple-element.117), channel_id=1, source_target_pairs={{0,124},{4,0},{8,4},{12,8},{16,12},{20,16},{24,20},{28,24},{32,28}... | collective-permute-start | bytes 294920 | tf_op jit(solution)/shard_map/ppermute | solution.py:785
  112.9 2.6 %collective-permute-start.22 = (f32[64,384]{1,0:T(8,128)S(1)}, f32[64,384]{1,0:T(8,128)S(1)}, u32[]{:S(2)}, u32[]{:S(2)}) collective-permute-start(f32[64,384]{1,0:T(8,128)S(1)} %get-tuple-element.129), channel_id=1, source_target_pairs={{0,4},{4,8},{8,12},{12,16},{16,20},{20,24},{24,28},{28,32},{32,36}... | collective-permute-start | bytes 294920 | tf_op jit(solution)/shard_map/ppermute | solution.py:785
  113.0 7.4 %collective-permute-start.23 = (f32[64,384]{1,0:T(8,128)S(1)}, f32[64,384]{1,0:T(8,128)S(1)}, u32[]{:S(2)}, u32[]{:S(2)}) collective-permute-start(f32[64,384]{1,0:T(8,128)S(1)} %get-tuple-element.130), channel_id=1, source_target_pairs={{0,124},{4,0},{8,4},{12,8},{16,12},{20,16},{24,20},{28,24},{32,28}... | collective-permute-start | bytes 294920 | tf_op jit(solution)/shard_map/ppermute | solution.py:785

commit v3 on v2

--- a/solution.py
+++ b/solution.py
@@ -28,6 +28,7 @@
 TILES = LANES // TILE
 TERMS = 32
 BATCH = 4
+EARLY = 20_000_000_000
 
 cheb_upper = 2.0
 cheb_ratio = 0.1
@@ -226,7 +227,8 @@
     return {
         "forward_inner": triple(forward_inner),
         "forward_outer": triple(forward_outer),
-        "backward": pair(backward),
+        "backward_outer": pair(backward[:, :32]),
+        "backward_inner": pair(backward[:, 32:]),
         "apply_inner": triple(apply_inner),
         "apply_outer": triple(apply_outer),
         "restrict": pair(restrict),
@@ -391,8 +393,10 @@
     return jnp.concatenate(rows).astype(jnp.bfloat16)
 
 
-def tables_kernel(geo, modes, own, lam, coef, kept):
-    kept[...] = own[...]
+def tables_kernel(geo, modes, own, lam, coef, kept, middle):
+    kept[0:128] = own[0:128]
+    kept[128:256] = own[384:512]
+    middle[...] = own[128:384]
     la, lb, lz = (geo[n : n + 1] for n in range(3))
     cz = la * lb / (2.0 * lz)
     ca = lz * lb / (2.0 * la)
@@ -417,7 +421,7 @@
     return join([*center, near, jnp.where(lane < half, first, last)])
 
 
-def outer_kernel(rot, left, own, right, geo, field, up, down, inner):
+def outer_kernel(rot, left, own, right, geo, field, up, down):
     factor = point_factor(LANES)
     for case in range(4):
 
@@ -425,7 +429,7 @@
         def _(case=case):
             for at, i in enumerate((0, 1, 6, 7)):
                 here = slice(at * 64, at * 64 + 64)
-                value = window(case, left, own[i * 64 : i * 64 + 64], right, here)
+                value = window(case, left, own[here], right, here)
                 field[here] = value * plane_factor(factor, i)
 
     up[0:128] = field[128:256]
@@ -433,7 +437,10 @@
     length = jnp.broadcast_to(geo[2:3], (PTS, LANES))
     up[128:136] = length
     down[128:136] = length
-    inner[...] = own[128:384]
+
+
+def follow_kernel(left, right, own, inner):
+    inner[...] = own[...]
 
 
 def inner_kernel(rot, left, own, right, field):
@@ -510,7 +517,7 @@
 
 def solve_outer_kernel(start_up, wide, tiles, *refs):
     field, below, above, spectrum, lam, fwd, bwd, bwd_low = refs[:8]
-    share, out, up, down, ext, parts, packed, modes = refs[8:]
+    share, modes, up, down, ext, parts, packed = refs[8:]
     lanes = tiles * TILE
     factor = point_factor(lanes)
     last = 192 if start_up else 448
@@ -536,18 +543,21 @@
         for start, stop in chunks(lanes):
             here = slice(c * MODES, (c + 1) * MODES)
             value = dot(fwd[c], packed[c, :, start:stop]) + spectrum[here, start:stop]
-            modes[0:MODES, start:stop], modes[MODES:, start:stop] = halves(value * lam[here, start:stop])
-        for start, stop in chunks(lanes):
-            value = dot(bwd[c], modes[:, start:stop])
-            value = value + dot(bwd_low[c], modes[0:MODES, start:stop])
-            store(parts, slice(0, 128), value, c * tiles + start // TILE)
-    for i in range(4):
-        for k in range(4):
-            classes = (load(parts, block(0, i * 4 + k), tiles, c * tiles) for c in range(4))
-            for (p, q), value in zip(mirrored(i, k), unfold(*classes)):
-                out[block(p, q)] = value * factor
-    up[...] = out[448:512]
-    down[...] = out[0:64]
+            modes[c, 0:MODES, start:stop], modes[c, MODES:, start:stop] = halves(value * lam[here, start:stop])
+    back(modes, bwd, bwd_low, parts, tiles, 32)
+    for k in range(4):
+        classes = (load(parts, block(0, k), tiles, c * tiles) for c in range(4))
+        values = unfold(*classes)
+        for (p, q), value in zip(mirrored(0, k), values):
+            (down if p == 0 else up)[block(0, q)] = value * factor
+
+
+def back(modes, bwd, bwd_low, parts, tiles, rows):
+    for c in range(4):
+        for start, stop in chunks(tiles * TILE):
+            value = dot(bwd[c], modes[c, :, start:stop])
+            value = value + dot(bwd_low[c], modes[c, 0:MODES, start:stop])
+            store(parts, slice(0, rows), value, c * tiles + start // TILE)
 
 
 def stepped(kind, value, before):
@@ -558,16 +568,22 @@
 
 def step_inner_kernel(kind, wide, tiles, *refs):
     take = iter(refs)
-    local = next(take)
+    modes = next(take)
     before = next(take) if kind in (1, 3) else None
     total = next(take) if kind != 0 else None
-    coef, app = next(take), next(take)
+    coef, app, bwd, bwd_low = (next(take) for _ in range(4))
     step = next(take) if kind in (0, 2) else None
     sum_out = next(take) if kind != 0 else None
     image, ext, parts, packed = take
     lanes = tiles * TILE
-    for i in range(6):
-        store(ext, slice(i * 64, i * 64 + 64), local[i * 64 + 64 : i * 64 + 128])
+    factor = point_factor(wide * TILE)
+    back(modes, bwd, bwd_low, parts, wide, 96)
+    for i in range(3):
+        for k in range(4):
+            classes = (load(parts, block(0, i * 4 + k), wide, c * wide) for c in range(4))
+            corners = ((i, k), (5 - i, k), (i, 7 - k), (5 - i, 7 - k))
+            for corner, value in zip(corners, unfold(*classes)):
+                store(ext, block(*corner), value * factor)
     assemble_sides(ext, range(6), wide)
     for i in range(6):
         here = slice(i * 64, i * 64 + 64)
@@ -594,7 +610,7 @@
 
 def step_outer_kernel(kind, wide, tiles, *refs):
     take = iter(refs)
-    local, below, above = next(take), next(take), next(take)
+    last, below, first, above = (next(take) for _ in range(4))
     before = next(take) if kind in (1, 3) else None
     total = next(take) if kind != 0 else None
     share_inner, share_outer, image, coef, app = (next(take) for _ in range(5))
@@ -606,8 +622,8 @@
     ext, parts, packed = next(take), next(take), next(take)
     split_field = next(take) if kind == 1 else None
     lanes = tiles * TILE
-    store(ext, slice(0, 64), local[0:64] + below[...])
-    store(ext, slice(64, 128), local[448:512] + above[...])
+    store(ext, slice(0, 64), first[...] + below[...])
+    store(ext, slice(64, 128), last[...] + above[...])
     assemble_sides(ext, range(2), wide)
     for at in range(2):
         here = slice(at * 64, at * 64 + 64)
@@ -687,37 +703,45 @@
     scale[...] = assemble_coarse(jnp.concatenate([first, value[16:48], last]))
 
 
-def coarse_kernel(local, below, above, scale, coef, prolong, *refs):
-    total_inner, total_outer, field, sum_inner, sum_outer, out, up, down, packed = refs
+def coarse_outer_kernel(local, below, above, scale, coef, prolong, field, out, pack, up, down):
     lanes = local.shape[1]
     value = local[...]
     value = jnp.concatenate([value[0:16] + below[...], value[16:48], value[48:64] + above[...]])
     value = assemble_coarse(value) / scale[...]
     high, low = halves(value)
-    packed[0:64] = high
-    packed[64:128] = low
-    packed[128:192] = high
-    for start, stop in chunks(lanes):
+    pack[0, 0:64] = high
+    pack[0, 64:128] = low
+    pack[0, 128:192] = high
+    for at, i in enumerate((0, 1, 6, 7)):
+        correct(i, slice(at * 64, at * 64 + 64), coef, prolong, pack, field, out)
+    up[...] = out[128:256]
+    down[...] = out[0:128]
+
+
+def coarse_inner_kernel(pack, coef, prolong, total_inner, total_outer, field, sum_inner, sum_outer, out):
+    for at, i in enumerate((2, 3, 4, 5)):
+        correct(i, slice(at * 64, at * 64 + 64), coef, prolong, pack, field, out)
+    for start, stop in chunks(pack.shape[2]):
         for i in range(PTS):
-            here = slice(i * 64, i * 64 + 64)
-            sides = (8, PTS, stop - start)
-            terms = [
-                dot(prolong[n * 512 + i * 64 : n * 512 + i * 64 + 64], packed[:, start:stop]) for n in range(4)
-            ]
+            value = dot(prolong[i * 64 : i * 64 + 64], pack[0, :, start:stop])
             if i in (0, 7):
                 at = slice(i // 7 * 64, i // 7 * 64 + 64)
-                sum_outer[at, start:stop] = total_outer[at, start:stop] + terms[0]
+                sum_outer[at, start:stop] = total_outer[at, start:stop] + value
             else:
                 at = slice(i * 64 - 64, i * 64)
-                sum_inner[at, start:stop] = total_inner[at, start:stop] + terms[0]
-            value = (
-                terms[1].reshape(sides) * coef[0:8, start:stop]
-                + terms[2].reshape(sides) * coef[8:16, start:stop]
-                + terms[3].reshape(sides) * coef[16:24, start:stop]
-            )
-            out[here, start:stop] = field[here, start:stop] - value.reshape(64, stop - start)
-    up[...] = out[384:512]
-    down[...] = out[0:128]
+                sum_inner[at, start:stop] = total_inner[at, start:stop] + value
+
+
+def correct(i, to, coef, prolong, pack, field, out):
+    here = slice(i * 64, i * 64 + 64)
+    for start, stop in chunks(pack.shape[2]):
+        sides = (8, PTS, stop - start)
+        value = 0.0
+        for n in range(3):
+            rows = slice((n + 1) * 512 + i * 64, (n + 1) * 512 + i * 64 + 64)
+            term = dot(prolong[rows], pack[0, :, start:stop]).reshape(sides)
+            value = value + term * coef[n * PTS : (n + 1) * PTS, start:stop]
+        out[to, start:stop] = field[here, start:stop] - value.reshape(64, stop - start)
 
 
 def finish_inner_kernel(rot, local, total_inner, total_outer, sol, res, ext):
@@ -756,13 +780,15 @@
             res[448:512] = load(ext, slice(64, 128), tiles)[:, start : start + OWN]
 
 
-def call(kernel, name, args, outs, scratch=(), scalars=0, flops=0):
-    in_specs = [
-        pl.BlockSpec(memory_space=pltpu.SMEM if n < scalars else pltpu.VMEM) for n in range(len(args))
-    ]
+def call(kernel, name, args, outs, scratch=(), scalars=0, flops=0, untouched=0):
+    spaces = [pltpu.SMEM] * scalars + [pl.ANY] * untouched
+    spaces += [pltpu.VMEM] * (len(args) - len(spaces))
+    in_specs = [pl.BlockSpec(memory_space=space) for space in spaces]
     return pl.pallas_call(
         kernel,
-        out_shape=[jax.ShapeDtypeStruct(out, jnp.float32) for out in outs],
+        out_shape=[
+            jax.ShapeDtypeStruct(out, jnp.float32 if len(out) == 2 else jnp.bfloat16) for out in outs
+        ],
         in_specs=in_specs,
         out_specs=[pl.BlockSpec(memory_space=pltpu.VMEM) for _ in outs],
         scratch_shapes=list(scratch),
@@ -807,19 +833,25 @@
         ]
     )
     geo = jnp.concatenate([geo, jnp.ones((5, LANES), wide)])
-    lam, coef, own = call(
-        tables_kernel, "tables", (geo, mats["modes"], own), ((4 * MODES, LANES), (24, LANES), (512, OWN))
-    )
-    outer, up, down, inner = call(
+    lam, coef, own, middle = call(
+        tables_kernel,
+        "tables",
+        (geo, mats["modes"], own),
+        ((4 * MODES, LANES), (24, LANES), (256, OWN), (256, OWN)),
+    )
+    (middle,) = call(follow_kernel, "follow", (left, right, middle), ((256, OWN),), untouched=2)
+    near, far = beside(middle)
+    outer, up, down = call(
         outer_kernel,
         "outer",
         (rot, left, own, right, geo),
-        ((256, LANES), (136, LANES), (136, LANES), (256, OWN)),
+        ((256, LANES), (136, LANES), (136, LANES)),
         scalars=1,
     )
     lower, upper = neighbours(up, down)
-    left, right = beside(inner)
-    (inner,) = call(inner_kernel, "inner", (rot, left, inner, right), ((256, LANES),), scalars=1)
+    (inner,) = call(
+        inner_kernel, "inner", (rot, near, middle, far), ((256, LANES),), scalars=1, flops=EARLY
+    )
 
     def solve(fields, below, above, before, tiles):
         lanes = tiles * TILE
@@ -835,19 +867,18 @@
                 vmem((4, 3 * INNER, lanes), narrow),
             ),
         )
-        share_outer, local, up, down = call(
+        share_outer, modes, up, down = call(
             functools.partial(solve_outer_kernel, start_up, before, tiles),
             "solve_outer",
-            (fields[0], below, above, spectrum, lam, mats["forward_outer"], *mats["backward"]),
-            shapes(tiles, 128, 512, 64, 64),
+            (fields[0], below, above, spectrum, lam, mats["forward_outer"], *mats["backward_outer"]),
+            (*shapes(tiles, 128), (4, 2 * MODES, lanes), *shapes(tiles, 64, 64)),
             (
                 vmem((before, 256, TILE), wide),
                 vmem((4 * tiles, 128, TILE), wide),
                 vmem((4, 3 * OUTER, lanes), narrow),
-                vmem((2 * MODES, lanes), narrow),
             ),
         )
-        return (share_inner, share_outer), local, neighbours(up, down)
+        return (share_inner, share_outer), (modes, up, down), neighbours(up, down)
 
     def advance(kind, local, messages, share, before, total, width, tiles):
         lanes = tiles * TILE
@@ -855,7 +886,7 @@
         def scratch(rows, folded):
             return [
                 vmem((width, rows, TILE), wide),
-                vmem((4 * tiles, 128, TILE), wide),
+                vmem((4 * width, 128, TILE), wide),
                 vmem((4, folded, lanes), narrow),
             ]
 
@@ -866,7 +897,7 @@
         *inner, image = call(
             functools.partial(step_inner_kernel, kind, width, tiles),
             f"step{kind}_inner",
-            (local, *pick(0), coef, mats["apply_inner"]),
+            (local[0], *pick(0), coef, mats["apply_inner"], *mats["backward_inner"]),
             shapes(tiles, *(384 for _ in kept), 512),
             scratch(384, 288),
         )
@@ -878,7 +909,8 @@
             functools.partial(step_outer_kernel, kind, width, tiles),
             f"step{kind}_outer",
             (
-                *(local, *messages, *pick(1), *share, image, coef, mats["apply_outer"]),
+                *(local[1], messages[0], local[2], messages[1]),
+                *(*pick(1), *share, image, coef, mats["apply_outer"]),
                 *(mats["restrict"] if kind == 1 else ()),
             ),
             shapes(tiles, *(128 for _ in kept), 512, sent, sent, *((64,) if kind == 1 else ())),
@@ -892,14 +924,20 @@
     share, local, messages = solve((field,), *messages, 5, 5)
     (total,), field, messages, coarse = advance(1, local, messages, share, step, step, 5, 4)
     (scale,) = call(diagonal_kernel, "diagonal", (lower, upper, geo, mats["coarse"]), shapes(4, 64))
-    *total, field, up, down = call(
-        coarse_kernel,
-        "coarse",
-        (coarse, *messages, scale, coef, mats["prolong"], *total, field),
-        shapes(4, 384, 128, 512, 128, 128),
-        (vmem((192, 4 * TILE), narrow),),
-    )
-    share, local, messages = solve((field,), *neighbours(up, down), 4, 4)
+    outer, terms, up, down = call(
+        coarse_outer_kernel,
+        "coarse_outer",
+        (coarse, *messages, scale, coef, mats["prolong"], field),
+        (*shapes(4, 256), (1, 192, 4 * TILE), *shapes(4, 128, 128)),
+    )
+    messages = neighbours(up, down)
+    *total, inner = call(
+        coarse_inner_kernel,
+        "coarse_inner",
+        (terms, coef, mats["prolong"], *total, field),
+        shapes(4, 384, 128, 256),
+    )
+    share, local, messages = solve((outer, inner), *messages, 4, 4)
     (step, total), field, messages = advance(2, local, messages, share, None, total, 4, 4)
     share, local, messages = solve((field,), *messages, 4, 3)
     (total,), field, messages = advance(3, local, messages, share, step, total, 3, 3)

time: 122 us -> 130 us (1.066); the launches traced: 122 us -> 127 us
  starting transfers between devices: 17.3 us -> 23.1 us
  waiting for transfers between devices: 65.6 us -> 62 us
    ppermute x24, starting transfers between devices: 17.3 us -> 23.1 us  [shifted(): lax.ppermute(value, axis, [(n, (n + steps) % count) for n in range(count)])]
    ppermute x24, waiting for transfers between devices: 65.6 us -> 62 us  [shifted(): lax.ppermute(value, axis, [(n, (n + steps) % count) for n in range(count)])]
    unnamed x24 -> x34, local copies, waits for them, and re-layouts: 1 us -> 3.02 us
    pallas_call x23 -> x25, Pallas kernels: 32 us -> 33.1 us  [call(): pl.pallas_call(kernel, out_shape=[jax.ShapeDtypeStruct(out, jnp.float32 i...]
  transfers between devices with their start and end apart: 24 -> 24, of which waited for: 18 -> 15; matrix products, arithmetic and copies ran while one was open for 3% -> 2% of each run, Pallas kernels for 13% -> 17%
where the time goes in v3:
time: 130 us; the launch traced here: 127 us
  waiting for transfers between devices  62 us (48%)
  Pallas kernels  33.1 us (25%)
  starting transfers between devices  23.1 us (18%)
  local copies, waits for them, and re-layouts  5.98 us (5%)
  between operations  1.89 us (1%)
    ppermute x24, waiting for transfers between devices, shifted(): lax.ppermute(value, axis, [(n, (n + steps) % count) for n in range(count)])  62 us
    pallas_call x25, Pallas kernels, call(): pl.pallas_call(kernel, out_shape=[jax.ShapeDtypeStruct(out, jnp.float32 i...  33.1 us
    ppermute x24, starting transfers between devices, shifted(): lax.ppermute(value, axis, [(n, (n + steps) % count) for n in range(count)])  23.1 us
    unnamed x34, local copies, waits for them, and re-layouts  3.02 us
  transfers between devices with their start and end apart: 24, of which 15 were waited for; matrix products, arithmetic and copies ran while one was open for 2% of the time, Pallas kernels for 17%

profile of v3, /device:TPU:31, one launch (start us, length us, event | category | flops | bytes accessed | tf_op | source)
XLA Modules:
  0.0 127.1 jit_solution(1392657807075472734)
XLA Ops:
  0.6 1.0 fusion
  1.7 3.8 %collective-permute-start.1 = (f32[256,256]{1,0:T(8,128)S(1)}, f32[256,256]{1,0:T(8,128)S(1)}, u32[]{:S(2)}, u32[]{:S(2)}) collective-permute-start(f32[256,256]{1,0:T(8,128)S(1)} %pad_maximum_fusion), channel_id=1, source_target_pairs={{0,3},{1,0},{2,1},{3,2},{4,7},{5,4},{6,5},{7,6},{8,11},{9,8},{10,9... | collective-permute-start | bytes 786440 | tf_op jit(solution)/shard_map/ppermute | solution.py:811
  5.5 0.8 pad_maximum_fusion.1
  7.4 0.1 concatenate.14
  7.5 0.1 stack_reshape.3
  7.6 0.7 tile.2
  8.3 0.1 stack_tile.3
  8.4 1.0 copy-done.8
  9.5 0.9 copy-done.10
  10.4 0.5 tables.1
  11.0 2.6 %collective-permute-done.left = f32[256,256]{1,0:T(8,128)S(1)} collective-permute-done((f32[256,256]{1,0:T(8,128)S(1)}, f32[256,256]{1,0:T(8,128)S(1)}, u32[]{:S(2)}, u32[]{:S(2)}) %collective-permute-start) | collective-permute-done | bytes 262176 | tf_op jit(solution)/shard_map/ppermute | solution.py:811
  13.6 0.8 collective-permute-start.5
  14.4 0.8 collective-permute-start.4
  15.1 0.6 dynamic_slice.6.rot
  15.7 0.9 copy-done.12
  16.7 1.2 outer.1
  17.9 2.2 %collective-permute-start.2 = (f32[136,640]{1,0:T(8,128)S(1)}, f32[136,640]{1,0:T(8,128)S(1)}, u32[]{:S(2)}, u32[]{:S(2)}) collective-permute-start(f32[136,640]{1,0:T(8,128)S(1)} %get-tuple-element.71), channel_id=1, source_target_pairs={{0,4},{4,8},{8,12},{12,16},{16,20},{20,24},{24,28},{28,32},{32,36}... | collective-permute-start | bytes 1044488 | tf_op jit(solution)/shard_map/ppermute | solution.py:811
  20.1 0.4 collective-permute-start.3
  20.5 1.5 %collective-permute-done.4.left = f32[256,256]{1,0:T(8,128)} collective-permute-done((f32[256,256]{1,0:T(8,128)S(1)}, f32[256,256]{1,0:T(8,128)}, u32[]{:S(2)}, u32[]{:S(2)}) %collective-permute-start.4) | collective-permute-done | bytes 262176 | tf_op jit(solution)/shard_map/ppermute | solution.py:811
  22.0 2.2 %inner.1.refs_1_ = f32[256,640]{1,0:T(8,128)S(1)} custom-call(s32[1]{0:T(128)} %dynamic_slice.6.rot, f32[256,256]{1,0:T(8,128)} %collective-permute-done.4.left, f32[256,256]{1,0:T(8,128)S(1)} %follow.1.own, f32[256,256]{1,0:T(8,128)} %collective-permute-done.5.right), custom_call_target="tpu_custom_call" | custom-call | flops 20000000000 | bytes 4000000 | tf_op jit(solution)/shard_map/inner/pallas_call | solution.py:787
  24.2 1.7 %solve_inner.4 = (f32[384,640]{1,0:T(8,128)S(1)}, f32[1024,640]{1,0:T(8,128)S(1)}) custom-call(f32[256,640]{1,0:T(8,128)S(1)} %get-tuple-element.70.refs_0_, f32[256,640]{1,0:T(8,128)S(1)} %inner.1.refs_1_, bf16[4,256,480]{2,1,0:T(8,128)(2,1)S(1)} %copy-done), custom_call_target="tpu_custom_call" | custom-call | bytes 4000000 | tf_op jit(solution)/shard_map/solve_inner/pallas_call | solution.py:787
  25.9 4.2 %collective-permute-done.3.refs_2_.upper = f32[136,640]{1,0:T(8,128)S(1)} collective-permute-done((f32[136,640]{1,0:T(8,128)S(1)}, f32[136,640]{1,0:T(8,128)S(1)}, u32[]{:S(2)}, u32[]{:S(2)}) %collective-permute-start.3) | collective-permute-done | bytes 348192 | tf_op jit(solution)/shard_map/ppermute | solution.py:811
  30.2 1.7 %solve_outer.4 = (f32[128,640]{1,0:T(8,128)S(1)}, bf16[4,512,640]{2,1,0:T(8,128)(2,1)S(1)}, f32[64,640]{1,0:T(8,128)S(1)}, f32[64,640]{1,0:T(8,128)S(1)}) custom-call(f32[256,640]{1,0:T(8,128)S(1)} %get-tuple-element.70.refs_0_, f32[136,640]{1,0:T(8,128)S(1)} %collective-permute-done.2.refs_1_.lower, f32[136,640]{1,0:T(8,128)S(1)} %collective-permute-done.3.refs_2_.upper, ...), custom_call_target="tpu_custom_call" | custom-call | bytes 4000000 | tf_op jit(solution)/shard_map/solve_outer/pallas_call | solution.py:787
  31.9 0.1 collective-permute-start.6
  32.0 0.7 collective-permute-start.7
  32.8 2.3 %step0_inner.1 = (f32[384,640]{1,0:T(8,128)S(1)}, f32[512,640]{1,0:T(8,128)S(1)}) custom-call(bf16[4,512,640]{2,1,0:T(8,128)(2,1)S(1)} %get-tuple-element.80.refs_0_, f32[24,640]{1,0:T(8,128)S(1)} %get-tuple-element.81.refs_1_.refs_7_.refs_3_.refs_9_.coef.refs_2_.refs_8_, bf16[4,320,288]{2,1,0:T(8,128)(2,1)S(1)} %copy-done.1, ...), custom_call_target="tpu_custom_call" | custom-call | bytes 4000000 | tf_op jit(solution)/shard_map/step0_inner/pallas_call | solution.py:787
  35.1 5.3 %collective-permute-done.7.refs_3_ = f32[64,640]{1,0:T(8,128)S(1)} collective-permute-done((f32[64,640]{1,0:T(8,128)S(1)}, f32[64,640]{1,0:T(8,128)S(1)}, u32[]{:S(2)}, u32[]{:S(2)}) %collective-permute-start.7) | collective-permute-done | bytes 163872 | tf_op jit(solution)/shard_map/ppermute | solution.py:811
  40.4 0.9 step0_outer.1
  41.4 0.5 collective-permute-start.9
  41.9 1.7 %solve_inner.5 = (f32[384,640]{1,0:T(8,128)S(1)}, f32[1024,640]{1,0:T(8,128)S(1)}) custom-call(f32[512,640]{1,0:T(8,128)S(1)} %get-tuple-element.83.refs_0_, bf16[4,256,480]{2,1,0:T(8,128)(2,1)S(1)} %copy-done), custom_call_target="tpu_custom_call" | custom-call | bytes 4000000 | tf_op jit(solution)/shard_map/solve_inner/pallas_call | solution.py:787
  43.6 1.8 %collective-permute-done.8.refs_1_ = f32[128,640]{1,0:T(8,128)S(1)} collective-permute-done((f32[128,640]{1,0:T(8,128)S(1)}, f32[128,640]{1,0:T(8,128)S(1)}, u32[]{:S(2)}, u32[]{:S(2)}) %collective-permute-start.8) | collective-permute-done | bytes 327712 | tf_op jit(solution)/shard_map/ppermute | solution.py:811
  45.4 5.9 %collective-permute-done.9.refs_2_ = f32[128,640]{1,0:T(8,128)S(1)} collective-permute-done((f32[128,640]{1,0:T(8,128)S(1)}, f32[128,640]{1,0:T(8,128)S(1)}, u32[]{:S(2)}, u32[]{:S(2)}) %collective-permute-start.9) | collective-permute-done | bytes 327712 | tf_op jit(solution)/shard_map/ppermute | solution.py:811
  51.2 1.6 %solve_outer.5 = (f32[128,640]{1,0:T(8,128)S(1)}, bf16[4,512,640]{2,1,0:T(8,128)(2,1)S(1)}, f32[64,640]{1,0:T(8,128)S(1)}, f32[64,640]{1,0:T(8,128)S(1)}) custom-call(f32[512,640]{1,0:T(8,128)S(1)} %get-tuple-element.83.refs_0_, f32[128,640]{1,0:T(8,128)S(1)} %collective-permute-done.8.refs_1_, f32[128,640]{1,0:T(8,128)S(1)} %collective-permute-done.9.refs_2_, ...), custom_call_target="tpu_custom_call" | custom-call | bytes 4000000 | tf_op jit(solution)/shard_map/solve_outer/pallas_call | solution.py:787
  52.9 0.5 collective-permute-start.11
  53.4 2.1 %step1_inner.1 = (f32[384,512]{1,0:T(8,128)S(1)}, f32[512,512]{1,0:T(8,128)S(1)}) custom-call(bf16[4,512,640]{2,1,0:T(8,128)(2,1)S(1)} %get-tuple-element.92.refs_0_, f32[384,640]{1,0:T(8,128)S(1)} %get-tuple-element.93.refs_1_.refs_2_, f32[384,640]{1,0:T(8,128)S(1)} %get-tuple-element.93.refs_1_.refs_2_, ...), custom_call_target="tpu_custom_call" | custom-call | bytes 4000000 | tf_op jit(solution)/shard_map/step1_inner/pallas_call | solution.py:787
  55.6 5.5 %collective-permute-done.11.refs_3_ = f32[64,640]{1,0:T(8,128)S(1)} collective-permute-done((f32[64,640]{1,0:T(8,128)S(1)}, f32[64,640]{1,0:T(8,128)S(1)}, u32[]{:S(2)}, u32[]{:S(2)}) %collective-permute-start.11) | collective-permute-done | bytes 163872 | tf_op jit(solution)/shard_map/ppermute | solution.py:811
  61.1 1.2 step1_outer.1
  62.3 0.5 collective-permute-start.13
  62.8 0.4 diagonal.1.scale
  63.2 0.3 collective-permute-done.12.below
  63.5 5.5 %collective-permute-done.13.above = f32[16,512]{1,0:T(8,128)S(1)} collective-permute-done((f32[16,512]{1,0:T(8,128)S(1)}, f32[16,512]{1,0:T(8,128)S(1)}, u32[]{:S(2)}, u32[]{:S(2)}) %collective-permute-start.13) | collective-permute-done | bytes 32800 | tf_op jit(solution)/shard_map/ppermute | solution.py:811
  69.1 0.7 coarse_outer.1
  69.8 10.3 %collective-permute-start.15 = (f32[128,512]{1,0:T(8,128)S(1)}, f32[128,512]{1,0:T(8,128)S(1)}, u32[]{:S(2)}, u32[]{:S(2)}) collective-permute-start(f32[128,512]{1,0:T(8,128)S(1)} %get-tuple-element.101), channel_id=1, source_target_pairs={{0,124},{4,0},{8,4},{12,8},{16,12},{20,16},{24,20},{28,24},{32,28}... | collective-permute-start | bytes 786440 | tf_op jit(solution)/shard_map/ppermute | solution.py:811
  80.1 0.9 coarse_inner.1
  81.0 1.5 %solve_inner.6 = (f32[384,512]{1,0:T(8,128)S(1)}, f32[1024,512]{1,0:T(8,128)S(1)}) custom-call(f32[256,512]{1,0:T(8,128)S(1)} %get-tuple-element.99.refs_0_, f32[256,512]{1,0:T(8,128)S(1)} %get-tuple-element.105.refs_1_, bf16[4,256,480]{2,1,0:T(8,128)(2,1)S(1)} %copy-done), custom_call_target="tpu_custom_call" | custom-call | bytes 4000000 | tf_op jit(solution)/shard_map/solve_inner/pallas_call | solution.py:787
  82.5 6.6 %collective-permute-done.15.refs_2_ = f32[128,512]{1,0:T(8,128)S(1)} collective-permute-done((f32[128,512]{1,0:T(8,128)S(1)}, f32[128,512]{1,0:T(8,128)S(1)}, u32[]{:S(2)}, u32[]{:S(2)}) %collective-permute-start.15) | collective-permute-done | bytes 262176 | tf_op jit(solution)/shard_map/ppermute | solution.py:811
  89.1 1.4 %solve_outer.6 = (f32[128,512]{1,0:T(8,128)S(1)}, bf16[4,512,512]{2,1,0:T(8,128)(2,1)S(1)}, f32[64,512]{1,0:T(8,128)S(1)}, f32[64,512]{1,0:T(8,128)S(1)}) custom-call(f32[256,512]{1,0:T(8,128)S(1)} %get-tuple-element.99.refs_0_, f32[128,512]{1,0:T(8,128)S(1)} %collective-permute-done.14.refs_1_, f32[128,512]{1,0:T(8,128)S(1)} %collective-permute-done.15.refs_2_, ...), custom_call_target="tpu_custom_call" | custom-call | bytes 4000000 | tf_op jit(solution)/shard_map/solve_outer/pallas_call | solution.py:787
  90.6 0.5 collective-permute-start.17
  91.1 2.1 %step2_inner.1 = (f32[384,512]{1,0:T(8,128)S(1)}, f32[384,512]{1,0:T(8,128)S(1)}, f32[512,512]{1,0:T(8,128)S(1)}) custom-call(bf16[4,512,512]{2,1,0:T(8,128)(2,1)S(1)} %get-tuple-element.112.refs_0_, f32[384,512]{1,0:T(8,128)S(1)} %get-tuple-element.113.refs_1_, f32[24,640]{1,0:T(8,128)S(1)} %get-tuple-element.81.refs_1_.refs_7_.refs_3_.refs_9_.coef.refs_2_.refs_8_, ...), custom_call_target="tpu_custom_call" | custom-call | bytes 4000000 | tf_op jit(solution)/shard_map/step2_inner/pallas_call | solution.py:787
  93.2 5.2 %collective-permute-done.17.refs_3_ = f32[64,512]{1,0:T(8,128)S(1)} collective-permute-done((f32[64,512]{1,0:T(8,128)S(1)}, f32[64,512]{1,0:T(8,128)S(1)}, u32[]{:S(2)}, u32[]{:S(2)}) %collective-permute-start.17) | collective-permute-done | bytes 131104 | tf_op jit(solution)/shard_map/ppermute | solution.py:811
  98.4 0.8 step2_outer.1
  99.2 0.5 collective-permute-start.19
  99.7 1.2 solve_inner.7
  101.0 1.6 %collective-permute-done.18.refs_1_ = f32[128,512]{1,0:T(8,128)S(1)} collective-permute-done((f32[128,512]{1,0:T(8,128)S(1)}, f32[128,512]{1,0:T(8,128)S(1)}, u32[]{:S(2)}, u32[]{:S(2)}) %collective-permute-start.18) | collective-permute-done | bytes 262176 | tf_op jit(solution)/shard_map/ppermute | solution.py:811
  102.5 5.9 %collective-permute-done.19.refs_2_ = f32[128,512]{1,0:T(8,128)S(1)} collective-permute-done((f32[128,512]{1,0:T(8,128)S(1)}, f32[128,512]{1,0:T(8,128)S(1)}, u32[]{:S(2)}, u32[]{:S(2)}) %collective-permute-start.19) | collective-permute-done | bytes 262176 | tf_op jit(solution)/shard_map/ppermute | solution.py:811
  108.4 1.1 solve_outer.7
  109.6 0.5 collective-permute-start.21
  110.1 1.7 %step3_inner.1 = (f32[384,384]{1,0:T(8,128)S(1)}, f32[512,384]{1,0:T(8,128)S(1)}) custom-call(bf16[4,512,384]{2,1,0:T(8,128)(2,1)S(1)} %get-tuple-element.125.refs_0_, f32[384,512]{1,0:T(8,128)S(1)} %get-tuple-element.126.refs_1_, f32[384,512]{1,0:T(8,128)S(1)} %get-tuple-element.127.refs_2_, ...), custom_call_target="tpu_custom_call" | custom-call | bytes 4000000 | tf_op jit(solution)/shard_map/step3_inner/pallas_call | solution.py:787
  111.8 5.3 %collective-permute-done.21.refs_3_ = f32[64,384]{1,0:T(8,128)S(1)} collective-permute-done((f32[64,384]{1,0:T(8,128)S(1)}, f32[64,384]{1,0:T(8,128)S(1)}, u32[]{:S(2)}, u32[]{:S(2)}) %collective-permute-start.21) | collective-permute-done | bytes 98336 | tf_op jit(solution)/shard_map/ppermute | solution.py:811
  117.0 0.6 step3_outer.1
  117.7 0.5 collective-permute-start.23
  118.2 2.0 %finish_inner.1 = (f32[512,256]{1,0:T(8,128)}, f32[384,256]{1,0:T(8,128)S(1)}) custom-call(s32[1]{0:T(128)} %dynamic_slice.6.rot, f32[512,384]{1,0:T(8,128)S(1)} %get-tuple-element.129.local, f32[384,384]{1,0:T(8,128)S(1)} %get-tuple-element.130.total_inner, f32[128,384]{1,0:T(8,128)S(1)} %get-tuple-element.131.total_outer), custom_call_target="tpu_custom_call" | custom-call | bytes 4000000 | tf_op jit(solution)/shard_map/finish_inner/pallas_call | solution.py:787
  120.3 4.9 %collective-permute-done.23.above = f32[64,384]{1,0:T(8,128)S(1)} collective-permute-done((f32[64,384]{1,0:T(8,128)S(1)}, f32[64,384]{1,0:T(8,128)S(1)}, u32[]{:S(2)}, u32[]{:S(2)}) %collective-permute-start.23) | collective-permute-done | bytes 98336 | tf_op jit(solution)/shard_map/ppermute | solution.py:811
  125.2 1.7 %finish_outer.1 = f32[512,256]{1,0:T(8,128)} custom-call(s32[1]{0:T(128)} %dynamic_slice.6.rot, f32[512,384]{1,0:T(8,128)S(1)} %get-tuple-element.129.local, f32[64,384]{1,0:T(8,128)S(1)} %collective-permute-done.22.below, f32[64,384]{1,0:T(8,128)S(1)} %collective-permute-done.23.above, f32[384,256]{1,0:T(8,128)S(1)} %get-tuple-element.135.inner), custom_call_target="tpu_custom_call" | custom-call | bytes 4000000 | tf_op jit(solution)/shard_map/finish_outer/pallas_call | solution.py:787
  (59 shorter events, 1.3 us)
Async XLA Ops:
  0.6 14.5 %copy-start.16 = (s32[32]{0:T(128)S(1)}, s32[32]{0:T(128)}, u32[]{:S(2)}) copy-start(s32[32]{0:T(128)} %param.22) | copy-start | bytes 388
  1.7 9.3 %collective-permute-start.1 = (f32[256,256]{1,0:T(8,128)S(1)}, f32[256,256]{1,0:T(8,128)S(1)}, u32[]{:S(2)}, u32[]{:S(2)}) collective-permute-start(f32[256,256]{1,0:T(8,128)S(1)} %pad_maximum_fusion), channel_id=1, source_target_pairs={{0,3},{1,0},{2,1},{3,2},{4,7},{5,4},{6,5},{7,6},{8,11},{9,8},{10,9... | collective-permute-start | bytes 786440 | tf_op jit(solution)/shard_map/ppermute | solution.py:811
  5.5 8.1 %collective-permute-start = (f32[256,256]{1,0:T(8,128)S(1)}, f32[256,256]{1,0:T(8,128)S(1)}, u32[]{:S(2)}, u32[]{:S(2)}) collective-permute-start(f32[256,256]{1,0:T(8,128)S(1)} %pad_maximum_fusion), channel_id=1, source_target_pairs={{0,1},{1,2},{2,3},{3,0},{4,5},{5,6},{6,7},{7,4},{8,9},{9,10},{10,1... | collective-permute-start | bytes 786440 | tf_op jit(solution)/shard_map/ppermute | solution.py:811
  8.4 1.0 copy-start.8
  9.5 0.9 copy-start.10
  11.0 2.6 %copy-start.11 = (f32[256,256]{1,0:T(8,128)}, f32[256,256]{1,0:T(8,128)S(1)}, u32[]{:S(2)}) copy-start(f32[256,256]{1,0:T(8,128)S(1)} %get-tuple-element.69.own) | copy-start | bytes 786436
  13.6 6.9 %collective-permute-start.5 = (f32[256,256]{1,0:T(8,128)S(1)}, f32[256,256]{1,0:T(8,128)}, u32[]{:S(2)}, u32[]{:S(2)}) collective-permute-start(f32[256,256]{1,0:T(8,128)S(1)} %follow.1.own), channel_id=1, source_target_pairs={{0,3},{1,0},{2,1},{3,2},{4,7},{5,4},{6,5},{7,6},{8,11},{9,8},{10,9... | collective-permute-start | bytes 786440 | tf_op jit(solution)/shard_map/ppermute | solution.py:811
  14.4 7.6 %collective-permute-start.4 = (f32[256,256]{1,0:T(8,128)S(1)}, f32[256,256]{1,0:T(8,128)}, u32[]{:S(2)}, u32[]{:S(2)}) collective-permute-start(f32[256,256]{1,0:T(8,128)S(1)} %follow.1.own), channel_id=1, source_target_pairs={{0,1},{1,2},{2,3},{3,0},{4,5},{5,6},{6,7},{7,4},{8,9},{9,10},{10,1... | collective-permute-start | bytes 786440 | tf_op jit(solution)/shard_map/ppermute | solution.py:811
  15.7 0.9 copy-start.12
  17.9 8.0 %collective-permute-start.2 = (f32[136,640]{1,0:T(8,128)S(1)}, f32[136,640]{1,0:T(8,128)S(1)}, u32[]{:S(2)}, u32[]{:S(2)}) collective-permute-start(f32[136,640]{1,0:T(8,128)S(1)} %get-tuple-element.71), channel_id=1, source_target_pairs={{0,4},{4,8},{8,12},{12,16},{16,20},{20,24},{24,28},{28,32},{32,36}... | collective-permute-start | bytes 1044488 | tf_op jit(solution)/shard_map/ppermute | solution.py:811
  20.1 4.1 %copy-start = (bf16[4,256,480]{2,1,0:T(8,128)(2,1)S(1)}, bf16[4,256,480]{2,1,0:T(8,128)(2,1)}, u32[]{:S(2)}) copy-start(bf16[4,256,480]{2,1,0:T(8,128)(2,1)} %constant.51.clone.refs_2_.refs_1_) | copy-start | bytes 2949124
  20.1 10.0 %collective-permute-start.3 = (f32[136,640]{1,0:T(8,128)S(1)}, f32[136,640]{1,0:T(8,128)S(1)}, u32[]{:S(2)}, u32[]{:S(2)}) collective-permute-start(f32[136,640]{1,0:T(8,128)S(1)} %get-tuple-element.72), channel_id=1, source_target_pairs={{0,124},{4,0},{8,4},{12,8},{16,12},{20,16},{24,20},{28,24},{32,28}... | collective-permute-start | bytes 1044488 | tf_op jit(solution)/shard_map/ppermute | solution.py:811
  24.2 6.0 %copy-start.2 = (bf16[4,256,240]{2,1,0:T(8,128)(2,1)S(1)}, bf16[4,256,240]{2,1,0:T(8,128)(2,1)}, u32[]{:S(2)}) copy-start(bf16[4,256,240]{2,1,0:T(8,128)(2,1)} %constant.52.clone.refs_5_) | copy-start | bytes 1474564
  24.2 6.0 %copy-start.7 = (bf16[4,32,512]{2,1,0:T(8,128)(2,1)S(1)}, bf16[4,32,512]{2,1,0:T(8,128)(2,1)}, u32[]{:S(2)}) copy-start(bf16[4,32,512]{2,1,0:T(8,128)(2,1)} %constant.53.clone.refs_6_) | copy-start | bytes 393220
  24.2 6.0 %copy-start.9 = (bf16[4,32,256]{2,1,0:T(8,128)(2,1)S(1)}, bf16[4,32,256]{2,1,0:T(8,128)(2,1)}, u32[]{:S(2)}) copy-start(bf16[4,32,256]{2,1,0:T(8,128)(2,1)} %constant.54.clone.refs_7_) | copy-start | bytes 196612
  30.2 2.6 %copy-start.1 = (bf16[4,320,288]{2,1,0:T(8,128)(2,1)S(1)}, bf16[4,320,288]{2,1,0:T(8,128)(2,1)}, u32[]{:S(2)}) copy-start(bf16[4,320,288]{2,1,0:T(8,128)(2,1)} %constant.57.clone.refs_2_.refs_4_.refs_3_) | copy-start | bytes 2211844
  30.2 2.6 %copy-start.3 = (bf16[4,96,512]{2,1,0:T(8,128)(2,1)S(1)}, bf16[4,96,512]{2,1,0:T(8,128)(2,1)}, u32[]{:S(2)}) copy-start(bf16[4,96,512]{2,1,0:T(8,128)(2,1)} %constant.55.clone.refs_3_.refs_5_.refs_4_) | copy-start | bytes 1179652
  30.2 2.6 %copy-start.5 = (bf16[4,96,256]{2,1,0:T(8,128)(2,1)S(1)}, bf16[4,96,256]{2,1,0:T(8,128)(2,1)}, u32[]{:S(2)}) copy-start(bf16[4,96,256]{2,1,0:T(8,128)(2,1)} %constant.56.clone.refs_4_.refs_6_.refs_5_) | copy-start | bytes 589828
  31.9 3.1 %collective-permute-start.6 = (f32[64,640]{1,0:T(8,128)S(1)}, f32[64,640]{1,0:T(8,128)S(1)}, u32[]{:S(2)}, u32[]{:S(2)}) collective-permute-start(f32[64,640]{1,0:T(8,128)S(1)} %get-tuple-element.76.refs_0_), channel_id=1, source_target_pairs={{0,4},{4,8},{8,12},{12,16},{16,20},{20,24},{24,28},{28,32},{32,36}... | collective-permute-start | bytes 491528 | tf_op jit(solution)/shard_map/ppermute | solution.py:811
  32.0 8.4 %collective-permute-start.7 = (f32[64,640]{1,0:T(8,128)S(1)}, f32[64,640]{1,0:T(8,128)S(1)}, u32[]{:S(2)}, u32[]{:S(2)}) collective-permute-start(f32[64,640]{1,0:T(8,128)S(1)} %get-tuple-element.77.refs_2_), channel_id=1, source_target_pairs={{0,124},{4,0},{8,4},{12,8},{16,12},{20,16},{24,20},{28,24},{32,28}... | collective-permute-start | bytes 491528 | tf_op jit(solution)/shard_map/ppermute | solution.py:811
  32.8 7.7 %copy-start.6 = (bf16[4,192,96]{2,1,0:T(8,128)(2,1)S(1)}, bf16[4,192,96]{2,1,0:T(8,128)(2,1)}, u32[]{:S(2)}) copy-start(bf16[4,192,96]{2,1,0:T(8,128)(2,1)} %constant.58.clone.refs_8_.refs_10_.refs_9_) | copy-start | bytes 442372
  41.3 4.1 %collective-permute-start.8 = (f32[128,640]{1,0:T(8,128)S(1)}, f32[128,640]{1,0:T(8,128)S(1)}, u32[]{:S(2)}, u32[]{:S(2)}) collective-permute-start(f32[128,640]{1,0:T(8,128)S(1)} %get-tuple-element.84), channel_id=1, source_target_pairs={{0,4},{4,8},{8,12},{12,16},{16,20},{20,24},{24,28},{28,32},{32,36}... | collective-permute-start | bytes 983048 | tf_op jit(solution)/shard_map/ppermute | solution.py:811
  41.4 9.9 %collective-permute-start.9 = (f32[128,640]{1,0:T(8,128)S(1)}, f32[128,640]{1,0:T(8,128)S(1)}, u32[]{:S(2)}, u32[]{:S(2)}) collective-permute-start(f32[128,640]{1,0:T(8,128)S(1)} %get-tuple-element.85), channel_id=1, source_target_pairs={{0,124},{4,0},{8,4},{12,8},{16,12},{20,16},{24,20},{28,24},{32,28}... | collective-permute-start | bytes 983048 | tf_op jit(solution)/shard_map/ppermute | solution.py:811
  52.8 2.7 %collective-permute-start.10 = (f32[64,640]{1,0:T(8,128)S(1)}, f32[64,640]{1,0:T(8,128)S(1)}, u32[]{:S(2)}, u32[]{:S(2)}) collective-permute-start(f32[64,640]{1,0:T(8,128)S(1)} %get-tuple-element.87.refs_0_), channel_id=1, source_target_pairs={{0,4},{4,8},{8,12},{12,16},{16,20},{20,24},{24,28},{28,32},{32,36}... | collective-permute-start | bytes 491528 | tf_op jit(solution)/shard_map/ppermute | solution.py:811
  52.9 8.1 %collective-permute-start.11 = (f32[64,640]{1,0:T(8,128)S(1)}, f32[64,640]{1,0:T(8,128)S(1)}, u32[]{:S(2)}, u32[]{:S(2)}) collective-permute-start(f32[64,640]{1,0:T(8,128)S(1)} %get-tuple-element.88.refs_2_), channel_id=1, source_target_pairs={{0,124},{4,0},{8,4},{12,8},{16,12},{20,16},{24,20},{28,24},{32,28}... | collective-permute-start | bytes 491528 | tf_op jit(solution)/shard_map/ppermute | solution.py:811
  53.4 7.6 %copy-start.13 = (bf16[64,1024]{1,0:T(8,128)(2,1)S(1)}, bf16[64,1024]{1,0:T(8,128)(2,1)}, u32[]{:S(2)}) copy-start(bf16[64,1024]{1,0:T(8,128)(2,1)} %constant.59.clone.refs_11_) | copy-start | bytes 393220
  53.4 7.6 %copy-start.14 = (bf16[64,512]{1,0:T(8,128)(2,1)S(1)}, bf16[64,512]{1,0:T(8,128)(2,1)}, u32[]{:S(2)}) copy-start(bf16[64,512]{1,0:T(8,128)(2,1)} %constant.60.clone.refs_12_) | copy-start | bytes 196612
  55.6 7.3 %copy-start.15 = (f32[64,8]{1,0:T(8,128)S(1)}, f32[64,8]{1,0:T(8,128)}, u32[]{:S(2)}) copy-start(f32[64,8]{1,0:T(8,128)} %constant.63.clone.table) | copy-start | bytes 6148
  61.1 8.0 %copy-start.4 = (bf16[2048,192]{1,0:T(8,128)(2,1)S(1)}, bf16[2048,192]{1,0:T(8,128)(2,1)}, u32[]{:S(2)}) copy-start(bf16[2048,192]{1,0:T(8,128)(2,1)} %constant.61.clone.prolong) | copy-start | bytes 2359300
  62.2 1.3 %collective-permute-start.12 = (f32[16,512]{1,0:T(8,128)S(1)}, f32[16,512]{1,0:T(8,128)S(1)}, u32[]{:S(2)}, u32[]{:S(2)}) collective-permute-start(f32[16,512]{1,0:T(8,128)S(1)} %get-tuple-element.96), channel_id=1, source_target_pairs={{0,4},{4,8},{8,12},{12,16},{16,20},{20,24},{24,28},{28,32},{32,36}... | collective-permute-start | bytes 98312 | tf_op jit(solution)/shard_map/ppermute | solution.py:811
  62.3 6.7 %collective-permute-start.13 = (f32[16,512]{1,0:T(8,128)S(1)}, f32[16,512]{1,0:T(8,128)S(1)}, u32[]{:S(2)}, u32[]{:S(2)}) collective-permute-start(f32[16,512]{1,0:T(8,128)S(1)} %get-tuple-element.97), channel_id=1, source_target_pairs={{0,124},{4,0},{8,4},{12,8},{16,12},{20,16},{24,20},{28,24},{32,28}... | collective-permute-start | bytes 98312 | tf_op jit(solution)/shard_map/ppermute | solution.py:811
  69.7 12.7 %collective-permute-start.14 = (f32[128,512]{1,0:T(8,128)S(1)}, f32[128,512]{1,0:T(8,128)S(1)}, u32[]{:S(2)}, u32[]{:S(2)}) collective-permute-start(f32[128,512]{1,0:T(8,128)S(1)} %get-tuple-element.100), channel_id=1, source_target_pairs={{0,4},{4,8},{8,12},{12,16},{16,20},{20,24},{24,28},{28,32},{32,36}... | collective-permute-start | bytes 786440 | tf_op jit(solution)/shard_map/ppermute | solution.py:811
  69.8 19.2 %collective-permute-start.15 = (f32[128,512]{1,0:T(8,128)S(1)}, f32[128,512]{1,0:T(8,128)S(1)}, u32[]{:S(2)}, u32[]{:S(2)}) collective-permute-start(f32[128,512]{1,0:T(8,128)S(1)} %get-tuple-element.101), channel_id=1, source_target_pairs={{0,124},{4,0},{8,4},{12,8},{16,12},{20,16},{24,20},{28,24},{32,28}... | collective-permute-start | bytes 786440 | tf_op jit(solution)/shard_map/ppermute | solution.py:811
  90.5 2.7 %collective-permute-start.16 = (f32[64,512]{1,0:T(8,128)S(1)}, f32[64,512]{1,0:T(8,128)S(1)}, u32[]{:S(2)}, u32[]{:S(2)}) collective-permute-start(f32[64,512]{1,0:T(8,128)S(1)} %get-tuple-element.107.refs_0_), channel_id=1, source_target_pairs={{0,4},{4,8},{8,12},{12,16},{16,20},{20,24},{24,28},{28,32},{32,36}... | collective-permute-start | bytes 393224 | tf_op jit(solution)/shard_map/ppermute | solution.py:811
  90.6 7.8 %collective-permute-start.17 = (f32[64,512]{1,0:T(8,128)S(1)}, f32[64,512]{1,0:T(8,128)S(1)}, u32[]{:S(2)}, u32[]{:S(2)}) collective-permute-start(f32[64,512]{1,0:T(8,128)S(1)} %get-tuple-element.108.refs_2_), channel_id=1, source_target_pairs={{0,124},{4,0},{8,4},{12,8},{16,12},{20,16},{24,20},{28,24},{32,28}... | collective-permute-start | bytes 393224 | tf_op jit(solution)/shard_map/ppermute | solution.py:811
  99.1 3.4 %collective-permute-start.18 = (f32[128,512]{1,0:T(8,128)S(1)}, f32[128,512]{1,0:T(8,128)S(1)}, u32[]{:S(2)}, u32[]{:S(2)}) collective-permute-start(f32[128,512]{1,0:T(8,128)S(1)} %get-tuple-element.116), channel_id=1, source_target_pairs={{0,4},{4,8},{8,12},{12,16},{16,20},{20,24},{24,28},{28,32},{32,36}... | collective-permute-start | bytes 786440 | tf_op jit(solution)/shard_map/ppermute | solution.py:811
  99.2 9.2 %collective-permute-start.19 = (f32[128,512]{1,0:T(8,128)S(1)}, f32[128,512]{1,0:T(8,128)S(1)}, u32[]{:S(2)}, u32[]{:S(2)}) collective-permute-start(f32[128,512]{1,0:T(8,128)S(1)} %get-tuple-element.117), channel_id=1, source_target_pairs={{0,124},{4,0},{8,4},{12,8},{16,12},{20,16},{24,20},{28,24},{32,28}... | collective-permute-start | bytes 786440 | tf_op jit(solution)/shard_map/ppermute | solution.py:811
  109.5 2.2 %collective-permute-start.20 = (f32[64,384]{1,0:T(8,128)S(1)}, f32[64,384]{1,0:T(8,128)S(1)}, u32[]{:S(2)}, u32[]{:S(2)}) collective-permute-start(f32[64,384]{1,0:T(8,128)S(1)} %get-tuple-element.119.refs_0_), channel_id=1, source_target_pairs={{0,4},{4,8},{8,12},{12,16},{16,20},{20,24},{24,28},{28,32},{32,36}... | collective-permute-start | bytes 294920 | tf_op jit(solution)/shard_map/ppermute | solution.py:811
  109.6 7.4 %collective-permute-start.21 = (f32[64,384]{1,0:T(8,128)S(1)}, f32[64,384]{1,0:T(8,128)S(1)}, u32[]{:S(2)}, u32[]{:S(2)}) collective-permute-start(f32[64,384]{1,0:T(8,128)S(1)} %get-tuple-element.120.refs_2_), channel_id=1, source_target_pairs={{0,124},{4,0},{8,4},{12,8},{16,12},{20,16},{24,20},{28,24},{32,28}... | collective-permute-start | bytes 294920 | tf_op jit(solution)/shard_map/ppermute | solution.py:811
  117.7 2.6 %collective-permute-start.22 = (f32[64,384]{1,0:T(8,128)S(1)}, f32[64,384]{1,0:T(8,128)S(1)}, u32[]{:S(2)}, u32[]{:S(2)}) collective-permute-start(f32[64,384]{1,0:T(8,128)S(1)} %get-tuple-element.133), channel_id=1, source_target_pairs={{0,4},{4,8},{8,12},{12,16},{16,20},{20,24},{24,28},{28,32},{32,36}... | collective-permute-start | bytes 294920 | tf_op jit(solution)/shard_map/ppermute | solution.py:811
  117.7 7.4 %collective-permute-start.23 = (f32[64,384]{1,0:T(8,128)S(1)}, f32[64,384]{1,0:T(8,128)S(1)}, u32[]{:S(2)}, u32[]{:S(2)}) collective-permute-start(f32[64,384]{1,0:T(8,128)S(1)} %get-tuple-element.134), channel_id=1, source_target_pairs={{0,124},{4,0},{8,4},{12,8},{16,12},{20,16},{24,20},{28,24},{32,28}... | collective-permute-start | bytes 294920 | tf_op jit(solution)/shard_map/ppermute | solution.py:811

commit v4 on v3

--- a/solution.py
+++ b/solution.py
@@ -359,14 +359,33 @@
     return sum_k + sum_m, sum_k - sum_m, diff_k + diff_m, diff_k - diff_m
 
 
-def pack(parts, packed, rows, tiles):
-    for c in range(4):
+def each_class(body, rolled):
+    if rolled:
+
+        def step(c, carry):
+            body(c)
+            return carry
+
+        lax.fori_loop(0, 4, step, 0)
+    else:
+        for c in range(4):
+            body(c)
+
+
+def class_rows(c, rows):
+    return slice(c * rows, (c + 1) * rows) if isinstance(c, int) else pl.ds(pl.multiple_of(c * rows, rows), rows)
+
+
+def pack(parts, packed, rows, tiles, rolled=False):
+    def body(c):
         for t in range(tiles):
             lanes = slice(t * TILE, (t + 1) * TILE)
             high, low = halves(parts[c * tiles + t, 0:rows, :])
             packed[c, 0:rows, lanes] = high
             packed[c, rows : 2 * rows, lanes] = low
             packed[c, 2 * rows : 3 * rows, lanes] = high
+
+    each_class(body, rolled)
 
 
 def unfold(ss, sa, as_, aa):
@@ -509,10 +528,13 @@
     lower, upper = radial_halos(parts, tiles, 16)
     put(parts, tiles, slice(128, 144), lower)
     put(parts, tiles, slice(144, 160), upper)
-    pack(parts, packed, INNER, tiles)
-    for c in range(4):
+    pack(parts, packed, INNER, tiles, True)
+
+    def forward(c):
         for start, stop in chunks(lanes):
-            spectrum[c * MODES : (c + 1) * MODES, start:stop] = dot(fwd[c], packed[c, :, start:stop])
+            spectrum[class_rows(c, MODES), start:stop] = dot(fwd[c], packed[c, :, start:stop])
+
+    each_class(forward, True)
 
 
 def solve_outer_kernel(start_up, wide, tiles, *refs):
@@ -544,7 +566,7 @@
             here = slice(c * MODES, (c + 1) * MODES)
             value = dot(fwd[c], packed[c, :, start:stop]) + spectrum[here, start:stop]
             modes[c, 0:MODES, start:stop], modes[c, MODES:, start:stop] = halves(value * lam[here, start:stop])
-    back(modes, bwd, bwd_low, parts, tiles, 32)
+    back(modes, bwd, bwd_low, parts, tiles, 32, False)
     for k in range(4):
         classes = (load(parts, block(0, k), tiles, c * tiles) for c in range(4))
         values = unfold(*classes)
@@ -552,12 +574,14 @@
             (down if p == 0 else up)[block(0, q)] = value * factor
 
 
-def back(modes, bwd, bwd_low, parts, tiles, rows):
-    for c in range(4):
+def back(modes, bwd, bwd_low, parts, tiles, rows, rolled):
+    def body(c):
         for start, stop in chunks(tiles * TILE):
             value = dot(bwd[c], modes[c, :, start:stop])
             value = value + dot(bwd_low[c], modes[c, 0:MODES, start:stop])
             store(parts, slice(0, rows), value, c * tiles + start // TILE)
+
+    each_class(body, rolled)
 
 
 def stepped(kind, value, before):
@@ -577,7 +601,7 @@
     image, ext, parts, packed = take
     lanes = tiles * TILE
     factor = point_factor(wide * TILE)
-    back(modes, bwd, bwd_low, parts, wide, 96)
+    back(modes, bwd, bwd_low, parts, wide, 96, True)
     for i in range(3):
         for k in range(4):
             classes = (load(parts, block(0, i * 4 + k), wide, c * wide) for c in range(4))
@@ -598,14 +622,17 @@
             corners = ((i, k), (5 - i, k), (i, 7 - k), (5 - i, 7 - k))
             values = fold(*(load(ext, block(p, q), tiles) for p, q in corners))
             put(parts, tiles, block(0, i * 4 + k), values)
-    pack(parts, packed, 96, tiles)
-    for c in range(4):
+    pack(parts, packed, 96, tiles, True)
+
+    def operate(c):
         for start, stop in chunks(lanes):
             terms = dot(app[c], packed[c, :, start:stop]).reshape(40, PTS, stop - start)
             value = terms[0:16] * coef[0:8, start:stop]
             sides = terms[16:28] * coef[8:16, start:stop] + terms[28:40] * coef[16:24, start:stop]
             value = jnp.concatenate([value[0:4], value[4:16] + sides])
-            image[c * 128 : (c + 1) * 128, start:stop] = value.reshape(128, stop - start)
+            image[class_rows(c, 128), start:stop] = value.reshape(128, stop - start)
+
+    each_class(operate, True)
 
 
 def step_outer_kernel(kind, wide, tiles, *refs):

time: 130 us -> 119 us (0.915); the launches traced: 127 us -> 118 us
  starting transfers between devices: 23.1 us -> 13.4 us
  Pallas kernels: 33.1 us -> 40.5 us
  waiting for transfers between devices: 62 us -> 55.9 us
    ppermute x24, starting transfers between devices: 23.1 us -> 13.4 us  [shifted(): lax.ppermute(value, axis, [(n, (n + steps) % count) for n in range(count)])]
    pallas_call x25, Pallas kernels: 33.1 us -> 40.5 us  [call(): pl.pallas_call(kernel, out_shape=[jax.ShapeDtypeStruct(out, jnp.float32 i...]
    ppermute x24, waiting for transfers between devices: 62 us -> 55.9 us  [shifted(): lax.ppermute(value, axis, [(n, (n + steps) % count) for n in range(count)])]
  transfers between devices with their start and end apart: 24 -> 24, of which waited for: 15 -> 15; matrix products, arithmetic and copies ran while one was open for 2% -> 2% of each run, Pallas kernels for 17% -> 24%
where the time goes in v4:
time: 119 us; the launch traced here: 118 us
  waiting for transfers between devices  55.9 us (47%)
  Pallas kernels  40.5 us (34%)
  starting transfers between devices  13.4 us (11%)
  local copies, waits for them, and re-layouts  5.98 us (5%)
  between operations  1.69 us (1%)
    ppermute x24, waiting for transfers between devices, shifted(): lax.ppermute(value, axis, [(n, (n + steps) % count) for n in range(count)])  55.9 us
    pallas_call x25, Pallas kernels, call(): pl.pallas_call(kernel, out_shape=[jax.ShapeDtypeStruct(out, jnp.float32 i...  40.5 us
    ppermute x24, starting transfers between devices, shifted(): lax.ppermute(value, axis, [(n, (n + steps) % count) for n in range(count)])  13.4 us
    unnamed x34, local copies, waits for them, and re-layouts  3.02 us
  transfers between devices with their start and end apart: 24, of which 15 were waited for; matrix products, arithmetic and copies ran while one was open for 2% of the time, Pallas kernels for 24%

profile of v4, /device:TPU:31, one launch (start us, length us, event | category | flops | bytes accessed | tf_op | source)
XLA Modules:
  0.0 118.4 jit_solution(9280838757159240497)
XLA Ops:
  0.6 1.0 fusion
  1.7 3.8 %collective-permute-start.1 = (f32[256,256]{1,0:T(8,128)S(1)}, f32[256,256]{1,0:T(8,128)S(1)}, u32[]{:S(2)}, u32[]{:S(2)}) collective-permute-start(f32[256,256]{1,0:T(8,128)S(1)} %pad_maximum_fusion), channel_id=1, source_target_pairs={{0,3},{1,0},{2,1},{3,2},{4,7},{5,4},{6,5},{7,6},{8,11},{9,8},{10,9... | collective-permute-start | bytes 786440 | tf_op jit(solution)/shard_map/ppermute | solution.py:838
  5.5 0.8 pad_maximum_fusion.1
  7.4 0.1 concatenate.14
  7.5 0.1 stack_reshape.3
  7.6 0.7 tile.2
  8.3 0.1 stack_tile.3
  8.4 1.0 copy-done.8
  9.5 0.9 copy-done.10
  10.4 0.6 tables.1
  11.0 2.5 %collective-permute-done.left = f32[256,256]{1,0:T(8,128)S(1)} collective-permute-done((f32[256,256]{1,0:T(8,128)S(1)}, f32[256,256]{1,0:T(8,128)S(1)}, u32[]{:S(2)}, u32[]{:S(2)}) %collective-permute-start) | collective-permute-done | bytes 262176 | tf_op jit(solution)/shard_map/ppermute | solution.py:838
  13.6 0.8 collective-permute-start.5
  14.4 0.8 collective-permute-start.4
  15.1 0.6 dynamic_slice.6.rot
  15.7 0.9 copy-done.12
  16.7 1.2 %outer.1 = (f32[256,640]{1,0:T(8,128)S(1)}, f32[136,640]{1,0:T(8,128)S(1)}, f32[136,640]{1,0:T(8,128)S(1)}) custom-call(s32[1]{0:T(128)} %dynamic_slice.6.rot, f32[256,256]{1,0:T(8,128)S(1)} %collective-permute-done.left, f32[256,256]{1,0:T(8,128)S(1)} %copy-done.12, f32[256,256]{1,0:T(8,128)S(1)} %collective-permute-done.1.right, ...), custom_call_target="tpu_custom_call" | custom-call | bytes 4000000 | tf_op jit(solution)/shard_map/outer/pallas_call | solution.py:814
  17.9 2.2 %collective-permute-start.2 = (f32[136,640]{1,0:T(8,128)S(1)}, f32[136,640]{1,0:T(8,128)S(1)}, u32[]{:S(2)}, u32[]{:S(2)}) collective-permute-start(f32[136,640]{1,0:T(8,128)S(1)} %get-tuple-element.71), channel_id=1, source_target_pairs={{0,4},{4,8},{8,12},{12,16},{16,20},{20,24},{24,28},{28,32},{32,36}... | collective-permute-start | bytes 1044488 | tf_op jit(solution)/shard_map/ppermute | solution.py:838
  20.1 0.3 collective-permute-start.3
  20.5 1.4 %collective-permute-done.4.left = f32[256,256]{1,0:T(8,128)} collective-permute-done((f32[256,256]{1,0:T(8,128)S(1)}, f32[256,256]{1,0:T(8,128)}, u32[]{:S(2)}, u32[]{:S(2)}) %collective-permute-start.4) | collective-permute-done | bytes 262176 | tf_op jit(solution)/shard_map/ppermute | solution.py:838
  21.9 2.2 %inner.1.refs_1_ = f32[256,640]{1,0:T(8,128)S(1)} custom-call(s32[1]{0:T(128)} %dynamic_slice.6.rot, f32[256,256]{1,0:T(8,128)} %collective-permute-done.4.left, f32[256,256]{1,0:T(8,128)S(1)} %follow.1.own, f32[256,256]{1,0:T(8,128)} %collective-permute-done.5.right), custom_call_target="tpu_custom_call" | custom-call | flops 20000000000 | bytes 4000000 | tf_op jit(solution)/shard_map/inner/pallas_call | solution.py:814
  24.2 2.4 %solve_inner.4 = (f32[384,640]{1,0:T(8,128)S(1)}, f32[1024,640]{1,0:T(8,128)S(1)}) custom-call(f32[256,640]{1,0:T(8,128)S(1)} %get-tuple-element.70.refs_0_, f32[256,640]{1,0:T(8,128)S(1)} %inner.1.refs_1_, bf16[4,256,480]{2,1,0:T(8,128)(2,1)S(1)} %copy-done), custom_call_target="tpu_custom_call" | custom-call | bytes 4000000 | tf_op jit(solution)/shard_map/solve_inner/pallas_call | solution.py:814
  26.6 3.5 %collective-permute-done.3.refs_2_.upper = f32[136,640]{1,0:T(8,128)S(1)} collective-permute-done((f32[136,640]{1,0:T(8,128)S(1)}, f32[136,640]{1,0:T(8,128)S(1)}, u32[]{:S(2)}, u32[]{:S(2)}) %collective-permute-start.3) | collective-permute-done | bytes 348192 | tf_op jit(solution)/shard_map/ppermute | solution.py:838
  30.2 1.7 %solve_outer.4 = (f32[128,640]{1,0:T(8,128)S(1)}, bf16[4,512,640]{2,1,0:T(8,128)(2,1)S(1)}, f32[64,640]{1,0:T(8,128)S(1)}, f32[64,640]{1,0:T(8,128)S(1)}) custom-call(f32[256,640]{1,0:T(8,128)S(1)} %get-tuple-element.70.refs_0_, f32[136,640]{1,0:T(8,128)S(1)} %collective-permute-done.2.refs_1_.lower, f32[136,640]{1,0:T(8,128)S(1)} %collective-permute-done.3.refs_2_.upper, ...), custom_call_target="tpu_custom_call" | custom-call | bytes 4000000 | tf_op jit(solution)/shard_map/solve_outer/pallas_call | solution.py:814
  32.0 0.5 collective-permute-start.7
  32.5 3.5 %step0_inner.1 = (f32[384,640]{1,0:T(8,128)S(1)}, f32[512,640]{1,0:T(8,128)S(1)}) custom-call(bf16[4,512,640]{2,1,0:T(8,128)(2,1)S(1)} %get-tuple-element.80.refs_0_, f32[24,640]{1,0:T(8,128)S(1)} %get-tuple-element.81.refs_1_.refs_7_.refs_3_.refs_9_.coef.refs_2_.refs_8_, bf16[4,320,288]{2,1,0:T(8,128)(2,1)S(1)} %copy-done.1, ...), custom_call_target="tpu_custom_call" | custom-call | bytes 4000000 | tf_op jit(solution)/shard_map/step0_inner/pallas_call | solution.py:814
  36.1 4.1 %collective-permute-done.7.refs_3_ = f32[64,640]{1,0:T(8,128)S(1)} collective-permute-done((f32[64,640]{1,0:T(8,128)S(1)}, f32[64,640]{1,0:T(8,128)S(1)}, u32[]{:S(2)}, u32[]{:S(2)}) %collective-permute-start.7) | collective-permute-done | bytes 163872 | tf_op jit(solution)/shard_map/ppermute | solution.py:838
  40.2 0.9 step0_outer.1
  41.0 0.6 collective-permute-start.8
  41.7 2.4 %solve_inner.5 = (f32[384,640]{1,0:T(8,128)S(1)}, f32[1024,640]{1,0:T(8,128)S(1)}) custom-call(f32[512,640]{1,0:T(8,128)S(1)} %get-tuple-element.83.refs_0_, bf16[4,256,480]{2,1,0:T(8,128)(2,1)S(1)} %copy-done), custom_call_target="tpu_custom_call" | custom-call | bytes 4000000 | tf_op jit(solution)/shard_map/solve_inner/pallas_call | solution.py:814
  44.1 1.6 %collective-permute-done.8.refs_1_ = f32[128,640]{1,0:T(8,128)S(1)} collective-permute-done((f32[128,640]{1,0:T(8,128)S(1)}, f32[128,640]{1,0:T(8,128)S(1)}, u32[]{:S(2)}, u32[]{:S(2)}) %collective-permute-start.8) | collective-permute-done | bytes 327712 | tf_op jit(solution)/shard_map/ppermute | solution.py:838
  45.7 5.8 %collective-permute-done.9.refs_2_ = f32[128,640]{1,0:T(8,128)S(1)} collective-permute-done((f32[128,640]{1,0:T(8,128)S(1)}, f32[128,640]{1,0:T(8,128)S(1)}, u32[]{:S(2)}, u32[]{:S(2)}) %collective-permute-start.9) | collective-permute-done | bytes 327712 | tf_op jit(solution)/shard_map/ppermute | solution.py:838
  51.5 1.6 %solve_outer.5 = (f32[128,640]{1,0:T(8,128)S(1)}, bf16[4,512,640]{2,1,0:T(8,128)(2,1)S(1)}, f32[64,640]{1,0:T(8,128)S(1)}, f32[64,640]{1,0:T(8,128)S(1)}) custom-call(f32[512,640]{1,0:T(8,128)S(1)} %get-tuple-element.83.refs_0_, f32[128,640]{1,0:T(8,128)S(1)} %collective-permute-done.8.refs_1_, f32[128,640]{1,0:T(8,128)S(1)} %collective-permute-done.9.refs_2_, ...), custom_call_target="tpu_custom_call" | custom-call | bytes 4000000 | tf_op jit(solution)/shard_map/solve_outer/pallas_call | solution.py:814
  53.2 0.5 collective-permute-start.11
  53.7 3.3 %step1_inner.1 = (f32[384,512]{1,0:T(8,128)S(1)}, f32[512,512]{1,0:T(8,128)S(1)}) custom-call(bf16[4,512,640]{2,1,0:T(8,128)(2,1)S(1)} %get-tuple-element.92.refs_0_, f32[384,640]{1,0:T(8,128)S(1)} %get-tuple-element.93.refs_1_.refs_2_, f32[384,640]{1,0:T(8,128)S(1)} %get-tuple-element.93.refs_1_.refs_2_, ...), custom_call_target="tpu_custom_call" | custom-call | bytes 4000000 | tf_op jit(solution)/shard_map/step1_inner/pallas_call | solution.py:814
  57.0 4.3 %collective-permute-done.11.refs_3_ = f32[64,640]{1,0:T(8,128)S(1)} collective-permute-done((f32[64,640]{1,0:T(8,128)S(1)}, f32[64,640]{1,0:T(8,128)S(1)}, u32[]{:S(2)}, u32[]{:S(2)}) %collective-permute-start.11) | collective-permute-done | bytes 163872 | tf_op jit(solution)/shard_map/ppermute | solution.py:838
  61.3 1.2 step1_outer.1
  62.5 0.5 collective-permute-start.12
  62.9 0.1 collective-permute-start.13
  63.1 0.4 diagonal.1.scale
  63.5 0.5 collective-permute-done.12.below
  64.0 5.6 %collective-permute-done.13.above = f32[16,512]{1,0:T(8,128)S(1)} collective-permute-done((f32[16,512]{1,0:T(8,128)S(1)}, f32[16,512]{1,0:T(8,128)S(1)}, u32[]{:S(2)}, u32[]{:S(2)}) %collective-permute-start.13) | collective-permute-done | bytes 32800 | tf_op jit(solution)/shard_map/ppermute | solution.py:838
  69.6 0.7 coarse_outer.1
  70.4 0.5 collective-permute-start.15
  70.9 0.9 coarse_inner.1
  71.8 2.1 %solve_inner.6 = (f32[384,512]{1,0:T(8,128)S(1)}, f32[1024,512]{1,0:T(8,128)S(1)}) custom-call(f32[256,512]{1,0:T(8,128)S(1)} %get-tuple-element.99.refs_0_, f32[256,512]{1,0:T(8,128)S(1)} %get-tuple-element.105.refs_1_, bf16[4,256,480]{2,1,0:T(8,128)(2,1)S(1)} %copy-done), custom_call_target="tpu_custom_call" | custom-call | bytes 4000000 | tf_op jit(solution)/shard_map/solve_inner/pallas_call | solution.py:814
  73.8 5.7 %collective-permute-done.15.refs_2_ = f32[128,512]{1,0:T(8,128)S(1)} collective-permute-done((f32[128,512]{1,0:T(8,128)S(1)}, f32[128,512]{1,0:T(8,128)S(1)}, u32[]{:S(2)}, u32[]{:S(2)}) %collective-permute-start.15) | collective-permute-done | bytes 262176 | tf_op jit(solution)/shard_map/ppermute | solution.py:838
  79.6 1.4 %solve_outer.6 = (f32[128,512]{1,0:T(8,128)S(1)}, bf16[4,512,512]{2,1,0:T(8,128)(2,1)S(1)}, f32[64,512]{1,0:T(8,128)S(1)}, f32[64,512]{1,0:T(8,128)S(1)}) custom-call(f32[256,512]{1,0:T(8,128)S(1)} %get-tuple-element.99.refs_0_, f32[128,512]{1,0:T(8,128)S(1)} %collective-permute-done.14.refs_1_, f32[128,512]{1,0:T(8,128)S(1)} %collective-permute-done.15.refs_2_, ...), custom_call_target="tpu_custom_call" | custom-call | bytes 4000000 | tf_op jit(solution)/shard_map/solve_outer/pallas_call | solution.py:814
  81.1 0.5 collective-permute-start.17
  81.5 3.2 %step2_inner.1 = (f32[384,512]{1,0:T(8,128)S(1)}, f32[384,512]{1,0:T(8,128)S(1)}, f32[512,512]{1,0:T(8,128)S(1)}) custom-call(bf16[4,512,512]{2,1,0:T(8,128)(2,1)S(1)} %get-tuple-element.112.refs_0_, f32[384,512]{1,0:T(8,128)S(1)} %get-tuple-element.113.refs_1_, f32[24,640]{1,0:T(8,128)S(1)} %get-tuple-element.81.refs_1_.refs_7_.refs_3_.refs_9_.coef.refs_2_.refs_8_, ...), custom_call_target="tpu_custom_call" | custom-call | bytes 4000000 | tf_op jit(solution)/shard_map/step2_inner/pallas_call | solution.py:814
  84.7 4.1 %collective-permute-done.17.refs_3_ = f32[64,512]{1,0:T(8,128)S(1)} collective-permute-done((f32[64,512]{1,0:T(8,128)S(1)}, f32[64,512]{1,0:T(8,128)S(1)}, u32[]{:S(2)}, u32[]{:S(2)}) %collective-permute-start.17) | collective-permute-done | bytes 131104 | tf_op jit(solution)/shard_map/ppermute | solution.py:838
  88.8 0.8 step2_outer.1
  89.6 0.8 collective-permute-start.18
  90.5 1.9 %solve_inner.7 = (f32[384,384]{1,0:T(8,128)S(1)}, f32[1024,384]{1,0:T(8,128)S(1)}) custom-call(f32[512,512]{1,0:T(8,128)S(1)} %get-tuple-element.115.refs_0_, bf16[4,256,480]{2,1,0:T(8,128)(2,1)S(1)} %copy-done), custom_call_target="tpu_custom_call" | custom-call | bytes 4000000 | tf_op jit(solution)/shard_map/solve_inner/pallas_call | solution.py:814
  92.4 1.4 %collective-permute-done.18.refs_1_ = f32[128,512]{1,0:T(8,128)S(1)} collective-permute-done((f32[128,512]{1,0:T(8,128)S(1)}, f32[128,512]{1,0:T(8,128)S(1)}, u32[]{:S(2)}, u32[]{:S(2)}) %collective-permute-start.18) | collective-permute-done | bytes 262176 | tf_op jit(solution)/shard_map/ppermute | solution.py:838
  93.8 5.8 %collective-permute-done.19.refs_2_ = f32[128,512]{1,0:T(8,128)S(1)} collective-permute-done((f32[128,512]{1,0:T(8,128)S(1)}, f32[128,512]{1,0:T(8,128)S(1)}, u32[]{:S(2)}, u32[]{:S(2)}) %collective-permute-start.19) | collective-permute-done | bytes 262176 | tf_op jit(solution)/shard_map/ppermute | solution.py:838
  99.6 1.1 solve_outer.7
  100.7 0.5 collective-permute-start.21
  101.2 2.7 %step3_inner.1 = (f32[384,384]{1,0:T(8,128)S(1)}, f32[512,384]{1,0:T(8,128)S(1)}) custom-call(bf16[4,512,384]{2,1,0:T(8,128)(2,1)S(1)} %get-tuple-element.125.refs_0_, f32[384,512]{1,0:T(8,128)S(1)} %get-tuple-element.126.refs_1_, f32[384,512]{1,0:T(8,128)S(1)} %get-tuple-element.127.refs_2_, ...), custom_call_target="tpu_custom_call" | custom-call | bytes 4000000 | tf_op jit(solution)/shard_map/step3_inner/pallas_call | solution.py:814
  104.0 4.2 %collective-permute-done.21.refs_3_ = f32[64,384]{1,0:T(8,128)S(1)} collective-permute-done((f32[64,384]{1,0:T(8,128)S(1)}, f32[64,384]{1,0:T(8,128)S(1)}, u32[]{:S(2)}, u32[]{:S(2)}) %collective-permute-start.21) | collective-permute-done | bytes 98336 | tf_op jit(solution)/shard_map/ppermute | solution.py:838
  108.2 0.6 step3_outer.1
  108.8 0.5 collective-permute-start.22
  109.4 2.0 %finish_inner.1 = (f32[512,256]{1,0:T(8,128)}, f32[384,256]{1,0:T(8,128)S(1)}) custom-call(s32[1]{0:T(128)} %dynamic_slice.6.rot, f32[512,384]{1,0:T(8,128)S(1)} %get-tuple-element.129.local, f32[384,384]{1,0:T(8,128)S(1)} %get-tuple-element.130.total_inner, f32[128,384]{1,0:T(8,128)S(1)} %get-tuple-element.131.total_outer), custom_call_target="tpu_custom_call" | custom-call | bytes 4000000 | tf_op jit(solution)/shard_map/finish_inner/pallas_call | solution.py:814
  111.5 5.3 %collective-permute-done.23.above = f32[64,384]{1,0:T(8,128)S(1)} collective-permute-done((f32[64,384]{1,0:T(8,128)S(1)}, f32[64,384]{1,0:T(8,128)S(1)}, u32[]{:S(2)}, u32[]{:S(2)}) %collective-permute-start.23) | collective-permute-done | bytes 98336 | tf_op jit(solution)/shard_map/ppermute | solution.py:838
  116.7 1.7 %finish_outer.1 = f32[512,256]{1,0:T(8,128)} custom-call(s32[1]{0:T(128)} %dynamic_slice.6.rot, f32[512,384]{1,0:T(8,128)S(1)} %get-tuple-element.129.local, f32[64,384]{1,0:T(8,128)S(1)} %collective-permute-done.22.below, f32[64,384]{1,0:T(8,128)S(1)} %collective-permute-done.23.above, f32[384,256]{1,0:T(8,128)S(1)} %get-tuple-element.135.inner), custom_call_target="tpu_custom_call" | custom-call | bytes 4000000 | tf_op jit(solution)/shard_map/finish_outer/pallas_call | solution.py:814
  (59 shorter events, 1.1 us)
Async XLA Ops:
  0.6 14.5 %copy-start.16 = (s32[32]{0:T(128)S(1)}, s32[32]{0:T(128)}, u32[]{:S(2)}) copy-start(s32[32]{0:T(128)} %param.22) | copy-start | bytes 388
  1.7 9.3 %collective-permute-start.1 = (f32[256,256]{1,0:T(8,128)S(1)}, f32[256,256]{1,0:T(8,128)S(1)}, u32[]{:S(2)}, u32[]{:S(2)}) collective-permute-start(f32[256,256]{1,0:T(8,128)S(1)} %pad_maximum_fusion), channel_id=1, source_target_pairs={{0,3},{1,0},{2,1},{3,2},{4,7},{5,4},{6,5},{7,6},{8,11},{9,8},{10,9... | collective-permute-start | bytes 786440 | tf_op jit(solution)/shard_map/ppermute | solution.py:838
  5.5 8.1 %collective-permute-start = (f32[256,256]{1,0:T(8,128)S(1)}, f32[256,256]{1,0:T(8,128)S(1)}, u32[]{:S(2)}, u32[]{:S(2)}) collective-permute-start(f32[256,256]{1,0:T(8,128)S(1)} %pad_maximum_fusion), channel_id=1, source_target_pairs={{0,1},{1,2},{2,3},{3,0},{4,5},{5,6},{6,7},{7,4},{8,9},{9,10},{10,1... | collective-permute-start | bytes 786440 | tf_op jit(solution)/shard_map/ppermute | solution.py:838
  8.4 1.0 copy-start.8
  9.5 0.9 copy-start.10
  11.0 2.6 %copy-start.11 = (f32[256,256]{1,0:T(8,128)}, f32[256,256]{1,0:T(8,128)S(1)}, u32[]{:S(2)}) copy-start(f32[256,256]{1,0:T(8,128)S(1)} %get-tuple-element.69.own) | copy-start | bytes 786436
  13.6 6.9 %collective-permute-start.5 = (f32[256,256]{1,0:T(8,128)S(1)}, f32[256,256]{1,0:T(8,128)}, u32[]{:S(2)}, u32[]{:S(2)}) collective-permute-start(f32[256,256]{1,0:T(8,128)S(1)} %follow.1.own), channel_id=1, source_target_pairs={{0,3},{1,0},{2,1},{3,2},{4,7},{5,4},{6,5},{7,6},{8,11},{9,8},{10,9... | collective-permute-start | bytes 786440 | tf_op jit(solution)/shard_map/ppermute | solution.py:838
  14.4 7.6 %collective-permute-start.4 = (f32[256,256]{1,0:T(8,128)S(1)}, f32[256,256]{1,0:T(8,128)}, u32[]{:S(2)}, u32[]{:S(2)}) collective-permute-start(f32[256,256]{1,0:T(8,128)S(1)} %follow.1.own), channel_id=1, source_target_pairs={{0,1},{1,2},{2,3},{3,0},{4,5},{5,6},{6,7},{7,4},{8,9},{9,10},{10,1... | collective-permute-start | bytes 786440 | tf_op jit(solution)/shard_map/ppermute | solution.py:838
  15.7 0.9 copy-start.12
  17.9 8.7 %collective-permute-start.2 = (f32[136,640]{1,0:T(8,128)S(1)}, f32[136,640]{1,0:T(8,128)S(1)}, u32[]{:S(2)}, u32[]{:S(2)}) collective-permute-start(f32[136,640]{1,0:T(8,128)S(1)} %get-tuple-element.71), channel_id=1, source_target_pairs={{0,4},{4,8},{8,12},{12,16},{16,20},{20,24},{24,28},{28,32},{32,36}... | collective-permute-start | bytes 1044488 | tf_op jit(solution)/shard_map/ppermute | solution.py:838
  20.1 4.0 %copy-start = (bf16[4,256,480]{2,1,0:T(8,128)(2,1)S(1)}, bf16[4,256,480]{2,1,0:T(8,128)(2,1)}, u32[]{:S(2)}) copy-start(bf16[4,256,480]{2,1,0:T(8,128)(2,1)} %constant.51.clone.refs_2_.refs_1_) | copy-start | bytes 2949124
  20.1 10.0 %collective-permute-start.3 = (f32[136,640]{1,0:T(8,128)S(1)}, f32[136,640]{1,0:T(8,128)S(1)}, u32[]{:S(2)}, u32[]{:S(2)}) collective-permute-start(f32[136,640]{1,0:T(8,128)S(1)} %get-tuple-element.72), channel_id=1, source_target_pairs={{0,124},{4,0},{8,4},{12,8},{16,12},{20,16},{24,20},{28,24},{32,28}... | collective-permute-start | bytes 1044488 | tf_op jit(solution)/shard_map/ppermute | solution.py:838
  24.1 6.1 %copy-start.2 = (bf16[4,256,240]{2,1,0:T(8,128)(2,1)S(1)}, bf16[4,256,240]{2,1,0:T(8,128)(2,1)}, u32[]{:S(2)}) copy-start(bf16[4,256,240]{2,1,0:T(8,128)(2,1)} %constant.52.clone.refs_5_) | copy-start | bytes 1474564
  24.1 6.0 %copy-start.7 = (bf16[4,32,512]{2,1,0:T(8,128)(2,1)S(1)}, bf16[4,32,512]{2,1,0:T(8,128)(2,1)}, u32[]{:S(2)}) copy-start(bf16[4,32,512]{2,1,0:T(8,128)(2,1)} %constant.53.clone.refs_6_) | copy-start | bytes 393220
  24.2 6.0 %copy-start.9 = (bf16[4,32,256]{2,1,0:T(8,128)(2,1)S(1)}, bf16[4,32,256]{2,1,0:T(8,128)(2,1)}, u32[]{:S(2)}) copy-start(bf16[4,32,256]{2,1,0:T(8,128)(2,1)} %constant.54.clone.refs_7_) | copy-start | bytes 196612
  30.2 2.3 %copy-start.1 = (bf16[4,320,288]{2,1,0:T(8,128)(2,1)S(1)}, bf16[4,320,288]{2,1,0:T(8,128)(2,1)}, u32[]{:S(2)}) copy-start(bf16[4,320,288]{2,1,0:T(8,128)(2,1)} %constant.57.clone.refs_2_.refs_4_.refs_3_) | copy-start | bytes 2211844
  30.2 2.3 %copy-start.3 = (bf16[4,96,512]{2,1,0:T(8,128)(2,1)S(1)}, bf16[4,96,512]{2,1,0:T(8,128)(2,1)}, u32[]{:S(2)}) copy-start(bf16[4,96,512]{2,1,0:T(8,128)(2,1)} %constant.55.clone.refs_3_.refs_5_.refs_4_) | copy-start | bytes 1179652
  30.2 2.3 %copy-start.5 = (bf16[4,96,256]{2,1,0:T(8,128)(2,1)S(1)}, bf16[4,96,256]{2,1,0:T(8,128)(2,1)}, u32[]{:S(2)}) copy-start(bf16[4,96,256]{2,1,0:T(8,128)(2,1)} %constant.56.clone.refs_4_.refs_6_.refs_5_) | copy-start | bytes 589828
  32.0 4.1 %collective-permute-start.6 = (f32[64,640]{1,0:T(8,128)S(1)}, f32[64,640]{1,0:T(8,128)S(1)}, u32[]{:S(2)}, u32[]{:S(2)}) collective-permute-start(f32[64,640]{1,0:T(8,128)S(1)} %get-tuple-element.76.refs_0_), channel_id=1, source_target_pairs={{0,4},{4,8},{8,12},{12,16},{16,20},{20,24},{24,28},{28,32},{32,36}... | collective-permute-start | bytes 491528 | tf_op jit(solution)/shard_map/ppermute | solution.py:838
  32.0 8.1 %collective-permute-start.7 = (f32[64,640]{1,0:T(8,128)S(1)}, f32[64,640]{1,0:T(8,128)S(1)}, u32[]{:S(2)}, u32[]{:S(2)}) collective-permute-start(f32[64,640]{1,0:T(8,128)S(1)} %get-tuple-element.77.refs_2_), channel_id=1, source_target_pairs={{0,124},{4,0},{8,4},{12,8},{16,12},{20,16},{24,20},{28,24},{32,28}... | collective-permute-start | bytes 491528 | tf_op jit(solution)/shard_map/ppermute | solution.py:838
  32.5 7.6 %copy-start.6 = (bf16[4,192,96]{2,1,0:T(8,128)(2,1)S(1)}, bf16[4,192,96]{2,1,0:T(8,128)(2,1)}, u32[]{:S(2)}) copy-start(bf16[4,192,96]{2,1,0:T(8,128)(2,1)} %constant.58.clone.refs_8_.refs_10_.refs_9_) | copy-start | bytes 442372
  41.0 4.6 %collective-permute-start.8 = (f32[128,640]{1,0:T(8,128)S(1)}, f32[128,640]{1,0:T(8,128)S(1)}, u32[]{:S(2)}, u32[]{:S(2)}) collective-permute-start(f32[128,640]{1,0:T(8,128)S(1)} %get-tuple-element.84), channel_id=1, source_target_pairs={{0,4},{4,8},{8,12},{12,16},{16,20},{20,24},{24,28},{28,32},{32,36}... | collective-permute-start | bytes 983048 | tf_op jit(solution)/shard_map/ppermute | solution.py:838
  41.7 9.8 %collective-permute-start.9 = (f32[128,640]{1,0:T(8,128)S(1)}, f32[128,640]{1,0:T(8,128)S(1)}, u32[]{:S(2)}, u32[]{:S(2)}) collective-permute-start(f32[128,640]{1,0:T(8,128)S(1)} %get-tuple-element.85), channel_id=1, source_target_pairs={{0,124},{4,0},{8,4},{12,8},{16,12},{20,16},{24,20},{28,24},{32,28}... | collective-permute-start | bytes 983048 | tf_op jit(solution)/shard_map/ppermute | solution.py:838
  53.1 3.9 %collective-permute-start.10 = (f32[64,640]{1,0:T(8,128)S(1)}, f32[64,640]{1,0:T(8,128)S(1)}, u32[]{:S(2)}, u32[]{:S(2)}) collective-permute-start(f32[64,640]{1,0:T(8,128)S(1)} %get-tuple-element.87.refs_0_), channel_id=1, source_target_pairs={{0,4},{4,8},{8,12},{12,16},{16,20},{20,24},{24,28},{28,32},{32,36}... | collective-permute-start | bytes 491528 | tf_op jit(solution)/shard_map/ppermute | solution.py:838
  53.2 8.1 %collective-permute-start.11 = (f32[64,640]{1,0:T(8,128)S(1)}, f32[64,640]{1,0:T(8,128)S(1)}, u32[]{:S(2)}, u32[]{:S(2)}) collective-permute-start(f32[64,640]{1,0:T(8,128)S(1)} %get-tuple-element.88.refs_2_), channel_id=1, source_target_pairs={{0,124},{4,0},{8,4},{12,8},{16,12},{20,16},{24,20},{28,24},{32,28}... | collective-permute-start | bytes 491528 | tf_op jit(solution)/shard_map/ppermute | solution.py:838
  53.7 7.6 %copy-start.13 = (bf16[64,1024]{1,0:T(8,128)(2,1)S(1)}, bf16[64,1024]{1,0:T(8,128)(2,1)}, u32[]{:S(2)}) copy-start(bf16[64,1024]{1,0:T(8,128)(2,1)} %constant.59.clone.refs_11_) | copy-start | bytes 393220
  53.7 7.6 %copy-start.14 = (bf16[64,512]{1,0:T(8,128)(2,1)S(1)}, bf16[64,512]{1,0:T(8,128)(2,1)}, u32[]{:S(2)}) copy-start(bf16[64,512]{1,0:T(8,128)(2,1)} %constant.60.clone.refs_12_) | copy-start | bytes 196612
  57.0 6.1 %copy-start.15 = (f32[64,8]{1,0:T(8,128)S(1)}, f32[64,8]{1,0:T(8,128)}, u32[]{:S(2)}) copy-start(f32[64,8]{1,0:T(8,128)} %constant.63.clone.table) | copy-start | bytes 6148
  61.3 8.3 %copy-start.4 = (bf16[2048,192]{1,0:T(8,128)(2,1)S(1)}, bf16[2048,192]{1,0:T(8,128)(2,1)}, u32[]{:S(2)}) copy-start(bf16[2048,192]{1,0:T(8,128)(2,1)} %constant.61.clone.prolong) | copy-start | bytes 2359300
  62.5 1.5 %collective-permute-start.12 = (f32[16,512]{1,0:T(8,128)S(1)}, f32[16,512]{1,0:T(8,128)S(1)}, u32[]{:S(2)}, u32[]{:S(2)}) collective-permute-start(f32[16,512]{1,0:T(8,128)S(1)} %get-tuple-element.96), channel_id=1, source_target_pairs={{0,4},{4,8},{8,12},{12,16},{16,20},{20,24},{24,28},{28,32},{32,36}... | collective-permute-start | bytes 98312 | tf_op jit(solution)/shard_map/ppermute | solution.py:838
  62.9 6.7 %collective-permute-start.13 = (f32[16,512]{1,0:T(8,128)S(1)}, f32[16,512]{1,0:T(8,128)S(1)}, u32[]{:S(2)}, u32[]{:S(2)}) collective-permute-start(f32[16,512]{1,0:T(8,128)S(1)} %get-tuple-element.97), channel_id=1, source_target_pairs={{0,124},{4,0},{8,4},{12,8},{16,12},{20,16},{24,20},{28,24},{32,28}... | collective-permute-start | bytes 98312 | tf_op jit(solution)/shard_map/ppermute | solution.py:838
  70.3 3.5 %collective-permute-start.14 = (f32[128,512]{1,0:T(8,128)S(1)}, f32[128,512]{1,0:T(8,128)S(1)}, u32[]{:S(2)}, u32[]{:S(2)}) collective-permute-start(f32[128,512]{1,0:T(8,128)S(1)} %get-tuple-element.100), channel_id=1, source_target_pairs={{0,4},{4,8},{8,12},{12,16},{16,20},{20,24},{24,28},{28,32},{32,36}... | collective-permute-start | bytes 786440 | tf_op jit(solution)/shard_map/ppermute | solution.py:838
  70.4 9.2 %collective-permute-start.15 = (f32[128,512]{1,0:T(8,128)S(1)}, f32[128,512]{1,0:T(8,128)S(1)}, u32[]{:S(2)}, u32[]{:S(2)}) collective-permute-start(f32[128,512]{1,0:T(8,128)S(1)} %get-tuple-element.101), channel_id=1, source_target_pairs={{0,124},{4,0},{8,4},{12,8},{16,12},{20,16},{24,20},{28,24},{32,28}... | collective-permute-start | bytes 786440 | tf_op jit(solution)/shard_map/ppermute | solution.py:838
  81.0 3.8 %collective-permute-start.16 = (f32[64,512]{1,0:T(8,128)S(1)}, f32[64,512]{1,0:T(8,128)S(1)}, u32[]{:S(2)}, u32[]{:S(2)}) collective-permute-start(f32[64,512]{1,0:T(8,128)S(1)} %get-tuple-element.107.refs_0_), channel_id=1, source_target_pairs={{0,4},{4,8},{8,12},{12,16},{16,20},{20,24},{24,28},{28,32},{32,36}... | collective-permute-start | bytes 393224 | tf_op jit(solution)/shard_map/ppermute | solution.py:838
  81.1 7.8 %collective-permute-start.17 = (f32[64,512]{1,0:T(8,128)S(1)}, f32[64,512]{1,0:T(8,128)S(1)}, u32[]{:S(2)}, u32[]{:S(2)}) collective-permute-start(f32[64,512]{1,0:T(8,128)S(1)} %get-tuple-element.108.refs_2_), channel_id=1, source_target_pairs={{0,124},{4,0},{8,4},{12,8},{16,12},{20,16},{24,20},{28,24},{32,28}... | collective-permute-start | bytes 393224 | tf_op jit(solution)/shard_map/ppermute | solution.py:838
  89.6 4.1 %collective-permute-start.18 = (f32[128,512]{1,0:T(8,128)S(1)}, f32[128,512]{1,0:T(8,128)S(1)}, u32[]{:S(2)}, u32[]{:S(2)}) collective-permute-start(f32[128,512]{1,0:T(8,128)S(1)} %get-tuple-element.116), channel_id=1, source_target_pairs={{0,4},{4,8},{8,12},{12,16},{16,20},{20,24},{24,28},{28,32},{32,36}... | collective-permute-start | bytes 786440 | tf_op jit(solution)/shard_map/ppermute | solution.py:838
  90.5 9.1 %collective-permute-start.19 = (f32[128,512]{1,0:T(8,128)S(1)}, f32[128,512]{1,0:T(8,128)S(1)}, u32[]{:S(2)}, u32[]{:S(2)}) collective-permute-start(f32[128,512]{1,0:T(8,128)S(1)} %get-tuple-element.117), channel_id=1, source_target_pairs={{0,124},{4,0},{8,4},{12,8},{16,12},{20,16},{24,20},{28,24},{32,28}... | collective-permute-start | bytes 786440 | tf_op jit(solution)/shard_map/ppermute | solution.py:838
  100.7 3.3 %collective-permute-start.20 = (f32[64,384]{1,0:T(8,128)S(1)}, f32[64,384]{1,0:T(8,128)S(1)}, u32[]{:S(2)}, u32[]{:S(2)}) collective-permute-start(f32[64,384]{1,0:T(8,128)S(1)} %get-tuple-element.119.refs_0_), channel_id=1, source_target_pairs={{0,4},{4,8},{8,12},{12,16},{16,20},{20,24},{24,28},{28,32},{32,36}... | collective-permute-start | bytes 294920 | tf_op jit(solution)/shard_map/ppermute | solution.py:838
  100.7 7.4 %collective-permute-start.21 = (f32[64,384]{1,0:T(8,128)S(1)}, f32[64,384]{1,0:T(8,128)S(1)}, u32[]{:S(2)}, u32[]{:S(2)}) collective-permute-start(f32[64,384]{1,0:T(8,128)S(1)} %get-tuple-element.120.refs_2_), channel_id=1, source_target_pairs={{0,124},{4,0},{8,4},{12,8},{16,12},{20,16},{24,20},{28,24},{32,28}... | collective-permute-start | bytes 294920 | tf_op jit(solution)/shard_map/ppermute | solution.py:838
  108.8 2.6 %collective-permute-start.22 = (f32[64,384]{1,0:T(8,128)S(1)}, f32[64,384]{1,0:T(8,128)S(1)}, u32[]{:S(2)}, u32[]{:S(2)}) collective-permute-start(f32[64,384]{1,0:T(8,128)S(1)} %get-tuple-element.133), channel_id=1, source_target_pairs={{0,4},{4,8},{8,12},{12,16},{16,20},{20,24},{24,28},{28,32},{32,36}... | collective-permute-start | bytes 294920 | tf_op jit(solution)/shard_map/ppermute | solution.py:838
  109.4 7.4 %collective-permute-start.23 = (f32[64,384]{1,0:T(8,128)S(1)}, f32[64,384]{1,0:T(8,128)S(1)}, u32[]{:S(2)}, u32[]{:S(2)}) collective-permute-start(f32[64,384]{1,0:T(8,128)S(1)} %get-tuple-element.134), channel_id=1, source_target_pairs={{0,124},{4,0},{8,4},{12,8},{16,12},{20,16},{24,20},{28,24},{32,28}... | collective-permute-start | bytes 294920 | tf_op jit(solution)/shard_map/ppermute | solution.py:838

commit v5 on v4

--- a/solution.py
+++ b/solution.py
@@ -412,9 +412,7 @@
     return jnp.concatenate(rows).astype(jnp.bfloat16)
 
 
-def tables_kernel(geo, modes, own, lam, coef, kept, middle):
-    kept[0:128] = own[0:128]
-    kept[128:256] = own[384:512]
+def tables_kernel(rot, geo, modes, own, lam, coef, middle):
     middle[...] = own[128:384]
     la, lb, lz = (geo[n : n + 1] for n in range(3))
     cz = la * lb / (2.0 * lz)
@@ -821,7 +819,7 @@
         scratch_shapes=list(scratch),
         name=name,
         cost_estimate=pl.CostEstimate(flops=flops, bytes_accessed=4_000_000, transcendentals=0),
-        compiler_params=pltpu.CompilerParams(vmem_limit_bytes=40 * 1024 * 1024),
+        compiler_params=pltpu.CompilerParams(vmem_limit_bytes=20 * 1024 * 1024),
     )(*args)
 
 
@@ -847,7 +845,8 @@
         return tuple((count, tiles * TILE) for count in rows)
 
     own = rhs.reshape(512, OWN)
-    left, right = beside(jnp.concatenate([own[0:128], own[384:512]]))
+    ends = jnp.concatenate([own[0:128], own[384:512]])
+    left, right = beside(ends)
     rot = lax.dynamic_slice(rotation, (group,), (1,))
     ring = jnp.concatenate([spacing_a, spacing_a, spacing_a])
     columns = lax.dynamic_slice(ring, (spacing_a.shape[0] + member * COLS_DEV - LEFT,), (WIN,))
@@ -860,18 +859,19 @@
         ]
     )
     geo = jnp.concatenate([geo, jnp.ones((5, LANES), wide)])
-    lam, coef, own, middle = call(
+    lam, coef, middle = call(
         tables_kernel,
         "tables",
-        (geo, mats["modes"], own),
-        ((4 * MODES, LANES), (24, LANES), (256, OWN), (256, OWN)),
+        (rot, geo, mats["modes"], own),
+        ((4 * MODES, LANES), (24, LANES), (256, OWN)),
+        scalars=1,
     )
     (middle,) = call(follow_kernel, "follow", (left, right, middle), ((256, OWN),), untouched=2)
     near, far = beside(middle)
     outer, up, down = call(
         outer_kernel,
         "outer",
-        (rot, left, own, right, geo),
+        (rot, left, ends, right, geo),
         ((256, LANES), (136, LANES), (136, LANES)),
         scalars=1,
     )

time: 119 us -> 117 us (0.983)
    unnamed x34 -> x28, local copies, waits for them, and re-layouts: 3.02 us -> 2.06 us
  transfers between devices with their start and end apart: 24 -> 24, of which waited for: 15 -> 16; matrix products, arithmetic and copies ran while one was open for 2% -> 3% of each run, Pallas kernels for 24% -> 24%
where the time goes in v5:
time: 117 us
  waiting for transfers between devices  55.5 us (47%)
  Pallas kernels  39.8 us (34%)
  starting transfers between devices  13.6 us (12%)
  local copies, waits for them, and re-layouts  5.62 us (5%)
  between operations  1.65 us (1%)
    ppermute x24, waiting for transfers between devices, shifted(): lax.ppermute(value, axis, [(n, (n + steps) % count) for n in range(count)])  55.5 us
    pallas_call x25, Pallas kernels, call(): pl.pallas_call(kernel, out_shape=[jax.ShapeDtypeStruct(out, jnp.float32 i...  39.8 us
    ppermute x24, starting transfers between devices, shifted(): lax.ppermute(value, axis, [(n, (n + steps) % count) for n in range(count)])  13.6 us
  transfers between devices with their start and end apart: 24, of which 16 were waited for; matrix products, arithmetic and copies ran while one was open for 3% of the time, Pallas kernels for 24%

profile of v5, /device:TPU:31, one launch (start us, length us, event | category | flops | bytes accessed | tf_op | source)
XLA Modules:
  0.0 117.1 jit_solution(2288873898570245586)
XLA Ops:
  0.6 1.0 fusion
  1.6 3.8 %collective-permute-start.1 = (f32[256,256]{1,0:T(8,128)S(1)}, f32[256,256]{1,0:T(8,128)S(1)}, u32[]{:S(2)}, u32[]{:S(2)}) collective-permute-start(f32[256,256]{1,0:T(8,128)S(1)} %pad_maximum_fusion.own), channel_id=1, source_target_pairs={{0,3},{1,0},{2,1},{3,2},{4,7},{5,4},{6,5},{7,6},{8,11},{9,8},{10,9... | collective-permute-start | bytes 786440 | tf_op jit(solution)/shard_map/ppermute | solution.py:836
  5.5 0.8 pad_maximum_fusion.1
  7.3 0.1 pad.3.clone
  7.3 0.1 concatenate.14
  7.5 0.1 stack_reshape.3
  7.6 0.7 tile.2
  8.3 0.1 stack_tile.3
  8.3 1.2 %dynamic_slice.6.rot = s32[1]{0:T(128)} dynamic-slice(s32[32]{0:T(128)} %param.22, s32[]{:T(128)S(6)} %select_n.6), dynamic_slice_sizes={1} | dynamic-slice | bytes 12 | tf_op jit(solution)/shard_map/dynamic_slice | solution.py:850
  9.6 1.0 copy-done.8
  10.7 0.9 copy-done.10
  11.6 1.1 tables.1
  12.7 0.8 collective-permute-done.left
  13.6 1.9 %collective-permute-start.5 = (f32[256,256]{1,0:T(8,128)S(1)}, f32[256,256]{1,0:T(8,128)S(1)}, u32[]{:S(2)}, u32[]{:S(2)}) collective-permute-start(f32[256,256]{1,0:T(8,128)S(1)} %follow.1.own), channel_id=1, source_target_pairs={{0,3},{1,0},{2,1},{3,2},{4,7},{5,4},{6,5},{7,6},{8,11},{9,8},{10,9... | collective-permute-start | bytes 786440 | tf_op jit(solution)/shard_map/ppermute | solution.py:836
  15.5 1.1 outer.1
  16.6 1.8 %collective-permute-start.2 = (f32[136,640]{1,0:T(8,128)S(1)}, f32[136,640]{1,0:T(8,128)S(1)}, u32[]{:S(2)}, u32[]{:S(2)}) collective-permute-start(f32[136,640]{1,0:T(8,128)S(1)} %get-tuple-element.69), channel_id=1, source_target_pairs={{0,4},{4,8},{8,12},{12,16},{16,20},{20,24},{24,28},{28,32},{32,36}... | collective-permute-start | bytes 1044488 | tf_op jit(solution)/shard_map/ppermute | solution.py:836
  18.5 0.4 collective-permute-start.3
  18.8 1.0 collective-permute-done.5.right
  19.8 3.1 %collective-permute-done.4.left = f32[256,256]{1,0:T(8,128)S(1)} collective-permute-done((f32[256,256]{1,0:T(8,128)S(1)}, f32[256,256]{1,0:T(8,128)S(1)}, u32[]{:S(2)}, u32[]{:S(2)}) %collective-permute-start.4) | collective-permute-done | bytes 262176 | tf_op jit(solution)/shard_map/ppermute | solution.py:836
  23.0 1.1 inner.1.refs_1_
  24.1 2.4 %solve_inner.4 = (f32[384,640]{1,0:T(8,128)S(1)}, f32[1024,640]{1,0:T(8,128)S(1)}) custom-call(f32[256,640]{1,0:T(8,128)S(1)} %get-tuple-element.68.refs_0_, f32[256,640]{1,0:T(8,128)S(1)} %inner.1.refs_1_, bf16[4,256,480]{2,1,0:T(8,128)(2,1)S(1)} %copy-done), custom_call_target="tpu_custom_call" | custom-call | bytes 4000000 | tf_op jit(solution)/shard_map/solve_inner/pallas_call | solution.py:812
  26.6 1.9 %collective-permute-done.3.refs_2_.upper = f32[136,640]{1,0:T(8,128)S(1)} collective-permute-done((f32[136,640]{1,0:T(8,128)S(1)}, f32[136,640]{1,0:T(8,128)S(1)}, u32[]{:S(2)}, u32[]{:S(2)}) %collective-permute-start.3) | collective-permute-done | bytes 348192 | tf_op jit(solution)/shard_map/ppermute | solution.py:836
  28.6 1.7 %solve_outer.4 = (f32[128,640]{1,0:T(8,128)S(1)}, bf16[4,512,640]{2,1,0:T(8,128)(2,1)S(1)}, f32[64,640]{1,0:T(8,128)S(1)}, f32[64,640]{1,0:T(8,128)S(1)}) custom-call(f32[256,640]{1,0:T(8,128)S(1)} %get-tuple-element.68.refs_0_, f32[136,640]{1,0:T(8,128)S(1)} %collective-permute-done.2.refs_1_.lower, f32[136,640]{1,0:T(8,128)S(1)} %collective-permute-done.3.refs_2_.upper, ...), custom_call_target="tpu_custom_call" | custom-call | bytes 4000000 | tf_op jit(solution)/shard_map/solve_outer/pallas_call | solution.py:812
  30.3 0.3 collective-permute-start.6
  30.7 0.3 collective-permute-start.7
  31.0 3.5 %step0_inner.1 = (f32[384,640]{1,0:T(8,128)S(1)}, f32[512,640]{1,0:T(8,128)S(1)}) custom-call(bf16[4,512,640]{2,1,0:T(8,128)(2,1)S(1)} %get-tuple-element.78.refs_0_, f32[24,640]{1,0:T(8,128)S(1)} %get-tuple-element.79.refs_1_.refs_7_.refs_3_.refs_9_.coef.refs_2_.refs_8_, bf16[4,320,288]{2,1,0:T(8,128)(2,1)S(1)} %copy-done.1, ...), custom_call_target="tpu_custom_call" | custom-call | bytes 4000000 | tf_op jit(solution)/shard_map/step0_inner/pallas_call | solution.py:812
  34.5 4.2 %collective-permute-done.7.refs_3_ = f32[64,640]{1,0:T(8,128)S(1)} collective-permute-done((f32[64,640]{1,0:T(8,128)S(1)}, f32[64,640]{1,0:T(8,128)S(1)}, u32[]{:S(2)}, u32[]{:S(2)}) %collective-permute-start.7) | collective-permute-done | bytes 163872 | tf_op jit(solution)/shard_map/ppermute | solution.py:836
  38.7 0.9 step0_outer.1
  39.6 0.6 collective-permute-start.8
  40.2 2.4 %solve_inner.5 = (f32[384,640]{1,0:T(8,128)S(1)}, f32[1024,640]{1,0:T(8,128)S(1)}) custom-call(f32[512,640]{1,0:T(8,128)S(1)} %get-tuple-element.81.refs_0_, bf16[4,256,480]{2,1,0:T(8,128)(2,1)S(1)} %copy-done), custom_call_target="tpu_custom_call" | custom-call | bytes 4000000 | tf_op jit(solution)/shard_map/solve_inner/pallas_call | solution.py:812
  42.7 1.6 %collective-permute-done.8.refs_1_ = f32[128,640]{1,0:T(8,128)S(1)} collective-permute-done((f32[128,640]{1,0:T(8,128)S(1)}, f32[128,640]{1,0:T(8,128)S(1)}, u32[]{:S(2)}, u32[]{:S(2)}) %collective-permute-start.8) | collective-permute-done | bytes 327712 | tf_op jit(solution)/shard_map/ppermute | solution.py:836
  44.3 5.8 %collective-permute-done.9.refs_2_ = f32[128,640]{1,0:T(8,128)S(1)} collective-permute-done((f32[128,640]{1,0:T(8,128)S(1)}, f32[128,640]{1,0:T(8,128)S(1)}, u32[]{:S(2)}, u32[]{:S(2)}) %collective-permute-start.9) | collective-permute-done | bytes 327712 | tf_op jit(solution)/shard_map/ppermute | solution.py:836
  50.1 1.6 %solve_outer.5 = (f32[128,640]{1,0:T(8,128)S(1)}, bf16[4,512,640]{2,1,0:T(8,128)(2,1)S(1)}, f32[64,640]{1,0:T(8,128)S(1)}, f32[64,640]{1,0:T(8,128)S(1)}) custom-call(f32[512,640]{1,0:T(8,128)S(1)} %get-tuple-element.81.refs_0_, f32[128,640]{1,0:T(8,128)S(1)} %collective-permute-done.8.refs_1_, f32[128,640]{1,0:T(8,128)S(1)} %collective-permute-done.9.refs_2_, ...), custom_call_target="tpu_custom_call" | custom-call | bytes 4000000 | tf_op jit(solution)/shard_map/solve_outer/pallas_call | solution.py:812
  51.7 0.5 collective-permute-start.11
  52.2 3.3 %step1_inner.1 = (f32[384,512]{1,0:T(8,128)S(1)}, f32[512,512]{1,0:T(8,128)S(1)}) custom-call(bf16[4,512,640]{2,1,0:T(8,128)(2,1)S(1)} %get-tuple-element.90.refs_0_, f32[384,640]{1,0:T(8,128)S(1)} %get-tuple-element.91.refs_1_.refs_2_, f32[384,640]{1,0:T(8,128)S(1)} %get-tuple-element.91.refs_1_.refs_2_, ...), custom_call_target="tpu_custom_call" | custom-call | bytes 4000000 | tf_op jit(solution)/shard_map/step1_inner/pallas_call | solution.py:812
  55.6 4.3 %collective-permute-done.11.refs_3_ = f32[64,640]{1,0:T(8,128)S(1)} collective-permute-done((f32[64,640]{1,0:T(8,128)S(1)}, f32[64,640]{1,0:T(8,128)S(1)}, u32[]{:S(2)}, u32[]{:S(2)}) %collective-permute-start.11) | collective-permute-done | bytes 163872 | tf_op jit(solution)/shard_map/ppermute | solution.py:836
  59.9 1.2 %step1_outer.1 = (f32[128,512]{1,0:T(8,128)S(1)}, f32[512,512]{1,0:T(8,128)S(1)}, f32[16,512]{1,0:T(8,128)S(1)}, f32[16,512]{1,0:T(8,128)S(1)}, f32[64,512]{1,0:T(8,128)S(1)}) custom-call(f32[64,640]{1,0:T(8,128)S(1)} %get-tuple-element.85.refs_0_, f32[64,640]{1,0:T(8,128)S(1)} %collective-permute-done.10.refs_1_, f32[64,640]{1,0:T(8,128)S(1)} %get-tuple-element.86.refs_2_, ...), custom_call_target="tpu_custom_call" | custom-call | bytes 4000000 | tf_op jit(solution)/shard_map/step1_outer/pallas_call | solution.py:812
  61.1 0.5 collective-permute-start.12
  61.7 0.4 diagonal.1.scale
  62.1 0.5 collective-permute-done.12.below
  62.6 5.6 %collective-permute-done.13.above = f32[16,512]{1,0:T(8,128)S(1)} collective-permute-done((f32[16,512]{1,0:T(8,128)S(1)}, f32[16,512]{1,0:T(8,128)S(1)}, u32[]{:S(2)}, u32[]{:S(2)}) %collective-permute-start.13) | collective-permute-done | bytes 32800 | tf_op jit(solution)/shard_map/ppermute | solution.py:836
  68.2 0.7 coarse_outer.1
  69.0 0.5 collective-permute-start.15
  69.5 0.9 coarse_inner.1
  70.4 2.1 %solve_inner.6 = (f32[384,512]{1,0:T(8,128)S(1)}, f32[1024,512]{1,0:T(8,128)S(1)}) custom-call(f32[256,512]{1,0:T(8,128)S(1)} %get-tuple-element.97.refs_0_, f32[256,512]{1,0:T(8,128)S(1)} %get-tuple-element.103.refs_1_, bf16[4,256,480]{2,1,0:T(8,128)(2,1)S(1)} %copy-done), custom_call_target="tpu_custom_call" | custom-call | bytes 4000000 | tf_op jit(solution)/shard_map/solve_inner/pallas_call | solution.py:812
  72.4 5.7 %collective-permute-done.15.refs_2_ = f32[128,512]{1,0:T(8,128)S(1)} collective-permute-done((f32[128,512]{1,0:T(8,128)S(1)}, f32[128,512]{1,0:T(8,128)S(1)}, u32[]{:S(2)}, u32[]{:S(2)}) %collective-permute-start.15) | collective-permute-done | bytes 262176 | tf_op jit(solution)/shard_map/ppermute | solution.py:836
  78.2 1.4 %solve_outer.6 = (f32[128,512]{1,0:T(8,128)S(1)}, bf16[4,512,512]{2,1,0:T(8,128)(2,1)S(1)}, f32[64,512]{1,0:T(8,128)S(1)}, f32[64,512]{1,0:T(8,128)S(1)}) custom-call(f32[256,512]{1,0:T(8,128)S(1)} %get-tuple-element.97.refs_0_, f32[128,512]{1,0:T(8,128)S(1)} %collective-permute-done.14.refs_1_, f32[128,512]{1,0:T(8,128)S(1)} %collective-permute-done.15.refs_2_, ...), custom_call_target="tpu_custom_call" | custom-call | bytes 4000000 | tf_op jit(solution)/shard_map/solve_outer/pallas_call | solution.py:812
  79.7 0.5 collective-permute-start.17
  80.2 3.2 %step2_inner.1 = (f32[384,512]{1,0:T(8,128)S(1)}, f32[384,512]{1,0:T(8,128)S(1)}, f32[512,512]{1,0:T(8,128)S(1)}) custom-call(bf16[4,512,512]{2,1,0:T(8,128)(2,1)S(1)} %get-tuple-element.110.refs_0_, f32[384,512]{1,0:T(8,128)S(1)} %get-tuple-element.111.refs_1_, f32[24,640]{1,0:T(8,128)S(1)} %get-tuple-element.79.refs_1_.refs_7_.refs_3_.refs_9_.coef.refs_2_.refs_8_, ...), custom_call_target="tpu_custom_call" | custom-call | bytes 4000000 | tf_op jit(solution)/shard_map/step2_inner/pallas_call | solution.py:812
  83.4 4.1 %collective-permute-done.17.refs_3_ = f32[64,512]{1,0:T(8,128)S(1)} collective-permute-done((f32[64,512]{1,0:T(8,128)S(1)}, f32[64,512]{1,0:T(8,128)S(1)}, u32[]{:S(2)}, u32[]{:S(2)}) %collective-permute-start.17) | collective-permute-done | bytes 131104 | tf_op jit(solution)/shard_map/ppermute | solution.py:836
  87.5 0.8 step2_outer.1
  88.3 0.8 collective-permute-start.18
  89.1 1.9 %solve_inner.7 = (f32[384,384]{1,0:T(8,128)S(1)}, f32[1024,384]{1,0:T(8,128)S(1)}) custom-call(f32[512,512]{1,0:T(8,128)S(1)} %get-tuple-element.113.refs_0_, bf16[4,256,480]{2,1,0:T(8,128)(2,1)S(1)} %copy-done), custom_call_target="tpu_custom_call" | custom-call | bytes 4000000 | tf_op jit(solution)/shard_map/solve_inner/pallas_call | solution.py:812
  91.0 1.4 %collective-permute-done.18.refs_1_ = f32[128,512]{1,0:T(8,128)S(1)} collective-permute-done((f32[128,512]{1,0:T(8,128)S(1)}, f32[128,512]{1,0:T(8,128)S(1)}, u32[]{:S(2)}, u32[]{:S(2)}) %collective-permute-start.18) | collective-permute-done | bytes 262176 | tf_op jit(solution)/shard_map/ppermute | solution.py:836
  92.4 5.8 %collective-permute-done.19.refs_2_ = f32[128,512]{1,0:T(8,128)S(1)} collective-permute-done((f32[128,512]{1,0:T(8,128)S(1)}, f32[128,512]{1,0:T(8,128)S(1)}, u32[]{:S(2)}, u32[]{:S(2)}) %collective-permute-start.19) | collective-permute-done | bytes 262176 | tf_op jit(solution)/shard_map/ppermute | solution.py:836
  98.2 1.1 solve_outer.7
  99.4 0.5 collective-permute-start.21
  99.9 2.8 %step3_inner.1 = (f32[384,384]{1,0:T(8,128)S(1)}, f32[512,384]{1,0:T(8,128)S(1)}) custom-call(bf16[4,512,384]{2,1,0:T(8,128)(2,1)S(1)} %get-tuple-element.123.refs_0_, f32[384,512]{1,0:T(8,128)S(1)} %get-tuple-element.124.refs_1_, f32[384,512]{1,0:T(8,128)S(1)} %get-tuple-element.125.refs_2_, ...), custom_call_target="tpu_custom_call" | custom-call | bytes 4000000 | tf_op jit(solution)/shard_map/step3_inner/pallas_call | solution.py:812
  102.7 4.2 %collective-permute-done.21.refs_3_ = f32[64,384]{1,0:T(8,128)S(1)} collective-permute-done((f32[64,384]{1,0:T(8,128)S(1)}, f32[64,384]{1,0:T(8,128)S(1)}, u32[]{:S(2)}, u32[]{:S(2)}) %collective-permute-start.21) | collective-permute-done | bytes 98336 | tf_op jit(solution)/shard_map/ppermute | solution.py:836
  106.8 0.6 step3_outer.1
  107.5 0.6 collective-permute-start.22
  108.1 2.0 %finish_inner.1 = (f32[512,256]{1,0:T(8,128)}, f32[384,256]{1,0:T(8,128)S(1)}) custom-call(s32[1]{0:T(128)} %dynamic_slice.6.rot, f32[512,384]{1,0:T(8,128)S(1)} %get-tuple-element.127.local, f32[384,384]{1,0:T(8,128)S(1)} %get-tuple-element.128.total_inner, f32[128,384]{1,0:T(8,128)S(1)} %get-tuple-element.129.total_outer), custom_call_target="tpu_custom_call" | custom-call | bytes 4000000 | tf_op jit(solution)/shard_map/finish_inner/pallas_call | solution.py:812
  110.1 5.4 %collective-permute-done.23.above = f32[64,384]{1,0:T(8,128)S(1)} collective-permute-done((f32[64,384]{1,0:T(8,128)S(1)}, f32[64,384]{1,0:T(8,128)S(1)}, u32[]{:S(2)}, u32[]{:S(2)}) %collective-permute-start.23) | collective-permute-done | bytes 98336 | tf_op jit(solution)/shard_map/ppermute | solution.py:836
  115.4 1.7 %finish_outer.1 = f32[512,256]{1,0:T(8,128)} custom-call(s32[1]{0:T(128)} %dynamic_slice.6.rot, f32[512,384]{1,0:T(8,128)S(1)} %get-tuple-element.127.local, f32[64,384]{1,0:T(8,128)S(1)} %collective-permute-done.22.below, f32[64,384]{1,0:T(8,128)S(1)} %collective-permute-done.23.above, f32[384,256]{1,0:T(8,128)S(1)} %get-tuple-element.133.inner), custom_call_target="tpu_custom_call" | custom-call | bytes 4000000 | tf_op jit(solution)/shard_map/finish_outer/pallas_call | solution.py:812
  (53 shorter events, 1.0 us)
Async XLA Ops:
  1.6 11.1 %collective-permute-start.1 = (f32[256,256]{1,0:T(8,128)S(1)}, f32[256,256]{1,0:T(8,128)S(1)}, u32[]{:S(2)}, u32[]{:S(2)}) collective-permute-start(f32[256,256]{1,0:T(8,128)S(1)} %pad_maximum_fusion.own), channel_id=1, source_target_pairs={{0,3},{1,0},{2,1},{3,2},{4,7},{5,4},{6,5},{7,6},{8,11},{9,8},{10,9... | collective-permute-start | bytes 786440 | tf_op jit(solution)/shard_map/ppermute | solution.py:836
  5.5 8.1 %collective-permute-start = (f32[256,256]{1,0:T(8,128)S(1)}, f32[256,256]{1,0:T(8,128)S(1)}, u32[]{:S(2)}, u32[]{:S(2)}) collective-permute-start(f32[256,256]{1,0:T(8,128)S(1)} %pad_maximum_fusion.own), channel_id=1, source_target_pairs={{0,1},{1,2},{2,3},{3,0},{4,5},{5,6},{6,7},{7,4},{8,9},{9,10},{10,1... | collective-permute-start | bytes 786440 | tf_op jit(solution)/shard_map/ppermute | solution.py:836
  9.6 1.0 copy-start.8
  10.7 0.9 copy-start.10
  13.6 6.3 %collective-permute-start.5 = (f32[256,256]{1,0:T(8,128)S(1)}, f32[256,256]{1,0:T(8,128)S(1)}, u32[]{:S(2)}, u32[]{:S(2)}) collective-permute-start(f32[256,256]{1,0:T(8,128)S(1)} %follow.1.own), channel_id=1, source_target_pairs={{0,3},{1,0},{2,1},{3,2},{4,7},{5,4},{6,5},{7,6},{8,11},{9,8},{10,9... | collective-permute-start | bytes 786440 | tf_op jit(solution)/shard_map/ppermute | solution.py:836
  15.5 7.5 %collective-permute-start.4 = (f32[256,256]{1,0:T(8,128)S(1)}, f32[256,256]{1,0:T(8,128)S(1)}, u32[]{:S(2)}, u32[]{:S(2)}) collective-permute-start(f32[256,256]{1,0:T(8,128)S(1)} %follow.1.own), channel_id=1, source_target_pairs={{0,1},{1,2},{2,3},{3,0},{4,5},{5,6},{6,7},{7,4},{8,9},{9,10},{10,1... | collective-permute-start | bytes 786440 | tf_op jit(solution)/shard_map/ppermute | solution.py:836
  16.6 9.9 %collective-permute-start.2 = (f32[136,640]{1,0:T(8,128)S(1)}, f32[136,640]{1,0:T(8,128)S(1)}, u32[]{:S(2)}, u32[]{:S(2)}) collective-permute-start(f32[136,640]{1,0:T(8,128)S(1)} %get-tuple-element.69), channel_id=1, source_target_pairs={{0,4},{4,8},{8,12},{12,16},{16,20},{20,24},{24,28},{28,32},{32,36}... | collective-permute-start | bytes 1044488 | tf_op jit(solution)/shard_map/ppermute | solution.py:836
  18.5 5.6 %copy-start = (bf16[4,256,480]{2,1,0:T(8,128)(2,1)S(1)}, bf16[4,256,480]{2,1,0:T(8,128)(2,1)}, u32[]{:S(2)}) copy-start(bf16[4,256,480]{2,1,0:T(8,128)(2,1)} %constant.51.clone.refs_2_.refs_1_) | copy-start | bytes 2949124
  18.5 10.0 %collective-permute-start.3 = (f32[136,640]{1,0:T(8,128)S(1)}, f32[136,640]{1,0:T(8,128)S(1)}, u32[]{:S(2)}, u32[]{:S(2)}) collective-permute-start(f32[136,640]{1,0:T(8,128)S(1)} %get-tuple-element.70), channel_id=1, source_target_pairs={{0,124},{4,0},{8,4},{12,8},{16,12},{20,16},{24,20},{28,24},{32,28}... | collective-permute-start | bytes 1044488 | tf_op jit(solution)/shard_map/ppermute | solution.py:836
  24.1 4.5 %copy-start.2 = (bf16[4,256,240]{2,1,0:T(8,128)(2,1)S(1)}, bf16[4,256,240]{2,1,0:T(8,128)(2,1)}, u32[]{:S(2)}) copy-start(bf16[4,256,240]{2,1,0:T(8,128)(2,1)} %constant.52.clone.refs_5_) | copy-start | bytes 1474564
  24.1 4.4 %copy-start.7 = (bf16[4,32,512]{2,1,0:T(8,128)(2,1)S(1)}, bf16[4,32,512]{2,1,0:T(8,128)(2,1)}, u32[]{:S(2)}) copy-start(bf16[4,32,512]{2,1,0:T(8,128)(2,1)} %constant.53.clone.refs_6_) | copy-start | bytes 393220
  24.1 4.4 %copy-start.9 = (bf16[4,32,256]{2,1,0:T(8,128)(2,1)S(1)}, bf16[4,32,256]{2,1,0:T(8,128)(2,1)}, u32[]{:S(2)}) copy-start(bf16[4,32,256]{2,1,0:T(8,128)(2,1)} %constant.54.clone.refs_7_) | copy-start | bytes 196612
  28.5 2.4 %copy-start.1 = (bf16[4,320,288]{2,1,0:T(8,128)(2,1)S(1)}, bf16[4,320,288]{2,1,0:T(8,128)(2,1)}, u32[]{:S(2)}) copy-start(bf16[4,320,288]{2,1,0:T(8,128)(2,1)} %constant.57.clone.refs_2_.refs_4_.refs_3_) | copy-start | bytes 2211844
  28.6 2.4 %copy-start.3 = (bf16[4,96,512]{2,1,0:T(8,128)(2,1)S(1)}, bf16[4,96,512]{2,1,0:T(8,128)(2,1)}, u32[]{:S(2)}) copy-start(bf16[4,96,512]{2,1,0:T(8,128)(2,1)} %constant.55.clone.refs_3_.refs_5_.refs_4_) | copy-start | bytes 1179652
  28.6 2.4 %copy-start.5 = (bf16[4,96,256]{2,1,0:T(8,128)(2,1)S(1)}, bf16[4,96,256]{2,1,0:T(8,128)(2,1)}, u32[]{:S(2)}) copy-start(bf16[4,96,256]{2,1,0:T(8,128)(2,1)} %constant.56.clone.refs_4_.refs_6_.refs_5_) | copy-start | bytes 589828
  30.3 4.2 %collective-permute-start.6 = (f32[64,640]{1,0:T(8,128)S(1)}, f32[64,640]{1,0:T(8,128)S(1)}, u32[]{:S(2)}, u32[]{:S(2)}) collective-permute-start(f32[64,640]{1,0:T(8,128)S(1)} %get-tuple-element.74.refs_0_), channel_id=1, source_target_pairs={{0,4},{4,8},{8,12},{12,16},{16,20},{20,24},{24,28},{28,32},{32,36}... | collective-permute-start | bytes 491528 | tf_op jit(solution)/shard_map/ppermute | solution.py:836
  30.7 8.1 %collective-permute-start.7 = (f32[64,640]{1,0:T(8,128)S(1)}, f32[64,640]{1,0:T(8,128)S(1)}, u32[]{:S(2)}, u32[]{:S(2)}) collective-permute-start(f32[64,640]{1,0:T(8,128)S(1)} %get-tuple-element.75.refs_2_), channel_id=1, source_target_pairs={{0,124},{4,0},{8,4},{12,8},{16,12},{20,16},{24,20},{28,24},{32,28}... | collective-permute-start | bytes 491528 | tf_op jit(solution)/shard_map/ppermute | solution.py:836
  31.0 7.7 %copy-start.6 = (bf16[4,192,96]{2,1,0:T(8,128)(2,1)S(1)}, bf16[4,192,96]{2,1,0:T(8,128)(2,1)}, u32[]{:S(2)}) copy-start(bf16[4,192,96]{2,1,0:T(8,128)(2,1)} %constant.58.clone.refs_8_.refs_10_.refs_9_) | copy-start | bytes 442372
  39.6 4.7 %collective-permute-start.8 = (f32[128,640]{1,0:T(8,128)S(1)}, f32[128,640]{1,0:T(8,128)S(1)}, u32[]{:S(2)}, u32[]{:S(2)}) collective-permute-start(f32[128,640]{1,0:T(8,128)S(1)} %get-tuple-element.82), channel_id=1, source_target_pairs={{0,4},{4,8},{8,12},{12,16},{16,20},{20,24},{24,28},{28,32},{32,36}... | collective-permute-start | bytes 983048 | tf_op jit(solution)/shard_map/ppermute | solution.py:836
  40.2 9.8 %collective-permute-start.9 = (f32[128,640]{1,0:T(8,128)S(1)}, f32[128,640]{1,0:T(8,128)S(1)}, u32[]{:S(2)}, u32[]{:S(2)}) collective-permute-start(f32[128,640]{1,0:T(8,128)S(1)} %get-tuple-element.83), channel_id=1, source_target_pairs={{0,124},{4,0},{8,4},{12,8},{16,12},{20,16},{24,20},{28,24},{32,28}... | collective-permute-start | bytes 983048 | tf_op jit(solution)/shard_map/ppermute | solution.py:836
  51.7 4.0 %collective-permute-start.10 = (f32[64,640]{1,0:T(8,128)S(1)}, f32[64,640]{1,0:T(8,128)S(1)}, u32[]{:S(2)}, u32[]{:S(2)}) collective-permute-start(f32[64,640]{1,0:T(8,128)S(1)} %get-tuple-element.85.refs_0_), channel_id=1, source_target_pairs={{0,4},{4,8},{8,12},{12,16},{16,20},{20,24},{24,28},{28,32},{32,36}... | collective-permute-start | bytes 491528 | tf_op jit(solution)/shard_map/ppermute | solution.py:836
  51.7 8.1 %collective-permute-start.11 = (f32[64,640]{1,0:T(8,128)S(1)}, f32[64,640]{1,0:T(8,128)S(1)}, u32[]{:S(2)}, u32[]{:S(2)}) collective-permute-start(f32[64,640]{1,0:T(8,128)S(1)} %get-tuple-element.86.refs_2_), channel_id=1, source_target_pairs={{0,124},{4,0},{8,4},{12,8},{16,12},{20,16},{24,20},{28,24},{32,28}... | collective-permute-start | bytes 491528 | tf_op jit(solution)/shard_map/ppermute | solution.py:836
  52.2 7.6 %copy-start.11 = (bf16[64,1024]{1,0:T(8,128)(2,1)S(1)}, bf16[64,1024]{1,0:T(8,128)(2,1)}, u32[]{:S(2)}) copy-start(bf16[64,1024]{1,0:T(8,128)(2,1)} %constant.59.clone.refs_11_) | copy-start | bytes 393220
  52.2 7.6 %copy-start.12 = (bf16[64,512]{1,0:T(8,128)(2,1)S(1)}, bf16[64,512]{1,0:T(8,128)(2,1)}, u32[]{:S(2)}) copy-start(bf16[64,512]{1,0:T(8,128)(2,1)} %constant.60.clone.refs_12_) | copy-start | bytes 196612
  55.6 6.0 %copy-start.13 = (f32[64,8]{1,0:T(8,128)S(1)}, f32[64,8]{1,0:T(8,128)}, u32[]{:S(2)}) copy-start(f32[64,8]{1,0:T(8,128)} %constant.63.clone.table) | copy-start | bytes 6148
  59.9 8.4 %copy-start.4 = (bf16[2048,192]{1,0:T(8,128)(2,1)S(1)}, bf16[2048,192]{1,0:T(8,128)(2,1)}, u32[]{:S(2)}) copy-start(bf16[2048,192]{1,0:T(8,128)(2,1)} %constant.61.clone.prolong) | copy-start | bytes 2359300
  61.1 1.5 %collective-permute-start.12 = (f32[16,512]{1,0:T(8,128)S(1)}, f32[16,512]{1,0:T(8,128)S(1)}, u32[]{:S(2)}, u32[]{:S(2)}) collective-permute-start(f32[16,512]{1,0:T(8,128)S(1)} %get-tuple-element.94), channel_id=1, source_target_pairs={{0,4},{4,8},{8,12},{12,16},{16,20},{20,24},{24,28},{28,32},{32,36}... | collective-permute-start | bytes 98312 | tf_op jit(solution)/shard_map/ppermute | solution.py:836
  61.6 6.7 %collective-permute-start.13 = (f32[16,512]{1,0:T(8,128)S(1)}, f32[16,512]{1,0:T(8,128)S(1)}, u32[]{:S(2)}, u32[]{:S(2)}) collective-permute-start(f32[16,512]{1,0:T(8,128)S(1)} %get-tuple-element.95), channel_id=1, source_target_pairs={{0,124},{4,0},{8,4},{12,8},{16,12},{20,16},{24,20},{28,24},{32,28}... | collective-permute-start | bytes 98312 | tf_op jit(solution)/shard_map/ppermute | solution.py:836
  68.9 3.5 %collective-permute-start.14 = (f32[128,512]{1,0:T(8,128)S(1)}, f32[128,512]{1,0:T(8,128)S(1)}, u32[]{:S(2)}, u32[]{:S(2)}) collective-permute-start(f32[128,512]{1,0:T(8,128)S(1)} %get-tuple-element.98), channel_id=1, source_target_pairs={{0,4},{4,8},{8,12},{12,16},{16,20},{20,24},{24,28},{28,32},{32,36}... | collective-permute-start | bytes 786440 | tf_op jit(solution)/shard_map/ppermute | solution.py:836
  69.0 9.2 %collective-permute-start.15 = (f32[128,512]{1,0:T(8,128)S(1)}, f32[128,512]{1,0:T(8,128)S(1)}, u32[]{:S(2)}, u32[]{:S(2)}) collective-permute-start(f32[128,512]{1,0:T(8,128)S(1)} %get-tuple-element.99), channel_id=1, source_target_pairs={{0,124},{4,0},{8,4},{12,8},{16,12},{20,16},{24,20},{28,24},{32,28}... | collective-permute-start | bytes 786440 | tf_op jit(solution)/shard_map/ppermute | solution.py:836
  79.6 3.8 %collective-permute-start.16 = (f32[64,512]{1,0:T(8,128)S(1)}, f32[64,512]{1,0:T(8,128)S(1)}, u32[]{:S(2)}, u32[]{:S(2)}) collective-permute-start(f32[64,512]{1,0:T(8,128)S(1)} %get-tuple-element.105.refs_0_), channel_id=1, source_target_pairs={{0,4},{4,8},{8,12},{12,16},{16,20},{20,24},{24,28},{28,32},{32,36}... | collective-permute-start | bytes 393224 | tf_op jit(solution)/shard_map/ppermute | solution.py:836
  79.7 7.8 %collective-permute-start.17 = (f32[64,512]{1,0:T(8,128)S(1)}, f32[64,512]{1,0:T(8,128)S(1)}, u32[]{:S(2)}, u32[]{:S(2)}) collective-permute-start(f32[64,512]{1,0:T(8,128)S(1)} %get-tuple-element.106.refs_2_), channel_id=1, source_target_pairs={{0,124},{4,0},{8,4},{12,8},{16,12},{20,16},{24,20},{28,24},{32,28}... | collective-permute-start | bytes 393224 | tf_op jit(solution)/shard_map/ppermute | solution.py:836
  88.3 4.2 %collective-permute-start.18 = (f32[128,512]{1,0:T(8,128)S(1)}, f32[128,512]{1,0:T(8,128)S(1)}, u32[]{:S(2)}, u32[]{:S(2)}) collective-permute-start(f32[128,512]{1,0:T(8,128)S(1)} %get-tuple-element.114), channel_id=1, source_target_pairs={{0,4},{4,8},{8,12},{12,16},{16,20},{20,24},{24,28},{28,32},{32,36}... | collective-permute-start | bytes 786440 | tf_op jit(solution)/shard_map/ppermute | solution.py:836
  89.1 9.1 %collective-permute-start.19 = (f32[128,512]{1,0:T(8,128)S(1)}, f32[128,512]{1,0:T(8,128)S(1)}, u32[]{:S(2)}, u32[]{:S(2)}) collective-permute-start(f32[128,512]{1,0:T(8,128)S(1)} %get-tuple-element.115), channel_id=1, source_target_pairs={{0,124},{4,0},{8,4},{12,8},{16,12},{20,16},{24,20},{28,24},{32,28}... | collective-permute-start | bytes 786440 | tf_op jit(solution)/shard_map/ppermute | solution.py:836
  99.3 3.3 %collective-permute-start.20 = (f32[64,384]{1,0:T(8,128)S(1)}, f32[64,384]{1,0:T(8,128)S(1)}, u32[]{:S(2)}, u32[]{:S(2)}) collective-permute-start(f32[64,384]{1,0:T(8,128)S(1)} %get-tuple-element.117.refs_0_), channel_id=1, source_target_pairs={{0,4},{4,8},{8,12},{12,16},{16,20},{20,24},{24,28},{28,32},{32,36}... | collective-permute-start | bytes 294920 | tf_op jit(solution)/shard_map/ppermute | solution.py:836
  99.4 7.4 %collective-permute-start.21 = (f32[64,384]{1,0:T(8,128)S(1)}, f32[64,384]{1,0:T(8,128)S(1)}, u32[]{:S(2)}, u32[]{:S(2)}) collective-permute-start(f32[64,384]{1,0:T(8,128)S(1)} %get-tuple-element.118.refs_2_), channel_id=1, source_target_pairs={{0,124},{4,0},{8,4},{12,8},{16,12},{20,16},{24,20},{28,24},{32,28}... | collective-permute-start | bytes 294920 | tf_op jit(solution)/shard_map/ppermute | solution.py:836
  107.5 2.6 %collective-permute-start.22 = (f32[64,384]{1,0:T(8,128)S(1)}, f32[64,384]{1,0:T(8,128)S(1)}, u32[]{:S(2)}, u32[]{:S(2)}) collective-permute-start(f32[64,384]{1,0:T(8,128)S(1)} %get-tuple-element.131), channel_id=1, source_target_pairs={{0,4},{4,8},{8,12},{12,16},{16,20},{20,24},{24,28},{28,32},{32,36}... | collective-permute-start | bytes 294920 | tf_op jit(solution)/shard_map/ppermute | solution.py:836
  108.1 7.4 %collective-permute-start.23 = (f32[64,384]{1,0:T(8,128)S(1)}, f32[64,384]{1,0:T(8,128)S(1)}, u32[]{:S(2)}, u32[]{:S(2)}) collective-permute-start(f32[64,384]{1,0:T(8,128)S(1)} %get-tuple-element.132), channel_id=1, source_target_pairs={{0,124},{4,0},{8,4},{12,8},{16,12},{20,16},{24,20},{28,24},{32,28}... | collective-permute-start | bytes 294920 | tf_op jit(solution)/shard_map/ppermute | solution.py:836

commit v6 on v5

--- a/solution.py
+++ b/solution.py
@@ -248,6 +248,17 @@
     return jnp.dot(left, right, preferred_element_type=jnp.float32)
 
 
+def sided(rot, off, near):
+    odd = rot[1] == 1
+    return jnp.where(odd, near, off), jnp.where(odd, off, near)
+
+
+def send(rot, off, near, up, down):
+    odd = rot[1] == 1
+    off[...] = jnp.where(odd, up, down)
+    near[...] = jnp.where(odd, down, up)
+
+
 def join(tiles):
     return jnp.concatenate(tiles, axis=1)
 
@@ -449,11 +460,8 @@
                 value = window(case, left, own[here], right, here)
                 field[here] = value * plane_factor(factor, i)
 
-    up[0:128] = field[128:256]
-    down[0:128] = field[0:128]
     length = jnp.broadcast_to(geo[2:3], (PTS, LANES))
-    up[128:136] = length
-    down[128:136] = length
+    send(rot, up, down, jnp.concatenate([field[128:256], length]), jnp.concatenate([field[0:128], length]))
 
 
 def follow_kernel(left, right, own, inner):
@@ -536,8 +544,10 @@
 
 
 def solve_outer_kernel(start_up, wide, tiles, *refs):
-    field, below, above, spectrum, lam, fwd, bwd, bwd_low = refs[:8]
-    share, modes, up, down, ext, parts, packed = refs[8:]
+    rot, field, off, near, spectrum, lam, fwd, bwd, bwd_low = refs[:9]
+    share, modes, up, down, to_off, to_near, ext, parts, packed = refs[9:]
+    below, above = sided(rot, off[0:128], near[0:128])
+    odd = rot[1] == 1
     lanes = tiles * TILE
     factor = point_factor(lanes)
     last = 192 if start_up else 448
@@ -568,8 +578,13 @@
     for k in range(4):
         classes = (load(parts, block(0, k), tiles, c * tiles) for c in range(4))
         values = unfold(*classes)
-        for (p, q), value in zip(mirrored(0, k), values):
-            (down if p == 0 else up)[block(0, q)] = value * factor
+        first, last, first_mirror, last_mirror = (value * factor for value in values)
+        for q, low, high in ((k, first, last), (PTS - 1 - k, first_mirror, last_mirror)):
+            here = block(0, q)
+            down[here] = low
+            up[here] = high
+            to_off[here] = jnp.where(odd, high, low)
+            to_near[here] = jnp.where(odd, low, high)
 
 
 def back(modes, bwd, bwd_low, parts, tiles, rows, rolled):
@@ -635,7 +650,8 @@
 
 def step_outer_kernel(kind, wide, tiles, *refs):
     take = iter(refs)
-    last, below, first, above = (next(take) for _ in range(4))
+    rot, last, below, first, above = (next(take) for _ in range(5))
+    below, above = sided(rot, below[...], above[...])
     before = next(take) if kind in (1, 3) else None
     total = next(take) if kind != 0 else None
     share_inner, share_outer, image, coef, app = (next(take) for _ in range(5))
@@ -647,8 +663,8 @@
     ext, parts, packed = next(take), next(take), next(take)
     split_field = next(take) if kind == 1 else None
     lanes = tiles * TILE
-    store(ext, slice(0, 64), first[...] + below[...])
-    store(ext, slice(64, 128), last[...] + above[...])
+    store(ext, slice(0, 64), first[...] + below)
+    store(ext, slice(64, 128), last[...] + above)
     assemble_sides(ext, range(2), wide)
     for at in range(2):
         here = slice(at * 64, at * 64 + 64)
@@ -685,14 +701,11 @@
         for start, stop in chunks(lanes):
             value = dot(res[...], split_field[:, start:stop])
             coarse[:, start:stop] = value + dot(res_low[...], split_field[0:512, start:stop])
-        up[...] = coarse[48:64]
-        down[...] = coarse[0:16]
+        send(rot, up, down, coarse[48:64], coarse[0:16])
     elif kind == 3:
-        up[...] = field[448:512]
-        down[...] = field[0:64]
+        send(rot, up, down, field[448:512], field[0:64])
     else:
-        up[...] = field[384:512]
-        down[...] = field[0:128]
+        send(rot, up, down, field[384:512], field[0:128])
 
 
 def assemble_coarse(value):
@@ -711,7 +724,7 @@
     return value + jnp.where(last, over, 0.0) + jnp.where(first, under, 0.0)
 
 
-def diagonal_kernel(lower, upper, geo, table, scale):
+def diagonal_kernel(rot, lower, upper, geo, table, scale):
     lanes = scale.shape[1]
     la, lb = geo[0:1, :lanes], geo[1:2, :lanes]
 
@@ -723,15 +736,17 @@
         )
 
     value = local(geo[2:3, :lanes], slice(0, 64))
-    first = value[0:16] + local(lower[128:129, :lanes], slice(48, 64))
-    last = value[48:64] + local(upper[128:129, :lanes], slice(0, 16))
+    lz_below, lz_above = sided(rot, lower[128:129, :lanes], upper[128:129, :lanes])
+    first = value[0:16] + local(lz_below, slice(48, 64))
+    last = value[48:64] + local(lz_above, slice(0, 16))
     scale[...] = assemble_coarse(jnp.concatenate([first, value[16:48], last]))
 
 
-def coarse_outer_kernel(local, below, above, scale, coef, prolong, field, out, pack, up, down):
+def coarse_outer_kernel(rot, local, below, above, scale, coef, prolong, field, out, pack, up, down):
     lanes = local.shape[1]
     value = local[...]
-    value = jnp.concatenate([value[0:16] + below[...], value[16:48], value[48:64] + above[...]])
+    below, above = sided(rot, below[...], above[...])
+    value = jnp.concatenate([value[0:16] + below, value[16:48], value[48:64] + above])
     value = assemble_coarse(value) / scale[...]
     high, low = halves(value)
     pack[0, 0:64] = high
@@ -739,8 +754,7 @@
     pack[0, 128:192] = high
     for at, i in enumerate((0, 1, 6, 7)):
         correct(i, slice(at * 64, at * 64 + 64), coef, prolong, pack, field, out)
-    up[...] = out[128:256]
-    down[...] = out[0:128]
+    send(rot, up, down, out[128:256], out[0:128])
 
 
 def coarse_inner_kernel(pack, coef, prolong, total_inner, total_outer, field, sum_inner, sum_outer, out):
@@ -792,8 +806,9 @@
 
 def finish_outer_kernel(rot, local, below, above, inner, res, ext):
     tiles = local.shape[1] // TILE
-    store(ext, slice(0, 64), local[0:64] + below[...])
-    store(ext, slice(64, 128), local[448:512] + above[...])
+    below, above = sided(rot, below[...], above[...])
+    store(ext, slice(0, 64), local[0:64] + below)
+    store(ext, slice(64, 128), local[448:512] + above)
     assemble_sides(ext, range(2), tiles)
     res[64:448] = inner[...]
     for case in range(4):
@@ -835,8 +850,11 @@
     def shifted(value, axis, count, steps):
         return lax.ppermute(value, axis, [(n, (n + steps) % count) for n in range(count)])
 
-    def neighbours(up, down):
-        return shifted(up, "grp", groups, 1), shifted(down, "grp", groups, -1)
+    swap_off = [(n, (n + 1) % groups if n % 2 else (n - 1) % groups) for n in range(groups)]
+    swap_near = [(n, n - 1 if n % 2 else n + 1) for n in range(groups)]
+
+    def neighbours(off, near):
+        return lax.ppermute(off, "grp", swap_off), lax.ppermute(near, "grp", swap_near)
 
     def beside(value):
         return shifted(value, "sub", members, 1), shifted(value, "sub", members, -1)
@@ -847,7 +865,7 @@
     own = rhs.reshape(512, OWN)
     ends = jnp.concatenate([own[0:128], own[384:512]])
     left, right = beside(ends)
-    rot = lax.dynamic_slice(rotation, (group,), (1,))
+    rot = jnp.concatenate([lax.dynamic_slice(rotation, (group,), (1,)), jnp.reshape(group % 2, (1,))])
     ring = jnp.concatenate([spacing_a, spacing_a, spacing_a])
     columns = lax.dynamic_slice(ring, (spacing_a.shape[0] + member * COLS_DEV - LEFT,), (WIN,))
     columns = jnp.concatenate([columns[start:stop] for start, stop in RINGS])
@@ -894,18 +912,19 @@
                 vmem((4, 3 * INNER, lanes), narrow),
             ),
         )
-        share_outer, modes, up, down = call(
+        share_outer, modes, up, down, off, near = call(
             functools.partial(solve_outer_kernel, start_up, before, tiles),
             "solve_outer",
-            (fields[0], below, above, spectrum, lam, mats["forward_outer"], *mats["backward_outer"]),
-            (*shapes(tiles, 128), (4, 2 * MODES, lanes), *shapes(tiles, 64, 64)),
+            (rot, fields[0], below, above, spectrum, lam, mats["forward_outer"], *mats["backward_outer"]),
+            (*shapes(tiles, 128), (4, 2 * MODES, lanes), *shapes(tiles, 64, 64, 64, 64)),
             (
                 vmem((before, 256, TILE), wide),
                 vmem((4 * tiles, 128, TILE), wide),
                 vmem((4, 3 * OUTER, lanes), narrow),
             ),
+            scalars=1,
         )
-        return (share_inner, share_outer), (modes, up, down), neighbours(up, down)
+        return (share_inner, share_outer), (modes, up, down), neighbours(off, near)
 
     def advance(kind, local, messages, share, before, total, width, tiles):
         lanes = tiles * TILE
@@ -936,12 +955,13 @@
             functools.partial(step_outer_kernel, kind, width, tiles),
             f"step{kind}_outer",
             (
-                *(local[1], messages[0], local[2], messages[1]),
+                *(rot, local[1], messages[0], local[2], messages[1]),
                 *(*pick(1), *share, image, coef, mats["apply_outer"]),
                 *(mats["restrict"] if kind == 1 else ()),
             ),
             shapes(tiles, *(128 for _ in kept), 512, sent, sent, *((64,) if kind == 1 else ())),
             extra,
+            scalars=1,
         )
         outer, (field, up, down, *coarse) = out[: len(kept)], out[len(kept) :]
         return list(zip(inner, outer)), field, neighbours(up, down), *coarse
@@ -950,12 +970,15 @@
     (step,), field, messages = advance(0, local, messages, share, None, None, 5, 5)
     share, local, messages = solve((field,), *messages, 5, 5)
     (total,), field, messages, coarse = advance(1, local, messages, share, step, step, 5, 4)
-    (scale,) = call(diagonal_kernel, "diagonal", (lower, upper, geo, mats["coarse"]), shapes(4, 64))
+    (scale,) = call(
+        diagonal_kernel, "diagonal", (rot, lower, upper, geo, mats["coarse"]), shapes(4, 64), scalars=1
+    )
     outer, terms, up, down = call(
         coarse_outer_kernel,
         "coarse_outer",
-        (coarse, *messages, scale, coef, mats["prolong"], field),
+        (rot, coarse, *messages, scale, coef, mats["prolong"], field),
         (*shapes(4, 256), (1, 192, 4 * TILE), *shapes(4, 128, 128)),
+        scalars=1,
     )
     messages = neighbours(up, down)
     *total, inner = call(

time: 117 us -> 121 us (1.034); the launches traced: 117 us -> 119 us
  waiting for transfers between devices: 55.5 us -> 36.4 us
  starting transfers between devices: 13.6 us -> 27.6 us
  Pallas kernels: 39.8 us -> 45.6 us
    ppermute x24 -> x4, waiting for transfers between devices: 55.5 us -> 4.73 us  [shifted(): lax.ppermute(value, axis, [(n, (n + steps) % count) for n in range(count)])]
    ppermute x0 -> x20, waiting for transfers between devices: none -> 31.7 us  [the longest x10 31.7 us: neighbours(): lax.ppermute(off, 'grp', swap_off)]
    ppermute x0 -> x20, starting transfers between devices: none -> 21.1 us  [the longest x10 20.4 us: neighbours(): lax.ppermute(off, 'grp', swap_off)]
    ppermute x24 -> x4, starting transfers between devices: 13.6 us -> 6.5 us  [shifted(): lax.ppermute(value, axis, [(n, (n + steps) % count) for n in range(count)])]
    pallas_call x25, Pallas kernels: 39.8 us -> 45.6 us  [call(): pl.pallas_call(kernel, out_shape=[jax.ShapeDtypeStruct(out, jnp.float32 i...]
  transfers between devices with their start and end apart: 24 -> 24, of which waited for: 16 -> 13; matrix products, arithmetic and copies ran while one was open for 3% -> 4% of each run, Pallas kernels for 24% -> 24%
where the time goes in v6:
time: 121 us; the launch traced here: 119 us
  Pallas kernels  45.6 us (38%)
  waiting for transfers between devices  36.4 us (30%)
  starting transfers between devices  27.6 us (23%)
  local copies, waits for them, and re-layouts  5.65 us (5%)
  other arithmetic  1.65 us (1%)
  between operations  1.6 us (1%)
    pallas_call x25, Pallas kernels, call(): pl.pallas_call(kernel, out_shape=[jax.ShapeDtypeStruct(out, jnp.float32 i...  45.6 us
    ppermute x10, waiting for transfers between devices, neighbours(): lax.ppermute(off, 'grp', swap_off)  31.7 us
    ppermute x10, starting transfers between devices, neighbours(): lax.ppermute(off, 'grp', swap_off)  20.4 us
    ppermute x4, starting transfers between devices, shifted(): lax.ppermute(value, axis, [(n, (n + steps) % count) for n in range(count)])  6.5 us
    ppermute x4, waiting for transfers between devices, shifted(): lax.ppermute(value, axis, [(n, (n + steps) % count) for n in range(count)])  4.73 us
  transfers between devices with their start and end apart: 24, of which 13 were waited for; matrix products, arithmetic and copies ran while one was open for 4% of the time, Pallas kernels for 24%

profile of v6, /device:TPU:31, one launch (start us, length us, event | category | flops | bytes accessed | tf_op | source)
XLA Modules:
  0.0 118.6 jit_solution(1037666166201693083)
XLA Ops:
  0.6 1.0 fusion
  1.6 3.8 %collective-permute-start.1 = (f32[256,256]{1,0:T(8,128)S(1)}, f32[256,256]{1,0:T(8,128)S(1)}, u32[]{:S(2)}, u32[]{:S(2)}) collective-permute-start(f32[256,256]{1,0:T(8,128)S(1)} %pad_maximum_fusion.own), channel_id=1, source_target_pairs={{0,3},{1,0},{2,1},{3,2},{4,7},{5,4},{6,5},{7,6},{8,11},{9,8},{10,9... | collective-permute-start | bytes 786440 | tf_op jit(solution)/shard_map/ppermute | solution.py:851
  5.5 0.8 pad_maximum_fusion.1
  6.3 0.1 dynamic_slice.7
  6.4 0.1 fusion.1
  6.5 1.2 %dynamic_slice.6 = s32[1]{0:T(128)} dynamic-slice(s32[32]{0:T(128)} %param.22, s32[]{:T(128)S(6)} %select_n.13), dynamic_slice_sizes={1} | dynamic-slice | bytes 12 | tf_op jit(solution)/shard_map/dynamic_slice | solution.py:868
  7.7 0.7 pad_add_fusion.rot.refs_0_
  9.2 0.1 pad.3.clone
  9.3 0.1 concatenate.18
  9.5 0.1 stack_reshape.3
  9.5 0.7 tile.2
  10.2 0.1 stack_tile.3
  10.4 1.0 copy-done.8
  11.4 0.9 copy-done.10
  12.4 1.1 tables.1
  13.5 0.1 collective-permute-done.left
  13.6 2.7 %collective-permute-start.5 = (f32[256,256]{1,0:T(8,128)S(1)}, f32[256,256]{1,0:T(8,128)S(1)}, u32[]{:S(2)}, u32[]{:S(2)}) collective-permute-start(f32[256,256]{1,0:T(8,128)S(1)} %follow.1.own), channel_id=1, source_target_pairs={{0,3},{1,0},{2,1},{3,2},{4,7},{5,4},{6,5},{7,6},{8,11},{9,8},{10,9... | collective-permute-start | bytes 786440 | tf_op jit(solution)/shard_map/ppermute | solution.py:851
  16.2 1.1 outer.1
  17.4 1.3 %collective-permute-start.2 = (f32[136,640]{1,0:T(8,128)S(1)}, f32[136,640]{1,0:T(8,128)S(1)}, u32[]{:S(2)}, u32[]{:S(2)}) collective-permute-start(f32[136,640]{1,0:T(8,128)S(1)} %get-tuple-element.77), channel_id=1, source_target_pairs={{0,124},{4,8},{8,4},{12,16},{16,12},{20,24},{24,20},{28,32},{32,28... | collective-permute-start | bytes 1044488 | tf_op jit(solution)/shard_map/ppermute | solution.py:857
  18.7 0.4 collective-permute-start.3
  19.1 1.5 %collective-permute-done.5.right = f32[256,256]{1,0:T(8,128)S(1)} collective-permute-done((f32[256,256]{1,0:T(8,128)S(1)}, f32[256,256]{1,0:T(8,128)S(1)}, u32[]{:S(2)}, u32[]{:S(2)}) %collective-permute-start.5) | collective-permute-done | bytes 262176 | tf_op jit(solution)/shard_map/ppermute | solution.py:851
  20.6 3.1 %collective-permute-done.4.left = f32[256,256]{1,0:T(8,128)S(1)} collective-permute-done((f32[256,256]{1,0:T(8,128)S(1)}, f32[256,256]{1,0:T(8,128)S(1)}, u32[]{:S(2)}, u32[]{:S(2)}) %collective-permute-start.4) | collective-permute-done | bytes 262176 | tf_op jit(solution)/shard_map/ppermute | solution.py:851
  23.7 1.1 inner.1.refs_1_
  24.9 2.4 %solve_inner.4 = (f32[384,640]{1,0:T(8,128)S(1)}, f32[1024,640]{1,0:T(8,128)S(1)}) custom-call(f32[256,640]{1,0:T(8,128)S(1)} %get-tuple-element.76.refs_0_.refs_1_, f32[256,640]{1,0:T(8,128)S(1)} %inner.1.refs_1_, bf16[4,256,480]{2,1,0:T(8,128)(2,1)S(1)} %copy-done), custom_call_target="tpu_custom_call" | custom-call | bytes 4000000 | tf_op jit(solution)/shard_map/solve_inner/pallas_call | solution.py:827
  27.3 0.2 collective-permute-done.2.refs_2_.lower
  27.6 2.4 %solve_outer.4 = (f32[128,640]{1,0:T(8,128)S(1)}, bf16[4,512,640]{2,1,0:T(8,128)(2,1)S(1)}, f32[64,640]{1,0:T(8,128)S(1)}, f32[64,640]{1,0:T(8,128)S(1)}, f32[64,640]{1,0:T(8,128)S(1)}, /*index=5*/f32[64,640]{1,0:T(8,128)S(1)}) custom-call(s32[2]{0:T(128)S(1)} %pad_add_fusion.rot.refs_0_, f32[256,640]{1,0:T(8,128)S(1)} %get-tuple-element.76.refs_0_.refs_1_, ...), custom_call_target="tpu_custom_call" | custom-call | bytes 4000000 | tf_op jit(solution)/shard_map/solve_outer/pallas_call | solution.py:827
  30.0 2.1 %collective-permute-start.6 = (f32[64,640]{1,0:T(8,128)S(1)}, f32[64,640]{1,0:T(8,128)S(1)}, u32[]{:S(2)}, u32[]{:S(2)}) collective-permute-start(f32[64,640]{1,0:T(8,128)S(1)} %get-tuple-element.83), channel_id=1, source_target_pairs={{0,124},{4,8},{8,4},{12,16},{16,12},{20,24},{24,20},{28,32},{32,28... | collective-permute-start | bytes 491528 | tf_op jit(solution)/shard_map/ppermute | solution.py:857
  32.1 0.4 collective-permute-start.7
  32.5 3.5 %step0_inner.1 = (f32[384,640]{1,0:T(8,128)S(1)}, f32[512,640]{1,0:T(8,128)S(1)}) custom-call(bf16[4,512,640]{2,1,0:T(8,128)(2,1)S(1)} %get-tuple-element.88.refs_0_, f32[24,640]{1,0:T(8,128)S(1)} %get-tuple-element.89.refs_1_.refs_8_.refs_3_.refs_10_.coef.refs_2_.refs_9_, bf16[4,320,288]{2,1,0:T(8,128)(2,1)S(1)} %copy-done.1, ...), custom_call_target="tpu_custom_call" | custom-call | bytes 4000000 | tf_op jit(solution)/shard_map/step0_inner/pallas_call | solution.py:827
  36.0 2.1 %collective-permute-done.6.refs_2_ = f32[64,640]{1,0:T(8,128)S(1)} collective-permute-done((f32[64,640]{1,0:T(8,128)S(1)}, f32[64,640]{1,0:T(8,128)S(1)}, u32[]{:S(2)}, u32[]{:S(2)}) %collective-permute-start.6) | collective-permute-done | bytes 163872 | tf_op jit(solution)/shard_map/ppermute | solution.py:857
  38.2 1.4 %step0_outer.1 = (f32[128,640]{1,0:T(8,128)S(1)}, f32[512,640]{1,0:T(8,128)S(1)}, f32[128,640]{1,0:T(8,128)S(1)}, f32[128,640]{1,0:T(8,128)S(1)}) custom-call(s32[2]{0:T(128)S(1)} %pad_add_fusion.rot.refs_0_, f32[64,640]{1,0:T(8,128)S(1)} %get-tuple-element.82.refs_1_, f32[64,640]{1,0:T(8,128)S(1)} %collective-permute-done.6.refs_2_, ...), custom_call_target="tpu_custom_call" | custom-call | bytes 4000000 | tf_op jit(solution)/shard_map/step0_outer/pallas_call | solution.py:827
  39.6 2.1 %collective-permute-start.8 = (f32[128,640]{1,0:T(8,128)S(1)}, f32[128,640]{1,0:T(8,128)S(1)}, u32[]{:S(2)}, u32[]{:S(2)}) collective-permute-start(f32[128,640]{1,0:T(8,128)S(1)} %get-tuple-element.92), channel_id=1, source_target_pairs={{0,124},{4,8},{8,4},{12,16},{16,12},{20,24},{24,20},{28,32},{32,28... | collective-permute-start | bytes 983048 | tf_op jit(solution)/shard_map/ppermute | solution.py:857
  41.7 2.4 %solve_inner.5 = (f32[384,640]{1,0:T(8,128)S(1)}, f32[1024,640]{1,0:T(8,128)S(1)}) custom-call(f32[512,640]{1,0:T(8,128)S(1)} %get-tuple-element.91.refs_0_.refs_1_, bf16[4,256,480]{2,1,0:T(8,128)(2,1)S(1)} %copy-done), custom_call_target="tpu_custom_call" | custom-call | bytes 4000000 | tf_op jit(solution)/shard_map/solve_inner/pallas_call | solution.py:827
  44.1 5.3 %collective-permute-done.8.refs_2_ = f32[128,640]{1,0:T(8,128)S(1)} collective-permute-done((f32[128,640]{1,0:T(8,128)S(1)}, f32[128,640]{1,0:T(8,128)S(1)}, u32[]{:S(2)}, u32[]{:S(2)}) %collective-permute-start.8) | collective-permute-done | bytes 327712 | tf_op jit(solution)/shard_map/ppermute | solution.py:857
  49.5 2.3 %solve_outer.5 = (f32[128,640]{1,0:T(8,128)S(1)}, bf16[4,512,640]{2,1,0:T(8,128)(2,1)S(1)}, f32[64,640]{1,0:T(8,128)S(1)}, f32[64,640]{1,0:T(8,128)S(1)}, f32[64,640]{1,0:T(8,128)S(1)}, /*index=5*/f32[64,640]{1,0:T(8,128)S(1)}) custom-call(s32[2]{0:T(128)S(1)} %pad_add_fusion.rot.refs_0_, f32[512,640]{1,0:T(8,128)S(1)} %get-tuple-element.91.refs_0_.refs_1_, ...), custom_call_target="tpu_custom_call" | custom-call | bytes 4000000 | tf_op jit(solution)/shard_map/solve_outer/pallas_call | solution.py:827
  51.8 2.1 %collective-permute-start.10 = (f32[64,640]{1,0:T(8,128)S(1)}, f32[64,640]{1,0:T(8,128)S(1)}, u32[]{:S(2)}, u32[]{:S(2)}) collective-permute-start(f32[64,640]{1,0:T(8,128)S(1)} %get-tuple-element.96), channel_id=1, source_target_pairs={{0,124},{4,8},{8,4},{12,16},{16,12},{20,24},{24,20},{28,32},{32,28... | collective-permute-start | bytes 491528 | tf_op jit(solution)/shard_map/ppermute | solution.py:857
  53.9 3.3 %step1_inner.1 = (f32[384,512]{1,0:T(8,128)S(1)}, f32[512,512]{1,0:T(8,128)S(1)}) custom-call(bf16[4,512,640]{2,1,0:T(8,128)(2,1)S(1)} %get-tuple-element.102.refs_0_, f32[384,640]{1,0:T(8,128)S(1)} %get-tuple-element.103.refs_1_.refs_2_, f32[384,640]{1,0:T(8,128)S(1)} %get-tuple-element.103.refs_1_.refs_2_, ...), custom_call_target="tpu_custom_call" | custom-call | bytes 4000000 | tf_op jit(solution)/shard_map/step1_inner/pallas_call | solution.py:827
  57.3 2.7 %collective-permute-done.10.refs_2_ = f32[64,640]{1,0:T(8,128)S(1)} collective-permute-done((f32[64,640]{1,0:T(8,128)S(1)}, f32[64,640]{1,0:T(8,128)S(1)}, u32[]{:S(2)}, u32[]{:S(2)}) %collective-permute-start.10) | collective-permute-done | bytes 163872 | tf_op jit(solution)/shard_map/ppermute | solution.py:857
  59.9 1.7 %step1_outer.1 = (f32[128,512]{1,0:T(8,128)S(1)}, f32[512,512]{1,0:T(8,128)S(1)}, f32[16,512]{1,0:T(8,128)S(1)}, f32[16,512]{1,0:T(8,128)S(1)}, f32[64,512]{1,0:T(8,128)S(1)}) custom-call(s32[2]{0:T(128)S(1)} %pad_add_fusion.rot.refs_0_, f32[64,640]{1,0:T(8,128)S(1)} %get-tuple-element.95.refs_1_, f32[64,640]{1,0:T(8,128)S(1)} %collective-permute-done.10.refs_2_, ...), custom_call_target="tpu_custom_call" | custom-call | bytes 4000000 | tf_op jit(solution)/shard_map/step1_outer/pallas_call | solution.py:827
  61.7 2.1 %collective-permute-start.12 = (f32[16,512]{1,0:T(8,128)S(1)}, f32[16,512]{1,0:T(8,128)S(1)}, u32[]{:S(2)}, u32[]{:S(2)}) collective-permute-start(f32[16,512]{1,0:T(8,128)S(1)} %get-tuple-element.106), channel_id=1, source_target_pairs={{0,124},{4,8},{8,4},{12,16},{16,12},{20,24},{24,20},{28,32},{32,28... | collective-permute-start | bytes 98312 | tf_op jit(solution)/shard_map/ppermute | solution.py:857
  63.8 0.9 diagonal.1.scale
  64.7 3.7 %collective-permute-done.12.below = f32[16,512]{1,0:T(8,128)S(1)} collective-permute-done((f32[16,512]{1,0:T(8,128)S(1)}, f32[16,512]{1,0:T(8,128)S(1)}, u32[]{:S(2)}, u32[]{:S(2)}) %collective-permute-start.12) | collective-permute-done | bytes 32800 | tf_op jit(solution)/shard_map/ppermute | solution.py:857
  68.4 1.2 %coarse_outer.1 = (f32[256,512]{1,0:T(8,128)S(1)}, bf16[1,192,512]{2,1,0:T(8,128)(2,1)S(1)}, f32[128,512]{1,0:T(8,128)S(1)}, f32[128,512]{1,0:T(8,128)S(1)}) custom-call(s32[2]{0:T(128)S(1)} %pad_add_fusion.rot.refs_0_, f32[64,512]{1,0:T(8,128)S(1)} %get-tuple-element.105.local, f32[16,512]{1,0:T(8,128)S(1)} %collective-permute-done.12.below, ...), custom_call_target="tpu_custom_call" | custom-call | bytes 4000000 | tf_op jit(solution)/shard_map/coarse_outer/pallas_call | solution.py:827
  69.6 2.1 %collective-permute-start.14 = (f32[128,512]{1,0:T(8,128)S(1)}, f32[128,512]{1,0:T(8,128)S(1)}, u32[]{:S(2)}, u32[]{:S(2)}) collective-permute-start(f32[128,512]{1,0:T(8,128)S(1)} %get-tuple-element.110), channel_id=1, source_target_pairs={{0,124},{4,8},{8,4},{12,16},{16,12},{20,24},{24,20},{28,32},{32,28... | collective-permute-start | bytes 786440 | tf_op jit(solution)/shard_map/ppermute | solution.py:857
  71.8 0.9 coarse_inner.1
  72.6 2.1 %solve_inner.6 = (f32[384,512]{1,0:T(8,128)S(1)}, f32[1024,512]{1,0:T(8,128)S(1)}) custom-call(f32[256,512]{1,0:T(8,128)S(1)} %get-tuple-element.109.refs_0_.refs_1_, f32[256,512]{1,0:T(8,128)S(1)} %get-tuple-element.115.refs_1_, bf16[4,256,480]{2,1,0:T(8,128)(2,1)S(1)} %copy-done), custom_call_target="tpu_custom_call" | custom-call | bytes 4000000 | tf_op jit(solution)/shard_map/solve_inner/pallas_call | solution.py:827
  74.7 4.1 %collective-permute-done.14.refs_2_ = f32[128,512]{1,0:T(8,128)S(1)} collective-permute-done((f32[128,512]{1,0:T(8,128)S(1)}, f32[128,512]{1,0:T(8,128)S(1)}, u32[]{:S(2)}, u32[]{:S(2)}) %collective-permute-start.14) | collective-permute-done | bytes 262176 | tf_op jit(solution)/shard_map/ppermute | solution.py:857
  78.8 2.0 %solve_outer.6 = (f32[128,512]{1,0:T(8,128)S(1)}, bf16[4,512,512]{2,1,0:T(8,128)(2,1)S(1)}, f32[64,512]{1,0:T(8,128)S(1)}, f32[64,512]{1,0:T(8,128)S(1)}, f32[64,512]{1,0:T(8,128)S(1)}, /*index=5*/f32[64,512]{1,0:T(8,128)S(1)}) custom-call(s32[2]{0:T(128)S(1)} %pad_add_fusion.rot.refs_0_, f32[256,512]{1,0:T(8,128)S(1)} %get-tuple-element.109.refs_0_.refs_1_, ...), custom_call_target="tpu_custom_call" | custom-call | bytes 4000000 | tf_op jit(solution)/shard_map/solve_outer/pallas_call | solution.py:827
  80.9 2.1 %collective-permute-start.16 = (f32[64,512]{1,0:T(8,128)S(1)}, f32[64,512]{1,0:T(8,128)S(1)}, u32[]{:S(2)}, u32[]{:S(2)}) collective-permute-start(f32[64,512]{1,0:T(8,128)S(1)} %get-tuple-element.118), channel_id=1, source_target_pairs={{0,124},{4,8},{8,4},{12,16},{16,12},{20,24},{24,20},{28,32},{32,28... | collective-permute-start | bytes 393224 | tf_op jit(solution)/shard_map/ppermute | solution.py:857
  83.0 3.2 %step2_inner.1 = (f32[384,512]{1,0:T(8,128)S(1)}, f32[384,512]{1,0:T(8,128)S(1)}, f32[512,512]{1,0:T(8,128)S(1)}) custom-call(bf16[4,512,512]{2,1,0:T(8,128)(2,1)S(1)} %get-tuple-element.124.refs_0_, f32[384,512]{1,0:T(8,128)S(1)} %get-tuple-element.125.refs_1_, f32[24,640]{1,0:T(8,128)S(1)} %get-tuple-element.89.refs_1_.refs_8_.refs_3_.refs_10_.coef.refs_2_.refs_9_, ...), custom_call_target="tpu_custom_call" | custom-call | bytes 4000000 | tf_op jit(solution)/shard_map/step2_inner/pallas_call | solution.py:827
  86.2 2.5 %collective-permute-done.16.refs_2_ = f32[64,512]{1,0:T(8,128)S(1)} collective-permute-done((f32[64,512]{1,0:T(8,128)S(1)}, f32[64,512]{1,0:T(8,128)S(1)}, u32[]{:S(2)}, u32[]{:S(2)}) %collective-permute-start.16) | collective-permute-done | bytes 131104 | tf_op jit(solution)/shard_map/ppermute | solution.py:857
  88.7 1.3 %step2_outer.1 = (f32[128,512]{1,0:T(8,128)S(1)}, f32[128,512]{1,0:T(8,128)S(1)}, f32[512,512]{1,0:T(8,128)S(1)}, f32[128,512]{1,0:T(8,128)S(1)}, f32[128,512]{1,0:T(8,128)S(1)}) custom-call(s32[2]{0:T(128)S(1)} %pad_add_fusion.rot.refs_0_, f32[64,512]{1,0:T(8,128)S(1)} %get-tuple-element.117.refs_1_, f32[64,512]{1,0:T(8,128)S(1)} %collective-permute-done.16.refs_2_, ...), custom_call_target="tpu_custom_call" | custom-call | bytes 4000000 | tf_op jit(solution)/shard_map/step2_outer/pallas_call | solution.py:827
  90.0 2.1 %collective-permute-start.18 = (f32[128,512]{1,0:T(8,128)S(1)}, f32[128,512]{1,0:T(8,128)S(1)}, u32[]{:S(2)}, u32[]{:S(2)}) collective-permute-start(f32[128,512]{1,0:T(8,128)S(1)} %get-tuple-element.128), channel_id=1, source_target_pairs={{0,124},{4,8},{8,4},{12,16},{16,12},{20,24},{24,20},{28,32},{32,28... | collective-permute-start | bytes 786440 | tf_op jit(solution)/shard_map/ppermute | solution.py:857
  92.1 1.9 %solve_inner.7 = (f32[384,384]{1,0:T(8,128)S(1)}, f32[1024,384]{1,0:T(8,128)S(1)}) custom-call(f32[512,512]{1,0:T(8,128)S(1)} %get-tuple-element.127.refs_0_.refs_1_, bf16[4,256,480]{2,1,0:T(8,128)(2,1)S(1)} %copy-done), custom_call_target="tpu_custom_call" | custom-call | bytes 4000000 | tf_op jit(solution)/shard_map/solve_inner/pallas_call | solution.py:827
  94.1 5.1 %collective-permute-done.18.refs_2_ = f32[128,512]{1,0:T(8,128)S(1)} collective-permute-done((f32[128,512]{1,0:T(8,128)S(1)}, f32[128,512]{1,0:T(8,128)S(1)}, u32[]{:S(2)}, u32[]{:S(2)}) %collective-permute-start.18) | collective-permute-done | bytes 262176 | tf_op jit(solution)/shard_map/ppermute | solution.py:857
  99.2 1.7 %solve_outer.7 = (f32[128,384]{1,0:T(8,128)S(1)}, bf16[4,512,384]{2,1,0:T(8,128)(2,1)S(1)}, f32[64,384]{1,0:T(8,128)S(1)}, f32[64,384]{1,0:T(8,128)S(1)}, f32[64,384]{1,0:T(8,128)S(1)}, /*index=5*/f32[64,384]{1,0:T(8,128)S(1)}) custom-call(s32[2]{0:T(128)S(1)} %pad_add_fusion.rot.refs_0_, f32[512,512]{1,0:T(8,128)S(1)} %get-tuple-element.127.refs_0_.refs_1_, ...), custom_call_target="tpu_custom_call" | custom-call | bytes 4000000 | tf_op jit(solution)/shard_map/solve_outer/pallas_call | solution.py:827
  100.9 2.1 %collective-permute-start.20 = (f32[64,384]{1,0:T(8,128)S(1)}, f32[64,384]{1,0:T(8,128)S(1)}, u32[]{:S(2)}, u32[]{:S(2)}) collective-permute-start(f32[64,384]{1,0:T(8,128)S(1)} %get-tuple-element.132), channel_id=1, source_target_pairs={{0,124},{4,8},{8,4},{12,16},{16,12},{20,24},{24,20},{28,32},{32,28... | collective-permute-start | bytes 294920 | tf_op jit(solution)/shard_map/ppermute | solution.py:857
  103.0 2.7 %step3_inner.1 = (f32[384,384]{1,0:T(8,128)S(1)}, f32[512,384]{1,0:T(8,128)S(1)}) custom-call(bf16[4,512,384]{2,1,0:T(8,128)(2,1)S(1)} %get-tuple-element.139.refs_0_, f32[384,512]{1,0:T(8,128)S(1)} %get-tuple-element.140.refs_1_, f32[384,512]{1,0:T(8,128)S(1)} %get-tuple-element.141.refs_2_, ...), custom_call_target="tpu_custom_call" | custom-call | bytes 4000000 | tf_op jit(solution)/shard_map/step3_inner/pallas_call | solution.py:827
  105.7 2.6 %collective-permute-done.20.refs_2_ = f32[64,384]{1,0:T(8,128)S(1)} collective-permute-done((f32[64,384]{1,0:T(8,128)S(1)}, f32[64,384]{1,0:T(8,128)S(1)}, u32[]{:S(2)}, u32[]{:S(2)}) %collective-permute-start.20) | collective-permute-done | bytes 98336 | tf_op jit(solution)/shard_map/ppermute | solution.py:857
  108.3 1.2 step3_outer.1
  109.5 2.1 %collective-permute-start.22 = (f32[64,384]{1,0:T(8,128)S(1)}, f32[64,384]{1,0:T(8,128)S(1)}, u32[]{:S(2)}, u32[]{:S(2)}) collective-permute-start(f32[64,384]{1,0:T(8,128)S(1)} %get-tuple-element.147), channel_id=1, source_target_pairs={{0,124},{4,8},{8,4},{12,16},{16,12},{20,24},{24,20},{28,32},{32,28... | collective-permute-start | bytes 294920 | tf_op jit(solution)/shard_map/ppermute | solution.py:857
  111.6 2.0 %finish_inner.1 = (f32[512,256]{1,0:T(8,128)}, f32[384,256]{1,0:T(8,128)S(1)}) custom-call(s32[2]{0:T(128)S(1)} %pad_add_fusion.rot.refs_0_, f32[512,384]{1,0:T(8,128)S(1)} %get-tuple-element.143.local, f32[384,384]{1,0:T(8,128)S(1)} %get-tuple-element.144.total_inner, f32[128,384]{1,0:T(8,128)S(1)} %get-tuple-element.145.total_outer), custom_call_target="tpu_custom_call" | custom-call | bytes 4000000 | tf_op jit(solution)/shard_map/finish_inner/pallas_call | solution.py:827
  113.6 3.3 %collective-permute-done.22.below = f32[64,384]{1,0:T(8,128)S(1)} collective-permute-done((f32[64,384]{1,0:T(8,128)S(1)}, f32[64,384]{1,0:T(8,128)S(1)}, u32[]{:S(2)}, u32[]{:S(2)}) %collective-permute-start.22) | collective-permute-done | bytes 98336 | tf_op jit(solution)/shard_map/ppermute | solution.py:857
  116.9 1.7 %finish_outer.1 = f32[512,256]{1,0:T(8,128)} custom-call(s32[2]{0:T(128)S(1)} %pad_add_fusion.rot.refs_0_, f32[512,384]{1,0:T(8,128)S(1)} %get-tuple-element.143.local, f32[64,384]{1,0:T(8,128)S(1)} %collective-permute-done.22.below, f32[64,384]{1,0:T(8,128)S(1)} %collective-permute-done.23.above, f32[384,256]{1,0:T(8,128)S(1)} %get-tuple-element.149.inner), custom_call_target="tpu_custom_call" | custom-call | bytes 4000000 | tf_op jit(solution)/shard_map/finish_outer/pallas_call | solution.py:827
  (54 shorter events, 0.5 us)
Async XLA Ops:
  1.6 11.8 %collective-permute-start.1 = (f32[256,256]{1,0:T(8,128)S(1)}, f32[256,256]{1,0:T(8,128)S(1)}, u32[]{:S(2)}, u32[]{:S(2)}) collective-permute-start(f32[256,256]{1,0:T(8,128)S(1)} %pad_maximum_fusion.own), channel_id=1, source_target_pairs={{0,3},{1,0},{2,1},{3,2},{4,7},{5,4},{6,5},{7,6},{8,11},{9,8},{10,9... | collective-permute-start | bytes 786440 | tf_op jit(solution)/shard_map/ppermute | solution.py:851
  5.5 8.1 %collective-permute-start = (f32[256,256]{1,0:T(8,128)S(1)}, f32[256,256]{1,0:T(8,128)S(1)}, u32[]{:S(2)}, u32[]{:S(2)}) collective-permute-start(f32[256,256]{1,0:T(8,128)S(1)} %pad_maximum_fusion.own), channel_id=1, source_target_pairs={{0,1},{1,2},{2,3},{3,0},{4,5},{5,6},{6,7},{7,4},{8,9},{9,10},{10,1... | collective-permute-start | bytes 786440 | tf_op jit(solution)/shard_map/ppermute | solution.py:851
  10.4 1.0 copy-start.8
  11.4 0.9 copy-start.10
  13.6 7.0 %collective-permute-start.5 = (f32[256,256]{1,0:T(8,128)S(1)}, f32[256,256]{1,0:T(8,128)S(1)}, u32[]{:S(2)}, u32[]{:S(2)}) collective-permute-start(f32[256,256]{1,0:T(8,128)S(1)} %follow.1.own), channel_id=1, source_target_pairs={{0,3},{1,0},{2,1},{3,2},{4,7},{5,4},{6,5},{7,6},{8,11},{9,8},{10,9... | collective-permute-start | bytes 786440 | tf_op jit(solution)/shard_map/ppermute | solution.py:851
  16.2 7.5 %collective-permute-start.4 = (f32[256,256]{1,0:T(8,128)S(1)}, f32[256,256]{1,0:T(8,128)S(1)}, u32[]{:S(2)}, u32[]{:S(2)}) collective-permute-start(f32[256,256]{1,0:T(8,128)S(1)} %follow.1.own), channel_id=1, source_target_pairs={{0,1},{1,2},{2,3},{3,0},{4,5},{5,6},{6,7},{7,4},{8,9},{9,10},{10,1... | collective-permute-start | bytes 786440 | tf_op jit(solution)/shard_map/ppermute | solution.py:851
  17.4 10.1 %collective-permute-start.2 = (f32[136,640]{1,0:T(8,128)S(1)}, f32[136,640]{1,0:T(8,128)S(1)}, u32[]{:S(2)}, u32[]{:S(2)}) collective-permute-start(f32[136,640]{1,0:T(8,128)S(1)} %get-tuple-element.77), channel_id=1, source_target_pairs={{0,124},{4,8},{8,4},{12,16},{16,12},{20,24},{24,20},{28,32},{32,28... | collective-permute-start | bytes 1044488 | tf_op jit(solution)/shard_map/ppermute | solution.py:857
  18.7 6.1 %copy-start = (bf16[4,256,480]{2,1,0:T(8,128)(2,1)S(1)}, bf16[4,256,480]{2,1,0:T(8,128)(2,1)}, u32[]{:S(2)}) copy-start(bf16[4,256,480]{2,1,0:T(8,128)(2,1)} %constant.63.clone.refs_2_.refs_1_) | copy-start | bytes 2949124
  18.7 8.8 %collective-permute-start.3 = (f32[136,640]{1,0:T(8,128)S(1)}, f32[136,640]{1,0:T(8,128)S(1)}, u32[]{:S(2)}, u32[]{:S(2)}) collective-permute-start(f32[136,640]{1,0:T(8,128)S(1)} %get-tuple-element.78), channel_id=1, source_target_pairs={{0,4},{4,0},{8,12},{12,8},{16,20},{20,16},{24,28},{28,24},{32,36},... | collective-permute-start | bytes 1044488 | tf_op jit(solution)/shard_map/ppermute | solution.py:857
  24.8 2.7 %copy-start.2 = (bf16[4,256,240]{2,1,0:T(8,128)(2,1)S(1)}, bf16[4,256,240]{2,1,0:T(8,128)(2,1)}, u32[]{:S(2)}) copy-start(bf16[4,256,240]{2,1,0:T(8,128)(2,1)} %constant.64.clone.refs_6_) | copy-start | bytes 1474564
  24.8 2.7 %copy-start.7 = (bf16[4,32,512]{2,1,0:T(8,128)(2,1)S(1)}, bf16[4,32,512]{2,1,0:T(8,128)(2,1)}, u32[]{:S(2)}) copy-start(bf16[4,32,512]{2,1,0:T(8,128)(2,1)} %constant.65.clone.refs_7_) | copy-start | bytes 393220
  24.9 2.7 %copy-start.9 = (bf16[4,32,256]{2,1,0:T(8,128)(2,1)S(1)}, bf16[4,32,256]{2,1,0:T(8,128)(2,1)}, u32[]{:S(2)}) copy-start(bf16[4,32,256]{2,1,0:T(8,128)(2,1)} %constant.66.clone.refs_8_) | copy-start | bytes 196612
  27.5 5.0 %copy-start.1 = (bf16[4,320,288]{2,1,0:T(8,128)(2,1)S(1)}, bf16[4,320,288]{2,1,0:T(8,128)(2,1)}, u32[]{:S(2)}) copy-start(bf16[4,320,288]{2,1,0:T(8,128)(2,1)} %constant.69.clone.refs_2_.refs_4_.refs_3_) | copy-start | bytes 2211844
  27.5 5.0 %copy-start.3 = (bf16[4,96,512]{2,1,0:T(8,128)(2,1)S(1)}, bf16[4,96,512]{2,1,0:T(8,128)(2,1)}, u32[]{:S(2)}) copy-start(bf16[4,96,512]{2,1,0:T(8,128)(2,1)} %constant.67.clone.refs_3_.refs_5_.refs_4_) | copy-start | bytes 1179652
  27.5 4.9 %copy-start.5 = (bf16[4,96,256]{2,1,0:T(8,128)(2,1)S(1)}, bf16[4,96,256]{2,1,0:T(8,128)(2,1)}, u32[]{:S(2)}) copy-start(bf16[4,96,256]{2,1,0:T(8,128)(2,1)} %constant.68.clone.refs_4_.refs_6_.refs_5_) | copy-start | bytes 589828
  30.0 8.1 %collective-permute-start.6 = (f32[64,640]{1,0:T(8,128)S(1)}, f32[64,640]{1,0:T(8,128)S(1)}, u32[]{:S(2)}, u32[]{:S(2)}) collective-permute-start(f32[64,640]{1,0:T(8,128)S(1)} %get-tuple-element.83), channel_id=1, source_target_pairs={{0,124},{4,8},{8,4},{12,16},{16,12},{20,24},{24,20},{28,32},{32,28... | collective-permute-start | bytes 491528 | tf_op jit(solution)/shard_map/ppermute | solution.py:857
  32.1 6.0 %collective-permute-start.7 = (f32[64,640]{1,0:T(8,128)S(1)}, f32[64,640]{1,0:T(8,128)S(1)}, u32[]{:S(2)}, u32[]{:S(2)}) collective-permute-start(f32[64,640]{1,0:T(8,128)S(1)} %get-tuple-element.85), channel_id=1, source_target_pairs={{0,4},{4,0},{8,12},{12,8},{16,20},{20,16},{24,28},{28,24},{32,36},... | collective-permute-start | bytes 491528 | tf_op jit(solution)/shard_map/ppermute | solution.py:857
  32.5 5.7 %copy-start.6 = (bf16[4,192,96]{2,1,0:T(8,128)(2,1)S(1)}, bf16[4,192,96]{2,1,0:T(8,128)(2,1)}, u32[]{:S(2)}) copy-start(bf16[4,192,96]{2,1,0:T(8,128)(2,1)} %constant.70.clone.refs_9_.refs_11_.refs_10_) | copy-start | bytes 442372
  39.6 9.9 %collective-permute-start.8 = (f32[128,640]{1,0:T(8,128)S(1)}, f32[128,640]{1,0:T(8,128)S(1)}, u32[]{:S(2)}, u32[]{:S(2)}) collective-permute-start(f32[128,640]{1,0:T(8,128)S(1)} %get-tuple-element.92), channel_id=1, source_target_pairs={{0,124},{4,8},{8,4},{12,16},{16,12},{20,24},{24,20},{28,32},{32,28... | collective-permute-start | bytes 983048 | tf_op jit(solution)/shard_map/ppermute | solution.py:857
  41.7 7.8 %collective-permute-start.9 = (f32[128,640]{1,0:T(8,128)S(1)}, f32[128,640]{1,0:T(8,128)S(1)}, u32[]{:S(2)}, u32[]{:S(2)}) collective-permute-start(f32[128,640]{1,0:T(8,128)S(1)} %get-tuple-element.93), channel_id=1, source_target_pairs={{0,4},{4,0},{8,12},{12,8},{16,20},{20,16},{24,28},{28,24},{32,36},... | collective-permute-start | bytes 983048 | tf_op jit(solution)/shard_map/ppermute | solution.py:857
  51.8 8.1 %collective-permute-start.10 = (f32[64,640]{1,0:T(8,128)S(1)}, f32[64,640]{1,0:T(8,128)S(1)}, u32[]{:S(2)}, u32[]{:S(2)}) collective-permute-start(f32[64,640]{1,0:T(8,128)S(1)} %get-tuple-element.96), channel_id=1, source_target_pairs={{0,124},{4,8},{8,4},{12,16},{16,12},{20,24},{24,20},{28,32},{32,28... | collective-permute-start | bytes 491528 | tf_op jit(solution)/shard_map/ppermute | solution.py:857
  53.9 6.0 %collective-permute-start.11 = (f32[64,640]{1,0:T(8,128)S(1)}, f32[64,640]{1,0:T(8,128)S(1)}, u32[]{:S(2)}, u32[]{:S(2)}) collective-permute-start(f32[64,640]{1,0:T(8,128)S(1)} %get-tuple-element.98), channel_id=1, source_target_pairs={{0,4},{4,0},{8,12},{12,8},{16,20},{20,16},{24,28},{28,24},{32,36},... | collective-permute-start | bytes 491528 | tf_op jit(solution)/shard_map/ppermute | solution.py:857
  53.9 6.0 %copy-start.11 = (bf16[64,1024]{1,0:T(8,128)(2,1)S(1)}, bf16[64,1024]{1,0:T(8,128)(2,1)}, u32[]{:S(2)}) copy-start(bf16[64,1024]{1,0:T(8,128)(2,1)} %constant.71.clone.refs_12_) | copy-start | bytes 393220
  53.9 6.0 %copy-start.12 = (bf16[64,512]{1,0:T(8,128)(2,1)S(1)}, bf16[64,512]{1,0:T(8,128)(2,1)}, u32[]{:S(2)}) copy-start(bf16[64,512]{1,0:T(8,128)(2,1)} %constant.72.clone.refs_13_) | copy-start | bytes 196612
  57.3 6.5 %copy-start.13 = (f32[64,8]{1,0:T(8,128)S(1)}, f32[64,8]{1,0:T(8,128)}, u32[]{:S(2)}) copy-start(f32[64,8]{1,0:T(8,128)} %constant.75.clone.table) | copy-start | bytes 6148
  59.9 8.5 %copy-start.4 = (bf16[2048,192]{1,0:T(8,128)(2,1)S(1)}, bf16[2048,192]{1,0:T(8,128)(2,1)}, u32[]{:S(2)}) copy-start(bf16[2048,192]{1,0:T(8,128)(2,1)} %constant.73.clone.prolong) | copy-start | bytes 2359300
  61.7 6.7 %collective-permute-start.12 = (f32[16,512]{1,0:T(8,128)S(1)}, f32[16,512]{1,0:T(8,128)S(1)}, u32[]{:S(2)}, u32[]{:S(2)}) collective-permute-start(f32[16,512]{1,0:T(8,128)S(1)} %get-tuple-element.106), channel_id=1, source_target_pairs={{0,124},{4,8},{8,4},{12,16},{16,12},{20,24},{24,20},{28,32},{32,28... | collective-permute-start | bytes 98312 | tf_op jit(solution)/shard_map/ppermute | solution.py:857
  63.8 4.6 %collective-permute-start.13 = (f32[16,512]{1,0:T(8,128)S(1)}, f32[16,512]{1,0:T(8,128)S(1)}, u32[]{:S(2)}, u32[]{:S(2)}) collective-permute-start(f32[16,512]{1,0:T(8,128)S(1)} %get-tuple-element.107), channel_id=1, source_target_pairs={{0,4},{4,0},{8,12},{12,8},{16,20},{20,16},{24,28},{28,24},{32,36},... | collective-permute-start | bytes 98312 | tf_op jit(solution)/shard_map/ppermute | solution.py:857
  69.6 9.2 %collective-permute-start.14 = (f32[128,512]{1,0:T(8,128)S(1)}, f32[128,512]{1,0:T(8,128)S(1)}, u32[]{:S(2)}, u32[]{:S(2)}) collective-permute-start(f32[128,512]{1,0:T(8,128)S(1)} %get-tuple-element.110), channel_id=1, source_target_pairs={{0,124},{4,8},{8,4},{12,16},{16,12},{20,24},{24,20},{28,32},{32,28... | collective-permute-start | bytes 786440 | tf_op jit(solution)/shard_map/ppermute | solution.py:857
  71.8 7.1 %collective-permute-start.15 = (f32[128,512]{1,0:T(8,128)S(1)}, f32[128,512]{1,0:T(8,128)S(1)}, u32[]{:S(2)}, u32[]{:S(2)}) collective-permute-start(f32[128,512]{1,0:T(8,128)S(1)} %get-tuple-element.111), channel_id=1, source_target_pairs={{0,4},{4,0},{8,12},{12,8},{16,20},{20,16},{24,28},{28,24},{32,36},... | collective-permute-start | bytes 786440 | tf_op jit(solution)/shard_map/ppermute | solution.py:857
  80.9 7.8 %collective-permute-start.16 = (f32[64,512]{1,0:T(8,128)S(1)}, f32[64,512]{1,0:T(8,128)S(1)}, u32[]{:S(2)}, u32[]{:S(2)}) collective-permute-start(f32[64,512]{1,0:T(8,128)S(1)} %get-tuple-element.118), channel_id=1, source_target_pairs={{0,124},{4,8},{8,4},{12,16},{16,12},{20,24},{24,20},{28,32},{32,28... | collective-permute-start | bytes 393224 | tf_op jit(solution)/shard_map/ppermute | solution.py:857
  83.0 5.7 %collective-permute-start.17 = (f32[64,512]{1,0:T(8,128)S(1)}, f32[64,512]{1,0:T(8,128)S(1)}, u32[]{:S(2)}, u32[]{:S(2)}) collective-permute-start(f32[64,512]{1,0:T(8,128)S(1)} %get-tuple-element.120), channel_id=1, source_target_pairs={{0,4},{4,0},{8,12},{12,8},{16,20},{20,16},{24,28},{28,24},{32,36},... | collective-permute-start | bytes 393224 | tf_op jit(solution)/shard_map/ppermute | solution.py:857
  90.0 9.2 %collective-permute-start.18 = (f32[128,512]{1,0:T(8,128)S(1)}, f32[128,512]{1,0:T(8,128)S(1)}, u32[]{:S(2)}, u32[]{:S(2)}) collective-permute-start(f32[128,512]{1,0:T(8,128)S(1)} %get-tuple-element.128), channel_id=1, source_target_pairs={{0,124},{4,8},{8,4},{12,16},{16,12},{20,24},{24,20},{28,32},{32,28... | collective-permute-start | bytes 786440 | tf_op jit(solution)/shard_map/ppermute | solution.py:857
  92.1 7.1 %collective-permute-start.19 = (f32[128,512]{1,0:T(8,128)S(1)}, f32[128,512]{1,0:T(8,128)S(1)}, u32[]{:S(2)}, u32[]{:S(2)}) collective-permute-start(f32[128,512]{1,0:T(8,128)S(1)} %get-tuple-element.129), channel_id=1, source_target_pairs={{0,4},{4,0},{8,12},{12,8},{16,20},{20,16},{24,28},{28,24},{32,36},... | collective-permute-start | bytes 786440 | tf_op jit(solution)/shard_map/ppermute | solution.py:857
  100.9 7.4 %collective-permute-start.20 = (f32[64,384]{1,0:T(8,128)S(1)}, f32[64,384]{1,0:T(8,128)S(1)}, u32[]{:S(2)}, u32[]{:S(2)}) collective-permute-start(f32[64,384]{1,0:T(8,128)S(1)} %get-tuple-element.132), channel_id=1, source_target_pairs={{0,124},{4,8},{8,4},{12,16},{16,12},{20,24},{24,20},{28,32},{32,28... | collective-permute-start | bytes 294920 | tf_op jit(solution)/shard_map/ppermute | solution.py:857
  103.0 5.3 %collective-permute-start.21 = (f32[64,384]{1,0:T(8,128)S(1)}, f32[64,384]{1,0:T(8,128)S(1)}, u32[]{:S(2)}, u32[]{:S(2)}) collective-permute-start(f32[64,384]{1,0:T(8,128)S(1)} %get-tuple-element.134), channel_id=1, source_target_pairs={{0,4},{4,0},{8,12},{12,8},{16,20},{20,16},{24,28},{28,24},{32,36},... | collective-permute-start | bytes 294920 | tf_op jit(solution)/shard_map/ppermute | solution.py:857
  109.5 7.4 %collective-permute-start.22 = (f32[64,384]{1,0:T(8,128)S(1)}, f32[64,384]{1,0:T(8,128)S(1)}, u32[]{:S(2)}, u32[]{:S(2)}) collective-permute-start(f32[64,384]{1,0:T(8,128)S(1)} %get-tuple-element.147), channel_id=1, source_target_pairs={{0,124},{4,8},{8,4},{12,16},{16,12},{20,24},{24,20},{28,32},{32,28... | collective-permute-start | bytes 294920 | tf_op jit(solution)/shard_map/ppermute | solution.py:857
  111.6 5.3 %collective-permute-start.23 = (f32[64,384]{1,0:T(8,128)S(1)}, f32[64,384]{1,0:T(8,128)S(1)}, u32[]{:S(2)}, u32[]{:S(2)}) collective-permute-start(f32[64,384]{1,0:T(8,128)S(1)} %get-tuple-element.148), channel_id=1, source_target_pairs={{0,4},{4,0},{8,12},{12,8},{16,20},{20,16},{24,28},{28,24},{32,36},... | collective-permute-start | bytes 294920 | tf_op jit(solution)/shard_map/ppermute | solution.py:857
